TPU v7x, 32 devices: a whole 2x2x4 slice. The times are simulated.
32 devices in a mesh: path: 2 (over core), frames: 16 (over z, y, x).
Axes of the slice: x: 2, y: 2, z: 4, core: 2. Of those that a mesh axis runs over, the one named last changes fastest.
Arguments:
- slow_input: bfloat16 [512, 14, 14, 1024], P(('path', 'frames'))
- fast_input: bfloat16 [2048, 14, 14, 128], P(('path', 'frames'))
- clip_offset: int32 [512], P(('path', 'frames')), may hold values from 0 to 256, as said below
- fill: int32 [512], P(('path', 'frames')), may hold values from 0 to 1, as said below
- w_fast_in: bfloat16 [128, 32], replicated, may hold values from -0.5 to 0.5
- w_fast_mid: bfloat16 [3, 32, 32], replicated, may hold values from -0.625 to 0.625
- w_fast_out: bfloat16 [32, 128], replicated, may hold values from -1 to 1
- w_lateral: bfloat16 [5, 128, 256], replicated, may hold values from -0.25 to 0.25
- w_slow_in: bfloat16 [1280, 256], replicated, may hold values from -0.15625 to 0.15625
- w_slow_mid: bfloat16 [3, 3, 256, 256], replicated, may hold values from -0.125 to 0.125
- w_slow_out: bfloat16 [256, 1024], replicated, may hold values from -0.375 to 0.375
- w_shortcut: bfloat16 [1280, 1024], replicated, may hold values from -0.15625 to 0.15625
- gains: float32 [3008], replicated, may hold values from 0.25 to 1.75
- biases: float32 [3008], replicated, may hold values from -3 to 3
- slow_cot: bfloat16 [512, 14, 14, 1024], P(('path', 'frames')), may hold values from -6 to 6
- fast_cot: bfloat16 [2048, 14, 14, 128], P(('path', 'frames')), may hold values from -6 to 6
Outputs:
- slow_output: bfloat16 [512, 14, 14, 1024], P(('path', 'frames'))
- fast_output: bfloat16 [2048, 14, 14, 128], P(('path', 'frames'))
- slow_input_grad: bfloat16 [512, 14, 14, 1024], P(('path', 'frames'))
- fast_input_grad: bfloat16 [2048, 14, 14, 128], P(('path', 'frames'))
- w_fast_in_grad: float32 [128, 32], replicated
- w_fast_mid_grad: float32 [3, 32, 32], replicated
- w_fast_out_grad: float32 [32, 128], replicated
- w_lateral_grad: float32 [5, 128, 256], replicated
- w_slow_in_grad: float32 [1280, 256], replicated
- w_slow_mid_grad: float32 [3, 3, 256, 256], replicated
- w_slow_out_grad: float32 [256, 1024], replicated
- w_shortcut_grad: float32 [1280, 1024], replicated
- gains_grad: float32 [3008], replicated
- biases_grad: float32 [3008], replicated
Inputs may be any that keep to these rules, and one draw needn't show every extreme that they name: clip_offset[t] is t minus the first slow frame of t's clip; it is 0 exactly where a clip begins, always at t = 0 and never at a t > 0 with t % 16 == 0; the first clip holds the slow frames 0 to 256 and the next begins right after it. fill[0] = 1.
All inputs are finite; a program needn't handle non-finite values.
Results may differ from a plain program's by a relative error of at most 0.0075.
The roundings to bfloat16 on the way count: a program that leaves them out, or rounds other values in their place, can miss the bound.
Values may be sent and summed in bfloat16 or wider, within the bound.
A program may use at most 320 MiB of HBM per device.

v0:
```python
import jax
import jax.numpy as jnp
from jax import lax
from jax.sharding import PartitionSpec as P

norm_eps = 1e-05


def with_halo(array, sides, width):
    for axis, dim in sides:
        peers, length = (lax.axis_size(axis), array.shape[dim])
        up = [(i, (i + 1) % peers) for i in range(peers - 1)]
        down = [(j, i) for i, j in up]
        last = lax.slice_in_dim(array, length - width, length, axis=dim)
        leading = lax.slice_in_dim(array, 0, width, axis=dim)
        before = lax.ppermute(last, axis, up)
        after = lax.ppermute(leading, axis, down)
        array = jnp.concatenate([before, array, after], axis=dim)
    return array


def from_behind(array, axis, by):
    peers = lax.axis_size(axis)
    pairs = [(i, i + by) for i in range(peers) if 0 <= i + by < peers]
    return lax.ppermute(array, axis, pairs)


def silu_slope(inputs):
    logistic = jax.nn.sigmoid(inputs)
    return logistic * (1.0 + inputs * (1.0 - logistic))


def norm_forward(inputs, weight):
    local_count = jnp.sum(weight) * inputs.shape[1]
    row_total, total_count = lax.psum(
        (jnp.sum(inputs * weight, axis=(0, 1)), local_count), ("path", "frames")
    )
    average = row_total / total_count
    centered = inputs - average
    spread = lax.psum(jnp.sum(centered * centered * weight, axis=(0, 1)), ("path", "frames"))
    inv_scale = lax.rsqrt(spread / total_count + norm_eps)
    return (centered * inv_scale, inv_scale, total_count)


def norm_backward(grad_in, unit, inv_scale, total_count, gain_part, weight):
    grad_total, grad_dot = lax.psum(
        (jnp.sum(grad_in, axis=(0, 1)), jnp.sum(grad_in * unit, axis=(0, 1))), ("path", "frames")
    )
    change = (
        gain_part * inv_scale * (grad_in - weight * (grad_total + unit * grad_dot) / total_count)
    )
    return (change, grad_dot, grad_total)


def project(inputs, matrix):
    return jnp.einsum("fpc,cd->fpd", inputs, matrix, preferred_element_type=jnp.float32)


def project_back(grad_low, matrix):
    return jnp.einsum("fpd,cd->fpc", grad_low, matrix, preferred_element_type=jnp.float32)


def weight_grad(inputs, grad_low):
    return jnp.einsum("fpc,fpd->cd", inputs, grad_low, preferred_element_type=jnp.float32)


def per_device(
    slow_input,
    fast_input,
    clip_offset,
    fill,
    w_fast_in,
    w_fast_mid,
    w_fast_out,
    w_lateral,
    w_slow_in,
    w_slow_mid,
    w_slow_out,
    w_shortcut,
    gains,
    biases,
    slow_cot,
    fast_cot,
):
    frames = slow_input.shape[0]
    grid_side = slow_input.shape[1]
    pixels = grid_side * grid_side
    c_slow = slow_input.shape[3]
    fast_frames = fast_input.shape[0]
    c_fast = fast_input.shape[3]
    in_fast = w_fast_in.shape[1]
    in_slow = w_slow_in.shape[1]
    c_lat = w_lateral.shape[2]
    widths = [in_fast, in_fast, c_fast, c_lat, in_slow, in_slow, c_slow, c_slow]
    bounds = [0]
    for seg_width in widths:
        bounds.append(bounds[-1] + seg_width)
    gain_parts = [gains[bounds[segment] : bounds[segment + 1]] for segment in range(8)]
    bias_parts = [biases[bounds[segment] : bounds[segment + 1]] for segment in range(8)]
    fill_value = fill.astype(jnp.float32)
    slow_weight = fill_value[:, None, None]
    fast_weight = jnp.repeat(fill_value, 4)[:, None, None]
    within = (clip_offset >= 1).astype(jnp.float32)
    within_low = within.astype(jnp.bfloat16)[:, None, None, None]
    quarter = jnp.arange(4)
    prev_link = jnp.where(quarter[None, :] > 0, 1.0, within[:, None]).reshape(fast_frames)
    next_link = jnp.concatenate([prev_link[1:], jnp.ones((1,), jnp.float32)])
    prev_low = prev_link.astype(jnp.bfloat16)[:, None, None]
    next_low = next_link.astype(jnp.bfloat16)[:, None, None]
    fast_rows = fast_input.reshape(fast_frames, pixels, c_fast)
    fa_conv = project(fast_rows, w_fast_in)
    fa_unit, fa_scale, fast_count = norm_forward(fa_conv, fast_weight)
    fa_pre = fa_unit * gain_parts[0] + bias_parts[0]
    fa_act = jax.nn.silu(fa_pre).astype(jnp.bfloat16)
    fa_wide = with_halo(fa_act, ((("path", "frames"), 0),), 1)
    fb_taps = jnp.concatenate([fa_wide[:-2] * prev_low, fa_act, fa_wide[2:] * next_low], axis=2)
    mid_flat = w_fast_mid.reshape(3 * in_fast, in_fast)
    fb_conv = project(fb_taps, mid_flat)
    fb_unit, fb_scale, fast_count = norm_forward(fb_conv, fast_weight)
    fb_pre = fb_unit * gain_parts[1] + bias_parts[1]
    fb_act = jax.nn.silu(fb_pre).astype(jnp.bfloat16)
    fc_conv = project(fb_act, w_fast_out)
    fc_unit, fc_scale, fast_count = norm_forward(fc_conv, fast_weight)
    fast_pre = fc_unit * gain_parts[2] + bias_parts[2] + fast_rows.astype(jnp.float32)
    fast_output = (
        (jax.nn.silu(fast_pre) * fast_weight).astype(jnp.bfloat16).reshape(fast_input.shape)
    )
    groups = fast_rows.reshape(frames, 4, pixels, c_fast)
    tail_frames = from_behind(groups[frames - 1, 2:4], ("path", "frames"), 1)
    earlier = jnp.concatenate([tail_frames[None], groups[:-1, 2:4]], axis=0) * within_low
    lat_taps = jnp.concatenate([earlier, groups[:, 0:3]], axis=1)
    lat_conv = jnp.einsum("tkpc,kcd->tpd", lat_taps, w_lateral, preferred_element_type=jnp.float32)
    lat_unit, lat_scale, slow_count = norm_forward(lat_conv, slow_weight)
    lat_pre = lat_unit * gain_parts[3] + bias_parts[3]
    lat_act = jax.nn.silu(lat_pre).astype(jnp.bfloat16)
    joined = jnp.concatenate([slow_input.reshape(frames, pixels, c_slow), lat_act], axis=2)
    sa_conv = project(joined, w_slow_in)
    sa_unit, sa_scale, slow_count = norm_forward(sa_conv, slow_weight)
    sa_pre = sa_unit * gain_parts[4] + bias_parts[4]
    sa_act = jax.nn.silu(sa_pre).astype(jnp.bfloat16)
    padded_grid = jnp.pad(
        sa_act.reshape(frames, grid_side, grid_side, in_slow), ((0, 0), (1, 1), (1, 1), (0, 0))
    )
    patches = jnp.concatenate(
        [
            padded_grid[:, row_step : row_step + grid_side, col_step : col_step + grid_side]
            for row_step in range(3)
            for col_step in range(3)
        ],
        axis=3,
    ).reshape(frames, pixels, 9 * in_slow)
    spatial_flat = w_slow_mid.reshape(9 * in_slow, in_slow)
    sb_conv = project(patches, spatial_flat)
    sb_unit, sb_scale, slow_count = norm_forward(sb_conv, slow_weight)
    sb_pre = sb_unit * gain_parts[5] + bias_parts[5]
    sb_act = jax.nn.silu(sb_pre).astype(jnp.bfloat16)
    sc_conv = project(sb_act, w_slow_out)
    sp_conv = project(joined, w_shortcut)
    sc_unit, sc_scale, slow_count = norm_forward(sc_conv, slow_weight)
    sp_unit, sp_scale, slow_count = norm_forward(sp_conv, slow_weight)
    slow_pre = sc_unit * gain_parts[6] + bias_parts[6] + sp_unit * gain_parts[7] + bias_parts[7]
    slow_output = (
        (jax.nn.silu(slow_pre) * slow_weight).astype(jnp.bfloat16).reshape(slow_input.shape)
    )
    slow_grad = (
        slow_cot.reshape(frames, pixels, c_slow).astype(jnp.float32)
        * slow_weight
        * silu_slope(slow_pre)
    )
    sc_change, sc_gain, sc_bias = norm_backward(
        slow_grad, sc_unit, sc_scale, slow_count, gain_parts[6], slow_weight
    )
    sp_change, sp_gain, sp_bias = norm_backward(
        slow_grad, sp_unit, sp_scale, slow_count, gain_parts[7], slow_weight
    )
    sc_low = sc_change.astype(jnp.bfloat16)
    sp_low = sp_change.astype(jnp.bfloat16)
    grad_slow_out = weight_grad(sb_act, sc_low)
    grad_shortcut = weight_grad(joined, sp_low)
    sb_back = project_back(sc_low, w_slow_out) * silu_slope(sb_pre)
    sb_change, sb_gain, sb_bias = norm_backward(
        sb_back, sb_unit, sb_scale, slow_count, gain_parts[5], slow_weight
    )
    sb_low = sb_change.astype(jnp.bfloat16)
    grad_slow_mid = weight_grad(patches, sb_low).reshape(w_slow_mid.shape)
    patch_back = project_back(sb_low, spatial_flat).reshape(
        frames, grid_side, grid_side, 9, in_slow
    )
    grid_back = jnp.zeros((frames, grid_side + 2, grid_side + 2, in_slow), jnp.float32)
    for row_step in range(3):
        for col_step in range(3):
            grid_back = grid_back.at[
                :, row_step : row_step + grid_side, col_step : col_step + grid_side
            ].add(patch_back[:, :, :, 3 * row_step + col_step])
    sa_back = grid_back[:, 1 : grid_side + 1, 1 : grid_side + 1].reshape(
        frames, pixels, in_slow
    ) * silu_slope(sa_pre)
    sa_change, sa_gain, sa_bias = norm_backward(
        sa_back, sa_unit, sa_scale, slow_count, gain_parts[4], slow_weight
    )
    sa_low = sa_change.astype(jnp.bfloat16)
    grad_slow_in = weight_grad(joined, sa_low)
    joined_back = project_back(sa_low, w_slow_in) + project_back(sp_low, w_shortcut)
    slow_input_grad = joined_back[:, :, :c_slow].astype(jnp.bfloat16).reshape(slow_input.shape)
    lat_back = joined_back[:, :, c_slow:] * silu_slope(lat_pre)
    lat_change, lat_gain, lat_bias = norm_backward(
        lat_back, lat_unit, lat_scale, slow_count, gain_parts[3], slow_weight
    )
    lat_low = lat_change.astype(jnp.bfloat16)
    grad_lateral = jnp.einsum(
        "tkpc,tpd->kcd", lat_taps, lat_low, preferred_element_type=jnp.float32
    )
    lead_row = from_behind(lat_low[0:1] * within_low[0:1, 0], ("path", "frames"), -1)
    following = jnp.concatenate([lat_low[1:] * within_low[1:, 0], lead_row], axis=0)
    own_part = jnp.einsum(
        "tpd,kcd->tkpc", lat_low, w_lateral[2:5], preferred_element_type=jnp.float32
    )
    late_part = jnp.einsum(
        "tpd,kcd->tkpc", following, w_lateral[0:2], preferred_element_type=jnp.float32
    )
    group_back = jnp.concatenate(
        [own_part[:, 0:2], own_part[:, 2:3] + late_part[:, 0:1], late_part[:, 1:2]], axis=1
    ).reshape(fast_frames, pixels, c_fast)
    fast_grad = (
        fast_cot.reshape(fast_frames, pixels, c_fast).astype(jnp.float32)
        * fast_weight
        * silu_slope(fast_pre)
    )
    fc_change, fc_gain, fc_bias = norm_backward(
        fast_grad, fc_unit, fc_scale, fast_count, gain_parts[2], fast_weight
    )
    fc_low = fc_change.astype(jnp.bfloat16)
    grad_fast_out = weight_grad(fb_act, fc_low)
    fb_back = project_back(fc_low, w_fast_out) * silu_slope(fb_pre)
    fb_change, fb_gain, fb_bias = norm_backward(
        fb_back, fb_unit, fb_scale, fast_count, gain_parts[1], fast_weight
    )
    fb_low = fb_change.astype(jnp.bfloat16)
    grad_fast_mid = weight_grad(fb_taps, fb_low).reshape(w_fast_mid.shape)
    fb_wide = with_halo(fb_low, ((("path", "frames"), 0),), 1)
    back_taps = jnp.concatenate([fb_wide[2:] * next_low, fb_low, fb_wide[:-2] * prev_low], axis=2)
    mid_back = jnp.transpose(w_fast_mid, (0, 2, 1)).reshape(3 * in_fast, in_fast)
    fa_back = project(back_taps, mid_back) * silu_slope(fa_pre)
    fa_change, fa_gain, fa_bias = norm_backward(
        fa_back, fa_unit, fa_scale, fast_count, gain_parts[0], fast_weight
    )
    fa_low = fa_change.astype(jnp.bfloat16)
    grad_fast_in = weight_grad(fast_rows, fa_low)
    fast_back = fast_grad + project_back(fa_low, w_fast_in) + group_back
    fast_input_grad = fast_back.astype(jnp.bfloat16).reshape(fast_input.shape)
    (
        grad_fast_in,
        grad_fast_mid,
        grad_fast_out,
        grad_lateral,
        grad_slow_in,
        grad_slow_mid,
        grad_slow_out,
        grad_shortcut,
    ) = lax.psum(
        (
            grad_fast_in,
            grad_fast_mid,
            grad_fast_out,
            grad_lateral,
            grad_slow_in,
            grad_slow_mid,
            grad_slow_out,
            grad_shortcut,
        ),
        ("path", "frames"),
    )
    gains_grad = jnp.concatenate(
        [fa_gain, fb_gain, fc_gain, lat_gain, sa_gain, sb_gain, sc_gain, sp_gain]
    )
    biases_grad = jnp.concatenate(
        [fa_bias, fb_bias, fc_bias, lat_bias, sa_bias, sb_bias, sc_bias, sp_bias]
    )
    return (
        slow_output,
        fast_output,
        slow_input_grad,
        fast_input_grad,
        grad_fast_in,
        grad_fast_mid,
        grad_fast_out,
        grad_lateral,
        grad_slow_in,
        grad_slow_mid,
        grad_slow_out,
        grad_shortcut,
        gains_grad,
        biases_grad,
    )


def solution(mesh):
    in_specs = (
        P(("path", "frames"), None, None, None),
        P(("path", "frames"), None, None, None),
        P(("path", "frames")),
        P(("path", "frames")),
        P(),
        P(),
        P(),
        P(),
        P(),
        P(),
        P(),
        P(),
        P(),
        P(),
        P(("path", "frames"), None, None, None),
        P(("path", "frames"), None, None, None),
    )
    out_specs = (
        P(("path", "frames"), None, None, None),
        P(("path", "frames"), None, None, None),
        P(("path", "frames"), None, None, None),
        P(("path", "frames"), None, None, None),
        P(),
        P(),
        P(),
        P(),
        P(),
        P(),
        P(),
        P(),
        P(),
        P(),
    )
    return jax.shard_map(
        per_device, mesh=mesh, in_specs=in_specs, out_specs=out_specs, check_vma=False
    )
```

profile of v0, /device:TPU:0, one launch (start us, length us, event | category | flops | bytes accessed | tf_op | source)
XLA Modules:
  0.0 1170.9 jit_solution(17869527145298170295)
XLA Ops:
  8.5 4.8 collective-permute-start
  18.6 4.6 slice.561
  30.0 5.5 copy.105
  35.4 3.7 bitcast_convert_fusion.1
  39.2 6.4 copy.56
  45.6 6.8 bitcast_convert_fusion
  52.4 5.2 multiply_reduce_fusion.22
  57.9 3.2 fusion.5
  61.2 40.4 %all-reduce.12 = (f32[256]{0:T(256)S(1)}, f32[]{:T(128)}) all-reduce(f32[256]{0:T(256)S(1)} %get-tuple-element.269, f32[]{:T(128)S(6)} %mul.664), channel_id=1, replica_groups=mesh['path'=2,'frames'=16] {'path','frames'}, use_global_device_ids=true, to_apply=%region_1.2 | all-reduce | flops 257 | bytes 2056 | tf_op jit(solution)/shard_map/psum | solution.py:35
  104.8 40.3 %psum.310 = f32[256]{0:T(256)S(1)} all-reduce(f32[256]{0:T(256)S(1)} %multiply_reduce_fusion.16), channel_id=1, replica_groups=mesh['path'=2,'frames'=16] {'path','frames'}, use_global_device_ids=true, to_apply=%region_5.6 | all-reduce | flops 256 | bytes 2048 | tf_op jit(solution)/shard_map/psum | solution.py:40
  146.3 2.9 multiply_convert_fusion.10
  149.3 7.5 multiply_reduce_fusion.15
  156.8 39.9 %psum.311 = f32[256]{0:T(256)S(1)} all-reduce(f32[256]{0:T(256)S(1)} %get-tuple-element.271), channel_id=1, replica_groups=mesh['path'=2,'frames'=16] {'path','frames'}, use_global_device_ids=true, to_apply=%region_7.8 | all-reduce | flops 256 | bytes 2048 | tf_op jit(solution)/shard_map/psum | solution.py:35
  199.9 40.1 %all-reduce.11 = (f32[256]{0:T(256)S(1)}, f32[32]{0:T(128)S(1)}, f32[]{:T(128)}) all-reduce(f32[256]{0:T(256)S(1)} %multiply_reduce_fusion.14, f32[32]{0:T(128)S(1)} %get-tuple-element.273, f32[]{:T(128)S(6)} %mul.708), channel_id=1, replica_groups=mesh['path'=2,'frames'=16] {'path','frames'}, use_global_device_ids=true, to_apply=%region_9.10 | all-reduce | flops 289 | bytes 2312 | tf_op jit(solution)/shard_map/psum | solution.py:40
  241.2 2.9 multiply_convert_fusion.9
  255.0 6.4 multiply_reduce_fusion.13
  261.4 40.1 %all-reduce.10 = (f32[256]{0:T(256)S(1)}, f32[32]{0:T(128)S(1)}) all-reduce(f32[256]{0:T(256)S(1)} %get-tuple-element.275, f32[32]{0:T(128)S(1)} %multiply_reduce_fusion.21), channel_id=1, replica_groups=mesh['path'=2,'frames'=16] {'path','frames'}, use_global_device_ids=true, to_apply=%region_11.12 | all-reduce | flops 288 | bytes 2304 | tf_op jit(solution)/shard_map/psum | solution.py:35
  306.6 4.2 collective-permute-start.1
  314.9 19.6 %reshape.622 = bf16[3,3,256,16,196]{2,1,0,4,3:T(4,128)(2,1)} reshape(bf16[2304,16,196]{0,2,1:T(8,128)(2,1)} %bitcast.268) | data formatting | bytes 28901376 | tf_op jit(solution)/shard_map/fpc,fpd->cd/dot_general | solution.py:64
  336.6 4.1 multiply_reduce_fusion.20
  340.7 40.5 %all-reduce.9 = (f32[256]{0:T(256)S(1)}, f32[32]{0:T(128)S(1)}) all-reduce(f32[256]{0:T(256)S(1)} %multiply_reduce_fusion.12, f32[32]{0:T(128)S(1)} %get-tuple-element.277), channel_id=1, replica_groups=mesh['path'=2,'frames'=16] {'path','frames'}, use_global_device_ids=true, to_apply=%region_13.14 | all-reduce | flops 288 | bytes 2304 | tf_op jit(solution)/shard_map/psum | solution.py:40
  384.7 9.1 multiply_reduce_fusion.5
  393.8 41.2 %all-reduce.8 = (f32[1024]{0:T(1024)S(1)}, f32[32]{0:T(128)S(1)}) all-reduce(f32[1024]{0:T(1024)S(1)} %get-tuple-element.279, f32[32]{0:T(128)S(1)} %multiply_reduce_fusion.19), channel_id=1, replica_groups=mesh['path'=2,'frames'=16] {'path','frames'}, use_global_device_ids=true, to_apply=%region_15.16 | all-reduce | flops 1056 | bytes 8448 | tf_op jit(solution)/shard_map/psum | solution.py:35
  436.4 17.5 %multiply_reduce_fusion.4 = (f32[1024]{0:T(1024)S(1)}, f32[1024]{0:T(1024)S(1)}, f32[16,196,1024]{2,1,0:T(8,128)}) fusion(f32[16,196,1024]{2,1,0:T(8,128)} %get-tuple-element.280, f32[1024]{0:T(1024)S(1)} %broadcast_divide_fusion.1, f32[16]{0:T(128)S(1)} %convert_element_type.89, bf16[1280,1024]{1,0:T(8,128)(2,1)S(1)} %copy-done, ...), kind=kOutput, calls=%fused_computation.15 | convolution fusion | flops 8256157696 | bytes 36352064 | tf_op jit(solution)/shard_map/fpc,cd->fpd/dot_general | solution.py:56
  453.8 5.7 multiply_reduce_fusion.8
  459.6 39.4 %all-reduce.7 = (f32[1024]{0:T(1024)S(1)}, f32[128]{0:T(128)S(1)}) all-reduce(f32[1024]{0:T(1024)S(1)} %get-tuple-element.166, f32[128]{0:T(128)S(1)} %get-tuple-element.282), channel_id=1, replica_groups=mesh['path'=2,'frames'=16] {'path','frames'}, use_global_device_ids=true, to_apply=%region_19.20 | all-reduce | flops 1152 | bytes 9216 | tf_op jit(solution)/shard_map/psum | solution.py:35
  500.3 4.7 multiply_reduce_fusion.7
  505.0 6.7 multiply_reduce_fusion.2
  511.7 41.0 %all-reduce.6 = (f32[1024]{0:T(1024)S(1)}, f32[1024]{0:T(1024)S(1)}, f32[128]{0:T(128)S(1)}) all-reduce(f32[1024]{0:T(1024)S(1)} %multiply_reduce_fusion.2, f32[1024]{0:T(1024)S(1)} %get-tuple-element.165, f32[128]{0:T(128)S(1)} %multiply_reduce_fusion.7), channel_id=1, replica_groups=mesh['path'=2,'frames'=16] {'path','frames'}, use_global_device_ids=true, to_apply=%region_21.22 | all-reduce | flops 2176 | bytes 17408 | tf_op jit(solution)/shard_map/psum | solution.py:40
  554.2 13.3 %fusion.84 = (f32[128]{0:T(128)S(1)}, f32[128]{0:T(128)S(1)}, f32[64,196,128]{2,1,0:T(8,128)}, bf16[64,196,128]{2,1,0:T(8,128)(2,1)}) fusion(f32[128]{0:T(128)S(1)} %get-tuple-element.221, f32[64,196,128]{2,1,0:T(8,128)} %get-tuple-element.283, f32[128]{0:T(128)S(1)} %broadcast_divide_fusion.5, bf16[64,196,128]{2,0,1:T(8,128)(2,1)} %bitcast.261, ...), kind=kLoop, calls=%fused_computation.228 | loop fusion | flops 33718016 | bytes 25693440 | tf_op jit(solution)/shard_map/reduce_sum | solution.py:47
  567.5 21.0 %multiply_reduce_fusion.1 = (f32[1024]{0:T(1024)S(1)}, f32[1024]{0:T(1024)S(1)}, f32[1024]{0:T(1024)S(1)}, f32[16,196,1024]{2,1,0:T(8,128)}, bf16[16,196,1024]{2,1,0:T(8,128)(2,1)}) fusion(f32[16,196,1024]{2,1,0:T(8,128)} %get-tuple-element.280, f32[1024]{0:T(1024)S(1)} %get-tuple-element.223, f32[1024]{0:T(1024)S(1)} %broadcast_divide_fusion.1, ...), kind=kLoop, calls=%fused_computation.9 | loop fusion | flops 83489792 | bytes 57847872 | tf_op jit(solution)/shard_map/reduce_sum | solution.py:47
  588.5 39.6 %all-reduce.5 = (f32[1024]{0:T(1024)S(1)}, f32[1024]{0:T(1024)S(1)}, f32[128]{0:T(128)S(1)}, f32[128]{0:T(128)S(1)}) all-reduce(f32[1024]{0:T(1024)S(1)} %get-tuple-element.152, f32[1024]{0:T(1024)S(1)} %get-tuple-element.150, f32[128]{0:T(128)S(1)} %get-tuple-element.154, ...), channel_id=1, replica_groups=mesh['path'=2,'frames'=16] {'path','frames'}, use_global_device_ids=true, to_apply=%region_37.38 | all-reduce | flops 2304 | bytes 18432 | tf_op jit(solution)/shard_map/psum | solution.py:46
  628.1 7.0 multiply_convert_fusion.3
  637.1 3.6 fusion.89
  642.1 6.2 multiply_convert_fusion.1
  648.3 6.2 convolution_bitcast_fusion.4
  654.5 4.9 fusion.87
  659.4 41.4 %all-reduce.4 = (f32[256]{0:T(256)S(1)}, f32[256]{0:T(256)S(1)}, f32[32]{0:T(128)S(1)}, f32[32]{0:T(128)S(1)}) all-reduce(f32[256]{0:T(256)S(1)} %get-tuple-element.160, f32[256]{0:T(256)S(1)} %get-tuple-element.159, f32[32]{0:T(128)S(1)} %get-tuple-element.164, ...), channel_id=1, replica_groups=mesh['path'=2,'frames'=16] {'path','frames'}, use_global_device_ids=true, to_apply=%region_43.44 | all-reduce | flops 576 | bytes 4608 | tf_op jit(solution)/shard_map/psum | solution.py:46
  700.8 4.9 multiply_convert_fusion.12
  707.0 4.8 collective-permute-start.4
  711.8 3.5 multiply_convert_fusion.7
  715.6 12.6 %fusion.38 = f32[3,3,256,256]{3,2,1,0:T(8,128)} fusion(bf16[3,3,256,16,196]{2,1,0,4,3:T(4,128)(2,1)} %reshape.622, bf16[16,196,256]{2,1,0:T(8,128)(2,1)S(1)} %multiply_convert_fusion.7), kind=kOutput, calls=%fused_computation.137 | convolution fusion | flops 3699376128 | bytes 18415616 | tf_op jit(solution)/shard_map/fpc,fpd->cd/dot_general | solution.py:64
  728.2 11.7 fusion.99
  742.8 5.3 fusion.20
  748.1 5.8 fusion.6
  760.9 4.4 fusion.86
  768.7 5.1 fusion.88
  773.8 41.5 %all-reduce.3 = (f32[1024]{0:T(1024)S(1)}, f32[256]{0:T(256)S(1)}, f32[256]{0:T(256)S(1)}, f32[32]{0:T(128)S(1)}, f32[32]{0:T(128)S(1)}) all-reduce(f32[1024]{0:T(1024)S(1)} %get-tuple-element.151, f32[256]{0:T(256)S(1)} %copy-done.79, f32[256]{0:T(256)S(1)} %copy-done.78, ...), channel_id=1, replica_groups=mesh['path'=2,'frames'=16] {'path','frames'}, use_global_device_ids=true, to_apply=%region_50.51 | all-reduce | flops 1600 | bytes 12800 | tf_op jit(solution)/shard_map/psum | solution.py:46
  815.4 10.6 multiply_convert_fusion
  826.0 13.1 %convolution_bitcast_fusion = f32[1280,1024]{1,0:T(8,128)} fusion(bf16[16,196,1024]{2,1,0:T(8,128)(2,1)S(1)} %multiply_convert_fusion, bf16[16,196,256]{2,1,0:T(8,128)(2,1)S(1)} %copy-done.34, bf16[16,196,1024]{2,1,0:T(8,128)(2,1)} %copy.56), kind=kOutput, calls=%fused_computation.35 | convolution fusion | flops 8236892160 | bytes 19693568 | tf_op jit(solution)/shard_map/fpc,fpd->cd/dot_general | solution.py:64
  839.1 11.7 %fusion.30 = f32[16,196,1280]{2,1,0:T(8,128)} fusion(bf16[16,196,1024]{2,1,0:T(8,128)(2,1)S(1)} %multiply_convert_fusion, bf16[1280,1024]{1,0:T(8,128)(2,1)S(1)} %copy-done), kind=kOutput, calls=%fused_computation.101 | convolution fusion | flops 8220835840 | bytes 25100288 | tf_op jit(solution)/shard_map/fpd,cd->fpc/dot_general | solution.py:60
  850.9 3.0 multiply_convert_fusion.11
  854.0 3.8 fusion.54
  859.4 4.0 convolution_bitcast_fusion.1
  863.4 13.9 %convolution_add_fusion = f32[16,196,1280]{2,1,0:T(8,128)} fusion(f32[16,196,1280]{2,1,0:T(8,128)} %fusion.30, bf16[16,196,256]{2,1,0:T(8,128)(2,1)S(1)} %multiply_convert_fusion.6, bf16[1280,256]{1,0:T(8,128)(2,1)S(1)} %copy-done.43), kind=kOutput, calls=%fused_computation | convolution fusion | flops 2059223040 | bytes 34373632 | tf_op jit(solution)/shard_map/fpd,cd->fpc/dot_general | solution.py:60
  877.4 4.4 fusion.85
  881.7 42.2 %all-reduce.2 = (f32[256]{0:T(256)S(1)}, f32[256]{0:T(256)S(1)}, f32[128,32]{0,1:T(8,128)}, f32[3,32,32]{1,0,2:T(4,128)S(1)}, f32[32,128]{1,0:T(8,128)}) all-reduce(f32[256]{0:T(256)S(1)} %get-tuple-element.156, f32[256]{0:T(256)S(1)} %get-tuple-element.155, ...), channel_id=1, replica_groups=mesh['path'=2,'frames'=16] {'path','frames'}, use_global_device_ids=true, to_apply=%region_66.67 | all-reduce | flops 11776 | bytes 94208 | tf_op jit(solution)/shard_map/psum | solution.py:46
  923.9 4.9 multiply_convert_fusion.5
  933.0 4.5 copy.70
  937.4 10.1 copy.66
  949.1 3.4 convolution_bitcast_fusion.2
  953.8 8.7 slice.666
  963.9 9.3 copy.82
  985.8 167.3 %all-reduce.16.cloned.1.call-done = (f32[5,128,256]{2,1,0:T(8,128)}, f32[1280,256]{1,0:T(8,128)}, f32[3,3,256,256]{3,2,1,0:T(8,128)}, f32[256,1024]{1,0:T(8,128)}, f32[1280,1024]{1,0:T(8,128)}) async-done(((f32[5,128,256]{2,1,0:T(8,128)}, f32[1280,256]{1,0:T(8,128)}, f32[3,3,256,256]{3,2,1,0:T(8,128)}, f32[256,1024]{1,0:T(8,128)}, f32[1280,1024]{1,0:T(8,128)}), (f32[5,128,256]{2,1,0:T(8,128)}, ...) | async-done | bytes 10616848 | tf_op jit(solution)/shard_map/psum | solution.py:260
  (352 shorter events, 101.4 us)
Async XLA Ops:
  7.2 429.2 %copy-start = (bf16[1280,1024]{1,0:T(8,128)(2,1)S(1)}, bf16[1280,1024]{1,0:T(8,128)(2,1)}, u32[]{:S(2)}) copy-start(bf16[1280,1024]{1,0:T(8,128)(2,1)} %param.45) | copy-start | bytes 7864324
  7.2 19.3 %copy-start.96 = (s32[4]{0:T(128)S(1)}, s32[4]{0:T(128)}, u32[]{:S(2)}) copy-start(s32[4]{0:T(128)} %constant.301.clone.1) | copy-start | bytes 52
  7.2 19.2 %copy-start.99 = (s32[16]{0:T(128)S(1)}, s32[16]{0:T(128)}, u32[]{:S(2)}) copy-start(s32[16]{0:T(128)} %param.36) | copy-start | bytes 196
  7.2 20.4 %copy-start.54 = (bf16[3,32,32]{2,1,0:T(8,128)(2,1)S(1)}, bf16[3,32,32]{2,1,0:T(8,128)(2,1)}, u32[]{:S(2)}) copy-start(bf16[3,32,32]{2,1,0:T(8,128)(2,1)} %param.39) | copy-start | bytes 18436
  7.2 1145.9 %all-reduce.16.cloned.1.call-start = ((), (), s32[]{:S(2)}) async-start(), calls=%async_computation | async-start | bytes 21233664 | tf_op jit(solution)/shard_map/psum | solution.py:260
  8.5 49.2 %collective-permute-start = (bf16[2,196,128]{2,1,0:T(8,128)(2,1)S(1)}, bf16[2,196,128]{2,1,0:T(8,128)(2,1)S(1)}, u32[]{:S(2)}, u32[]{:S(2)}) collective-permute-start(bf16[2,196,128]{2,1,0:T(8,128)(2,1)S(1)} %bitcast.293), channel_id=1, source_target_pairs={{0,1},{1,2},{2,3},{3,4},{4,5},{5,6},{6,7},{7,8},{8,9},{9,10},{10,1... | collective-permute-start | bytes 301064 | tf_op jit(solution)/shard_map/ppermute | solution.py:25
  16.9 286.5 %copy-start.94 = (f32[32]{0:T(128)}, f32[32]{0:T(128)S(1)}, u32[]{:S(2)}) copy-start(f32[32]{0:T(128)S(1)} %get-tuple-element.255) | copy-start | bytes 388
  17.7 128.5 %copy-start.65 = (f32[256]{0:T(256)}, f32[256]{0:T(256)S(1)}, u32[]{:S(2)}) copy-start(f32[256]{0:T(256)S(1)} %get-tuple-element.260) | copy-start | bytes 3076
  17.7 231.8 %copy-start.60 = (f32[256]{0:T(256)}, f32[256]{0:T(256)S(1)}, u32[]{:S(2)}) copy-start(f32[256]{0:T(256)S(1)} %get-tuple-element.259) | copy-start | bytes 3076
  26.5 31.2 %copy-start.92 = (bf16[16]{0:T(256)(128)(2,1)}, bf16[16]{0:T(256)(128)(2,1)S(1)}, u32[]{:S(2)}) copy-start(bf16[16]{0:T(256)(128)(2,1)S(1)} %get-tuple-element.268) | copy-start | bytes 100
  27.4 307.2 %copy-start.69 = (bf16[64]{0:T(256)(128)(2,1)}, bf16[64]{0:T(256)(128)(2,1)S(1)}, u32[]{:S(2)}) copy-start(bf16[64]{0:T(256)(128)(2,1)S(1)} %reshape.593) | copy-start | bytes 388
  29.9 9.2 slice-start.17
  57.7 276.9 %copy-start.82 = (bf16[64]{0:T(256)(128)(2,1)}, bf16[64]{0:T(256)(128)(2,1)S(1)}, u32[]{:S(2)}) copy-start(bf16[64]{0:T(256)(128)(2,1)S(1)} %pad_maximum_fusion.16) | copy-start | bytes 388
  61.2 83.9 %copy-start.64 = (f32[3008]{0:T(1024)S(1)}, f32[3008]{0:T(1024)}, u32[]{:S(2)}) copy-start(f32[3008]{0:T(1024)} %param.46) | copy-start | bytes 36100
  102.2 47.1 %copy-start.50 = (f32[256]{0:T(256)}, f32[256]{0:T(256)S(1)}, u32[]{:S(2)}) copy-start(f32[256]{0:T(256)S(1)} %broadcast_divide_fusion.4) | copy-start | bytes 3076
  104.8 44.5 %copy-start.42 = (bf16[1280,256]{1,0:T(8,128)(2,1)S(1)}, bf16[1280,256]{1,0:T(8,128)(2,1)}, u32[]{:S(2)}) copy-start(bf16[1280,256]{1,0:T(8,128)(2,1)} %param.42) | copy-start | bytes 1966084
  146.3 10.5 copy-start.58
  146.3 10.5 copy-start.67
  197.3 52.2 %copy-start.46 = (f32[256]{0:T(256)}, f32[256]{0:T(256)S(1)}, u32[]{:S(2)}) copy-start(f32[256]{0:T(256)S(1)} %broadcast_divide_fusion.3) | copy-start | bytes 3076
  252.1 51.2 %copy-start.70 = (f32[32]{0:T(128)}, f32[32]{0:T(128)S(1)}, u32[]{:S(2)}) copy-start(f32[32]{0:T(128)S(1)} %broadcast_divide_fusion.7) | copy-start | bytes 388
  303.3 31.2 %copy-start.72 = (f32[32]{0:T(128)}, f32[32]{0:T(128)S(1)}, u32[]{:S(2)}) copy-start(f32[32]{0:T(128)S(1)} %get-tuple-element.209) | copy-start | bytes 388
  303.3 31.2 %copy-start.95 = (f32[32]{0:T(128)}, f32[32]{0:T(128)S(1)}, u32[]{:S(2)}) copy-start(f32[32]{0:T(128)S(1)} %get-tuple-element.257) | copy-start | bytes 388
  306.6 27.9 %collective-permute-start.1 = (bf16[1,196,32]{1,2,0:T(8,128)(2,1)S(1)}, bf16[1,196,32]{1,2,0:T(8,128)(2,1)S(1)}, u32[]{:S(2)}, u32[]{:S(2)}) collective-permute-start(bf16[1,196,32]{1,2,0:T(8,128)(2,1)S(1)} %get-tuple-element.244), channel_id=1, source_target_pairs={{0,1},{1,2},{2,3},{3,4},{4,5},{5,6},{6,7},{7,8},{8,9},{9,10},{10,1... | collective-permute-start | bytes 37640 | tf_op jit(solution)/shard_map/ppermute | solution.py:16
  310.8 23.7 %collective-permute-start.2 = (bf16[1,196,32]{1,2,0:T(8,128)(2,1)S(1)}, bf16[1,196,32]{1,2,0:T(8,128)(2,1)S(1)}, u32[]{:S(2)}, u32[]{:S(2)}) collective-permute-start(bf16[1,196,32]{1,2,0:T(8,128)(2,1)S(1)} %get-tuple-element.245), channel_id=1, source_target_pairs={{1,0},{2,1},{3,2},{4,3},{5,4},{6,5},{7,6},{8,7},{9,8},{10,9},{11,1... | collective-permute-start | bytes 37640 | tf_op jit(solution)/shard_map/ppermute | solution.py:17
  336.5 48.1 %copy-start.97 = (bf16[256,1024]{1,0:T(8,128)(2,1)S(1)}, bf16[256,1024]{1,0:T(8,128)(2,1)}, u32[]{:S(2)}) copy-start(bf16[256,1024]{1,0:T(8,128)(2,1)} %param.44) | copy-start | bytes 1572868
  436.4 17.5 %copy-start.18 = (f32[64,196,32]{1,2,0:T(8,128)S(1)}, f32[64,196,32]{1,2,0:T(8,128)}, u32[]{:S(2)}) copy-start(f32[64,196,32]{1,2,0:T(8,128)} %get-tuple-element.278) | copy-start | bytes 4816900
  436.4 17.5 %copy-start.98 = (bf16[32,128]{1,0:T(8,128)(2,1)S(1)}, bf16[32,128]{1,0:T(8,128)(2,1)}, u32[]{:S(2)}) copy-start(bf16[32,128]{1,0:T(8,128)(2,1)} %param.40) | copy-start | bytes 24580
  554.1 13.3 %slice-start = ((s8[13107200]{0:T(1024)(128)(4,1)}), s8[4194304]{0:T(1024)(128)(4,1)S(1)}, s32[]{:S(2)}) async-start(s8[13107200]{0:T(1024)(128)(4,1)} %bitcast.254), calls=%async_computation.1 | async-start | bytes 8388608
  554.1 13.3 %slice-start.1 = ((s8[13107200]{0:T(1024)(128)(4,1)}), s8[4194304]{0:T(1024)(128)(4,1)S(1)}, s32[]{:S(2)}) async-start(s8[13107200]{0:T(1024)(128)(4,1)} %bitcast.254), calls=%async_computation.2 | async-start | bytes 8388608
  554.1 13.3 %slice-start.2 = ((s8[13107200]{0:T(1024)(128)(4,1)}), s8[4194304]{0:T(1024)(128)(4,1)S(1)}, s32[]{:S(2)}) async-start(s8[13107200]{0:T(1024)(128)(4,1)} %bitcast.254), calls=%async_computation.3 | async-start | bytes 8388608
  554.1 13.3 %slice-start.3 = ((s8[13107200]{0:T(1024)(128)(4,1)}), s8[524288]{0:T(1024)(128)(4,1)S(1)}, s32[]{:S(2)}) async-start(s8[13107200]{0:T(1024)(128)(4,1)} %bitcast.254), calls=%async_computation.4 | async-start | bytes 1048576
  628.0 12.7 %copy-start.55 = (f32[1024]{0:T(1024)}, f32[1024]{0:T(1024)S(1)}, u32[]{:S(2)}) copy-start(f32[1024]{0:T(1024)S(1)} %get-tuple-element.182) | copy-start | bytes 12292
  628.1 12.7 %slice-start.10 = ((s8[13107200]{0:T(1024)(128)(4,1)}), s8[4194304]{0:T(1024)(128)(4,1)S(1)}, s32[]{:S(2)}) async-start(s8[13107200]{0:T(1024)(128)(4,1)} %bitcast.266), calls=%async_computation.11 | async-start | bytes 8388608
  628.1 12.7 %slice-start.11 = ((s8[13107200]{0:T(1024)(128)(4,1)}), s8[4194304]{0:T(1024)(128)(4,1)S(1)}, s32[]{:S(2)}) async-start(s8[13107200]{0:T(1024)(128)(4,1)} %bitcast.266), calls=%async_computation.12 | async-start | bytes 8388608
  700.7 14.5 %copy-start.74 = (f32[256]{0:T(256)}, f32[256]{0:T(256)S(1)}, u32[]{:S(2)}) copy-start(f32[256]{0:T(256)S(1)} %get-tuple-element.178) | copy-start | bytes 3076
  700.7 14.6 %copy-start.76 = (f32[256]{0:T(256)}, f32[256]{0:T(256)S(1)}, u32[]{:S(2)}) copy-start(f32[256]{0:T(256)S(1)} %get-tuple-element.177) | copy-start | bytes 3076
  700.7 11.1 copy-start.14
  705.7 59.7 %copy-start.25 = (bf16[64,196,32]{1,2,0:T(8,128)(2,1)}, bf16[64,196,32]{1,2,0:T(8,128)(2,1)S(1)}, u32[]{:S(2)}) copy-start(bf16[64,196,32]{1,2,0:T(8,128)(2,1)S(1)} %multiply_convert_fusion.12) | copy-start | bytes 2408452
  705.7 60.9 %collective-permute-start.3 = (bf16[1,196,32]{1,2,0:T(8,128)(2,1)S(1)}, bf16[1,196,32]{1,2,0:T(8,128)(2,1)S(1)}, u32[]{:S(2)}, u32[]{:S(2)}) collective-permute-start(bf16[1,196,32]{1,2,0:T(8,128)(2,1)S(1)} %get-tuple-element.240), channel_id=1, source_target_pairs={{1,0},{2,1},{3,2},{4,3},{5,4},{6,5},{7,6},{8,7},{9,8},{10,9},{11,1... | collective-permute-start | bytes 37640 | tf_op jit(solution)/shard_map/ppermute | solution.py:17
  707.0 59.6 %collective-permute-start.4 = (bf16[1,196,32]{1,2,0:T(8,128)(2,1)S(1)}, bf16[1,196,32]{1,2,0:T(8,128)(2,1)S(1)}, u32[]{:S(2)}, u32[]{:S(2)}) collective-permute-start(bf16[1,196,32]{1,2,0:T(8,128)(2,1)S(1)} %get-tuple-element.241), channel_id=1, source_target_pairs={{0,1},{1,2},{2,3},{3,4},{4,5},{5,6},{6,7},{7,8},{8,9},{9,10},{10,1... | collective-permute-start | bytes 37640 | tf_op jit(solution)/shard_map/ppermute | solution.py:16
  715.6 12.6 %copy-start.36 = (bf16[3,3,256,256]{3,2,1,0:T(8,128)(2,1)S(1)}, bf16[3,3,256,256]{3,2,1,0:T(8,128)(2,1)}, u32[]{:S(2)}) copy-start(bf16[3,3,256,256]{3,2,1,0:T(8,128)(2,1)} %param.43) | copy-start | bytes 3538948
  739.9 14.0 %copy-start.1 = (f32[16,14,14,9,256]{4,0,3,2,1:T(8,128)S(1)}, f32[16,14,14,9,256]{4,0,3,2,1:T(8,128)}, u32[]{:S(2)}) copy-start(f32[16,14,14,9,256]{4,0,3,2,1:T(8,128)} %fusion.99) | copy-start | bytes 86704128
  815.4 10.6 copy-start.34
  826.0 33.4 %slice-start.15 = ((s8[6553600]{0:T(1024)(128)(4,1)}), s8[4194304]{0:T(1024)(128)(4,1)S(1)}, s32[]{:S(2)}) async-start(s8[6553600]{0:T(1024)(128)(4,1)} %bitcast.270), calls=%async_computation.16 | async-start | bytes 8388608
  839.1 11.8 %copy-start.9 = (f32[64,196,32]{1,2,0:T(8,128)S(1)}, f32[64,196,32]{1,2,0:T(8,128)}, u32[]{:S(2)}) copy-start(f32[64,196,32]{1,2,0:T(8,128)} %get-tuple-element.274) | copy-start | bytes 4816900
  839.1 11.8 %copy-start.30 = (f32[64,196,32]{1,2,0:T(8,128)S(1)}, f32[64,196,32]{1,2,0:T(8,128)}, u32[]{:S(2)}) copy-start(f32[64,196,32]{1,2,0:T(8,128)} %get-tuple-element.286) | copy-start | bytes 4816900
  839.1 11.8 %copy-start.71 = (f32[32]{0:T(128)S(1)}, f32[32]{0:T(128)}, u32[]{:S(2)}) copy-start(f32[32]{0:T(128)} %copy-done.70) | copy-start | bytes 388
  839.1 11.8 %copy-start.73 = (f32[32]{0:T(128)S(1)}, f32[32]{0:T(128)}, u32[]{:S(2)}) copy-start(f32[32]{0:T(128)} %copy-done.72) | copy-start | bytes 388
  839.1 11.8 %copy-start.91 = (f32[32]{0:T(128)S(1)}, f32[32]{0:T(128)}, u32[]{:S(2)}) copy-start(f32[32]{0:T(128)} %get-tuple-element.208) | copy-start | bytes 388
  839.1 18.7 %copy-start.15 = (f32[16,196,256]{2,1,0:T(8,128)S(1)}, f32[16,196,256]{2,1,0:T(8,128)}, u32[]{:S(2)}) copy-start(f32[16,196,256]{2,1,0:T(8,128)} %get-tuple-element.217) | copy-start | bytes 9633796
  839.1 20.3 %slice-start.16 = ((s8[6553600]{0:T(1024)(128)(4,1)}), s8[2359296]{0:T(1024)(128)(4,1)S(1)}, s32[]{:S(2)}) async-start(s8[6553600]{0:T(1024)(128)(4,1)} %bitcast.270), calls=%async_computation.17 | async-start | bytes 4718592
  863.4 13.9 %copy-start.7 = (f32[16,196,256,1]{2,1,3,0:T(8,128)S(1)}, f32[16,196,256,1]{2,1,3,0:T(8,128)}, u32[]{:S(2)}) copy-start(f32[16,196,256,1]{2,1,3,0:T(8,128)} %get-tuple-element.270) | copy-start | bytes 9633796
  863.4 13.9 %copy-start.51 = (f32[256]{0:T(256)S(1)}, f32[256]{0:T(256)}, u32[]{:S(2)}) copy-start(f32[256]{0:T(256)} %copy-done.50) | copy-start | bytes 3076
  863.4 13.9 %copy-start.59 = (f32[256]{0:T(256)S(1)}, f32[256]{0:T(256)}, u32[]{:S(2)}) copy-start(f32[256]{0:T(256)} %copy-done.58) | copy-start | bytes 3076
  863.4 13.9 %copy-start.66 = (f32[256]{0:T(256)S(1)}, f32[256]{0:T(256)}, u32[]{:S(2)}) copy-start(f32[256]{0:T(256)} %copy-done.65) | copy-start | bytes 3076
  863.4 13.9 %copy-start.68 = (f32[256]{0:T(256)S(1)}, f32[256]{0:T(256)}, u32[]{:S(2)}) copy-start(f32[256]{0:T(256)} %copy-done.67) | copy-start | bytes 3076
  877.4 46.6 %copy-start.80 = (f32[256]{0:T(256)S(1)}, f32[256]{0:T(256)}, u32[]{:S(2)}) copy-start(f32[256]{0:T(256)} %get-tuple-element.206) | copy-start | bytes 3076
  937.4 10.1 copy-start.12
  937.4 11.6 copy-start.45
  947.6 26.4 %collective-permute-start.5 = (bf16[1,196,256]{2,1,0:T(8,128)(2,1)S(1)}, bf16[1,196,256]{2,1,0:T(8,128)(2,1)S(1)}, u32[]{:S(2)}, u32[]{:S(2)}) collective-permute-start(bf16[1,196,256]{2,1,0:T(8,128)(2,1)S(1)} %slice_multiply_fusion.2), channel_id=1, source_target_pairs={{1,0},{2,1},{3,2},{4,3},{5,4},{6,5},{7,6},{8,7},{9,8},{10,9},{11,1... | collective-permute-start | bytes 301064 | tf_op jit(solution)/shard_map/ppermute | solution.py:25
  953.8 8.7 copy-start.90
  953.8 9.4 copy-start.75
  953.8 9.4 copy-start.84
  953.8 9.4 copy-start.88
  (64 other events, 294.5 us)
Sparse Core Ops, SparseCore 0:
  932.4 220.6 all-reduce.15
where the time goes:
time: 1180 us; the launch traced here: 1170 us
  blocking collectives  528 us (45%)
  waiting for transfers between devices  167 us (14%)
  other arithmetic  165 us (14%)
  matrix products  161 us (14%)
  local copies, waits for them, and re-layouts  115 us (10%)
  starting transfers between devices  18.2 us (2%)
  between operations  17.1 us (1%)
    psum x5, blocking collectives, norm_forward(): lax.psum((jnp.sum(inputs * weight, axis=(0, 1)), local_count), ('path', '...  201 us
    psum x1, waiting for transfers between devices, per_device(): lax.psum((grad_fast_in, grad_fast_mid, grad_fast_out, grad_lateral, grad_...  167 us
    psum x4, blocking collectives, norm_backward(): lax.psum((jnp.sum(grad_in, axis=(0, 1)), jnp.sum(grad_in * unit, axis=(0,...  165 us
    psum x4, blocking collectives, norm_forward(): lax.psum(jnp.sum(centered * centered * weight, axis=(0, 1)), ('path', 'fr...  162 us
    dot_general x8, matrix products, project(): jnp.einsum('fpc,cd->fpd', inputs, matrix, preferred_element_type=jnp.floa...  60.8 us
    dot_general x6, matrix products, project_back(): jnp.einsum('fpd,cd->fpc', grad_low, matrix, preferred_element_type=jnp.fl...  47.8 us
    dot_general x7, matrix products, weight_grad(): jnp.einsum('fpc,fpd->cd', inputs, grad_low, preferred_element_type=jnp.fl...  42.7 us
    unnamed x256, local copies, waits for them, and re-layouts  32.8 us
  transfers between devices with their start and end apart: 7, of which 1 were waited for; matrix products, arithmetic and copies ran while one was open for 14% of the time, Pallas kernels for 0%

commit v1 on v0

v1 whole, which is shorter than its diff:
```python
import functools

import jax
import jax.numpy as jnp
from jax import lax
from jax.experimental import pallas as pl
from jax.experimental.pallas import tpu as pltpu
from jax.sharding import PartitionSpec as P

norm_eps = 1e-05
F32 = jnp.float32
BF16 = jnp.bfloat16
MESH = pl.DeviceIdType.MESH
AXES = ("path", "frames")
STEPS = 7
LANES = 128
VMEM_LIMIT = 56 * 1024 * 1024


def dot(a, b):
    return jnp.dot(a, b, preferred_element_type=F32)


def dot_nt(a, b):
    return lax.dot_general(a, b, (((1,), (1,)), ((), ())), preferred_element_type=F32)


def dot_tn(a, b):
    return lax.dot_general(a, b, (((0,), (0,)), ((), ())), preferred_element_type=F32)


def sig(v):
    return 0.5 * jnp.tanh(0.5 * v) + 0.5


def slope(v):
    s = sig(v)
    return s + (v * s) * (1.0 - s)


def rows(ref, slab, first, count):
    parts = [ref[slab, first + j : first + j + 1, :] for j in range(count)]
    return parts[0] if count == 1 else jnp.concatenate(parts, axis=1)


def put_rows(ref, first, value):
    for j in range(value.shape[1] // LANES):
        ref[first + j : first + j + 1, :] = value[:, j * LANES : (j + 1) * LANES]


def zero_ref(ref):
    ref[...] = jnp.zeros(ref.shape, ref.dtype)


def spread_add(step, z, mean_ref, m2_ref, cols=slice(None)):
    count = z.shape[0]
    mean = jnp.sum(z, axis=0) * (1.0 / count)
    d = z - mean
    m2 = jnp.sum(d * d, axis=0)
    first = step == 0
    old_mean = jnp.where(first, 0.0, mean_ref[:, cols])
    old_m2 = jnp.where(first, 0.0, m2_ref[:, cols])
    done = jnp.full((1, z.shape[-1]), step, jnp.int32).astype(F32)
    share = 1.0 / (done + 1.0)
    delta = mean - old_mean
    mean_ref[:, cols] = old_mean + delta * share
    m2_ref[:, cols] = old_m2 + m2 + delta * delta * (done * share * count)


def spread_end(mean_ref, m2_ref, fill, positions):
    filled = jnp.sum(fill, axis=0, keepdims=True)
    mean = jnp.sum(fill * mean_ref[...], axis=0, keepdims=True) / jnp.maximum(filled, 1.0)
    d = mean_ref[...] - mean
    m2 = jnp.sum(fill * (m2_ref[...] + positions * (d * d)), axis=0, keepdims=True)
    return mean, m2


def sum_add(step, value, ref, cols=slice(None)):
    ref[:, cols] = jnp.where(step == 0, 0.0, ref[:, cols]) + jnp.sum(value, axis=0)


def sum_end(ref):
    return jnp.sum(ref[...], axis=0, keepdims=True)


def pad8(n):
    return -(-n // 8) * 8


def exchange_kernel(cfg, *refs):
    fwd, bwd, n_coefs, has_up, has_down = cfg
    nf = sum(c[2] for c in fwd)
    nb = max((c[6] + c[4] for c in bwd), default=0)
    nn = sum(c[4] for c in bwd)
    n_row = 2 * nf + nb
    it = iter(refs)
    stats_ref, gb_ref = next(it), next(it)
    coef_refs = [next(it) for _ in range(n_coefs)]
    up_ref = next(it) if has_up else None
    down_ref = next(it) if has_down else None
    coef_out = next(it) if nf else None
    pq_out = next(it) if nb else None
    from_prev = next(it) if has_up else None
    from_next = next(it) if has_down else None
    slots1, slots2, mid, tot, send1, recv1, send2, recv2 = (next(it) for _ in range(8))
    if has_up:
        up_land, up_sems = next(it), next(it)
    if has_down:
        down_land, down_sems = next(it), next(it)

    paths, length = lax.axis_size("path"), lax.axis_size("frames")
    near = 4
    g1, g2 = paths * near, length // near
    me_p, me_f = lax.axis_index("path"), lax.axis_index("frames")
    me = me_p * length + me_f
    total = paths * length
    r1 = me_p * near + lax.rem(me_f, near)
    r2 = lax.div(me_f, near)

    def peer1(k):
        r = lax.rem(r1 + k, g1)
        return (lax.div(r, near), r2 * near + lax.rem(r, near))

    def peer2(k):
        r = lax.rem(r2 + k, g2)
        return (me_p, r * near + lax.rem(me_f, near))

    def split(index):
        return (lax.div(index, length), lax.rem(index, length))

    nxt, prv = split(lax.rem(me + 1, total)), split(lax.rem(me + total - 1, total))

    barrier = pltpu.get_barrier_semaphore()
    greeted = 0
    for k in range(1, g1):
        pl.semaphore_signal(barrier, inc=1, device_id=peer1(k), device_id_type=MESH)
        greeted += 1
    for k in range(1, g2):
        pl.semaphore_signal(barrier, inc=1, device_id=peer2(k), device_id_type=MESH)
        greeted += 1
    if has_up or has_down:
        pl.semaphore_signal(barrier, inc=1, device_id=nxt, device_id_type=MESH)
        pl.semaphore_signal(barrier, inc=1, device_id=prv, device_id_type=MESH)
        greeted += 2
    pl.semaphore_wait(barrier, greeted)

    halos = []
    copies = []
    for k in range(1, g1):
        copies.append(
            pltpu.make_async_remote_copy(
                src_ref=stats_ref,
                dst_ref=slots1.at[r1],
                send_sem=send1.at[k],
                recv_sem=recv1.at[k],
                device_id=peer1(k),
                device_id_type=MESH,
            )
        )
        copies[-1].start()
    if has_up:
        halos.append(
            pltpu.make_async_remote_copy(
                src_ref=up_ref,
                dst_ref=up_land,
                send_sem=up_sems.at[0],
                recv_sem=up_sems.at[1],
                device_id=nxt,
                device_id_type=MESH,
            )
        )
        halos[-1].start()
    if has_down:
        halos.append(
            pltpu.make_async_remote_copy(
                src_ref=down_ref,
                dst_ref=down_land,
                send_sem=down_sems.at[0],
                recv_sem=down_sems.at[1],
                device_id=prv,
                device_id_type=MESH,
            )
        )
        halos[-1].start()
    slots1[r1] = stats_ref[...]
    for c in copies:
        c.wait_recv()

    def combine(slots, count, out):
        if nf:
            n = slots[0, n_row : n_row + 1, :]
            for g in range(1, count):
                n = n + slots[g, n_row : n_row + 1, :]
            acc = slots[0, n_row : n_row + 1, :] * slots[0, 0:nf, :]
            for g in range(1, count):
                acc = acc + slots[g, n_row : n_row + 1, :] * slots[g, 0:nf, :]
            mean = acc / jnp.maximum(n, 1.0)
            m2 = None
            for g in range(count):
                d = slots[g, 0:nf, :] - mean
                part = slots[g, nf : 2 * nf, :] + slots[g, n_row : n_row + 1, :] * (d * d)
                m2 = part if m2 is None else m2 + part
            out[0:nf, :] = mean
            out[nf : 2 * nf, :] = m2
            out[n_row : n_row + 1, :] = n
        if nb:
            acc = slots[0, 2 * nf : n_row, :]
            for g in range(1, count):
                acc = acc + slots[g, 2 * nf : n_row, :]
            out[2 * nf : n_row, :] = acc

    zero_ref(mid)
    combine(slots1, g1, mid)
    copies2 = []
    for k in range(1, g2):
        copies2.append(
            pltpu.make_async_remote_copy(
                src_ref=mid,
                dst_ref=slots2.at[r2],
                send_sem=send2.at[k],
                recv_sem=recv2.at[k],
                device_id=peer2(k),
                device_id_type=MESH,
            )
        )
        copies2[-1].start()
    slots2[r2] = mid[...]
    for c in copies2:
        c.wait_recv()
    combine(slots2, g2, tot)

    def lanes4(v):
        w = v + pltpu.roll(v, 64, 1)
        return w + pltpu.roll(w, 32, 1)

    at = 0
    for kind, g_row, count in fwd:
        n = tot[n_row : n_row + 1, :]
        mean = tot[at : at + count, :]
        m2 = tot[nf + at : nf + at + count, :]
        if kind == "lane4":
            whole = lanes4(mean) * 0.25
            d = mean - whole
            var = lanes4(m2 + n * (d * d)) / (4.0 * n)
            mean = whole
        elif kind == "row4":
            whole = jnp.sum(mean, axis=0, keepdims=True) * 0.25
            d = mean - whole
            var = jnp.sum(m2 + n * (d * d), axis=0, keepdims=True) / (4.0 * n)
            var = jnp.broadcast_to(var, (count, LANES))
            mean = jnp.broadcast_to(whole, (count, LANES))
        else:
            var = m2 / n
        inv = lax.rsqrt(var + norm_eps)
        scale = inv * gb_ref[0, g_row : g_row + count, :]
        coef_out[0, at : at + count, :] = scale
        coef_out[1, at : at + count, :] = gb_ref[1, g_row : g_row + count, :] - mean * scale
        coef_out[2, at : at + count, :] = inv
        coef_out[3, at : at + count, :] = mean * inv
        coef_out[4, at : at + count, :] = jnp.broadcast_to(n, (count, LANES))
        at += count
    at = 0
    for kind, coef, row, _, count, db_at, dg_at in bwd:
        db = tot[2 * nf + db_at : 2 * nf + db_at + count, :]
        dg = tot[2 * nf + dg_at : 2 * nf + dg_at + count, :]
        c = coef_refs[coef]
        scale, inv = c[0, row : row + count, :], c[2, row : row + count, :]
        mi, n = c[3, row : row + count, :], c[4, row : row + count, :]
        if kind == "lane4":
            db, dg, n = lanes4(db), lanes4(dg), 4.0 * n
        elif kind == "row4":
            db = jnp.broadcast_to(jnp.sum(db, axis=0, keepdims=True), (count, LANES))
            dg = jnp.broadcast_to(jnp.sum(dg, axis=0, keepdims=True), (count, LANES))
            n = 4.0 * n
        pq_out[0, at : at + count, :] = scale / n * (db - mi * dg)
        pq_out[1, at : at + count, :] = scale / n * inv * dg
        pq_out[2, at : at + count, :] = db
        pq_out[3, at : at + count, :] = dg
        at += count

    for c in halos:
        c.wait()
    if has_up:
        from_prev[...] = up_land[...]
    if has_down:
        from_next[...] = down_land[...]
    for c in copies:
        c.wait_send()
    for c in copies2:
        c.wait_send()


def exchange(mesh_sizes, cid, stats, gb, fwd=(), bwd=(), coefs=(), up=None, down=None):
    paths, length = mesh_sizes
    g1, g2 = paths * 4, length // 4
    nf = sum(c[2] for c in fwd)
    nn = sum(c[4] for c in bwd)
    r = stats.shape[0]
    vm = pl.BlockSpec(memory_space=pltpu.VMEM)
    operands = [stats, gb, *coefs]
    outs = []
    if nf:
        outs.append(jax.ShapeDtypeStruct((5, nf, LANES), F32))
    if nn:
        outs.append(jax.ShapeDtypeStruct((4, nn, LANES), F32))
    scratch = [
        pltpu.VMEM((g1, r, LANES), F32),
        pltpu.VMEM((g2, r, LANES), F32),
        pltpu.VMEM((r, LANES), F32),
        pltpu.VMEM((r, LANES), F32),
        pltpu.SemaphoreType.DMA((g1,)),
        pltpu.SemaphoreType.DMA((g1,)),
        pltpu.SemaphoreType.DMA((g2,)),
        pltpu.SemaphoreType.DMA((g2,)),
    ]
    for halo in (up, down):
        if halo is not None:
            operands.append(halo)
            outs.append(jax.ShapeDtypeStruct(halo.shape, halo.dtype))
            scratch += [pltpu.VMEM(halo.shape, halo.dtype), pltpu.SemaphoreType.DMA((2,))]
    cfg = (fwd, bwd, len(coefs), up is not None, down is not None)
    return pl.pallas_call(
        functools.partial(exchange_kernel, cfg),
        out_shape=outs,
        in_specs=[vm] * len(operands),
        out_specs=[vm] * len(outs),
        scratch_shapes=scratch,
        compiler_params=pltpu.CompilerParams(collective_id=cid, has_side_effects=True),
        name=f"exchange_{cid}",
    )(*operands)


def call(kernel, ins, outs, scratch=(), name=None):
    return pl.pallas_call(
        kernel,
        grid=(STEPS,),
        in_specs=[pl.BlockSpec(b, m) for _, b, m in ins],
        out_specs=[pl.BlockSpec(b, m) for _, _, b, m in outs],
        out_shape=[jax.ShapeDtypeStruct(s, d) for s, d, _, _ in outs],
        scratch_shapes=list(scratch),
        compiler_params=pltpu.CompilerParams(
            dimension_semantics=("arbitrary",), vmem_limit_bytes=VMEM_LIMIT
        ),
        name=name,
    )(*[a for a, _, _ in ins])


def whole(array):
    zeros = (0,) * array.ndim
    return (array, array.shape, lambda i: zeros)


def blocked(array, axis, size):
    block = array.shape[:axis] + (size,) + array.shape[axis + 1 :]
    return (array, block, lambda i: tuple(i if d == axis else 0 for d in range(array.ndim)))


def out_whole(shape, dtype):
    zeros = (0,) * len(shape)
    return (shape, dtype, shape, lambda i: zeros)


def out_blocked(shape, dtype, axis, size):
    block = shape[:axis] + (size,) + shape[axis + 1 :]
    return (shape, dtype, block, lambda i: tuple(i if d == axis else 0 for d in range(len(shape))))


def flat(value):
    return value.reshape(-1, value.shape[-1])


def spread_rows(ref, index, count, height):
    return [jnp.broadcast_to(ref[(*index, slice(p, p + 1))], (height, ref.shape[-1])) for p in range(count)]


def k_first(x_ref, tail_ref, m16_ref, m64_ref, wfa_ref, wlat_ref,
            fa_ref, lat_ref, taps_ref, st_ref, up_ref, down_ref, xs, fm, fv, lm, lv):
    i = pl.program_id(0)
    x = x_ref[...]
    s_n, p_n, f_n, _ = x.shape
    packed = jnp.concatenate([flat(x[s]) for s in range(s_n)], axis=1)
    fa = dot(packed, wfa_ref[...])
    fa_ref[...] = fa.reshape(fa_ref.shape)
    zero_ref(up_ref)
    zero_ref(down_ref)
    for p in range(p_n):
        down_ref[0, p : p + 1, :] = fa[p * f_n : p * f_n + 1, :]
        up_ref[0, p : p + 1, :] = fa[p * f_n + f_n - 1 : p * f_n + f_n, :]
    spread_add(i, fa.reshape(p_n, f_n, LANES), fm, fv)

    xs[...] = flat(x).astype(F32)
    n = xs.shape[0] // 4
    quarter = [xs[pl.ds(k, n, stride=4), :] for k in range(4)]
    t_n = f_n // 4
    first = lax.broadcasted_iota(jnp.int32, (n // t_n, t_n, LANES), 1) == 0
    link = m16_ref[1:2]
    taps = []
    for k in range(2):
        halo = jnp.concatenate(
            [
                jnp.broadcast_to(tail_ref[0, s, p : p + 1, k * LANES : (k + 1) * LANES], (t_n, LANES))
                for s in range(s_n)
                for p in range(p_n)
            ],
            axis=0,
        )
        moved = pltpu.roll(quarter[2 + k], 1, 0).reshape(n // t_n, t_n, LANES)
        taps.append(flat(jnp.where(first, halo.reshape(moved.shape), moved) * link))
    taps = jnp.concatenate([*taps, *quarter[:3]], axis=1).astype(BF16)
    taps_ref[...] = taps.reshape(taps_ref.shape)
    lat = dot(taps, wlat_ref[...])
    lat_ref[...] = lat.reshape(lat_ref.shape)
    spread_add(i, lat.reshape(n // t_n, t_n, lat.shape[1]), lm, lv)

    @pl.when(i == STEPS - 1)
    def _():
        zero_ref(st_ref)
        fill = m16_ref[0, :, 0:1]
        mean, m2 = spread_end(fm, fv, m64_ref[0, :, 0:1], STEPS * p_n)
        put_rows(st_ref, 0, mean)
        put_rows(st_ref, 3, m2)
        mean, m2 = spread_end(lm, lv, fill, STEPS * p_n * s_n)
        put_rows(st_ref, 1, mean)
        put_rows(st_ref, 4, m2)
        put_rows(st_ref, 6, count_row(m16_ref, STEPS * p_n * s_n))


def count_row(m16_ref, positions):
    return jnp.sum(m16_ref[0], axis=0, keepdims=True) * float(positions)


def shifted(value, first_rows, last_rows, f_n):
    n = value.shape[0]
    shape = (n // f_n, f_n, value.shape[1])
    place = lax.broadcasted_iota(jnp.int32, shape, 1)
    before = jnp.where(place == 0, first_rows, pltpu.roll(value, 1, 0).reshape(shape))
    after = jnp.where(place == f_n - 1, last_rows, pltpu.roll(value, n - 1, 0).reshape(shape))
    return before, after


def k_join(x_ref, lat_ref, fa_ref, hp_ref, hn_ref, c1_ref, m16_ref, m64_ref, wj_ref, wmid_ref,
           lact_ref, ftap_ref, sa_ref, sp_ref, fb_ref, st_ref, am, av, pm, pv, bm, bv):
    i = pl.program_id(0)
    s_n, p_n, t_n, c_slow = x_ref.shape
    c_lat = lat_ref.shape[-1]
    v = flat(lat_ref[...]) * rows(c1_ref, 0, 1, 2) + rows(c1_ref, 1, 1, 2)
    lact = (v * sig(v)).astype(BF16)
    lact_ref[...] = lact.reshape(lact_ref.shape)
    joined = jnp.concatenate([flat(x_ref[...]), lact], axis=1)
    wide = c_lat
    for n in range(wj_ref.shape[1] // wide):
        z = dot(joined, wj_ref[:, n * wide : (n + 1) * wide])
        z4 = z.reshape(s_n, p_n, t_n, wide)
        z3 = z.reshape(s_n * p_n, t_n, wide)
        if n == 0:
            sa_ref[...] = z4
            spread_add(i, z3, am, av)
        else:
            cols = slice((n - 1) * wide, n * wide)
            sp_ref[:, :, :, cols] = z4
            spread_add(i, z3, pm, pv, cols)

    f_n = fa_ref.shape[1]
    scale, shift = rows(c1_ref, 0, 0, 1), rows(c1_ref, 1, 0, 1)

    def act(z):
        w = z * scale + shift
        return (w * sig(w)).astype(BF16).astype(F32)

    fact = act(flat(fa_ref[...]))
    ends = []
    for ref in (hp_ref, hn_ref):
        small = act(ref[0])
        ends.append(
            jnp.concatenate(
                [jnp.broadcast_to(small[p : p + 1, :], (f_n, LANES)) for p in range(p_n)], axis=0
            ).reshape(p_n, f_n, LANES)
        )
    before, after = shifted(fact, ends[0], ends[1], f_n)
    ftap = jnp.concatenate(
        [flat(before * m64_ref[1:2]), fact, flat(after * m64_ref[2:3])], axis=1
    ).astype(BF16)
    ftap_ref[...] = ftap.reshape(ftap_ref.shape)
    fb = dot(ftap, wmid_ref[...])
    fb_ref[...] = fb.reshape(fb_ref.shape)
    spread_add(i, fb.reshape(p_n, f_n, LANES), bm, bv)

    @pl.when(i == STEPS - 1)
    def _():
        zero_ref(st_ref)
        fill = m16_ref[0, :, 0:1]
        positions = STEPS * p_n * s_n
        mean, m2 = spread_end(bm, bv, m64_ref[0, :, 0:1], STEPS * p_n)
        put_rows(st_ref, 0, mean)
        put_rows(st_ref, 11, m2)
        mean, m2 = spread_end(am, av, fill, positions)
        put_rows(st_ref, 1, mean)
        put_rows(st_ref, 12, m2)
        mean, m2 = spread_end(pm, pv, fill, positions)
        put_rows(st_ref, 3, mean)
        put_rows(st_ref, 14, m2)
        put_rows(st_ref, 22, count_row(m16_ref, positions))


def k_spatial(sa_ref, fb_ref, c2_ref, m16_ref, m64_ref, wsp_ref, wout_ref,
              pad_ref, sb_ref, fact_ref, st_ref, sm, sv, cm, cv):
    i = pl.program_id(0)
    h_n, w_n, t_n, c = sa_ref.shape

    @pl.when(i == 0)
    def _():
        scale, shift = rows(c2_ref, 0, 1, 2), rows(c2_ref, 1, 1, 2)
        zero_ref(pad_ref)

        @pl.loop(0, h_n)
        def _(h):
            v = flat(sa_ref[h]) * scale + shift
            pad_ref[h + 1, 1 : w_n + 1] = (v * sig(v)).astype(BF16).reshape(w_n, t_n, c)

    per = h_n // STEPS
    h0 = i * per
    acc = None
    for a in range(3):
        for b in range(3):
            k = 3 * a + b
            part = dot(flat(pad_ref[pl.ds(h0 + a, per), b : b + w_n].reshape(per * w_n, t_n, c)), wsp_ref[k])
            acc = part if acc is None else acc + part
    sb_ref[...] = acc.reshape(sb_ref.shape)
    spread_add(i, acc.reshape(per * w_n, t_n, acc.shape[1]), sm, sv)

    p_n, f_n, _ = fb_ref.shape
    v = flat(fb_ref[...]) * rows(c2_ref, 0, 0, 1) + rows(c2_ref, 1, 0, 1)
    fact = (v * sig(v)).astype(BF16)
    fact_ref[...] = fact.reshape(fact_ref.shape)
    fc = dot(fact, wout_ref[...])
    spread_add(i, fc.reshape(p_n, f_n, fc.shape[1]), cm, cv)

    @pl.when(i == STEPS - 1)
    def _():
        zero_ref(st_ref)
        mean, m2 = spread_end(cm, cv, m64_ref[0, :, 0:1], STEPS * p_n)
        put_rows(st_ref, 0, mean)
        put_rows(st_ref, 6, m2)
        mean, m2 = spread_end(sm, sv, m16_ref[0, :, 0:1], h_n * w_n)
        put_rows(st_ref, 4, mean)
        put_rows(st_ref, 10, m2)
        put_rows(st_ref, 12, count_row(m16_ref, h_n * w_n))


def k_expand(sb_ref, fact_ref, x_ref, cot_ref, c3_ref, m16_ref, m64_ref, wso_ref, wout_ref,
             sact_ref, fout_ref, df_ref, st_ref, cm, cv, s1, s2):
    i = pl.program_id(0)
    s_n, p_n, t_n, c = sb_ref.shape
    v = flat(sb_ref[...]) * rows(c3_ref, 0, 4, 2) + rows(c3_ref, 1, 4, 2)
    sact = (v * sig(v)).astype(BF16)
    sact_ref[...] = sact.reshape(sact_ref.shape)
    wide = 256
    for n in range(wso_ref.shape[1] // wide):
        cols = slice(n * wide, (n + 1) * wide)
        z = dot(sact, wso_ref[:, cols])
        spread_add(i, z.reshape(s_n * p_n, t_n, wide), cm, cv, cols)

    f_n = fact_ref.shape[1]
    fc = dot(flat(fact_ref[...]), wout_ref[...])
    fill = m64_ref[0:1]
    for s in range(s_n):
        cols = slice(s * LANES, (s + 1) * LANES)
        z = fc[:, cols].reshape(p_n, f_n, LANES)
        unit = z * rows(c3_ref, 2, s, 1) - rows(c3_ref, 3, s, 1)
        pre = z * rows(c3_ref, 0, s, 1) + rows(c3_ref, 1, s, 1) + x_ref[s].astype(F32)
        g = sig(pre)
        y = pre * g
        fout_ref[s] = (y * fill).astype(BF16)
        d = cot_ref[s].astype(F32) * fill * (g + y * (1.0 - g))
        df_ref[:, :, cols] = d
        sum_add(i, d, s1, cols)
        sum_add(i, d * unit, s2, cols)

    @pl.when(i == STEPS - 1)
    def _():
        zero_ref(st_ref)
        positions = STEPS * p_n * s_n
        mean, m2 = spread_end(cm, cv, m16_ref[0, :, 0:1], positions)
        put_rows(st_ref, 0, mean)
        put_rows(st_ref, 8, m2)
        put_rows(st_ref, 16, sum_end(s1))
        put_rows(st_ref, 20, sum_end(s2))
        put_rows(st_ref, 24, count_row(m16_ref, positions))


def back_norm(scale, p, q, dy, z, fill):
    return scale * dy - fill * (p + z * q)


def k_out(sact_ref, sp_ref, cot_ref, df_ref, fact_ref, fb_ref, c2_ref, c3_ref, c4_ref, q4_ref,
          m16_ref, m64_ref, wso_ref, wout_ref,
          out_ref, dy_ref, dfb_ref, gout_ref, up_ref, down_ref, st_ref, s1, s2, s3, t1, t2):
    i = pl.program_id(0)
    s_n, p_n, t_n, _ = sact_ref.shape
    sact = flat(sact_ref[...])
    fill = m16_ref[0:1, :, 0:1]
    wide = 256
    for n in range(wso_ref.shape[1] // wide):
        cols = slice(n * wide, (n + 1) * wide)
        shape = (s_n * p_n, t_n, wide)
        sc = dot(sact, wso_ref[:, cols]).reshape(shape)
        sp = sp_ref[:, :, :, cols].reshape(shape)
        u6 = sc * rows(c4_ref, 2, 2 * n, 2) - rows(c4_ref, 3, 2 * n, 2)
        u7 = sp * rows(c2_ref, 2, 3 + 2 * n, 2) - rows(c2_ref, 3, 3 + 2 * n, 2)
        pre = (
            sc * rows(c4_ref, 0, 2 * n, 2)
            + sp * rows(c2_ref, 0, 3 + 2 * n, 2)
            + (rows(c4_ref, 1, 2 * n, 2) + rows(c2_ref, 1, 3 + 2 * n, 2))
        )
        g = sig(pre)
        y = pre * g
        out_ref[:, :, :, cols] = (y * fill).astype(BF16).reshape(s_n, p_n, t_n, wide)
        d = cot_ref[:, :, :, cols].reshape(shape).astype(F32) * fill * (g + y * (1.0 - g))
        dy_ref[:, :, :, cols] = d.reshape(s_n, p_n, t_n, wide)
        sum_add(i, d, s1, cols)
        sum_add(i, d * u6, s2, cols)
        sum_add(i, d * u7, s3, cols)

    f_n = fact_ref.shape[1]
    fact = flat(fact_ref[...])
    fc = dot(fact, wout_ref[...])
    fill4 = m64_ref[0:1]
    parts = []
    for s in range(s_n):
        cols = slice(s * LANES, (s + 1) * LANES)
        d = back_norm(
            rows(c3_ref, 0, s, 1), rows(q4_ref, 0, s, 1), rows(q4_ref, 1, s, 1),
            df_ref[:, :, cols], fc[:, cols].reshape(p_n, f_n, LANES), fill4,
        )
        parts.append(flat(d).astype(BF16))
    dfc = jnp.concatenate(parts, axis=1)
    gout_ref[...] = jnp.where(i == 0, 0.0, gout_ref[...]) + dot_tn(fact, dfc)
    z = fb_ref[...]
    back = dot_nt(dfc, wout_ref[...]).reshape(p_n, f_n, LANES) * slope(
        z * rows(c2_ref, 0, 0, 1) + rows(c2_ref, 1, 0, 1)
    )
    dfb_ref[...] = back
    sum_add(i, back, t1)
    sum_add(i, back * (z * rows(c2_ref, 2, 0, 1) - rows(c2_ref, 3, 0, 1)), t2)
    for k, value in enumerate((back, z)):
        value = flat(value)
        for p in range(p_n):
            down_ref[0, k, p : p + 1, :] = value[p * f_n : p * f_n + 1, :]
            up_ref[0, k, p : p + 1, :] = value[p * f_n + f_n - 1 : p * f_n + f_n, :]
        down_ref[0, k, p_n : p_n + 1, :] = m64_ref[0, 0:1, :]
        up_ref[0, k, p_n : p_n + 1, :] = m64_ref[0, f_n - 1 : f_n, :]

    @pl.when(i == STEPS - 1)
    def _():
        zero_ref(st_ref)
        put_rows(st_ref, 0, sum_end(s1))
        put_rows(st_ref, 8, sum_end(s2))
        put_rows(st_ref, 16, sum_end(s3))
        put_rows(st_ref, 24, sum_end(t1))
        put_rows(st_ref, 25, sum_end(t2))


def k_back_out(dy_ref, sp_ref, sact_ref, sb_ref, dfb_ref, fb_ref, fa_ref, ftap_ref, hp_ref, hn_ref,
               c1_ref, c2_ref, c3_ref, c4_ref, q5_ref, m16_ref, m64_ref, wso_ref, wback_ref,
               dsc_ref, dsp_ref, dsb_ref, dfa_ref, gmid_ref, st_ref, s1, s2, t1, t2):
    i = pl.program_id(0)
    s_n, p_n, t_n, c = sb_ref.shape
    sact = flat(sact_ref[...])
    fill = m16_ref[0:1, :, 0:1]
    wide = 256
    back = None
    for n in range(wso_ref.shape[1] // wide):
        cols = slice(n * wide, (n + 1) * wide)
        shape = (s_n * p_n, t_n, wide)
        d = dy_ref[:, :, :, cols].reshape(shape)
        sc = dot(sact, wso_ref[:, cols]).reshape(shape)
        dsc = back_norm(rows(c4_ref, 0, 2 * n, 2), rows(q5_ref, 0, 2 * n, 2), rows(q5_ref, 1, 2 * n, 2), d, sc, fill)
        dsc = dsc.astype(BF16)
        dsc_ref[:, :, :, cols] = dsc.reshape(s_n, p_n, t_n, wide)
        sp = sp_ref[:, :, :, cols].reshape(shape)
        dsp = back_norm(
            rows(c2_ref, 0, 3 + 2 * n, 2), rows(q5_ref, 0, 8 + 2 * n, 2), rows(q5_ref, 1, 8 + 2 * n, 2), d, sp, fill
        )
        dsp_ref[:, :, :, cols] = dsp.astype(BF16).reshape(s_n, p_n, t_n, wide)
        part = dot_nt(flat(dsc), wso_ref[:, cols])
        back = part if back is None else back + part
    z = sb_ref[...].reshape(s_n * p_n, t_n, c)
    back = back.reshape(z.shape) * slope(z * rows(c3_ref, 0, 4, 2) + rows(c3_ref, 1, 4, 2))
    dsb_ref[...] = back.reshape(dsb_ref.shape)
    sum_add(i, back, s1)
    sum_add(i, back * (z * rows(c3_ref, 2, 4, 2) - rows(c3_ref, 3, 4, 2)), s2)

    f_n = fb_ref.shape[1]
    scale, p_row, q_row = rows(c2_ref, 0, 0, 1), rows(q5_ref, 0, 16, 1), rows(q5_ref, 1, 16, 1)
    dfb = back_norm(scale, p_row, q_row, dfb_ref[...], fb_ref[...], m64_ref[0:1])
    dfb_low = flat(dfb).astype(BF16)
    gmid_ref[...] = jnp.where(i == 0, 0.0, gmid_ref[...]) + dot_tn(dfb_low, flat(ftap_ref[...]))
    own = dfb_low.astype(F32)
    ends = []
    for ref in (hp_ref, hn_ref):
        small = back_norm(scale, p_row, q_row, ref[0, 0], ref[0, 1], ref[0, 0, p_n : p_n + 1, :])
        small = small.astype(BF16).astype(F32)
        ends.append(
            jnp.concatenate(
                [jnp.broadcast_to(small[p : p + 1, :], (f_n, LANES)) for p in range(p_n)], axis=0
            ).reshape(p_n, f_n, LANES)
        )
    before, after = shifted(own, ends[0], ends[1], f_n)
    taps = jnp.concatenate(
        [flat(after * m64_ref[2:3]), own, flat(before * m64_ref[1:2])], axis=1
    ).astype(BF16)
    z = fa_ref[...]
    back = dot(taps, wback_ref[...]).reshape(z.shape) * slope(
        z * rows(c1_ref, 0, 0, 1) + rows(c1_ref, 1, 0, 1)
    )
    dfa_ref[...] = back
    sum_add(i, back, t1)
    sum_add(i, back * (z * rows(c1_ref, 2, 0, 1) - rows(c1_ref, 3, 0, 1)), t2)

    @pl.when(i == STEPS - 1)
    def _():
        zero_ref(st_ref)
        put_rows(st_ref, 0, sum_end(s1))
        put_rows(st_ref, 2, sum_end(s2))
        put_rows(st_ref, 4, sum_end(t1))
        put_rows(st_ref, 5, sum_end(t2))


def k_back_spatial(dsb_ref, sb_ref, sa_ref, x_ref, dfa_ref, fa_ref, c1_ref, c2_ref, c3_ref, q6_ref,
                   m16_ref, m64_ref, wsp_ref,
                   pad_ref, dsa_ref, dlow_ref, gin_ref, st_ref, s1, s2):
    i = pl.program_id(0)
    h_n, w_n, t_n, c = sb_ref.shape

    @pl.when(i == 0)
    def _():
        scale = rows(c3_ref, 0, 4, 2)
        p_row, q_row = rows(q6_ref, 0, 0, 2), rows(q6_ref, 1, 0, 2)
        zero_ref(pad_ref)

        @pl.loop(0, h_n)
        def _(h):
            d = back_norm(scale, p_row, q_row, dsb_ref[h], sb_ref[h], m16_ref[0:1, :, 0:1])
            pad_ref[h + 1, 1 : w_n + 1] = d.astype(BF16)

    per = h_n // STEPS
    h0 = i * per
    acc = None
    for a in range(3):
        for b in range(3):
            k = 3 * a + b
            block = pad_ref[pl.ds(h0 + 2 - a, per), 2 - b : 2 - b + w_n]
            part = dot_nt(flat(block), wsp_ref[k])
            acc = part if acc is None else acc + part
    z = sa_ref[...].reshape(per * w_n, t_n, c)
    back = acc.reshape(z.shape) * slope(z * rows(c2_ref, 0, 1, 2) + rows(c2_ref, 1, 1, 2))
    dsa_ref[...] = back.reshape(dsa_ref.shape)
    sum_add(i, back, s1)
    sum_add(i, back * (z * rows(c2_ref, 2, 1, 2) - rows(c2_ref, 3, 1, 2)), s2)

    low = back_norm(
        rows(c1_ref, 0, 0, 1), rows(q6_ref, 0, 2, 1), rows(q6_ref, 1, 2, 1), dfa_ref[...], fa_ref[...], m64_ref[0:1]
    ).astype(BF16)
    dlow_ref[...] = low
    packed = jnp.concatenate([flat(x_ref[s]) for s in range(x_ref.shape[0])], axis=1)
    gin_ref[...] = jnp.where(i == 0, 0.0, gin_ref[...]) + dot_tn(flat(low), packed)

    @pl.when(i == STEPS - 1)
    def _():
        zero_ref(st_ref)
        put_rows(st_ref, 0, sum_end(s1))
        put_rows(st_ref, 2, sum_end(s2))


def k_back_join(dsa_ref, sa_ref, dsp_ref, lat_ref, c1_ref, c2_ref, q7_ref, m16_ref, wj_ref,
                low_ref, gx_ref, dlat_ref, down_ref, st_ref, s1, s2):
    i = pl.program_id(0)
    s_n, p_n, t_n, c = sa_ref.shape
    shape = (s_n * p_n, t_n, c)
    low = back_norm(
        rows(c2_ref, 0, 1, 2), rows(q7_ref, 0, 0, 2), rows(q7_ref, 1, 0, 2),
        dsa_ref[...].reshape(shape), sa_ref[...].reshape(shape), m16_ref[0:1, :, 0:1],
    ).astype(BF16)
    low_ref[...] = low.reshape(low_ref.shape)
    both = jnp.concatenate([flat(low), flat(dsp_ref[...])], axis=1)
    wide = 256
    blocks = wj_ref.shape[0] // wide
    for n in range(blocks):
        d = dot_nt(both, wj_ref[n * wide : (n + 1) * wide, :])
        if n < blocks - 1:
            gx_ref[:, :, :, n * wide : (n + 1) * wide] = d.astype(BF16).reshape(s_n, p_n, t_n, wide)
    z = lat_ref[...].reshape(shape)
    back = d.reshape(shape) * slope(z * rows(c1_ref, 0, 1, 2) + rows(c1_ref, 1, 1, 2))
    dlat_ref[...] = back.reshape(dlat_ref.shape)
    sum_add(i, back, s1)
    sum_add(i, back * (z * rows(c1_ref, 2, 1, 2) - rows(c1_ref, 3, 1, 2)), s2)
    fill = jnp.broadcast_to(m16_ref[0, 0:1, 0:1], (1, c))
    for k, value in enumerate((flat(back), flat(z))):
        for s in range(s_n):
            for p in range(p_n):
                r = (s * p_n + p) * t_n
                down_ref[0, k, s, p : p + 1, :] = value[r : r + 1, :]
            down_ref[0, k, s, p_n : p_n + 1, :] = fill

    @pl.when(i == STEPS - 1)
    def _():
        zero_ref(st_ref)
        put_rows(st_ref, 0, sum_end(s1))
        put_rows(st_ref, 2, sum_end(s2))


def k_last(dlat_ref, lat_ref, taps_ref, hn_ref, df_ref, dlow_ref, c1_ref, q8_ref, m16_ref,
           wlat_ref, wfa_ref, gx_ref, glat_ref, gs):
    i = pl.program_id(0)
    s_n, p_n, t_n, c = lat_ref.shape
    shape = (s_n * p_n, t_n, c)
    scale, p_row, q_row = rows(c1_ref, 0, 1, 2), rows(q8_ref, 0, 0, 2), rows(q8_ref, 1, 0, 2)
    low = flat(
        back_norm(scale, p_row, q_row, dlat_ref[...].reshape(shape), lat_ref[...].reshape(shape), m16_ref[0:1, :, 0:1])
    ).astype(BF16)
    glat_ref[...] = jnp.where(i == 0, 0.0, glat_ref[...]) + dot_tn(low, flat(taps_ref[...]))
    ends = []
    for s in range(s_n):
        small = back_norm(
            scale, p_row, q_row, hn_ref[0, 0, s], hn_ref[0, 1, s], hn_ref[0, 0, s, p_n : p_n + 1, :]
        )
        small = small.astype(BF16).astype(F32)
        ends += [jnp.broadcast_to(small[p : p + 1, :], (t_n, c)) for p in range(p_n)]
    ends = jnp.concatenate(ends, axis=0).reshape(shape)
    n = low.shape[0]
    moved = pltpu.roll(low.astype(F32), n - 1, 0).reshape(shape)
    place = lax.broadcasted_iota(jnp.int32, shape, 1)
    following = flat(jnp.where(place == t_n - 1, ends, moved) * m16_ref[2:3, :, 0:1]).astype(BF16)
    own = dot_nt(low, wlat_ref[2 * LANES : 5 * LANES, :])
    late = dot_nt(following, wlat_ref[0 : 2 * LANES, :])
    gs[pl.ds(0, n, stride=4), :] = own[:, 0:LANES]
    gs[pl.ds(1, n, stride=4), :] = own[:, LANES : 2 * LANES]
    gs[pl.ds(2, n, stride=4), :] = own[:, 2 * LANES :] + late[:, 0:LANES]
    gs[pl.ds(3, n, stride=4), :] = late[:, LANES:]
    back = dot_nt(flat(dlow_ref[...]), wfa_ref[...])
    for s in range(s_n):
        cols = slice(s * LANES, (s + 1) * LANES)
        total = flat(df_ref[:, :, cols]) + back[:, cols] + gs[s * n : (s + 1) * n, :]
        gx_ref[s] = total.astype(BF16).reshape(gx_ref.shape[1:])


def blockdiag(matrix, count):
    a, b = matrix.shape
    eye = jnp.eye(count, dtype=matrix.dtype)
    return (eye[:, None, :, None] * matrix[None, :, None, :]).reshape(count * a, count * b)


def fold_diag(value, count, a, b):
    blocks = value.reshape(count, a, count, b)
    return sum(blocks[s, :, s, :] for s in range(count))


def per_device(slow_input, fast_input, clip_offset, fill, w_fast_in, w_fast_mid, w_fast_out, w_lateral,
               w_slow_in, w_slow_mid, w_slow_out, w_shortcut, gains, biases, slow_cot, fast_cot):
    sizes = (lax.axis_size("path"), lax.axis_size("frames"))
    total = sizes[0] * sizes[1]
    me = lax.axis_index("path") * sizes[1] + lax.axis_index("frames")
    t_n, side, _, c_slow = slow_input.shape
    f_n, c_fast = fast_input.shape[0], fast_input.shape[3]
    in_fast, in_slow, c_lat = w_fast_in.shape[1], w_slow_in.shape[1], w_lateral.shape[2]
    pixels = side * side
    groups = LANES // in_fast
    inner = pixels // groups
    p_n = inner // STEPS

    def slow_view(a):
        return jnp.transpose(a, (1, 2, 0, 3)).reshape(groups, inner, t_n, a.shape[3])

    def fast_view(a):
        return jnp.transpose(a, (1, 2, 0, 3)).reshape(groups, inner, f_n, a.shape[3])

    def unview(a):
        return jnp.transpose(a.reshape(side, side, a.shape[2], a.shape[3]), (2, 0, 1, 3))

    x_slow, cot_slow = slow_view(slow_input), slow_view(slow_cot)
    x_fast, cot_fast = fast_view(fast_input), fast_view(fast_cot)

    filled = fill.astype(F32)
    link = (clip_offset >= 1).astype(F32)
    next_link = jnp.concatenate([link[1:], (me < total - 1).astype(F32)[None]])
    m16 = jnp.broadcast_to(jnp.stack([filled, link, next_link])[:, :, None], (3, t_n, LANES))
    ones = jnp.ones((t_n, 3), F32)
    before = jnp.concatenate([link[:, None], ones], axis=1).reshape(f_n)
    after = jnp.concatenate([ones, next_link[:, None]], axis=1).reshape(f_n)
    m64 = jnp.broadcast_to(jnp.stack([jnp.repeat(filled, 4), before, after])[:, :, None], (3, f_n, LANES))

    def norm_rows(a):
        at = [0]
        for w in (in_fast, in_fast, c_fast, c_lat, in_slow, in_slow, c_slow, c_slow):
            at.append(at[-1] + w)
        seg = [a[at[k] : at[k + 1]] for k in range(8)]
        return jnp.concatenate(
            [seg[0]] * groups + [seg[1]] * groups + [seg[2]] * groups + seg[3:]
        ).reshape(-1, LANES)

    gb = jnp.stack([norm_rows(gains), norm_rows(biases)])

    tail = x_fast.reshape(pixels, f_n, c_fast)[:, f_n - 2 :].reshape(groups, STEPS, p_n, 2 * c_fast)
    ups = [(k, k + 1) for k in range(total - 1)]
    tail = lax.ppermute(tail, AXES, ups)
    tail = jnp.pad(jnp.transpose(tail, (1, 0, 2, 3)).astype(F32), ((0, 0), (0, 0), (0, 8 - p_n), (0, 0)))

    wfa = blockdiag(w_fast_in, groups)
    wmid = jnp.concatenate([blockdiag(w_fast_mid[k], groups) for k in range(3)], axis=0)
    wback = jnp.concatenate([blockdiag(w_fast_mid[k].T, groups) for k in range(3)], axis=0)
    wout = blockdiag(w_fast_out, groups)
    wlat = w_lateral.reshape(-1, c_lat)
    wj = jnp.concatenate([w_slow_in, w_shortcut], axis=1)
    wsp = w_slow_mid.reshape(9, in_slow, in_slow)

    sl = (groups, inner, t_n)
    fp = (inner, f_n)

    def slow_out(width, dtype):
        return out_blocked(sl + (width,), dtype, 1, p_n)

    def fast_out(width, dtype):
        return out_blocked(fp + (width,), dtype, 0, p_n)

    def sb_(a):
        return blocked(a, 1, p_n)

    def fb_(a):
        return blocked(a, 0, p_n)

    def stat(n):
        return out_whole((pad8(n), LANES), F32)

    def acc(rows_n, width, count):
        return [pltpu.VMEM((rows_n, width), F32)] * count

    halo_small = out_blocked((STEPS, 8, LANES), F32, 0, 1)

    fa, lat, taps, st, up, down = call(
        k_first,
        [sb_(x_fast), blocked(tail, 0, 1), whole(m16), whole(m64), whole(wfa), whole(wlat)],
        [fast_out(LANES, F32), slow_out(c_lat, F32), slow_out(5 * c_fast, BF16), stat(7), halo_small, halo_small],
        [pltpu.VMEM((groups * p_n * f_n, c_fast), F32), *acc(f_n, LANES, 2), *acc(t_n, c_lat, 2)],
        "first",
    )
    c1, hp, hn = exchange(sizes, 1, st, gb, fwd=(("lane4", 0, 1), ("plain", 6, 2)), up=up, down=down)

    lact, ftap, sa, sp, fb, st = call(
        k_join,
        [sb_(x_slow), sb_(lat), fb_(fa), blocked(hp, 0, 1), blocked(hn, 0, 1), whole(c1), whole(m16), whole(m64),
         whole(wj), whole(wmid)],
        [slow_out(c_lat, BF16), fast_out(3 * LANES, BF16), slow_out(in_slow, F32), slow_out(c_slow, F32),
         fast_out(LANES, F32), stat(23)],
        [*acc(t_n, in_slow, 2), *acc(t_n, c_slow, 2), *acc(f_n, LANES, 2)],
        "join",
    )
    (c2,) = exchange(sizes, 2, st, gb, fwd=(("lane4", 1, 1), ("plain", 8, 2), ("plain", 20, 8)))

    rows_n = side // STEPS
    pad, sb, fact, st = call(
        k_spatial,
        [whole(sa.reshape(side, side, t_n, in_slow)),
         fb_(fb), whole(c2), whole(m16), whole(m64), whole(wsp), whole(wout)],
        [out_whole((side + 2, side + 2, t_n, in_slow), BF16),
         out_blocked((side, side, t_n, in_slow), F32, 0, rows_n), fast_out(LANES, BF16), stat(13)],
        [*acc(t_n, in_slow, 2), *acc(f_n, groups * c_fast, 2)],
        "spatial",
    )
    (c3,) = exchange(sizes, 3, st, gb, fwd=(("row4", 2, 4), ("plain", 10, 2)))

    sb4 = sb.reshape(sl + (in_slow,))
    sact, fast_y, df, st = call(
        k_expand,
        [sb_(sb4), fb_(fact), sb_(x_fast), sb_(cot_fast), whole(c3), whole(m16), whole(m64), whole(w_slow_out), whole(wout)],
        [slow_out(in_slow, BF16), out_blocked((groups, inner, f_n, c_fast), BF16, 1, p_n),
         fast_out(groups * c_fast, F32), stat(25)],
        [*acc(t_n, c_slow, 2), *acc(f_n, groups * c_fast, 2)],
        "expand",
    )
    c4, q4 = exchange(sizes, 4, st, gb, fwd=(("plain", 12, 8),), bwd=(("row4", 0, 0, 2, 4, 0, 4),), coefs=(c3,))

    halo_pair = out_blocked((STEPS, 2, 8, LANES), F32, 0, 1)
    slow_y, dy, dfb, g_fout, up, down, st = call(
        k_out,
        [sb_(sact), sb_(sp), sb_(cot_slow), fb_(df), fb_(fact), fb_(fb), whole(c2), whole(c3), whole(c4), whole(q4),
         whole(m16), whole(m64), whole(w_slow_out), whole(wout)],
        [slow_out(c_slow, BF16), slow_out(c_slow, F32), fast_out(LANES, F32),
         out_whole((LANES, groups * c_fast), F32), halo_pair, halo_pair, stat(26)],
        [*acc(t_n, c_slow, 3), *acc(f_n, LANES, 2)],
        "out",
    )
    q5, hp, hn = exchange(
        sizes, 5, st, gb,
        bwd=(("plain", 0, 0, 12, 8, 0, 8), ("plain", 1, 3, 20, 8, 0, 16), ("lane4", 1, 0, 1, 1, 24, 25)),
        coefs=(c4, c2), up=up, down=down,
    )

    dsc, dsp, dsb, dfa, g_fmid, st = call(
        k_back_out,
        [sb_(dy), sb_(sp), sb_(sact), sb_(sb4), fb_(dfb), fb_(fb), fb_(fa), fb_(ftap), blocked(hp, 0, 1), blocked(hn, 0, 1),
         whole(c1), whole(c2), whole(c3), whole(c4), whole(q5), whole(m16), whole(m64), whole(w_slow_out), whole(wback)],
        [slow_out(c_slow, BF16), slow_out(c_slow, BF16), slow_out(in_slow, F32), fast_out(LANES, F32),
         out_whole((LANES, 3 * LANES), F32), stat(6)],
        [*acc(t_n, in_slow, 2), *acc(f_n, LANES, 2)],
        "back_out",
    )
    (q6,) = exchange(
        sizes, 6, st, gb, bwd=(("plain", 0, 4, 10, 2, 0, 2), ("lane4", 1, 0, 0, 1, 4, 5)), coefs=(c3, c1)
    )

    grid = (side, side, t_n, in_slow)
    dpad, dsa, dfa_low, g_fin, st = call(
        k_back_spatial,
        [whole(dsb.reshape(grid)), whole(sb), blocked(sa.reshape(grid), 0, rows_n), sb_(x_fast), fb_(dfa), fb_(fa),
         whole(c1), whole(c2), whole(c3), whole(q6), whole(m16), whole(m64), whole(wsp)],
        [out_whole((side + 2, side + 2, t_n, in_slow), BF16), out_blocked(grid, F32, 0, rows_n), fast_out(LANES, BF16),
         out_whole((LANES, groups * c_fast), F32), stat(4)],
        [*acc(t_n, in_slow, 2)],
        "back_spatial",
    )
    (q7,) = exchange(sizes, 7, st, gb, bwd=(("plain", 0, 1, 8, 2, 0, 2),), coefs=(c2,))

    dsa_low, slow_gx, dlat, down, st = call(
        k_back_join,
        [sb_(dsa.reshape(sl + (in_slow,))), sb_(sa), sb_(dsp), sb_(lat), whole(c1), whole(c2), whole(q7), whole(m16), whole(wj)],
        [slow_out(in_slow, BF16), slow_out(c_slow, BF16), slow_out(c_lat, F32),
         out_blocked((STEPS, 2, groups, 8, c_lat), F32, 0, 1), stat(4)],
        [*acc(t_n, c_lat, 2)],
        "back_join",
    )
    q8, hn = exchange(sizes, 8, st, gb, bwd=(("plain", 0, 1, 6, 2, 0, 2),), coefs=(c1,), down=down)

    fast_gx, g_lat = call(
        k_last,
        [sb_(dlat), sb_(lat), sb_(taps), blocked(hn, 0, 1), fb_(df), fb_(dfa_low), whole(c1), whole(q8), whole(m16),
         whole(wlat), whole(wfa)],
        [out_blocked((groups, inner, f_n, c_fast), BF16, 1, p_n), out_whole((c_lat, 5 * c_fast), F32)],
        [pltpu.VMEM((groups * p_n * f_n, c_fast), F32)],
        "last",
    )

    def wgrad(a, b):
        return dot_tn(a.reshape(-1, a.shape[-1]), b.reshape(-1, b.shape[-1]))

    g_sout = wgrad(sact, dsc)
    g_short = jnp.concatenate([wgrad(x_slow, dsp), wgrad(lact, dsp)], axis=0)
    g_sin = jnp.concatenate([wgrad(x_slow, dsa_low), wgrad(lact, dsa_low)], axis=0)
    patches = jnp.concatenate(
        [pad[a : a + side, b : b + side] for a in range(3) for b in range(3)], axis=3
    )
    g_smid = wgrad(patches, dpad[1 : side + 1, 1 : side + 1]).reshape(w_slow_mid.shape)
    g_fin = fold_diag(g_fin, groups, in_fast, c_fast).T
    g_fmid = jnp.stack(
        [fold_diag(g_fmid[:, k * LANES : (k + 1) * LANES], groups, in_fast, in_fast).T for k in range(3)]
    )
    g_fout = fold_diag(g_fout, groups, in_fast, c_fast)
    g_lat = g_lat.T.reshape(w_lateral.shape)
    grads = lax.psum((g_fin, g_fmid, g_fout, g_lat, g_sin, g_smid, g_sout, g_short), AXES)

    def norm_grads(slab):
        def row(q, at, n):
            return q[slab, at : at + n].reshape(-1)

        return jnp.concatenate(
            [row(q6, 2, 1)[:in_fast], row(q5, 16, 1)[:in_fast], row(q4, 0, 1), row(q8, 0, 2), row(q7, 0, 2),
             row(q6, 0, 2), row(q5, 0, 8), row(q5, 8, 8)]
        )

    return (
        unview(slow_y),
        unview(fast_y),
        unview(slow_gx),
        unview(fast_gx),
        *grads,
        norm_grads(3),
        norm_grads(2),
    )


def solution(mesh):
    frames = P(("path", "frames"), None, None, None)
    in_specs = (frames, frames, P(AXES), P(AXES), *([P()] * 10), frames, frames)
    out_specs = (*([frames] * 4), *([P()] * 10))
    return jax.shard_map(per_device, mesh=mesh, in_specs=in_specs, out_specs=out_specs, check_vma=False)
```

time: 1180 us -> 610 us (0.52)
  blocking collectives: 528 us -> 42.9 us
  Pallas kernels: 0 us -> 242 us
  other arithmetic: 165 us -> 16 us
  matrix products: 161 us -> 29.6 us
  local copies, waits for them, and re-layouts: 115 us -> 84.9 us
  starting transfers between devices: 18.2 us -> 5.53 us
    psum x13 -> x1, blocking collectives: 528 us -> 42.9 us  [per_device(): lax.psum((g_fin, g_fmid, g_fout, g_lat, g_sin, g_smid, g_sout, g_short),...]
    pallas_call x0 -> x17, Pallas kernels: none -> 242 us  [the longest x9 147 us: call(): pl.pallas_call(kernel, grid=(STEPS,), in_specs=[pl.BlockSpec(b, m) for _,...]
    dot_general x25 -> x6, matrix products: 161 us -> 29.6 us  [dot_tn(): lax.dot_general(a, b, (((0,), (0,)), ((), ())), preferred_element_type=F32)]
    reduce_sum x13 -> x0, other arithmetic: 66.7 us -> none  [the longest x3 22.1 us: norm_backward(): jnp.sum(grad_in, axis=(0, 1))]
    convert_element_type x16 -> x2, other arithmetic: 61 us -> 1.25 us  [the longest x1 1.24 us: per_device(): filled = fill.astype(F32)]
    dot_general x1 -> x0, local copies, waits for them, and re-layouts: 19.6 us -> none  [weight_grad(): jnp.einsum('fpc,fpd->cd', inputs, grad_low, preferred_element_type=jnp.fl...]
    convert_element_type x6 -> x1, local copies, waits for them, and re-layouts: 17.8 us -> 0.69 us  [blockdiag(): eye = jnp.eye(count, dtype=matrix.dtype)]
    scatter-add x8 -> x0, other arithmetic: 16.1 us -> none  [per_device(): grid_back = grid_back.at[:, row_step:row_step + grid_side, col_step:col_s...]
  transfers between devices with their start and end apart: 7 -> 2, of which waited for: 1 -> 1; matrix products, arithmetic and copies ran while one was open for 14% -> 8% of each run, Pallas kernels for 0% -> 0%
where the time goes in v1:
time: 610 us; the launch traced here: 607 us
  Pallas kernels  242 us (40%)
  waiting for transfers between devices  172 us (28%)
  local copies, waits for them, and re-layouts  84.9 us (14%)
  blocking collectives  42.9 us (7%)
  matrix products  29.6 us (5%)
  other arithmetic  16 us (3%)
  between operations  14.6 us (2%)
    psum x1, waiting for transfers between devices, per_device(): lax.psum((g_fin, g_fmid, g_fout, g_lat, g_sin, g_smid, g_sout, g_short),...  172 us
    pallas_call x9, Pallas kernels, call(): pl.pallas_call(kernel, grid=(STEPS,), in_specs=[pl.BlockSpec(b, m) for _,...  147 us
    pallas_call x8, Pallas kernels, exchange(): pl.pallas_call(functools.partial(exchange_kernel, cfg), out_shape=outs, i...  94.9 us
    psum x1, blocking collectives, per_device(): lax.psum((g_fin, g_fmid, g_fout, g_lat, g_sin, g_smid, g_sout, g_short),...  42.9 us
    dot_general x6, matrix products, dot_tn(): lax.dot_general(a, b, (((0,), (0,)), ((), ())), preferred_element_type=F32)  29.6 us
    unnamed x92, local copies, waits for them, and re-layouts  21.9 us
    reshape x1, local copies, waits for them, and re-layouts, wgrad(): return dot_tn(a.reshape(-1, a.shape[-1]), b.reshape(-1, b.shape[-1]))  19.3 us
  transfers between devices with their start and end apart: 2, of which 1 were waited for; matrix products, arithmetic and copies ran while one was open for 8% of the time, Pallas kernels for 0%

profile of v1, /device:TPU:0, one launch (start us, length us, event | category | flops | bytes accessed | tf_op | source)
XLA Modules:
  0.0 606.9 jit_solution(15258821859188214482)
XLA Ops:
  7.2 1.1 slice.301
  9.1 5.5 collective-permute-start
  14.6 1.3 fusion.12
  15.9 1.3 slice.242
  17.2 1.3 slice.243
  18.5 1.4 slice.244
  19.9 1.4 fusion.11
  21.3 1.2 slice.234
  22.5 1.3 slice.236
  23.8 1.3 slice.237
  25.9 1.2 fusion.3
  27.2 1.2 fusion.13
  32.1 0.8 broadcast_multiply_fusion.7
  33.7 1.1 constant_dynamic-update-slice_fusion.1
  34.8 1.3 slice_bitcast_fusion.4
  38.2 1.9 broadcast_multiply_fusion.2
  40.1 1.7 mul.162
  41.7 1.7 mul.158
  43.4 1.7 mul.154
  45.1 0.8 broadcast_multiply_fusion.3
  46.6 1.7 mul.175
  49.7 0.8 concatenate.45
  50.6 0.8 concatenate.44
  52.0 2.0 constant_dynamic-update-slice_fusion.wj_ref
  54.8 1.0 pad_maximum_fusion.2.wmid_ref
  57.1 1.6 pad_convert_fusion.tail_ref
  60.1 9.0 %first.1 = (f32[49,64,128]{2,1,0:T(8,128)}, f32[4,49,16,256]{3,2,1,0:T(8,128)}, bf16[4,49,16,640]{3,2,1,0:T(8,128)(2,1)}, f32[8,128]{1,0:T(8,128)}, f32[7,8,128]{2,1,0:T(8,128)}, /*index=5*/f32[7,8,128]{2,1,0:T(8,128)}) custom-call(bf16[4,49,64,128]{3,2,1,0:T(8,128)(2,1)} %bitcast.184, f32[7,4,8,256]{3,2,1,0:T(8,128)} %pad_convert_fusion.tail_ref, ...), custom_call_target="tpu_custom_call" | custom-call | tf_op jit(solution)/shard_map/first/pallas_call | solution.py:334
  69.1 11.6 %exchange_1.1 = (f32[5,3,128]{2,1,0:T(4,128)}, f32[7,8,128]{2,1,0:T(8,128)}, f32[7,8,128]{2,1,0:T(8,128)}) custom-call(f32[8,128]{1,0:T(8,128)} %get-tuple-element.71.refs_0_, f32[2,28,128]{2,1,0:T(8,128)} %pad_maximum_fusion.5.refs_1_, f32[7,8,128]{2,1,0:T(8,128)} %get-tuple-element.72.refs_2_, f32[7,8,128]{2,1,0:T(8,128)} %get-tuple-element.73.refs_3_), custom_call_target="tpu_custom_call" | custom-call | tf_op jit(solution)/shard_map/exchange_1/pallas_call | solution.py:322
  80.7 19.5 %join.1 = (bf16[4,49,16,256]{3,2,1,0:T(8,128)(2,1)}, bf16[49,64,384]{2,1,0:T(8,128)(2,1)}, f32[4,49,16,256]{3,2,1,0:T(8,128)}, f32[4,49,16,1024]{3,2,1,0:T(8,128...) custom-call(bf16[4,49,16,1024]{3,2,1,0:T(8,128)(2,1)} %bitcast.178, f32[4,49,16,256]{3,2,1,0:T(8,128)} %get-tuple-element.69.lat_ref, ...), custom_call_target="tpu_custom_call" | custom-call | tf_op jit(solution)/shard_map/join/pallas_call | solution.py:334
  100.2 11.4 %exchange_2.1.c2_ref.refs_3_.refs_2_ = f32[5,11,128]{2,1,0:T(8,128)} custom-call(f32[24,128]{1,0:T(8,128)} %get-tuple-element.79.refs_0_, f32[2,28,128]{2,1,0:T(8,128)} %pad_maximum_fusion.5.refs_1_), custom_call_target="tpu_custom_call" | custom-call | tf_op jit(solution)/shard_map/exchange_2/pallas_call | solution.py:322
  111.6 12.5 %spatial.1 = (bf16[16,16,16,256]{3,2,1,0:T(8,128)(2,1)}, f32[14,14,16,256]{3,2,1,0:T(8,128)}, bf16[49,64,128]{2,1,0:T(8,128)(2,1)}, f32[16,128]{1,0:T(8,128)}) custom-call(f32[14,14,16,256]{3,2,1,0:T(8,128)} %bitcast.189, f32[49,64,128]{2,1,0:T(8,128)} %get-tuple-element.78.fb_ref, f32[5,11,128]{2,1,0:T(8,128)} %exchange_2.1.c2_ref.refs_3_.refs_2_, ...), custom_call_target="tpu_custom_call" | custom-call | tf_op jit(solution)/shard_map/spatial/pallas_call | solution.py:334
  124.0 10.3 %exchange_3.1.c3_ref.refs_2_ = f32[5,6,128]{2,1,0:T(8,128)} custom-call(f32[16,128]{1,0:T(8,128)} %get-tuple-element.82.refs_0_, f32[2,28,128]{2,1,0:T(8,128)} %pad_maximum_fusion.5.refs_1_), custom_call_target="tpu_custom_call" | custom-call | tf_op jit(solution)/shard_map/exchange_3/pallas_call | solution.py:322
  134.3 13.8 %expand.1 = (bf16[4,49,16,256]{3,2,1,0:T(8,128)(2,1)}, bf16[4,49,64,128]{3,2,1,0:T(8,128)(2,1)}, f32[49,64,512]{2,1,0:T(8,128)}, f32[32,128]{1,0:T(8,128)}) custom-call(f32[4,49,16,256]{3,2,1,0:T(8,128)} %bitcast.187, bf16[49,64,128]{2,1,0:T(8,128)(2,1)} %get-tuple-element.81.fact_ref, bf16[4,49,64,128]{3,2,1,0:T(8,128)(2,1)} %bitcast.185, ...), custom_call_target="tpu_custom_call" | custom-call | tf_op jit(solution)/shard_map/expand/pallas_call | solution.py:334
  148.1 10.9 %exchange_4.1 = (f32[5,8,128]{2,1,0:T(8,128)}, f32[4,4,128]{2,1,0:T(4,128)}) custom-call(f32[32,128]{1,0:T(8,128)} %get-tuple-element.86.refs_0_, f32[2,28,128]{2,1,0:T(8,128)} %pad_maximum_fusion.5.refs_1_, f32[5,6,128]{2,1,0:T(8,128)} %exchange_3.1.c3_ref.refs_2_), custom_call_target="tpu_custom_call" | custom-call | tf_op jit(solution)/shard_map/exchange_4/pallas_call | solution.py:322
  159.0 24.0 %out.1 = (bf16[4,49,16,1024]{3,2,1,0:T(8,128)(2,1)}, f32[4,49,16,1024]{3,2,1,0:T(8,128)}, f32[49,64,128]{2,1,0:T(8,128)}, f32[128,512]{1,0:T(8,128)}, f32[7,2,8,...) custom-call(bf16[4,49,16,256]{3,2,1,0:T(8,128)(2,1)} %get-tuple-element.83.sact_ref, ...), custom_call_target="tpu_custom_call" | custom-call | tf_op jit(solution)/shard_map/out/pallas_call | solution.py:334
  183.0 12.8 %exchange_5.1 = (f32[4,17,128]{2,1,0:T(8,128)}, f32[7,2,8,128]{3,2,1,0:T(8,128)}, f32[7,2,8,128]{3,2,1,0:T(8,128)}) custom-call(f32[32,128]{1,0:T(8,128)} %get-tuple-element.94.refs_0_, f32[2,28,128]{2,1,0:T(8,128)} %pad_maximum_fusion.5.refs_1_, f32[5,8,128]{2,1,0:T(8,128)} %get-tuple-element.87.c4_ref.refs_2_, ...), custom_call_target="tpu_custom_call" | custom-call | tf_op jit(solution)/shard_map/exchange_5/pallas_call | solution.py:322
  195.8 23.0 %back_out.1 = (bf16[4,49,16,1024]{3,2,1,0:T(8,128)(2,1)}, bf16[4,49,16,1024]{3,2,1,0:T(8,128)(2,1)}, f32[4,49,16,256]{3,2,1,0:T(8,128)}, f32[49,64,128]{2,1,0:T(...) custom-call(f32[4,49,16,1024]{3,2,1,0:T(8,128)} %get-tuple-element.91.dy_ref, ...), custom_call_target="tpu_custom_call" | custom-call | tf_op jit(solution)/shard_map/back_out/pallas_call | solution.py:334
  218.8 9.9 %exchange_6.1.q6_ref = f32[4,3,128]{2,1,0:T(4,128)} custom-call(f32[8,128]{1,0:T(8,128)} %get-tuple-element.102.refs_0_, f32[2,28,128]{2,1,0:T(8,128)} %pad_maximum_fusion.5.refs_1_, f32[5,6,128]{2,1,0:T(8,128)} %exchange_3.1.c3_ref.refs_2_, f32[5,3,128]{2,1,0:T(4,128)} %get-tuple-element.76.c1_ref.refs_3_.refs_2_), custom_call_target="tpu_custom_call" | custom-call | tf_op jit(solution)/shard_map/exchange_6/pallas_call | solution.py:322
  228.7 15.3 %back_spatial.1 = (bf16[16,16,16,256]{3,2,1,0:T(8,128)(2,1)}, f32[14,14,16,256]{3,2,1,0:T(8,128)}, bf16[49,64,128]{2,1,0:T(8,128)(2,1)}, f32[128,512]{1,0:T(8,128)}, f32[8,128]{1,0:T(8,128)}) custom-call(f32[14,14,16,256]{3,2,1,0:T(8,128)} %bitcast.202, f32[14,14,16,256]{3,2,1,0:T(8,128)} %get-tuple-element.80.sb_ref, f32[14,14,16,256]{3,2,1,0:T(8,128)} %bitcast.190, ...), custom_call_target="tpu_custom_call" | custom-call | tf_op jit(solution)/shard_map/back_spatial/pallas_call | solution.py:334
  244.1 11.1 %exchange_7.1.q7_ref = f32[4,2,128]{2,1,0:T(2,128)} custom-call(f32[8,128]{1,0:T(8,128)} %get-tuple-element.105.refs_0_, f32[2,28,128]{2,1,0:T(8,128)} %pad_maximum_fusion.5.refs_1_, f32[5,11,128]{2,1,0:T(8,128)} %exchange_2.1.c2_ref.refs_3_.refs_2_), custom_call_target="tpu_custom_call" | custom-call | tf_op jit(solution)/shard_map/exchange_7/pallas_call | solution.py:322
  255.2 18.1 %back_join.1 = (bf16[4,49,16,256]{3,2,1,0:T(8,128)(2,1)}, bf16[4,49,16,1024]{3,2,1,0:T(8,128)(2,1)}, f32[4,49,16,256]{3,2,1,0:T(8,128)}, f32[7,2,4,8,256]{4,3,2,1,0:T(8,128)}, f32[8,128]{1,0:T(8,128)}) custom-call(f32[4,49,16,256]{3,2,1,0:T(8,128)} %bitcast.204, f32[4,49,16,256]{3,2,1,0:T(8,128)} %get-tuple-element.77.sa_ref, ...), custom_call_target="tpu_custom_call" | custom-call | tf_op jit(solution)/shard_map/back_join/pallas_call | solution.py:334
  273.2 17.0 %exchange_8.1 = (f32[4,2,128]{2,1,0:T(2,128)}, f32[7,2,4,8,256]{4,3,2,1,0:T(8,128)}) custom-call(f32[8,128]{1,0:T(8,128)} %get-tuple-element.109.refs_0_, f32[2,28,128]{2,1,0:T(8,128)} %pad_maximum_fusion.5.refs_1_, f32[5,3,128]{2,1,0:T(4,128)} %get-tuple-element.76.c1_ref.refs_3_.refs_2_, f32[7,2,4,8,256]{4,3,2,1,0:T(8,128)} %get-tuple-element.110.refs_3_), custom_call_target="tpu_custom_call" | custom-call | tf_op jit(solution)/shard_map/exchange_8/pallas_call | solution.py:322
  290.3 11.9 %last.1 = (bf16[4,49,64,128]{3,2,1,0:T(8,128)(2,1)}, f32[256,640]{1,0:T(8,128)}) custom-call(f32[4,49,16,256]{3,2,1,0:T(8,128)} %get-tuple-element.107.dlat_ref, f32[4,49,16,256]{3,2,1,0:T(8,128)} %get-tuple-element.69.lat_ref, bf16[4,49,16,640]{3,2,1,0:T(8,128)(2,1)} %get-tuple-element.108.taps_ref, f32[7,2,4,8,256]{4,3,2,1,0:T(8,128)} %get-tuple-element.111.hn_ref, ...), custom_call_target="tpu_custom_call" | custom-call | tf_op jit(solution)/shard_map/last/pallas_call | solution.py:334
  302.1 2.2 copy.95
  304.3 5.9 convolution_bitcast_fusion.2
  310.9 0.8 copy-done
  313.0 5.1 copy-done.1
  318.1 19.3 %copy.99 = bf16[3136,2304]{0,1:T(8,128)(2,1)} copy(bf16[3136,2304]{1,0:T(8,128)(2,1)} %bitcast.194) | data formatting | bytes 28901376 | tf_op jit(solution)/shard_map/reshape | solution.py:1043
  337.4 2.8 slice.280
  340.2 5.9 convolution_bitcast_fusion.3
  346.2 2.0 convolution_bitcast_fusion.1
  348.2 9.1 %convolution_bitcast_fusion = f32[1024,1024]{1,0:T(8,128)} fusion(bf16[3136,1024]{1,0:T(8,128)(2,1)S(1)} %bitcast.193, bf16[3136,1024]{1,0:T(8,128)(2,1)S(1)} %bitcast.182), kind=kOutput, calls=%fused_computation.1 | convolution fusion | flops 6576668672 | bytes 17039360 | tf_op jit(solution)/shard_map/dot_general | solution.py:29
  357.3 1.2 pad_maximum_fusion.1
  358.5 5.9 fusion.14
  364.4 2.9 pad_maximum_fusion
  367.4 0.9 copy-done.12
  374.5 42.9 %all-reduce.3 = (f32[128,32]{0,1:T(8,128)}, f32[3,32,32]{2,1,0:T(8,128)}, f32[32,128]{1,0:T(8,128)}) all-reduce(f32[128,32]{0,1:T(8,128)S(1)} %get-tuple-element.225, f32[3,32,32]{2,1,0:T(8,128)S(1)} %pad_maximum_fusion.4, f32[32,128]{1,0:T(8,128)S(1)} %get-tuple-element.224), channel_id=1, replica_groups=mesh['path'=2,'frames'=16] {'path','frames'}, use_global_device_ids=true, to_apply=%region_0.1 | all-reduce | flops 11264 | bytes 90112 | tf_op jit(solution)/shard_map/psum | solution.py:1058
  417.4 171.5 %all-reduce.7.cloned.1.call-done = (f32[5,128,256]{2,1,0:T(8,128)}, f32[1280,256]{0,1:T(8,128)}, f32[3,3,256,256]{3,2,1,0:T(8,128)}, f32[256,1024]{1,0:T(8,128)}, f32[1280,1024]{1,0:T(8,128)}) async-done(((f32[5,128,256]{2,1,0:T(8,128)}, f32[1280,256]{0,1:T(8,128)}, f32[3,3,256,256]{3,2,1,0:T(8,128)}, f32[256,1024]{1,0:T(8,128)}, f32[1280,1024]{1,0:T(8,128)}), (f32[5,128,256]{2,1,0:T(8,128)}, ...) | async-done | bytes 10616848 | tf_op jit(solution)/shard_map/psum | solution.py:1058
  588.9 2.9 copy.105
  591.9 2.1 copy.160
  593.9 1.4 copy.161
  595.3 1.0 copy.162
  596.3 1.3 copy-done.4
  597.6 2.4 copy.163
  (139 shorter events, 22.4 us)
Async XLA Ops:
  7.2 42.5 %slice-start.8 = ((f32[3008]{0:T(1024)}), f32[64]{0:T(128)S(1)}, s32[]{:S(2)}) async-start(f32[3008]{0:T(1024)} %param.29), calls=%async_computation.9 | async-start | bytes 1024 | tf_op jit(solution)/shard_map/slice | solution.py:896
  7.2 581.7 %all-reduce.7.cloned.1.call-start = ((), (), s32[]{:S(2)}) async-start(), calls=%async_computation | async-start | bytes 21233664 | tf_op jit(solution)/shard_map/psum | solution.py:1058
  9.1 48.0 %collective-permute-start = (bf16[4,7,7,256]{3,2,0,1:T(8,128)(2,1)}, bf16[4,7,7,256]{3,2,0,1:T(8,128)(2,1)}, u32[]{:S(2)}, u32[]{:S(2)}) collective-permute-start(bf16[4,7,7,256]{3,2,0,1:T(8,128)(2,1)} %copy.65), channel_id=1, source_target_pairs={{0,1},{1,2},{2,3},{3,4},{4,5},{5,6},{6,7},{7,8},{8,9},{9,10},{10,1... | collective-permute-start | bytes 301064 | tf_op jit(solution)/shard_map/ppermute | solution.py:905
  49.0 5.8 copy-start.15
  49.0 5.8 copy-start.16
  49.0 5.8 copy-start.17
  49.0 6.8 %copy-start.18 = (bf16[128,128]{1,0:T(8,128)(2,1)S(1)}, bf16[128,128]{1,0:T(8,128)(2,1)}, u32[]{:S(2)}) copy-start(bf16[128,128]{1,0:T(8,128)(2,1)} %mul.175) | copy-start | bytes 98308
  49.7 6.0 copy-start.19
  49.7 6.0 copy-start.20
  54.0 26.7 %copy-start.2 = (bf16[1280,1280]{1,0:T(8,128)(2,1)}, bf16[1280,1280]{1,0:T(8,128)(2,1)S(1)}, u32[]{:S(2)}) copy-start(bf16[1280,1280]{1,0:T(8,128)(2,1)S(1)} %constant_dynamic-update-slice_fusion.wj_ref) | copy-start | bytes 9830404
  290.3 14.0 %copy-start.10 = (bf16[4,49,16,256]{3,2,1,0:T(8,128)(2,1)S(1)}, bf16[4,49,16,256]{3,2,1,0:T(8,128)(2,1)}, u32[]{:S(2)}) copy-start(bf16[4,49,16,256]{3,2,1,0:T(8,128)(2,1)} %get-tuple-element.120) | copy-start | bytes 4816900
  304.3 5.9 copy-start.5
  310.2 1.6 copy-start
  313.0 5.1 copy-start.1
  337.4 2.8 copy-start.3
  337.4 8.8 %slice-start = ((s8[6422528]{0:T(1024)(128)(4,1)}), s8[4194304]{0:T(1024)(128)(4,1)S(1)}, s32[]{:S(2)}) async-start(s8[6422528]{0:T(1024)(128)(4,1)} %bitcast.179), calls=%async_computation.1 | async-start | bytes 8388608
  340.2 5.9 slice-start.1
  340.2 7.9 %slice-start.2 = ((s8[6422528]{0:T(1024)(128)(4,1)}), s8[4194304]{0:T(1024)(128)(4,1)S(1)}, s32[]{:S(2)}) async-start(s8[6422528]{0:T(1024)(128)(4,1)} %bitcast.191), calls=%async_computation.3 | async-start | bytes 8388608
  346.1 2.0 slice-start.3
  346.1 12.3 %slice-start.4 = ((s8[14745600]{0:T(1024)(128)(4,1)}), s8[4194304]{0:T(1024)(128)(4,1)S(1)}, s32[]{:S(2)}) async-start(s8[14745600]{0:T(1024)(128)(4,1)} %bitcast.195), calls=%async_computation.5 | async-start | bytes 8388608
  348.1 10.3 %slice-start.5 = ((s8[14745600]{0:T(1024)(128)(4,1)}), s8[4194304]{0:T(1024)(128)(4,1)S(1)}, s32[]{:S(2)}) async-start(s8[14745600]{0:T(1024)(128)(4,1)} %bitcast.195), calls=%async_computation.6 | async-start | bytes 8388608
  348.2 10.3 %slice-start.6 = ((s8[14745600]{0:T(1024)(128)(4,1)}), s8[4194304]{0:T(1024)(128)(4,1)S(1)}, s32[]{:S(2)}) async-start(s8[14745600]{0:T(1024)(128)(4,1)} %bitcast.195), calls=%async_computation.7 | async-start | bytes 8388608
  348.2 10.3 %slice-start.7 = ((s8[14745600]{0:T(1024)(128)(4,1)}), s8[2162688]{0:T(1024)(128)(4,1)S(1)}, s32[]{:S(2)}) async-start(s8[14745600]{0:T(1024)(128)(4,1)} %bitcast.195), calls=%async_computation.8 | async-start | bytes 4325376
  348.2 10.3 %copy-start.9 = (bf16[14,14,16,256]{3,2,1,0:T(8,128)(2,1)S(1)}, bf16[14,14,16,256]{3,2,1,0:T(8,128)(2,1)}, u32[]{:S(2)}) copy-start(bf16[14,14,16,256]{3,2,1,0:T(8,128)(2,1)} %slice.280) | copy-start | bytes 4816900
  358.5 5.9 copy-start.6
  358.5 5.9 copy-start.7
  367.4 0.9 copy-start.12
  367.4 1.0 copy-start.13
  367.4 1.2 copy-start.14
  367.4 3.5 copy-start.22
  367.4 3.5 copy-start.21
  588.9 5.0 copy-start.8
  591.8 3.5 copy-start.11
  593.9 3.7 copy-start.4
Sparse Core Ops, SparseCore 0:
  367.5 221.3 all-reduce.6

commit v2 on v1

--- a/solution.py
+++ b/solution.py
@@ -379,7 +379,7 @@
     x = x_ref[...]
     s_n, p_n, f_n, _ = x.shape
     packed = jnp.concatenate([flat(x[s]) for s in range(s_n)], axis=1)
-    fa = dot(packed, wfa_ref[...])
+    fa = dot_nt(packed, wfa_ref[...])
     fa_ref[...] = fa.reshape(fa_ref.shape)
     zero_ref(up_ref)
     zero_ref(down_ref)
@@ -438,7 +438,7 @@
     return before, after
 
 
-def k_join(x_ref, lat_ref, fa_ref, hp_ref, hn_ref, c1_ref, m16_ref, m64_ref, wj_ref, wmid_ref,
+def k_join(x_ref, lat_ref, fa_ref, hp_ref, hn_ref, c1_ref, m16_ref, m64_ref, win_ref, wsc_ref, wmid_ref,
            lact_ref, ftap_ref, sa_ref, sp_ref, fb_ref, st_ref, am, av, pm, pv, bm, bv):
     i = pl.program_id(0)
     s_n, p_n, t_n, c_slow = x_ref.shape
@@ -448,8 +448,8 @@
     lact_ref[...] = lact.reshape(lact_ref.shape)
     joined = jnp.concatenate([flat(x_ref[...]), lact], axis=1)
     wide = c_lat
-    for n in range(wj_ref.shape[1] // wide):
-        z = dot(joined, wj_ref[:, n * wide : (n + 1) * wide])
+    for n in range(1 + wsc_ref.shape[1] // wide):
+        z = dot(joined, win_ref[...] if n == 0 else wsc_ref[:, (n - 1) * wide : n * wide])
         z4 = z.reshape(s_n, p_n, t_n, wide)
         z3 = z.reshape(s_n * p_n, t_n, wide)
         if n == 0:
@@ -594,7 +594,7 @@
 
 def k_out(sact_ref, sp_ref, cot_ref, df_ref, fact_ref, fb_ref, c2_ref, c3_ref, c4_ref, q4_ref,
           m16_ref, m64_ref, wso_ref, wout_ref,
-          out_ref, dy_ref, dfb_ref, gout_ref, up_ref, down_ref, st_ref, s1, s2, s3, t1, t2):
+          out_ref, dy_ref, dfb_ref, gout_ref, up_ref, down_ref, st_ref, s1, s2, s3, t1, t2, gout):
     i = pl.program_id(0)
     s_n, p_n, t_n, _ = sact_ref.shape
     sact = flat(sact_ref[...])
@@ -634,7 +634,7 @@
         )
         parts.append(flat(d).astype(BF16))
     dfc = jnp.concatenate(parts, axis=1)
-    gout_ref[...] = jnp.where(i == 0, 0.0, gout_ref[...]) + dot_tn(fact, dfc)
+    add_to(i, gout, dot_tn(fact, dfc))
     z = fb_ref[...]
     back = dot_nt(dfc, wout_ref[...]).reshape(p_n, f_n, LANES) * slope(
         z * rows(c2_ref, 0, 0, 1) + rows(c2_ref, 1, 0, 1)
@@ -658,31 +658,53 @@
         put_rows(st_ref, 16, sum_end(s3))
         put_rows(st_ref, 24, sum_end(t1))
         put_rows(st_ref, 25, sum_end(t2))
-
-
-def k_back_out(dy_ref, sp_ref, sact_ref, sb_ref, dfb_ref, fb_ref, fa_ref, ftap_ref, hp_ref, hn_ref,
+        gout_ref[...] = fold_wide(gout, s_n)
+
+
+def add_to(step, ref, value):
+    ref[...] = jnp.where(step == 0, 0.0, ref[...]) + value
+
+
+def fold_wide(ref, count):
+    a = ref.shape[0] // count
+    return sum(ref[s * a : (s + 1) * a, s * LANES : (s + 1) * LANES] for s in range(count))
+
+
+def fold_lanes(value, count):
+    a = value.shape[0] // count
+    parts = [value[s * a : (s + 1) * a, :] for s in range(count)]
+    return sum(p if s == 0 else pltpu.roll(p, LANES - s * a, 1) for s, p in enumerate(parts))
+
+
+def k_back_out(x_ref, lact_ref, dy_ref, sp_ref, sact_ref, sb_ref, dfb_ref, fb_ref, fa_ref, ftap_ref, hp_ref, hn_ref,
                c1_ref, c2_ref, c3_ref, c4_ref, q5_ref, m16_ref, m64_ref, wso_ref, wback_ref,
-               dsc_ref, dsp_ref, dsb_ref, dfa_ref, gmid_ref, st_ref, s1, s2, t1, t2):
+               gw_ref, dsp_ref, dsb_ref, dfa_ref, gmid_ref, st_ref, s1, s2, t1, t2, gsc, gso, gmid):
     i = pl.program_id(0)
     s_n, p_n, t_n, c = sb_ref.shape
     sact = flat(sact_ref[...])
     fill = m16_ref[0:1, :, 0:1]
     wide = 256
     back = None
+    turned = jnp.concatenate([flat(x_ref[...]), flat(lact_ref[...])], axis=1).T
+    sact_turned = sact.T
     for n in range(wso_ref.shape[1] // wide):
         cols = slice(n * wide, (n + 1) * wide)
         shape = (s_n * p_n, t_n, wide)
         d = dy_ref[:, :, :, cols].reshape(shape)
         sc = dot(sact, wso_ref[:, cols]).reshape(shape)
         dsc = back_norm(rows(c4_ref, 0, 2 * n, 2), rows(q5_ref, 0, 2 * n, 2), rows(q5_ref, 1, 2 * n, 2), d, sc, fill)
-        dsc = dsc.astype(BF16)
-        dsc_ref[:, :, :, cols] = dsc.reshape(s_n, p_n, t_n, wide)
+        dsc = flat(dsc.astype(BF16))
+        old = jnp.where(i == 0, 0.0, gso[:, cols])
+        gso[:, cols] = old + dot(sact_turned, dsc)
         sp = sp_ref[:, :, :, cols].reshape(shape)
         dsp = back_norm(
             rows(c2_ref, 0, 3 + 2 * n, 2), rows(q5_ref, 0, 8 + 2 * n, 2), rows(q5_ref, 1, 8 + 2 * n, 2), d, sp, fill
         )
-        dsp_ref[:, :, :, cols] = dsp.astype(BF16).reshape(s_n, p_n, t_n, wide)
-        part = dot_nt(flat(dsc), wso_ref[:, cols])
+        dsp = flat(dsp.astype(BF16))
+        dsp_ref[:, :, :, cols] = dsp.reshape(s_n, p_n, t_n, wide)
+        old = jnp.where(i == 0, 0.0, gsc[:, cols])
+        gsc[:, cols] = old + dot(turned, dsp)
+        part = dot_nt(dsc, wso_ref[:, cols])
         back = part if back is None else back + part
     z = sb_ref[...].reshape(s_n * p_n, t_n, c)
     back = back.reshape(z.shape) * slope(z * rows(c3_ref, 0, 4, 2) + rows(c3_ref, 1, 4, 2))
@@ -694,7 +716,7 @@
     scale, p_row, q_row = rows(c2_ref, 0, 0, 1), rows(q5_ref, 0, 16, 1), rows(q5_ref, 1, 16, 1)
     dfb = back_norm(scale, p_row, q_row, dfb_ref[...], fb_ref[...], m64_ref[0:1])
     dfb_low = flat(dfb).astype(BF16)
-    gmid_ref[...] = jnp.where(i == 0, 0.0, gmid_ref[...]) + dot_tn(dfb_low, flat(ftap_ref[...]))
+    add_to(i, gmid, dot_tn(dfb_low, flat(ftap_ref[...])))
     own = dfb_low.astype(F32)
     ends = []
     for ref in (hp_ref, hn_ref):
@@ -724,11 +746,20 @@
         put_rows(st_ref, 2, sum_end(s2))
         put_rows(st_ref, 4, sum_end(t1))
         put_rows(st_ref, 5, sum_end(t2))
-
-
-def k_back_spatial(dsb_ref, sb_ref, sa_ref, x_ref, dfa_ref, fa_ref, c1_ref, c2_ref, c3_ref, q6_ref,
+        for k in range(3):
+            gmid_ref[k * 32 : (k + 1) * 32, :] = fold_lanes(gmid[:, k * LANES : (k + 1) * LANES], s_n)
+        tall, low_tall = gsc.shape[0], gso.shape[0]
+        blocks = gsc.shape[1] // wide
+        for n in range(blocks):
+            cols = slice(n * wide, (n + 1) * wide)
+            gw_ref[n * tall : (n + 1) * tall, :] = gsc[:, cols].astype(BF16)
+            at = blocks * tall + n * low_tall
+            gw_ref[at : at + low_tall, :] = gso[:, cols].astype(BF16)
+
+
+def k_back_spatial(dsb_ref, sb_ref, sa_ref, spad_ref, x_ref, dfa_ref, fa_ref, gout_ref, gmid_ref, c1_ref, c2_ref, c3_ref, q6_ref,
                    m16_ref, m64_ref, wsp_ref,
-                   pad_ref, dsa_ref, dlow_ref, gin_ref, st_ref, s1, s2):
+                   dsa_ref, dlow_ref, gw_ref, gf_ref, st_ref, s1, s2, pad_ref, gsp, gin):
     i = pl.program_id(0)
     h_n, w_n, t_n, c = sb_ref.shape
 
@@ -746,9 +777,13 @@
     per = h_n // STEPS
     h0 = i * per
     acc = None
+    turned = flat(pad_ref[pl.ds(h0 + 1, per), 1 : w_n + 1]).T
     for a in range(3):
         for b in range(3):
             k = 3 * a + b
+            patch = flat(spad_ref[pl.ds(h0 + a, per), b : b + w_n])
+            cols = slice(k * c, (k + 1) * c)
+            gsp[:, cols] = jnp.where(i == 0, 0.0, gsp[:, cols]) + dot(turned, patch)
             block = pad_ref[pl.ds(h0 + 2 - a, per), 2 - b : 2 - b + w_n]
             part = dot_nt(flat(block), wsp_ref[k])
             acc = part if acc is None else acc + part
@@ -763,17 +798,25 @@
     ).astype(BF16)
     dlow_ref[...] = low
     packed = jnp.concatenate([flat(x_ref[s]) for s in range(x_ref.shape[0])], axis=1)
-    gin_ref[...] = jnp.where(i == 0, 0.0, gin_ref[...]) + dot_tn(flat(low), packed)
+    add_to(i, gin, dot_tn(flat(low), packed))
 
     @pl.when(i == STEPS - 1)
     def _():
         zero_ref(st_ref)
         put_rows(st_ref, 0, sum_end(s1))
         put_rows(st_ref, 2, sum_end(s2))
-
-
-def k_back_join(dsa_ref, sa_ref, dsp_ref, lat_ref, c1_ref, c2_ref, q7_ref, m16_ref, wj_ref,
-                low_ref, gx_ref, dlat_ref, down_ref, st_ref, s1, s2):
+        for k in range(9):
+            gw_ref[k * c : (k + 1) * c, :] = gsp[:, k * c : (k + 1) * c].T.astype(BF16)
+        gf_ref[0:32, 0:LANES] = fold_wide(gin, x_ref.shape[0])
+        gf_ref[0:32, LANES:] = gout_ref[...]
+        gf_ref[32:64, 0:LANES] = gmid_ref[0:32, :]
+        gf_ref[32:64, LANES:] = gmid_ref[32:64, :]
+        gf_ref[64:96, 0:LANES] = gmid_ref[64:96, :]
+        gf_ref[64:96, LANES:] = jnp.zeros((32, LANES), F32)
+
+
+def k_back_join(x_ref, lact_ref, dsa_ref, sa_ref, dsp_ref, lat_ref, c1_ref, c2_ref, q7_ref, m16_ref, win_ref, wsc_ref,
+                gw_ref, gx_ref, dlat_ref, down_ref, st_ref, s1, s2, gsi):
     i = pl.program_id(0)
     s_n, p_n, t_n, c = sa_ref.shape
     shape = (s_n * p_n, t_n, c)
@@ -781,12 +824,16 @@
         rows(c2_ref, 0, 1, 2), rows(q7_ref, 0, 0, 2), rows(q7_ref, 1, 0, 2),
         dsa_ref[...].reshape(shape), sa_ref[...].reshape(shape), m16_ref[0:1, :, 0:1],
     ).astype(BF16)
-    low_ref[...] = low.reshape(low_ref.shape)
-    both = jnp.concatenate([flat(low), flat(dsp_ref[...])], axis=1)
+    low = flat(low)
+    dsp = flat(dsp_ref[...])
+    turned = low.T
     wide = 256
-    blocks = wj_ref.shape[0] // wide
+    blocks = win_ref.shape[0] // wide
     for n in range(blocks):
-        d = dot_nt(both, wj_ref[n * wide : (n + 1) * wide, :])
+        part = slice(n * wide, (n + 1) * wide)
+        joined = flat(x_ref[:, :, :, part] if n < blocks - 1 else lact_ref[...])
+        gsi[:, part] = jnp.where(i == 0, 0.0, gsi[:, part]) + dot(turned, joined)
+        d = dot_nt(dsp, wsc_ref[part, :]) + dot_nt(low, win_ref[part, :])
         if n < blocks - 1:
             gx_ref[:, :, :, n * wide : (n + 1) * wide] = d.astype(BF16).reshape(s_n, p_n, t_n, wide)
     z = lat_ref[...].reshape(shape)
@@ -807,10 +854,13 @@
         zero_ref(st_ref)
         put_rows(st_ref, 0, sum_end(s1))
         put_rows(st_ref, 2, sum_end(s2))
+        for n in range(blocks):
+            part = slice(n * wide, (n + 1) * wide)
+            gw_ref[part, :] = gsi[:, part].T.astype(BF16)
 
 
 def k_last(dlat_ref, lat_ref, taps_ref, hn_ref, df_ref, dlow_ref, c1_ref, q8_ref, m16_ref,
-           wlat_ref, wfa_ref, gx_ref, glat_ref, gs):
+           wlat_ref, wfa_ref, gx_ref, gw_ref, gs, glat):
     i = pl.program_id(0)
     s_n, p_n, t_n, c = lat_ref.shape
     shape = (s_n * p_n, t_n, c)
@@ -818,7 +868,7 @@
     low = flat(
         back_norm(scale, p_row, q_row, dlat_ref[...].reshape(shape), lat_ref[...].reshape(shape), m16_ref[0:1, :, 0:1])
     ).astype(BF16)
-    glat_ref[...] = jnp.where(i == 0, 0.0, glat_ref[...]) + dot_tn(low, flat(taps_ref[...]))
+    add_to(i, glat, dot_tn(low, flat(taps_ref[...])))
     ends = []
     for s in range(s_n):
         small = back_norm(
@@ -837,29 +887,303 @@
     gs[pl.ds(1, n, stride=4), :] = own[:, LANES : 2 * LANES]
     gs[pl.ds(2, n, stride=4), :] = own[:, 2 * LANES :] + late[:, 0:LANES]
     gs[pl.ds(3, n, stride=4), :] = late[:, LANES:]
-    back = dot_nt(flat(dlow_ref[...]), wfa_ref[...])
+    back = dot(flat(dlow_ref[...]), wfa_ref[...])
     for s in range(s_n):
         cols = slice(s * LANES, (s + 1) * LANES)
         total = flat(df_ref[:, :, cols]) + back[:, cols] + gs[s * n : (s + 1) * n, :]
         gx_ref[s] = total.astype(BF16).reshape(gx_ref.shape[1:])
 
-
-def blockdiag(matrix, count):
-    a, b = matrix.shape
-    eye = jnp.eye(count, dtype=matrix.dtype)
-    return (eye[:, None, :, None] * matrix[None, :, None, :]).reshape(count * a, count * b)
-
-
-def fold_diag(value, count, a, b):
-    blocks = value.reshape(count, a, count, b)
-    return sum(blocks[s, :, s, :] for s in range(count))
+    @pl.when(i == STEPS - 1)
+    def _():
+        for k in range(glat.shape[1] // LANES):
+            part = slice(k * LANES, (k + 1) * LANES)
+            gw_ref[part, :] = glat[:, part].T.astype(BF16)
+
+
+def each(first, last, body):
+    def step(k, carry):
+        body(k)
+        return carry
+    lax.fori_loop(first, last, step, 0)
+
+
+NEAR = 4
+
+
+def reduce_kernel(cfg, *refs):
+    offsets, heights, ch, far = cfg
+    n_in = len(offsets)
+    ins = refs[:n_in]
+    (out_ref, x, land_a, buf_b, land_b, buf_c, land_c, acc,
+     sem_a, sem_b, sem_c, sem_d, sem_e, sem_f) = refs[n_in:]
+    me_p, me_f = lax.axis_index("path"), lax.axis_index("frames")
+    me_q, me_r = lax.rem(me_f, NEAR), lax.div(me_f, NEAR)
+    other = 1 - me_p
+
+    def at(path, q, r):
+        return pl.ds(pl.multiple_of(((path * NEAR + q) * far + r) * ch, 16), ch)
+
+    def q_of(k):
+        return lax.rem(me_q + k, NEAR)
+
+    def r_of(k):
+        return lax.rem(me_r + k, far)
+
+    barrier = pltpu.get_barrier_semaphore()
+    pl.semaphore_signal(barrier, inc=1, device_id=(other, me_f), device_id_type=MESH)
+    each(1, NEAR, lambda k: pl.semaphore_signal(
+        barrier, inc=1, device_id=(me_p, me_r * NEAR + q_of(k)), device_id_type=MESH))
+    each(1, far, lambda k: pl.semaphore_signal(
+        barrier, inc=1, device_id=(me_p, r_of(k) * NEAR + me_q), device_id_type=MESH))
+    end = 0
+    for ref, off, height in zip(ins, offsets, heights):
+        x[off : off + height, :] = ref[...].astype(BF16)
+        end = off + height
+    if end < x.shape[0]:
+        x[end:, :] = jnp.zeros((x.shape[0] - end, x.shape[1]), BF16)
+    pl.semaphore_wait(barrier, NEAR + far - 1)
+
+    def copy(src, dst, sem, index, device):
+        return pltpu.make_async_remote_copy(
+            src_ref=src, dst_ref=dst, send_sem=sem.at[(0, *index)], recv_sem=sem.at[(1, *index)],
+            device_id=device, device_id_type=MESH)
+
+    sibling = (other, me_f)
+
+    def pair(k, m):
+        return copy(x.at[at(other, q_of(k), r_of(m + 1))], land_a.at[k, m], sem_a, (k, m), sibling)
+
+    def plane(k, m):
+        return copy(buf_b.at[k, m], land_b.at[k, m], sem_b, (k, m), (me_p, me_r * NEAR + q_of(k)))
+
+    def line(m):
+        return copy(buf_c.at[m], land_c.at[m], sem_c, (m,), (me_p, r_of(m + 1) * NEAR + me_q))
+
+    def own(q, r):
+        return out_ref.at[at(me_p, q, r)]
+
+    def line_back(k):
+        return copy(own(me_q, me_r), own(me_q, me_r), sem_d, (k,), (me_p, r_of(k) * NEAR + me_q))
+
+    def plane_back(k, m):
+        part = own(me_q, r_of(far - m))
+        return copy(part, part, sem_e, (k, m), (me_p, me_r * NEAR + q_of(k)))
+
+    def pair_back(k, m):
+        part = own(q_of(NEAR - k), r_of(far - m))
+        return copy(part, part, sem_f, (k, m), sibling)
+
+    def both(body, first=0):
+        each(0, far, lambda m: each(first, NEAR, lambda k: body(k, m)))
+
+    def start_pair(m):
+        each(1, NEAR, lambda k: pair(k, m).start())
+        pair(0, m).start()
+
+    each(0, far, start_pair)
+
+    def add_pair(k, m):
+        pair(k, m).wait_recv()
+        buf_b[k, m] = (x[at(me_p, q_of(k), r_of(m + 1)), :].astype(F32) + land_a[k, m].astype(F32)).astype(BF16)
+        plane(k, m).start()
+
+    both(add_pair, 1)
+
+    def add_plane(m):
+        pair(0, m).wait_recv()
+        acc[...] = x[at(me_p, me_q, r_of(m + 1)), :].astype(F32) + land_a[0, m].astype(F32)
+
+        def more(k):
+            plane(k, m).wait_recv()
+            acc[...] += land_b[k, m].astype(F32)
+
+        each(1, NEAR, more)
+
+    def send_line(m):
+        add_plane(m)
+        buf_c[m] = acc[...].astype(BF16)
+        line(m).start()
+
+    each(0, far - 1, send_line)
+    add_plane(far - 1)
+
+    def add_line(m):
+        line(m).wait_recv()
+        acc[...] += land_c[m].astype(F32)
+
+    each(0, far - 1, add_line)
+    out_ref[at(me_p, me_q, me_r), :] = acc[...].astype(BF16)
+    each(1, far, lambda k: line_back(k).start())
+
+    def share(m):
+        each(1, NEAR, lambda k: plane_back(k, m).start())
+        pair_back(0, m).start()
+
+    share(0)
+
+    def relay(m):
+        line_back(m).wait_recv()
+        share(m)
+
+    each(1, far, relay)
+
+    def hand_on(k, m):
+        plane_back(k, m).wait_recv()
+        pair_back(k, m).start()
+
+    both(hand_on, 1)
+    both(lambda k, m: pair_back(k, m).wait())
+    both(lambda k, m: pair(k, m).wait_send())
+    both(lambda k, m: plane(k, m).wait_send(), 1)
+    each(0, far - 1, lambda m: line(m).wait_send())
+    each(1, far, lambda k: line_back(k).wait_send())
+    both(lambda k, m: plane_back(k, m).wait_send(), 1)
+
+
+def reduce_all(sizes, cid, parts):
+    paths, length = sizes
+    far = length // NEAR
+    unit = 16 * paths * length
+    heights = tuple(p.shape[0] for p in parts)
+    offsets = tuple(sum(heights[:k]) for k in range(len(parts)))
+    total = -(-sum(heights) // unit) * unit
+    ch = total // (paths * length)
+    vm = pl.BlockSpec(memory_space=pltpu.VMEM)
+    width = parts[0].shape[1]
+    quad = pltpu.VMEM((NEAR, far, ch, width), BF16)
+    single = pltpu.VMEM((far, ch, width), BF16)
+    out = pl.pallas_call(
+        functools.partial(reduce_kernel, (offsets, heights, ch, far)),
+        out_shape=jax.ShapeDtypeStruct((total, width), BF16),
+        in_specs=[vm] * len(parts),
+        out_specs=vm,
+        scratch_shapes=[
+            pltpu.VMEM((total, width), BF16), quad, quad, quad, single, single,
+            pltpu.VMEM((ch, width), F32),
+            *[pltpu.SemaphoreType.DMA((2, NEAR, far))] * 2,
+            *[pltpu.SemaphoreType.DMA((2, far))] * 2,
+            *[pltpu.SemaphoreType.DMA((2, NEAR, far))] * 2,
+        ],
+        compiler_params=pltpu.CompilerParams(collective_id=cid, has_side_effects=True, vmem_limit_bytes=VMEM_LIMIT),
+        name=f"reduce_{cid}",
+    )(*parts)
+    return [out[o : o + h] for o, h in zip(offsets, heights)]
+
+
+def k_prep(x_hbm, fill_ref, clip_ref, norm_ref, wfi_ref, wfm_ref, wfo_ref,
+           tail_ref, gb_ref, m16_ref, m64_ref, wfa_ref, wmid_ref, wback_ref, wout_ref,
+           near, rows_f, sent, land, sems, local):
+    length = lax.axis_size("frames")
+    total = lax.axis_size("path") * length
+    me = lax.axis_index("path") * length + lax.axis_index("frames")
+
+    def place(index):
+        return (lax.div(index, length), lax.rem(index, length))
+
+    nxt, prv = place(lax.rem(me + 1, total)), place(lax.rem(me + total - 1, total))
+    barrier = pltpu.get_barrier_semaphore()
+    pl.semaphore_signal(barrier, inc=1, device_id=nxt, device_id_type=MESH)
+    pl.semaphore_signal(barrier, inc=1, device_id=prv, device_id_type=MESH)
+    s_n, inner, t_n, c = near.shape
+    f_n = x_hbm.shape[2]
+    fetch = pltpu.make_async_copy(x_hbm.at[:, :, pl.ds(f_n - t_n, t_n), :], near, local)
+    fetch.start()
+    fetch.wait()
+    p_n = inner // STEPS
+    rows_f[...] = near[...].reshape(rows_f.shape).astype(F32)
+    zero_ref(sent)
+    count = s_n * inner
+    for k in range(2):
+        line = rows_f[pl.ds(t_n - 2 + k, count, stride=t_n), :]
+        for s in range(s_n):
+            for step in range(STEPS):
+                at = s * inner + step * p_n
+                sent[step, s, 0:p_n, k * c : (k + 1) * c] = line[at : at + p_n, :]
+    pl.semaphore_wait(barrier, 2)
+    copy = pltpu.make_async_remote_copy(
+        src_ref=sent, dst_ref=land, send_sem=sems.at[0], recv_sem=sems.at[1], device_id=nxt, device_id_type=MESH
+    )
+    copy.start()
+
+    lane = lax.broadcasted_iota(jnp.int32, (1, LANES), 1)
+    for k in range(2):
+        half = pltpu.roll(norm_ref[k], LANES // 2, 1)
+        main = jnp.where(lane < LANES // 2, half[0:23], half[1:24])
+        for j in range(2):
+            v = jnp.where(lane // 32 == j, norm_ref[k, 0:1, :], 0.0)
+            v = v + pltpu.roll(v, 64, 1)
+            gb_ref[k, j : j + 1, :] = v + pltpu.roll(v, 32, 1)
+        for j in range(4):
+            gb_ref[k, 2 + j : 3 + j, :] = main[0:1]
+        gb_ref[k, 6:28, :] = main[1:23]
+        gb_ref[k, 28:32, :] = jnp.zeros((4, LANES), F32)
+
+    def row(value):
+        return jnp.full((1, LANES), value, F32)
+
+    last = jnp.where(me < total - 1, 1.0, 0.0)
+    link = [jnp.where(clip_ref[t] >= 1, 1.0, 0.0) for t in range(t_n)]
+    for t in range(t_n):
+        filled = row(fill_ref[t].astype(F32))
+        after = row(link[t + 1] if t + 1 < t_n else last)
+        m16_ref[0, t : t + 1, :] = filled
+        m16_ref[1, t : t + 1, :] = row(link[t])
+        m16_ref[2, t : t + 1, :] = after
+        m64_ref[0, 4 * t : 4 * t + 4, :] = jnp.broadcast_to(filled, (4, LANES))
+        m64_ref[1, 4 * t : 4 * t + 1, :] = row(link[t])
+        m64_ref[1, 4 * t + 1 : 4 * t + 4, :] = jnp.ones((3, LANES), F32)
+        m64_ref[2, 4 * t : 4 * t + 3, :] = jnp.ones((3, LANES), F32)
+        m64_ref[2, 4 * t + 3 : 4 * t + 4, :] = after
+
+    zero_ref(wfa_ref)
+    zero_ref(wout_ref)
+    a = wfi_ref.shape[0]
+    for s in range(s_n):
+        wfa_ref[s * a : (s + 1) * a, s * LANES : (s + 1) * LANES] = wfi_ref[...]
+        wout_ref[s * a : (s + 1) * a, s * LANES : (s + 1) * LANES] = wfo_ref[...]
+    tall = (LANES, a)
+    spread = (lax.broadcasted_iota(jnp.int32, tall, 0) % a == lax.broadcasted_iota(jnp.int32, tall, 1)).astype(BF16)
+    square = (LANES, LANES)
+    diag = lax.broadcasted_iota(jnp.int32, square, 0) // a == lax.broadcasted_iota(jnp.int32, square, 1) // a
+    for k in range(3):
+        left = dot(spread, wfm_ref[k]).astype(BF16)
+        wmid_ref[k * LANES : (k + 1) * LANES, :] = jnp.where(diag, dot_nt(left, spread), 0.0).astype(BF16)
+        right = dot_nt(spread, wfm_ref[k]).astype(BF16)
+        wback_ref[k * LANES : (k + 1) * LANES, :] = jnp.where(diag, dot_nt(right, spread), 0.0).astype(BF16)
+    copy.wait()
+    tail_ref[...] = land[...]
+
+
+def prepare(x_fast, fill, clip_offset, norms, w_fast_in, w_fast_mid, w_fast_out):
+    s_n, inner, f_n, c = x_fast.shape
+    t_n = fill.shape[0]
+    p_n = inner // STEPS
+    vm = pl.BlockSpec(memory_space=pltpu.VMEM)
+    sm = pl.BlockSpec(memory_space=pltpu.SMEM)
+    tail = (STEPS, s_n, 8, 2 * c)
+    outs = [(tail, F32), ((2, 32, LANES), F32), ((3, t_n, LANES), F32), ((3, f_n, LANES), F32),
+            ((LANES, s_n * c), BF16), ((3 * LANES, LANES), BF16), ((3 * LANES, LANES), BF16), ((LANES, s_n * c), BF16)]
+    return pl.pallas_call(
+        k_prep,
+        out_shape=[jax.ShapeDtypeStruct(s, d) for s, d in outs],
+        in_specs=[pl.BlockSpec(memory_space=pl.ANY), sm, sm, vm, vm, vm, vm],
+        out_specs=[vm] * len(outs),
+        scratch_shapes=[
+            pltpu.VMEM((s_n, inner, t_n, c), BF16),
+            pltpu.VMEM((s_n * inner * t_n, c), F32),
+            pltpu.VMEM(tail, F32),
+            pltpu.VMEM(tail, F32),
+            pltpu.SemaphoreType.DMA((2,)),
+            pltpu.SemaphoreType.DMA,
+        ],
+        compiler_params=pltpu.CompilerParams(collective_id=10, has_side_effects=True, vmem_limit_bytes=VMEM_LIMIT),
+        name="prepare",
+    )(x_fast, fill, clip_offset, norms, w_fast_in.T, w_fast_mid, w_fast_out)
 
 
 def per_device(slow_input, fast_input, clip_offset, fill, w_fast_in, w_fast_mid, w_fast_out, w_lateral,
                w_slow_in, w_slow_mid, w_slow_out, w_shortcut, gains, biases, slow_cot, fast_cot):
     sizes = (lax.axis_size("path"), lax.axis_size("frames"))
-    total = sizes[0] * sizes[1]
-    me = lax.axis_index("path") * sizes[1] + lax.axis_index("frames")
     t_n, side, _, c_slow = slow_input.shape
     f_n, c_fast = fast_input.shape[0], fast_input.shape[3]
     in_fast, in_slow, c_lat = w_fast_in.shape[1], w_slow_in.shape[1], w_lateral.shape[2]
@@ -880,37 +1204,12 @@
     x_slow, cot_slow = slow_view(slow_input), slow_view(slow_cot)
     x_fast, cot_fast = fast_view(fast_input), fast_view(fast_cot)
 
-    filled = fill.astype(F32)
-    link = (clip_offset >= 1).astype(F32)
-    next_link = jnp.concatenate([link[1:], (me < total - 1).astype(F32)[None]])
-    m16 = jnp.broadcast_to(jnp.stack([filled, link, next_link])[:, :, None], (3, t_n, LANES))
-    ones = jnp.ones((t_n, 3), F32)
-    before = jnp.concatenate([link[:, None], ones], axis=1).reshape(f_n)
-    after = jnp.concatenate([ones, next_link[:, None]], axis=1).reshape(f_n)
-    m64 = jnp.broadcast_to(jnp.stack([jnp.repeat(filled, 4), before, after])[:, :, None], (3, f_n, LANES))
-
-    def norm_rows(a):
-        at = [0]
-        for w in (in_fast, in_fast, c_fast, c_lat, in_slow, in_slow, c_slow, c_slow):
-            at.append(at[-1] + w)
-        seg = [a[at[k] : at[k + 1]] for k in range(8)]
-        return jnp.concatenate(
-            [seg[0]] * groups + [seg[1]] * groups + [seg[2]] * groups + seg[3:]
-        ).reshape(-1, LANES)
-
-    gb = jnp.stack([norm_rows(gains), norm_rows(biases)])
-
-    tail = x_fast.reshape(pixels, f_n, c_fast)[:, f_n - 2 :].reshape(groups, STEPS, p_n, 2 * c_fast)
-    ups = [(k, k + 1) for k in range(total - 1)]
-    tail = lax.ppermute(tail, AXES, ups)
-    tail = jnp.pad(jnp.transpose(tail, (1, 0, 2, 3)).astype(F32), ((0, 0), (0, 0), (0, 8 - p_n), (0, 0)))
-
-    wfa = blockdiag(w_fast_in, groups)
-    wmid = jnp.concatenate([blockdiag(w_fast_mid[k], groups) for k in range(3)], axis=0)
-    wback = jnp.concatenate([blockdiag(w_fast_mid[k].T, groups) for k in range(3)], axis=0)
-    wout = blockdiag(w_fast_out, groups)
+    norms = jnp.stack([gains, biases])
+    norms = jnp.pad(norms, ((0, 0), (0, -norms.shape[1] % (8 * LANES)))).reshape(2, -1, LANES)
+    tail, gb, m16, m64, wfa, wmid, wback, wout = prepare(
+        x_fast, fill, clip_offset, norms, w_fast_in, w_fast_mid, w_fast_out
+    )
     wlat = w_lateral.reshape(-1, c_lat)
-    wj = jnp.concatenate([w_slow_in, w_shortcut], axis=1)
     wsp = w_slow_mid.reshape(9, in_slow, in_slow)
 
     sl = (groups, inner, t_n)
@@ -948,7 +1247,7 @@
     lact, ftap, sa, sp, fb, st = call(
         k_join,
         [sb_(x_slow), sb_(lat), fb_(fa), blocked(hp, 0, 1), blocked(hn, 0, 1), whole(c1), whole(m16), whole(m64),
-         whole(wj), whole(wmid)],
+         whole(w_slow_in), whole(w_shortcut), whole(wmid)],
         [slow_out(c_lat, BF16), fast_out(3 * LANES, BF16), slow_out(in_slow, F32), slow_out(c_slow, F32),
          fast_out(LANES, F32), stat(23)],
         [*acc(t_n, in_slow, 2), *acc(t_n, c_slow, 2), *acc(f_n, LANES, 2)],
@@ -985,8 +1284,8 @@
         [sb_(sact), sb_(sp), sb_(cot_slow), fb_(df), fb_(fact), fb_(fb), whole(c2), whole(c3), whole(c4), whole(q4),
          whole(m16), whole(m64), whole(w_slow_out), whole(wout)],
         [slow_out(c_slow, BF16), slow_out(c_slow, F32), fast_out(LANES, F32),
-         out_whole((LANES, groups * c_fast), F32), halo_pair, halo_pair, stat(26)],
-        [*acc(t_n, c_slow, 3), *acc(f_n, LANES, 2)],
+         out_whole((in_fast, c_fast), F32), halo_pair, halo_pair, stat(26)],
+        [*acc(t_n, c_slow, 3), *acc(f_n, LANES, 2), *acc(LANES, groups * c_fast, 1)],
         "out",
     )
     q5, hp, hn = exchange(
@@ -995,13 +1294,15 @@
         coefs=(c4, c2), up=up, down=down,
     )
 
-    dsc, dsp, dsb, dfa, g_fmid, st = call(
+    c_cat = w_slow_in.shape[0]
+    gw_out, dsp, dsb, dfa, g_fmid, st = call(
         k_back_out,
-        [sb_(dy), sb_(sp), sb_(sact), sb_(sb4), fb_(dfb), fb_(fb), fb_(fa), fb_(ftap), blocked(hp, 0, 1), blocked(hn, 0, 1),
+        [sb_(x_slow), sb_(lact), sb_(dy), sb_(sp), sb_(sact), sb_(sb4), fb_(dfb), fb_(fb), fb_(fa), fb_(ftap), blocked(hp, 0, 1), blocked(hn, 0, 1),
          whole(c1), whole(c2), whole(c3), whole(c4), whole(q5), whole(m16), whole(m64), whole(w_slow_out), whole(wback)],
-        [slow_out(c_slow, BF16), slow_out(c_slow, BF16), slow_out(in_slow, F32), fast_out(LANES, F32),
-         out_whole((LANES, 3 * LANES), F32), stat(6)],
-        [*acc(t_n, in_slow, 2), *acc(f_n, LANES, 2)],
+        [out_whole(((c_cat + in_slow) * c_slow // in_slow, in_slow), BF16), slow_out(c_slow, BF16),
+         slow_out(in_slow, F32), fast_out(LANES, F32), out_whole((3 * in_fast, LANES), F32), stat(6)],
+        [*acc(t_n, in_slow, 2), *acc(f_n, LANES, 2), *acc(c_cat, c_slow, 1), *acc(in_slow, c_slow, 1),
+         *acc(LANES, 3 * LANES, 1)],
         "back_out",
     )
     (q6,) = exchange(
@@ -1009,53 +1310,58 @@
     )
 
     grid = (side, side, t_n, in_slow)
-    dpad, dsa, dfa_low, g_fin, st = call(
+    dsa, dfa_low, gw_mid, gw_fast, st = call(
         k_back_spatial,
-        [whole(dsb.reshape(grid)), whole(sb), blocked(sa.reshape(grid), 0, rows_n), sb_(x_fast), fb_(dfa), fb_(fa),
-         whole(c1), whole(c2), whole(c3), whole(q6), whole(m16), whole(m64), whole(wsp)],
-        [out_whole((side + 2, side + 2, t_n, in_slow), BF16), out_blocked(grid, F32, 0, rows_n), fast_out(LANES, BF16),
-         out_whole((LANES, groups * c_fast), F32), stat(4)],
-        [*acc(t_n, in_slow, 2)],
+        [whole(dsb.reshape(grid)), whole(sb), blocked(sa.reshape(grid), 0, rows_n), whole(pad), sb_(x_fast), fb_(dfa), fb_(fa),
+         whole(g_fout), whole(g_fmid), whole(c1), whole(c2), whole(c3), whole(q6), whole(m16), whole(m64), whole(wsp)],
+        [out_blocked(grid, F32, 0, rows_n), fast_out(LANES, BF16), out_whole((9 * in_slow, in_slow), BF16),
+         out_whole((3 * in_fast, 2 * LANES), F32), stat(4)],
+        [*acc(t_n, in_slow, 2), pltpu.VMEM((side + 2, side + 2, t_n, in_slow), BF16), *acc(in_slow, 9 * in_slow, 1),
+         *acc(LANES, groups * c_fast, 1)],
         "back_spatial",
     )
     (q7,) = exchange(sizes, 7, st, gb, bwd=(("plain", 0, 1, 8, 2, 0, 2),), coefs=(c2,))
 
-    dsa_low, slow_gx, dlat, down, st = call(
+    gw_in, slow_gx, dlat, down, st = call(
         k_back_join,
-        [sb_(dsa.reshape(sl + (in_slow,))), sb_(sa), sb_(dsp), sb_(lat), whole(c1), whole(c2), whole(q7), whole(m16), whole(wj)],
-        [slow_out(in_slow, BF16), slow_out(c_slow, BF16), slow_out(c_lat, F32),
+        [sb_(x_slow), sb_(lact), sb_(dsa.reshape(sl + (in_slow,))), sb_(sa), sb_(dsp), sb_(lat), whole(c1), whole(c2), whole(q7), whole(m16),
+         whole(w_slow_in), whole(w_shortcut)],
+        [out_whole((c_cat, in_slow), BF16), slow_out(c_slow, BF16), slow_out(c_lat, F32),
          out_blocked((STEPS, 2, groups, 8, c_lat), F32, 0, 1), stat(4)],
-        [*acc(t_n, c_lat, 2)],
+        [*acc(t_n, c_lat, 2), *acc(in_slow, c_cat, 1)],
         "back_join",
     )
     q8, hn = exchange(sizes, 8, st, gb, bwd=(("plain", 0, 1, 6, 2, 0, 2),), coefs=(c1,), down=down)
 
-    fast_gx, g_lat = call(
+    fast_gx, gw_lat = call(
         k_last,
         [sb_(dlat), sb_(lat), sb_(taps), blocked(hn, 0, 1), fb_(df), fb_(dfa_low), whole(c1), whole(q8), whole(m16),
          whole(wlat), whole(wfa)],
-        [out_blocked((groups, inner, f_n, c_fast), BF16, 1, p_n), out_whole((c_lat, 5 * c_fast), F32)],
-        [pltpu.VMEM((groups * p_n * f_n, c_fast), F32)],
+        [out_blocked((groups, inner, f_n, c_fast), BF16, 1, p_n), out_whole((5 * c_fast, c_lat), BF16)],
+        [pltpu.VMEM((groups * p_n * f_n, c_fast), F32), *acc(c_lat, 5 * c_fast, 1)],
         "last",
     )
 
-    def wgrad(a, b):
-        return dot_tn(a.reshape(-1, a.shape[-1]), b.reshape(-1, b.shape[-1]))
-
-    g_sout = wgrad(sact, dsc)
-    g_short = jnp.concatenate([wgrad(x_slow, dsp), wgrad(lact, dsp)], axis=0)
-    g_sin = jnp.concatenate([wgrad(x_slow, dsa_low), wgrad(lact, dsa_low)], axis=0)
-    patches = jnp.concatenate(
-        [pad[a : a + side, b : b + side] for a in range(3) for b in range(3)], axis=3
-    )
-    g_smid = wgrad(patches, dpad[1 : side + 1, 1 : side + 1]).reshape(w_slow_mid.shape)
-    g_fin = fold_diag(g_fin, groups, in_fast, c_fast).T
-    g_fmid = jnp.stack(
-        [fold_diag(g_fmid[:, k * LANES : (k + 1) * LANES], groups, in_fast, in_fast).T for k in range(3)]
-    )
-    g_fout = fold_diag(g_fout, groups, in_fast, c_fast)
-    g_lat = g_lat.T.reshape(w_lateral.shape)
-    grads = lax.psum((g_fin, g_fmid, g_fout, g_lat, g_sin, g_smid, g_sout, g_short), AXES)
+    gw_out, gw_mid, gw_in, gw_lat, gw_fast = [
+        g.astype(F32) for g in reduce_all(sizes, 9, [gw_out, gw_mid, gw_in, gw_lat, gw_fast])
+    ]
+    blocks = c_slow // in_slow
+    g_short, g_sout = [
+        jnp.transpose(g.reshape(blocks, -1, in_slow), (1, 0, 2)).reshape(-1, c_slow)
+        for g in (gw_out[: blocks * c_cat], gw_out[blocks * c_cat :])
+    ]
+    taps_t = [gw_fast[in_fast : 2 * in_fast, :in_fast], gw_fast[in_fast : 2 * in_fast, c_fast : c_fast + in_fast],
+              gw_fast[2 * in_fast :, :in_fast]]
+    grads = (
+        gw_fast[:in_fast, :c_fast].T,
+        jnp.transpose(jnp.stack(taps_t), (0, 2, 1)),
+        gw_fast[:in_fast, c_fast:],
+        gw_lat.reshape(w_lateral.shape),
+        gw_in,
+        gw_mid.reshape(w_slow_mid.shape),
+        g_sout,
+        g_short,
+    )
 
     def norm_grads(slab):
         def row(q, at, n):

time: 610 us -> 366 us (0.60)
  waiting for transfers between devices: 172 us -> 0 us
  Pallas kernels: 242 us -> 343 us
  local copies, waits for them, and re-layouts: 84.9 us -> 15 us
  blocking collectives: 42.9 us -> 0 us
  matrix products: 29.6 us -> 0 us
  between operations: 14.6 us -> 0.86 us
  other arithmetic: 16 us -> 5.83 us
    psum x1 -> x0, waiting for transfers between devices: 172 us -> none  [per_device(): lax.psum((g_fin, g_fmid, g_fout, g_lat, g_sin, g_smid, g_sout, g_short),...]
    pallas_call x0 -> x2, Pallas kernels: none -> 90.8 us  [the longest x1 76 us: reduce_all(): pl.pallas_call(functools.partial(reduce_kernel, (offsets, heights, ch, fa...]
    psum x1 -> x0, blocking collectives: 42.9 us -> none  [per_device(): lax.psum((g_fin, g_fmid, g_fout, g_lat, g_sin, g_smid, g_sout, g_short),...]
    dot_general x6 -> x0, matrix products: 29.6 us -> none  [dot_tn(): lax.dot_general(a, b, (((0,), (0,)), ((), ())), preferred_element_type=F32)]
    unnamed x92 -> x10, local copies, waits for them, and re-layouts: 21.9 us -> 4.73 us
    reshape x8 -> x2, local copies, waits for them, and re-layouts: 20.7 us -> 4.1 us  [per_device(): jnp.transpose(g.reshape(blocks, -1, in_slow), (1, 0, 2)).reshape(-1, c_slow)]
    slice x20 -> x7, local copies, waits for them, and re-layouts: 15.8 us -> 1.96 us  [the longest x3 1 us: reduce_all(): return [out[o:o + h] for o, h in zip(offsets, heights)]]
    pallas_call x9, Pallas kernels: 147 us -> 158 us  [call(): pl.pallas_call(kernel, grid=(STEPS,), in_specs=[pl.BlockSpec(b, m) for _,...]
  transfers between devices with their start and end apart: 2 -> 0, of which waited for: 1 -> 0; matrix products, arithmetic and copies ran while one was open for 8% -> 0% of each run, Pallas kernels for 0% -> 0%
where the time goes in v2:
time: 366 us; the launch traced here: 364 us
  Pallas kernels  343 us (94%)
  local copies, waits for them, and re-layouts  15 us (4%)
  other arithmetic  5.83 us (2%)
    pallas_call x9, Pallas kernels, call(): pl.pallas_call(kernel, grid=(STEPS,), in_specs=[pl.BlockSpec(b, m) for _,...  158 us
    pallas_call x8, Pallas kernels, exchange(): pl.pallas_call(functools.partial(exchange_kernel, cfg), out_shape=outs, i...  93.8 us
    pallas_call x1, Pallas kernels, reduce_all(): pl.pallas_call(functools.partial(reduce_kernel, (offsets, heights, ch, fa...  76 us
    pallas_call x1, Pallas kernels, prepare(): pl.pallas_call(k_prep, out_shape=[jax.ShapeDtypeStruct(s, d) for s, d in...  14.9 us

profile of v2, /device:TPU:0, one launch (start us, length us, event | category | flops | bytes accessed | tf_op | source)
XLA Modules:
  0.0 364.3 jit_solution(1545579808129923958)
XLA Ops:
  0.6 0.8 fusion
  1.4 0.6 copy.37
  2.0 14.9 %prepare.1 = (f32[7,4,8,256]{3,2,1,0:T(8,128)}, f32[2,32,128]{2,1,0:T(8,128)}, f32[3,16,128]{2,1,0:T(8,128)}, f32[3,64,128]{2,1,0:T(8,128)}, bf16[128,512]{1,0:T...) custom-call(bf16[4,49,64,128]{3,2,1,0:T(8,128)(2,1)} %bitcast.97, ...), custom_call_target="tpu_custom_call" | custom-call | tf_op jit(solution)/shard_map/prepare/pallas_call | solution.py:1166
  16.9 9.0 %first.1 = (f32[49,64,128]{2,1,0:T(8,128)}, f32[4,49,16,256]{3,2,1,0:T(8,128)}, bf16[4,49,16,640]{3,2,1,0:T(8,128)(2,1)}, f32[8,128]{1,0:T(8,128)}, f32[7,8,128]{2,1,0:T(8,128)}, /*index=5*/f32[7,8,128]{2,1,0:T(8,128)}) custom-call(bf16[4,49,64,128]{3,2,1,0:T(8,128)(2,1)} %bitcast.98, f32[7,4,8,256]{3,2,1,0:T(8,128)} %get-tuple-element.77.tail_ref, ...), custom_call_target="tpu_custom_call" | custom-call | tf_op jit(solution)/shard_map/first/pallas_call | solution.py:334
  25.9 11.8 %exchange_1.1 = (f32[5,3,128]{2,1,0:T(4,128)}, f32[7,8,128]{2,1,0:T(8,128)}, f32[7,8,128]{2,1,0:T(8,128)}) custom-call(f32[8,128]{1,0:T(8,128)} %get-tuple-element.83.refs_0_, f32[2,32,128]{2,1,0:T(8,128)} %get-tuple-element.84.refs_1_, f32[7,8,128]{2,1,0:T(8,128)} %get-tuple-element.85.refs_2_, f32[7,8,128]{2,1,0:T(8,128)} %get-tuple-element.86.refs_3_), custom_call_target="tpu_custom_call" | custom-call | tf_op jit(solution)/shard_map/exchange_1/pallas_call | solution.py:322
  37.7 19.6 %join.1 = (bf16[4,49,16,256]{3,2,1,0:T(8,128)(2,1)}, bf16[49,64,384]{2,1,0:T(8,128)(2,1)}, f32[4,49,16,256]{3,2,1,0:T(8,128)}, f32[4,49,16,1024]{3,2,1,0:T(8,128...) custom-call(bf16[4,49,16,1024]{3,2,1,0:T(8,128)(2,1)} %bitcast.94, f32[4,49,16,256]{3,2,1,0:T(8,128)} %get-tuple-element.81.lat_ref, ...), custom_call_target="tpu_custom_call" | custom-call | tf_op jit(solution)/shard_map/join/pallas_call | solution.py:334
  57.3 10.1 %exchange_2.1.c2_ref.refs_3_.refs_2_ = f32[5,11,128]{2,1,0:T(8,128)} custom-call(f32[24,128]{1,0:T(8,128)} %get-tuple-element.93.refs_0_, f32[2,32,128]{2,1,0:T(8,128)} %get-tuple-element.84.refs_1_), custom_call_target="tpu_custom_call" | custom-call | tf_op jit(solution)/shard_map/exchange_2/pallas_call | solution.py:322
  67.4 12.5 %spatial.1 = (bf16[16,16,16,256]{3,2,1,0:T(8,128)(2,1)}, f32[14,14,16,256]{3,2,1,0:T(8,128)}, bf16[49,64,128]{2,1,0:T(8,128)(2,1)}, f32[16,128]{1,0:T(8,128)}) custom-call(f32[14,14,16,256]{3,2,1,0:T(8,128)} %bitcast.103, f32[49,64,128]{2,1,0:T(8,128)} %get-tuple-element.92.fb_ref, f32[5,11,128]{2,1,0:T(8,128)} %exchange_2.1.c2_ref.refs_3_.refs_2_, ...), custom_call_target="tpu_custom_call" | custom-call | tf_op jit(solution)/shard_map/spatial/pallas_call | solution.py:334
  79.9 11.1 %exchange_3.1.c3_ref.refs_2_ = f32[5,6,128]{2,1,0:T(8,128)} custom-call(f32[16,128]{1,0:T(8,128)} %get-tuple-element.97.refs_0_, f32[2,32,128]{2,1,0:T(8,128)} %get-tuple-element.84.refs_1_), custom_call_target="tpu_custom_call" | custom-call | tf_op jit(solution)/shard_map/exchange_3/pallas_call | solution.py:322
  90.9 13.8 %expand.1 = (bf16[4,49,16,256]{3,2,1,0:T(8,128)(2,1)}, bf16[4,49,64,128]{3,2,1,0:T(8,128)(2,1)}, f32[49,64,512]{2,1,0:T(8,128)}, f32[32,128]{1,0:T(8,128)}) custom-call(f32[4,49,16,256]{3,2,1,0:T(8,128)} %bitcast.101, bf16[49,64,128]{2,1,0:T(8,128)(2,1)} %get-tuple-element.96.fact_ref, bf16[4,49,64,128]{3,2,1,0:T(8,128)(2,1)} %bitcast.99, ...), custom_call_target="tpu_custom_call" | custom-call | tf_op jit(solution)/shard_map/expand/pallas_call | solution.py:334
  104.7 10.1 %exchange_4.1 = (f32[5,8,128]{2,1,0:T(8,128)}, f32[4,4,128]{2,1,0:T(4,128)}) custom-call(f32[32,128]{1,0:T(8,128)} %get-tuple-element.101.refs_0_, f32[2,32,128]{2,1,0:T(8,128)} %get-tuple-element.84.refs_1_, f32[5,6,128]{2,1,0:T(8,128)} %exchange_3.1.c3_ref.refs_2_), custom_call_target="tpu_custom_call" | custom-call | tf_op jit(solution)/shard_map/exchange_4/pallas_call | solution.py:322
  114.9 0.7 slice_bitcast_fusion.14
  115.5 23.8 %out.1 = (bf16[4,49,16,1024]{3,2,1,0:T(8,128)(2,1)}, f32[4,49,16,1024]{3,2,1,0:T(8,128)}, f32[49,64,128]{2,1,0:T(8,128)}, f32[32,128]{1,0:T(8,128)}, f32[7,2,8,1...) custom-call(bf16[4,49,16,256]{3,2,1,0:T(8,128)(2,1)} %get-tuple-element.98.sact_ref, ...), custom_call_target="tpu_custom_call" | custom-call | tf_op jit(solution)/shard_map/out/pallas_call | solution.py:334
  139.4 12.8 %exchange_5.1 = (f32[4,17,128]{2,1,0:T(8,128)}, f32[7,2,8,128]{3,2,1,0:T(8,128)}, f32[7,2,8,128]{3,2,1,0:T(8,128)}) custom-call(f32[32,128]{1,0:T(8,128)} %get-tuple-element.110.refs_0_, f32[2,32,128]{2,1,0:T(8,128)} %get-tuple-element.84.refs_1_, f32[5,8,128]{2,1,0:T(8,128)} %get-tuple-element.102.c4_ref.refs_2_, ...), custom_call_target="tpu_custom_call" | custom-call | tf_op jit(solution)/shard_map/exchange_5/pallas_call | solution.py:322
  152.2 28.2 %back_out.1 = (bf16[6144,256]{1,0:T(8,128)(2,1)}, bf16[4,49,16,1024]{3,2,1,0:T(8,128)(2,1)}, f32[4,49,16,256]{3,2,1,0:T(8,128)}, f32[49,64,128]{2,1,0:T(8,128)}, f32[96,128]{1,0:T(8,128)}, /*index=5*/f32[8,128]{1,0:T(8,128)}) custom-call(bf16[4,49,16,1024]{3,2,1,0:T(8,128)(2,1)} %bitcast.95, bf16[4,49,16,256]{3,2,1,0:T(8,128)(2,1)} %get-tuple-element.106.lact_ref, ...), custom_call_target="tpu_custom_call" | custom-call | tf_op jit(solution)/shard_map/back_out/pallas_call | solution.py:334
  180.3 9.8 %exchange_6.1.q6_ref = f32[4,3,128]{2,1,0:T(4,128)} custom-call(f32[8,128]{1,0:T(8,128)} %get-tuple-element.122.refs_0_, f32[2,32,128]{2,1,0:T(8,128)} %get-tuple-element.84.refs_1_, f32[5,6,128]{2,1,0:T(8,128)} %exchange_3.1.c3_ref.refs_2_, f32[5,3,128]{2,1,0:T(4,128)} %get-tuple-element.89.c1_ref.refs_3_.refs_2_), custom_call_target="tpu_custom_call" | custom-call | tf_op jit(solution)/shard_map/exchange_6/pallas_call | solution.py:322
  190.2 18.3 %back_spatial.1 = (f32[14,14,16,256]{3,2,1,0:T(8,128)}, bf16[49,64,128]{2,1,0:T(8,128)(2,1)}, bf16[2304,256]{1,0:T(8,128)(2,1)}, f32[96,256]{1,0:T(8,128)}, f32[8,128]{1,0:T(8,128)}) custom-call(f32[14,14,16,256]{3,2,1,0:T(8,128)} %bitcast.114, f32[14,14,16,256]{3,2,1,0:T(8,128)} %get-tuple-element.95.sb_ref, f32[14,14,16,256]{3,2,1,0:T(8,128)} %bitcast.104, ...), custom_call_target="tpu_custom_call" | custom-call | tf_op jit(solution)/shard_map/back_spatial/pallas_call | solution.py:334
  208.5 0.7 slice_bitcast_fusion.15
  209.2 0.7 slice_bitcast_fusion.4
  209.9 11.1 %exchange_7.1.q7_ref = f32[4,2,128]{2,1,0:T(2,128)} custom-call(f32[8,128]{1,0:T(8,128)} %get-tuple-element.125.refs_0_, f32[2,32,128]{2,1,0:T(8,128)} %get-tuple-element.84.refs_1_, f32[5,11,128]{2,1,0:T(8,128)} %exchange_2.1.c2_ref.refs_3_.refs_2_), custom_call_target="tpu_custom_call" | custom-call | tf_op jit(solution)/shard_map/exchange_7/pallas_call | solution.py:322
  221.0 0.0 copy-start.2
  221.0 20.5 %back_join.1 = (bf16[1280,256]{1,0:T(8,128)(2,1)}, bf16[4,49,16,1024]{3,2,1,0:T(8,128)(2,1)}, f32[4,49,16,256]{3,2,1,0:T(8,128)}, f32[7,2,4,8,256]{4,3,2,1,0:T(8,128)}, f32[8,128]{1,0:T(8,128)}) custom-call(bf16[4,49,16,1024]{3,2,1,0:T(8,128)(2,1)} %bitcast.96, bf16[4,49,16,256]{3,2,1,0:T(8,128)(2,1)} %get-tuple-element.106.lact_ref, ...), custom_call_target="tpu_custom_call" | custom-call | tf_op jit(solution)/shard_map/back_join/pallas_call | solution.py:334
  241.6 0.0 copy-done.2
  241.6 0.7 slice_bitcast_fusion.8
  242.3 17.0 %exchange_8.1 = (f32[4,2,128]{2,1,0:T(2,128)}, f32[7,2,4,8,256]{4,3,2,1,0:T(8,128)}) custom-call(f32[8,128]{1,0:T(8,128)} %get-tuple-element.129.refs_0_, f32[2,32,128]{2,1,0:T(8,128)} %get-tuple-element.84.refs_1_, f32[5,3,128]{2,1,0:T(4,128)} %get-tuple-element.89.c1_ref.refs_3_.refs_2_, f32[7,2,4,8,256]{4,3,2,1,0:T(8,128)} %get-tuple-element.130.refs_3_), custom_call_target="tpu_custom_call" | custom-call | tf_op jit(solution)/shard_map/exchange_8/pallas_call | solution.py:322
  259.3 0.0 copy-start.3
  259.3 12.4 %last.1 = (bf16[4,49,64,128]{3,2,1,0:T(8,128)(2,1)}, bf16[640,256]{1,0:T(8,128)(2,1)}) custom-call(f32[4,49,16,256]{3,2,1,0:T(8,128)} %get-tuple-element.127.dlat_ref, f32[4,49,16,256]{3,2,1,0:T(8,128)} %get-tuple-element.81.lat_ref, bf16[4,49,16,640]{3,2,1,0:T(8,128)(2,1)} %get-tuple-element.128.taps_ref, f32[7,2,4,8,256]{4,3,2,1,0:T(8,128)} %get-tuple-element.131.hn_ref, ...), custom_call_target="tpu_custom_call" | custom-call | tf_op jit(solution)/shard_map/last/pallas_call | solution.py:334
  271.7 0.0 copy-done.3
  271.7 0.7 concatenate.7
  272.4 0.7 concatenate.6
  273.1 76.0 %reduce_9.1 = bf16[10752,256]{1,0:T(8,128)(2,1)} custom-call(bf16[6144,256]{1,0:T(8,128)(2,1)} %get-tuple-element.135.refs_0_, bf16[2304,256]{1,0:T(8,128)(2,1)} %get-tuple-element.136.refs_1_, bf16[1280,256]{1,0:T(8,128)(2,1)} %get-tuple-element.137.refs_2_, bf16[640,256]{1,0:T(8,128)(2,1)} %get-tuple-element.138.refs_3_, f32[96,256]{1,0:T(8,128)} %get-tuple-element.139.refs_4_), custom_call_target="tpu_custom_call" | custom-call | tf_op jit(solution)/shard_map/reduce_9/pallas_call | solution.py:1055
  349.0 0.0 slice-start.1
  349.1 0.9 slice_convert_fusion.2
  350.0 0.6 fusion.1
  350.6 0.7 copy.32
  351.3 1.0 slice.110
  352.3 0.0 copy-start.1
  352.3 0.9 convert.2
  353.2 0.0 slice-done.1
  353.2 1.6 convert.3
  354.8 1.1 copy-done.1
  355.9 1.2 slice_convert_fusion.1
  357.1 0.5 slice_convert_fusion
  357.6 0.0 copy-start
  357.6 0.3 slice.142
  358.0 2.3 copy-done
  360.2 0.0 slice-start
  360.2 3.0 copy.34
  363.3 0.0 slice-done
  363.3 1.1 copy.33
  (3 shorter events, 0.0 us)
Async XLA Ops:
  221.0 20.6 %copy-start.2 = (f32[4,2,128]{2,1,0:T(2,128)S(1)}, f32[4,2,128]{2,1,0:T(2,128)}, u32[]{:S(2)}) copy-start(f32[4,2,128]{2,1,0:T(2,128)} %exchange_7.1.q7_ref) | copy-start | bytes 12292
  259.3 12.4 %copy-start.3 = (f32[4,2,128]{2,1,0:T(2,128)S(1)}, f32[4,2,128]{2,1,0:T(2,128)}, u32[]{:S(2)}) copy-start(f32[4,2,128]{2,1,0:T(2,128)} %get-tuple-element.133.q8_ref) | copy-start | bytes 12292
  349.0 4.1 %slice-start.1 = ((bf16[10752,256]{1,0:T(8,128)(2,1)}), bf16[2304,256]{1,0:T(8,128)(2,1)S(1)}, s32[]{:S(2)}) async-start(bf16[10752,256]{1,0:T(8,128)(2,1)} %reduce_9.1), calls=%async_computation.1 | async-start | bytes 2359296 | tf_op jit(solution)/shard_map/slice | solution.py:1070
  352.3 3.6 %copy-start.1 = (bf16[10752,256]{1,0:T(8,128)(2,1)S(1)}, bf16[10752,256]{1,0:T(8,128)(2,1)}, u32[]{:S(2)}) copy-start(bf16[10752,256]{1,0:T(8,128)(2,1)} %reduce_9.1) | copy-start | bytes 16515076
  357.6 2.6 copy-start
  360.2 3.0 slice-start

commit v3 on v2

--- a/solution.py
+++ b/solution.py
@@ -87,27 +87,7 @@
     return -(-n // 8) * 8
 
 
-def exchange_kernel(cfg, *refs):
-    fwd, bwd, n_coefs, has_up, has_down = cfg
-    nf = sum(c[2] for c in fwd)
-    nb = max((c[6] + c[4] for c in bwd), default=0)
-    nn = sum(c[4] for c in bwd)
-    n_row = 2 * nf + nb
-    it = iter(refs)
-    stats_ref, gb_ref = next(it), next(it)
-    coef_refs = [next(it) for _ in range(n_coefs)]
-    up_ref = next(it) if has_up else None
-    down_ref = next(it) if has_down else None
-    coef_out = next(it) if nf else None
-    pq_out = next(it) if nb else None
-    from_prev = next(it) if has_up else None
-    from_next = next(it) if has_down else None
-    slots1, slots2, mid, tot, send1, recv1, send2, recv2 = (next(it) for _ in range(8))
-    if has_up:
-        up_land, up_sems = next(it), next(it)
-    if has_down:
-        down_land, down_sems = next(it), next(it)
-
+def exchange_peers(cfg):
     paths, length = lax.axis_size("path"), lax.axis_size("frames")
     near = 4
     g1, g2 = paths * near, length // near
@@ -129,20 +109,33 @@
         return (lax.div(index, length), lax.rem(index, length))
 
     nxt, prv = split(lax.rem(me + 1, total)), split(lax.rem(me + total - 1, total))
-
-    barrier = pltpu.get_barrier_semaphore()
-    greeted = 0
-    for k in range(1, g1):
-        pl.semaphore_signal(barrier, inc=1, device_id=peer1(k), device_id_type=MESH)
-        greeted += 1
-    for k in range(1, g2):
-        pl.semaphore_signal(barrier, inc=1, device_id=peer2(k), device_id_type=MESH)
-        greeted += 1
-    if has_up or has_down:
-        pl.semaphore_signal(barrier, inc=1, device_id=nxt, device_id_type=MESH)
-        pl.semaphore_signal(barrier, inc=1, device_id=prv, device_id_type=MESH)
-        greeted += 2
-    pl.semaphore_wait(barrier, greeted)
+    return g1, g2, r1, r2, peer1, peer2, nxt, prv
+
+
+def exchange_hello(cfg):
+    g1, g2, _, _, peer1, peer2, nxt, prv = exchange_peers(cfg)
+    peers = [peer1(k) for k in range(1, g1)] + [peer2(k) for k in range(1, g2)]
+    if cfg.up or cfg.down:
+        peers += [nxt, prv]
+    for peer in peers:
+        pl.semaphore_signal(pltpu.get_barrier_semaphore(), inc=1, device_id=peer, device_id_type=MESH)
+    return len(peers)
+
+
+def exchange_run(cfg, ins, outs, scratch, meanwhile=None):
+    fwd, bwd = cfg.fwd, cfg.bwd
+    nf = sum(c[2] for c in fwd)
+    nb = max((c[6] + c[4] for c in bwd), default=0)
+    n_row = 2 * nf + nb
+    stats_ref, up_ref, down_ref = scratch[:3]
+    gb_ref, *coef_refs = ins
+    outs = list(outs)
+    coef_out = outs.pop(0) if nf else None
+    pq_out = outs.pop(0) if nb else None
+    from_prev = outs.pop(0) if cfg.up else None
+    from_next = outs.pop(0) if cfg.down else None
+    slots1, slots2, mid, tot, send1, recv1, send2, recv2, up_land, up_sems, down_land, down_sems = scratch[3:]
+    g1, g2, r1, r2, peer1, peer2, nxt, prv = exchange_peers(cfg)
 
     halos = []
     copies = []
@@ -158,31 +151,25 @@
             )
         )
         copies[-1].start()
-    if has_up:
-        halos.append(
-            pltpu.make_async_remote_copy(
-                src_ref=up_ref,
-                dst_ref=up_land,
-                send_sem=up_sems.at[0],
-                recv_sem=up_sems.at[1],
-                device_id=nxt,
-                device_id_type=MESH,
+    for used, src, land, sems, peer in (
+        (cfg.up, up_ref, up_land, up_sems, nxt),
+        (cfg.down, down_ref, down_land, down_sems, prv),
+    ):
+        if used:
+            halos.append(
+                pltpu.make_async_remote_copy(
+                    src_ref=src,
+                    dst_ref=land,
+                    send_sem=sems.at[0],
+                    recv_sem=sems.at[1],
+                    device_id=peer,
+                    device_id_type=MESH,
+                )
             )
-        )
-        halos[-1].start()
-    if has_down:
-        halos.append(
-            pltpu.make_async_remote_copy(
-                src_ref=down_ref,
-                dst_ref=down_land,
-                send_sem=down_sems.at[0],
-                recv_sem=down_sems.at[1],
-                device_id=prv,
-                device_id_type=MESH,
-            )
-        )
-        halos[-1].start()
+            halos[-1].start()
     slots1[r1] = stats_ref[...]
+    if meanwhile is not None:
+        meanwhile()
     for c in copies:
         c.wait_recv()
 
@@ -280,9 +267,9 @@
 
     for c in halos:
         c.wait()
-    if has_up:
+    if cfg.up:
         from_prev[...] = up_land[...]
-    if has_down:
+    if cfg.down:
         from_next[...] = down_land[...]
     for c in copies:
         c.wait_send()
@@ -290,59 +277,115 @@
         c.wait_send()
 
 
-def exchange(mesh_sizes, cid, stats, gb, fwd=(), bwd=(), coefs=(), up=None, down=None):
-    paths, length = mesh_sizes
-    g1, g2 = paths * 4, length // 4
-    nf = sum(c[2] for c in fwd)
-    nn = sum(c[4] for c in bwd)
-    r = stats.shape[0]
+class Exchange:
+    def __init__(self, sizes, cid, rows_n, fwd=(), bwd=(), up=None, down=None):
+        self.cid, self.fwd, self.bwd, self.up, self.down = cid, fwd, bwd, up, down
+        g1, g2, r = sizes[0] * 4, sizes[1] // 4, pad8(rows_n)
+        self.outs = []
+        nf, nn = sum(c[2] for c in fwd), sum(c[4] for c in bwd)
+        if nf:
+            self.outs.append(((5, nf, LANES), F32))
+        if nn:
+            self.outs.append(((4, nn, LANES), F32))
+        self.outs += [(h, F32) for h in (up, down) if h]
+        none = (8, LANES)
+        self.stats = (r, LANES)
+        self.work = [
+            pltpu.VMEM((g1, r, LANES), F32),
+            pltpu.VMEM((g2, r, LANES), F32),
+            pltpu.VMEM((r, LANES), F32),
+            pltpu.VMEM((r, LANES), F32),
+            pltpu.SemaphoreType.DMA((g1,)),
+            pltpu.SemaphoreType.DMA((g1,)),
+            pltpu.SemaphoreType.DMA((g2,)),
+            pltpu.SemaphoreType.DMA((g2,)),
+            pltpu.VMEM(up or none, F32),
+            pltpu.SemaphoreType.DMA((2,)),
+            pltpu.VMEM(down or none, F32),
+            pltpu.SemaphoreType.DMA((2,)),
+        ]
+        self.local = [pltpu.VMEM(self.stats, F32), pltpu.VMEM(up or none, F32), pltpu.VMEM(down or none, F32)]
+
+
+def exchange_alone(ex, stats, gb, coefs=(), up=None, down=None):
     vm = pl.BlockSpec(memory_space=pltpu.VMEM)
-    operands = [stats, gb, *coefs]
-    outs = []
-    if nf:
-        outs.append(jax.ShapeDtypeStruct((5, nf, LANES), F32))
-    if nn:
-        outs.append(jax.ShapeDtypeStruct((4, nn, LANES), F32))
-    scratch = [
-        pltpu.VMEM((g1, r, LANES), F32),
-        pltpu.VMEM((g2, r, LANES), F32),
-        pltpu.VMEM((r, LANES), F32),
-        pltpu.VMEM((r, LANES), F32),
-        pltpu.SemaphoreType.DMA((g1,)),
-        pltpu.SemaphoreType.DMA((g1,)),
-        pltpu.SemaphoreType.DMA((g2,)),
-        pltpu.SemaphoreType.DMA((g2,)),
-    ]
-    for halo in (up, down):
-        if halo is not None:
-            operands.append(halo)
-            outs.append(jax.ShapeDtypeStruct(halo.shape, halo.dtype))
-            scratch += [pltpu.VMEM(halo.shape, halo.dtype), pltpu.SemaphoreType.DMA((2,))]
-    cfg = (fwd, bwd, len(coefs), up is not None, down is not None)
-    return pl.pallas_call(
-        functools.partial(exchange_kernel, cfg),
-        out_shape=outs,
-        in_specs=[vm] * len(operands),
-        out_specs=[vm] * len(outs),
-        scratch_shapes=scratch,
-        compiler_params=pltpu.CompilerParams(collective_id=cid, has_side_effects=True),
-        name=f"exchange_{cid}",
-    )(*operands)
-
-
-def call(kernel, ins, outs, scratch=(), name=None):
+    operands = [stats, gb, *coefs] + [h for h in (up, down) if h is not None]
+    n_in, n_out = len(operands), len(ex.outs)
+
+    def kernel(*refs):
+        ins, outs, work = refs[:n_in], refs[n_in : n_in + n_out], refs[n_in + n_out :]
+        count = exchange_hello(ex)
+        pl.semaphore_wait(pltpu.get_barrier_semaphore(), count)
+        halos = list(ins[2 + len(coefs) :])
+        up_ref = halos.pop(0) if ex.up else None
+        down_ref = halos.pop(0) if ex.down else None
+        exchange_run(ex, ins[1 : 2 + len(coefs)], outs, [ins[0], up_ref, down_ref, *work])
+
     return pl.pallas_call(
         kernel,
+        out_shape=[jax.ShapeDtypeStruct(s, d) for s, d in ex.outs],
+        in_specs=[vm] * n_in,
+        out_specs=[vm] * n_out,
+        scratch_shapes=ex.work,
+        compiler_params=pltpu.CompilerParams(collective_id=ex.cid, has_side_effects=True),
+        name=f"exchange_{ex.cid}",
+    )(*operands)
+
+
+STAT, UP, DOWN = "stat", "up", "down"
+
+
+def call(kernel, ins, outs, scratch=(), name=None, ex=None, ex_ins=()):
+    real = [o for o in outs if not isinstance(o, str)]
+    extra_in = [whole(a) for a in ex_ins]
+    extra_out = [out_whole(s, d) for s, d in ex.outs] if ex else []
+    all_in, all_out = [*ins, *extra_in], [*real, *extra_out]
+    local = [*ex.local, *ex.work] if ex else []
+    sizes = [len(ins), len(extra_in), len(real), len(extra_out), len(scratch), len(local)]
+    ends = [sum(sizes[: k + 1]) for k in range(len(sizes))]
+
+    def body(*refs):
+        k_in, x_in, k_out, x_out, k_scr, x_scr = (refs[e - n : e] for e, n in zip(ends, sizes))
+        if ex is None:
+            kernel(*k_in, *k_out, *k_scr)
+            return
+        i = pl.program_id(0)
+
+        @pl.when(i == 0)
+        def _():
+            exchange_hello(ex)
+
+        named = {STAT: x_scr[0]}
+        if ex.up:
+            named[UP] = x_scr[1].at[pl.ds(i, 1)]
+        if ex.down:
+            named[DOWN] = x_scr[2].at[pl.ds(i, 1)]
+        it = iter(k_out)
+        late = kernel(*k_in, *[named[o] if isinstance(o, str) else next(it) for o in outs], *k_scr)
+
+        @pl.when(i == STEPS - 1)
+        def _():
+            pl.semaphore_wait(pltpu.get_barrier_semaphore(), len_peers(ex))
+            exchange_run(ex, x_in, x_out, x_scr, late)
+
+    params = {"collective_id": ex.cid, "has_side_effects": True} if ex else {}
+    return pl.pallas_call(
+        body,
         grid=(STEPS,),
-        in_specs=[pl.BlockSpec(b, m) for _, b, m in ins],
-        out_specs=[pl.BlockSpec(b, m) for _, _, b, m in outs],
-        out_shape=[jax.ShapeDtypeStruct(s, d) for s, d, _, _ in outs],
-        scratch_shapes=list(scratch),
+        in_specs=[pl.BlockSpec(b, m) for _, b, m in all_in],
+        out_specs=[pl.BlockSpec(b, m) for _, _, b, m in all_out],
+        out_shape=[jax.ShapeDtypeStruct(s, d) for s, d, _, _ in all_out],
+        scratch_shapes=[*scratch, *local],
         compiler_params=pltpu.CompilerParams(
-            dimension_semantics=("arbitrary",), vmem_limit_bytes=VMEM_LIMIT
+            dimension_semantics=("arbitrary",), vmem_limit_bytes=VMEM_LIMIT, **params
         ),
         name=name,
-    )(*[a for a, _, _ in ins])
+    )(*[a for a, _, _ in all_in])
+
+
+def len_peers(ex):
+    paths, length = lax.axis_size("path"), lax.axis_size("frames")
+    return paths * 4 - 1 + length // 4 - 1 + (2 if ex.up or ex.down else 0)
 
 
 def whole(array):
@@ -746,6 +789,8 @@
         put_rows(st_ref, 2, sum_end(s2))
         put_rows(st_ref, 4, sum_end(t1))
         put_rows(st_ref, 5, sum_end(t2))
+
+    def late():
         for k in range(3):
             gmid_ref[k * 32 : (k + 1) * 32, :] = fold_lanes(gmid[:, k * LANES : (k + 1) * LANES], s_n)
         tall, low_tall = gsc.shape[0], gso.shape[0]
@@ -755,6 +800,8 @@
             gw_ref[n * tall : (n + 1) * tall, :] = gsc[:, cols].astype(BF16)
             at = blocks * tall + n * low_tall
             gw_ref[at : at + low_tall, :] = gso[:, cols].astype(BF16)
+
+    return late
 
 
 def k_back_spatial(dsb_ref, sb_ref, sa_ref, spad_ref, x_ref, dfa_ref, fa_ref, gout_ref, gmid_ref, c1_ref, c2_ref, c3_ref, q6_ref,
@@ -805,6 +852,8 @@
         zero_ref(st_ref)
         put_rows(st_ref, 0, sum_end(s1))
         put_rows(st_ref, 2, sum_end(s2))
+
+    def late():
         for k in range(9):
             gw_ref[k * c : (k + 1) * c, :] = gsp[:, k * c : (k + 1) * c].T.astype(BF16)
         gf_ref[0:32, 0:LANES] = fold_wide(gin, x_ref.shape[0])
@@ -813,6 +862,8 @@
         gf_ref[32:64, LANES:] = gmid_ref[32:64, :]
         gf_ref[64:96, 0:LANES] = gmid_ref[64:96, :]
         gf_ref[64:96, LANES:] = jnp.zeros((32, LANES), F32)
+
+    return late
 
 
 def k_back_join(x_ref, lact_ref, dsa_ref, sa_ref, dsp_ref, lat_ref, c1_ref, c2_ref, q7_ref, m16_ref, win_ref, wsc_ref,
@@ -1067,7 +1118,49 @@
         compiler_params=pltpu.CompilerParams(collective_id=cid, has_side_effects=True, vmem_limit_bytes=VMEM_LIMIT),
         name=f"reduce_{cid}",
     )(*parts)
-    return [out[o : o + h] for o, h in zip(offsets, heights)]
+    return out
+
+
+def k_unpack(pieces, src_ref, *refs):
+    n_out = len(refs) - 4
+    outs, (low, wide, sem_in, sem_out) = refs[:n_out], refs[n_out:]
+
+    def fetch(k):
+        row, height = pieces[k][:2]
+        part = pl.ds(row, height)
+        return pltpu.make_async_copy(src_ref.at[part], low.at[part], sem_in.at[k])
+
+    def store(k):
+        row, height, out, col = pieces[k]
+        part = outs[out] if col is None else outs[out].at[:, pl.ds(col, src_ref.shape[1])]
+        return pltpu.make_async_copy(wide.at[pl.ds(row, height)], part, sem_out.at[k])
+
+    for k in range(len(pieces)):
+        fetch(k).start()
+    for k, (row, height, _, _) in enumerate(pieces):
+        fetch(k).wait()
+        wide[row : row + height, :] = low[row : row + height, :].astype(F32)
+        store(k).start()
+    for k in range(len(pieces)):
+        store(k).wait()
+
+
+def unpack(reduced, pieces, shapes):
+    hbm = pl.BlockSpec(memory_space=pl.ANY)
+    return pl.pallas_call(
+        functools.partial(k_unpack, pieces),
+        out_shape=[jax.ShapeDtypeStruct(s, F32) for s in shapes],
+        in_specs=[hbm],
+        out_specs=[hbm] * len(shapes),
+        scratch_shapes=[
+            pltpu.VMEM(reduced.shape, BF16),
+            pltpu.VMEM(reduced.shape, F32),
+            pltpu.SemaphoreType.DMA((len(pieces),)),
+            pltpu.SemaphoreType.DMA((len(pieces),)),
+        ],
+        compiler_params=pltpu.CompilerParams(vmem_limit_bytes=VMEM_LIMIT),
+        name="unpack",
+    )(reduced)
 
 
 def k_prep(x_hbm, fill_ref, clip_ref, norm_ref, wfi_ref, wfm_ref, wfo_ref,
@@ -1233,39 +1326,42 @@
     def acc(rows_n, width, count):
         return [pltpu.VMEM((rows_n, width), F32)] * count
 
-    halo_small = out_blocked((STEPS, 8, LANES), F32, 0, 1)
-
-    fa, lat, taps, st, up, down = call(
+    small = (STEPS, 8, LANES)
+
+    fa, lat, taps, c1, hp, hn = call(
         k_first,
         [sb_(x_fast), blocked(tail, 0, 1), whole(m16), whole(m64), whole(wfa), whole(wlat)],
-        [fast_out(LANES, F32), slow_out(c_lat, F32), slow_out(5 * c_fast, BF16), stat(7), halo_small, halo_small],
+        [fast_out(LANES, F32), slow_out(c_lat, F32), slow_out(5 * c_fast, BF16), STAT, UP, DOWN],
         [pltpu.VMEM((groups * p_n * f_n, c_fast), F32), *acc(f_n, LANES, 2), *acc(t_n, c_lat, 2)],
         "first",
-    )
-    c1, hp, hn = exchange(sizes, 1, st, gb, fwd=(("lane4", 0, 1), ("plain", 6, 2)), up=up, down=down)
-
-    lact, ftap, sa, sp, fb, st = call(
+        Exchange(sizes, 1, 7, fwd=(("lane4", 0, 1), ("plain", 6, 2)), up=small, down=small),
+        [gb],
+    )
+
+    lact, ftap, sa, sp, fb, c2 = call(
         k_join,
         [sb_(x_slow), sb_(lat), fb_(fa), blocked(hp, 0, 1), blocked(hn, 0, 1), whole(c1), whole(m16), whole(m64),
          whole(w_slow_in), whole(w_shortcut), whole(wmid)],
         [slow_out(c_lat, BF16), fast_out(3 * LANES, BF16), slow_out(in_slow, F32), slow_out(c_slow, F32),
-         fast_out(LANES, F32), stat(23)],
+         fast_out(LANES, F32), STAT],
         [*acc(t_n, in_slow, 2), *acc(t_n, c_slow, 2), *acc(f_n, LANES, 2)],
         "join",
-    )
-    (c2,) = exchange(sizes, 2, st, gb, fwd=(("lane4", 1, 1), ("plain", 8, 2), ("plain", 20, 8)))
+        Exchange(sizes, 2, 23, fwd=(("lane4", 1, 1), ("plain", 8, 2), ("plain", 20, 8))),
+        [gb],
+    )
 
     rows_n = side // STEPS
-    pad, sb, fact, st = call(
+    pad, sb, fact, c3 = call(
         k_spatial,
         [whole(sa.reshape(side, side, t_n, in_slow)),
          fb_(fb), whole(c2), whole(m16), whole(m64), whole(wsp), whole(wout)],
         [out_whole((side + 2, side + 2, t_n, in_slow), BF16),
-         out_blocked((side, side, t_n, in_slow), F32, 0, rows_n), fast_out(LANES, BF16), stat(13)],
+         out_blocked((side, side, t_n, in_slow), F32, 0, rows_n), fast_out(LANES, BF16), STAT],
         [*acc(t_n, in_slow, 2), *acc(f_n, groups * c_fast, 2)],
         "spatial",
-    )
-    (c3,) = exchange(sizes, 3, st, gb, fwd=(("row4", 2, 4), ("plain", 10, 2)))
+        Exchange(sizes, 3, 13, fwd=(("row4", 2, 4), ("plain", 10, 2))),
+        [gb],
+    )
 
     sb4 = sb.reshape(sl + (in_slow,))
     sact, fast_y, df, st = call(
@@ -1276,7 +1372,9 @@
         [*acc(t_n, c_slow, 2), *acc(f_n, groups * c_fast, 2)],
         "expand",
     )
-    c4, q4 = exchange(sizes, 4, st, gb, fwd=(("plain", 12, 8),), bwd=(("row4", 0, 0, 2, 4, 0, 4),), coefs=(c3,))
+    c4, q4 = exchange_alone(
+        Exchange(sizes, 4, 25, fwd=(("plain", 12, 8),), bwd=(("row4", 0, 0, 2, 4, 0, 4),)), st, gb, [c3]
+    )
 
     halo_pair = out_blocked((STEPS, 2, 8, LANES), F32, 0, 1)
     slow_y, dy, dfb, g_fout, up, down, st = call(
@@ -1288,39 +1386,41 @@
         [*acc(t_n, c_slow, 3), *acc(f_n, LANES, 2), *acc(LANES, groups * c_fast, 1)],
         "out",
     )
-    q5, hp, hn = exchange(
-        sizes, 5, st, gb,
+    pair = (STEPS, 2, 8, LANES)
+    ex5 = Exchange(
+        sizes, 5, 26,
         bwd=(("plain", 0, 0, 12, 8, 0, 8), ("plain", 1, 3, 20, 8, 0, 16), ("lane4", 1, 0, 1, 1, 24, 25)),
-        coefs=(c4, c2), up=up, down=down,
-    )
+        up=pair, down=pair,
+    )
+    q5, hp, hn = exchange_alone(ex5, st, gb, [c4, c2], up, down)
 
     c_cat = w_slow_in.shape[0]
-    gw_out, dsp, dsb, dfa, g_fmid, st = call(
+    gw_out, dsp, dsb, dfa, g_fmid, q6 = call(
         k_back_out,
         [sb_(x_slow), sb_(lact), sb_(dy), sb_(sp), sb_(sact), sb_(sb4), fb_(dfb), fb_(fb), fb_(fa), fb_(ftap), blocked(hp, 0, 1), blocked(hn, 0, 1),
          whole(c1), whole(c2), whole(c3), whole(c4), whole(q5), whole(m16), whole(m64), whole(w_slow_out), whole(wback)],
         [out_whole(((c_cat + in_slow) * c_slow // in_slow, in_slow), BF16), slow_out(c_slow, BF16),
-         slow_out(in_slow, F32), fast_out(LANES, F32), out_whole((3 * in_fast, LANES), F32), stat(6)],
+         slow_out(in_slow, F32), fast_out(LANES, F32), out_whole((3 * in_fast, LANES), F32), STAT],
         [*acc(t_n, in_slow, 2), *acc(f_n, LANES, 2), *acc(c_cat, c_slow, 1), *acc(in_slow, c_slow, 1),
          *acc(LANES, 3 * LANES, 1)],
         "back_out",
-    )
-    (q6,) = exchange(
-        sizes, 6, st, gb, bwd=(("plain", 0, 4, 10, 2, 0, 2), ("lane4", 1, 0, 0, 1, 4, 5)), coefs=(c3, c1)
+        Exchange(sizes, 6, 6, bwd=(("plain", 0, 4, 10, 2, 0, 2), ("lane4", 1, 0, 0, 1, 4, 5))),
+        [gb, c3, c1],
     )
 
     grid = (side, side, t_n, in_slow)
-    dsa, dfa_low, gw_mid, gw_fast, st = call(
+    dsa, dfa_low, gw_mid, gw_fast, q7 = call(
         k_back_spatial,
         [whole(dsb.reshape(grid)), whole(sb), blocked(sa.reshape(grid), 0, rows_n), whole(pad), sb_(x_fast), fb_(dfa), fb_(fa),
          whole(g_fout), whole(g_fmid), whole(c1), whole(c2), whole(c3), whole(q6), whole(m16), whole(m64), whole(wsp)],
         [out_blocked(grid, F32, 0, rows_n), fast_out(LANES, BF16), out_whole((9 * in_slow, in_slow), BF16),
-         out_whole((3 * in_fast, 2 * LANES), F32), stat(4)],
+         out_whole((3 * in_fast, 2 * LANES), F32), STAT],
         [*acc(t_n, in_slow, 2), pltpu.VMEM((side + 2, side + 2, t_n, in_slow), BF16), *acc(in_slow, 9 * in_slow, 1),
          *acc(LANES, groups * c_fast, 1)],
         "back_spatial",
-    )
-    (q7,) = exchange(sizes, 7, st, gb, bwd=(("plain", 0, 1, 8, 2, 0, 2),), coefs=(c2,))
+        Exchange(sizes, 7, 4, bwd=(("plain", 0, 1, 8, 2, 0, 2),)),
+        [gb, c2],
+    )
 
     gw_in, slow_gx, dlat, down, st = call(
         k_back_join,
@@ -1331,7 +1431,8 @@
         [*acc(t_n, c_lat, 2), *acc(in_slow, c_cat, 1)],
         "back_join",
     )
-    q8, hn = exchange(sizes, 8, st, gb, bwd=(("plain", 0, 1, 6, 2, 0, 2),), coefs=(c1,), down=down)
+    ex8 = Exchange(sizes, 8, 4, bwd=(("plain", 0, 1, 6, 2, 0, 2),), down=down.shape)
+    q8, hn = exchange_alone(ex8, st, gb, [c1], None, down)
 
     fast_gx, gw_lat = call(
         k_last,
@@ -1342,14 +1443,20 @@
         "last",
     )
 
-    gw_out, gw_mid, gw_in, gw_lat, gw_fast = [
-        g.astype(F32) for g in reduce_all(sizes, 9, [gw_out, gw_mid, gw_in, gw_lat, gw_fast])
-    ]
+    reduced = reduce_all(sizes, 9, [gw_out, gw_mid, gw_in, gw_lat, gw_fast])
     blocks = c_slow // in_slow
-    g_short, g_sout = [
-        jnp.transpose(g.reshape(blocks, -1, in_slow), (1, 0, 2)).reshape(-1, c_slow)
-        for g in (gw_out[: blocks * c_cat], gw_out[blocks * c_cat :])
-    ]
+    pieces, at = [], 0
+    for out, tall in ((0, c_cat), (1, in_slow)):
+        for n in range(blocks):
+            pieces.append((at, tall, out, n * in_slow))
+            at += tall
+    for out, tall in ((2, gw_mid.shape[0]), (3, c_cat), (4, gw_lat.shape[0]), (5, gw_fast.shape[0])):
+        pieces.append((at, tall, out, None))
+        at += tall
+    g_short, g_sout, gw_mid, gw_in, gw_lat, gw_fast = unpack(
+        reduced, tuple(pieces),
+        [(c_cat, c_slow), (in_slow, c_slow), gw_mid.shape, (c_cat, in_slow), gw_lat.shape, gw_fast.shape],
+    )
     taps_t = [gw_fast[in_fast : 2 * in_fast, :in_fast], gw_fast[in_fast : 2 * in_fast, c_fast : c_fast + in_fast],
               gw_fast[2 * in_fast :, :in_fast]]
     grads = (

time: 366 us -> 345 us (0.943)
  Pallas kernels: 343 us -> 334 us
  local copies, waits for them, and re-layouts: 15 us -> 7.56 us
  other arithmetic: 5.83 us -> 0.76 us
    pallas_call x17 -> x13, Pallas kernels: 252 us -> 244 us  [the longest x9 196 us: call(): pl.pallas_call(body, grid=(STEPS,), in_specs=[pl.BlockSpec(b, m) for _, b...]
    reshape x2 -> x0, local copies, waits for them, and re-layouts: 4.1 us -> none  [per_device(): jnp.transpose(g.reshape(blocks, -1, in_slow), (1, 0, 2)).reshape(-1, c_slow)]
where the time goes in v3:
time: 345 us; the launch traced here: 344 us
  Pallas kernels  334 us (97%)
  local copies, waits for them, and re-layouts  7.56 us (2%)
    pallas_call x9, Pallas kernels, call(): pl.pallas_call(body, grid=(STEPS,), in_specs=[pl.BlockSpec(b, m) for _, b...  196 us
    pallas_call x1, Pallas kernels, reduce_all(): pl.pallas_call(functools.partial(reduce_kernel, (offsets, heights, ch, fa...  76 us
    pallas_call x3, Pallas kernels, exchange_alone(): pl.pallas_call(kernel, out_shape=[jax.ShapeDtypeStruct(s, d) for s, d in...  42 us
    pallas_call x1, Pallas kernels, prepare(): pl.pallas_call(k_prep, out_shape=[jax.ShapeDtypeStruct(s, d) for s, d in...  14.8 us

profile of v3, /device:TPU:0, one launch (start us, length us, event | category | flops | bytes accessed | tf_op | source)
XLA Modules:
  0.0 343.5 jit_solution(17860235859514235470)
XLA Ops:
  0.6 0.8 fusion
  1.4 0.6 copy.33
  2.0 14.8 %prepare.1 = (f32[7,4,8,256]{3,2,1,0:T(8,128)}, f32[2,32,128]{2,1,0:T(8,128)}, f32[3,16,128]{2,1,0:T(8,128)}, f32[3,64,128]{2,1,0:T(8,128)}, bf16[128,512]{1,0:T...) custom-call(bf16[4,49,64,128]{3,2,1,0:T(8,128)(2,1)} %bitcast.85, ...), custom_call_target="tpu_custom_call" | custom-call | tf_op jit(solution)/shard_map/prepare/pallas_call | solution.py:1259
  16.8 15.3 %first.1 = (f32[49,64,128]{2,1,0:T(8,128)}, f32[4,49,16,256]{3,2,1,0:T(8,128)}, bf16[4,49,16,640]{3,2,1,0:T(8,128)(2,1)}, f32[5,3,128]{2,1,0:T(4,128)}, f32[7,8,128]{2,1,0:T(8,128)}, /*index=5*/f32[7,8,128]{2,1,0:T(8,128)}) custom-call(bf16[4,49,64,128]{3,2,1,0:T(8,128)(2,1)} %bitcast.86, f32[7,4,8,256]{3,2,1,0:T(8,128)} %get-tuple-element.80.refs_1_, ...), custom_call_target="tpu_custom_call" | custom-call | tf_op jit(solution)/shard_map/first/pallas_call | solution.py:372
  32.1 29.1 %join.1 = (bf16[4,49,16,256]{3,2,1,0:T(8,128)(2,1)}, bf16[49,64,384]{2,1,0:T(8,128)(2,1)}, f32[4,49,16,256]{3,2,1,0:T(8,128)}, f32[4,49,16,1024]{3,2,1,0:T(8,128...) custom-call(bf16[4,49,16,1024]{3,2,1,0:T(8,128)(2,1)} %bitcast.82, ...), custom_call_target="tpu_custom_call" | custom-call | tf_op jit(solution)/shard_map/join/pallas_call | solution.py:372
  61.3 18.8 %spatial.1 = (bf16[16,16,16,256]{3,2,1,0:T(8,128)(2,1)}, f32[14,14,16,256]{3,2,1,0:T(8,128)}, bf16[49,64,128]{2,1,0:T(8,128)(2,1)}, f32[5,6,128]{2,1,0:T(8,128)}) custom-call(f32[14,14,16,256]{3,2,1,0:T(8,128)} %bitcast.91, f32[49,64,128]{2,1,0:T(8,128)} %get-tuple-element.92.refs_1_.refs_5_.refs_7_, ...), custom_call_target="tpu_custom_call" | custom-call | tf_op jit(solution)/shard_map/spatial/pallas_call | solution.py:372
  80.1 13.8 %expand.1 = (bf16[4,49,16,256]{3,2,1,0:T(8,128)(2,1)}, bf16[4,49,64,128]{3,2,1,0:T(8,128)(2,1)}, f32[49,64,512]{2,1,0:T(8,128)}, f32[32,128]{1,0:T(8,128)}) custom-call(f32[4,49,16,256]{3,2,1,0:T(8,128)} %bitcast.89, bf16[49,64,128]{2,1,0:T(8,128)(2,1)} %get-tuple-element.96.refs_1_.refs_4_, bf16[4,49,64,128]{3,2,1,0:T(8,128)(2,1)} %bitcast.87, ...), custom_call_target="tpu_custom_call" | custom-call | tf_op jit(solution)/shard_map/expand/pallas_call | solution.py:372
  93.9 11.7 %exchange_4.1 = (f32[5,8,128]{2,1,0:T(8,128)}, f32[4,4,128]{2,1,0:T(4,128)}) custom-call(f32[32,128]{1,0:T(8,128)} %get-tuple-element.101.refs_0_, f32[2,32,128]{2,1,0:T(8,128)} %get-tuple-element.84.refs_6_.refs_11_.refs_7_.refs_1_.refs_21_.refs_16_, f32[5,6,128]{2,1,0:T(8,128)} %get-tuple-element.97.refs_4_.refs_2_.refs_7_.refs_14_.refs_22_.refs_11_), custom_call_target="tpu_custom_call" | custom-call | tf_op jit(solution)/shard_map/exchange_4/pallas_call | solution.py:324
  105.6 0.7 slice_bitcast_fusion.14
  106.3 23.8 %out.1 = (bf16[4,49,16,1024]{3,2,1,0:T(8,128)(2,1)}, f32[4,49,16,1024]{3,2,1,0:T(8,128)}, f32[49,64,128]{2,1,0:T(8,128)}, f32[32,128]{1,0:T(8,128)}, f32[7,2,8,1...) custom-call(bf16[4,49,16,256]{3,2,1,0:T(8,128)(2,1)} %get-tuple-element.98.refs_0_.refs_4_, ...), custom_call_target="tpu_custom_call" | custom-call | tf_op jit(solution)/shard_map/out/pallas_call | solution.py:372
  130.1 12.7 %exchange_5.1 = (f32[4,17,128]{2,1,0:T(8,128)}, f32[7,2,8,128]{3,2,1,0:T(8,128)}, f32[7,2,8,128]{3,2,1,0:T(8,128)}) custom-call(f32[32,128]{1,0:T(8,128)} %get-tuple-element.110.refs_0_, f32[2,32,128]{2,1,0:T(8,128)} %get-tuple-element.84.refs_6_.refs_11_.refs_7_.refs_1_.refs_21_.refs_16_, f32[5,8,128]{2,1,0:T(8,128)} %get-tuple-element.102.refs_8_.refs_2_.refs_15_, ...), custom_call_target="tpu_custom_call" | custom-call | tf_op jit(solution)/shard_map/exchange_5/pallas_call | solution.py:324
  142.9 38.2 %back_out.1 = (bf16[6144,256]{1,0:T(8,128)(2,1)}, bf16[4,49,16,1024]{3,2,1,0:T(8,128)(2,1)}, f32[4,49,16,256]{3,2,1,0:T(8,128)}, f32[49,64,128]{2,1,0:T(8,128)},...) custom-call(bf16[4,49,16,1024]{3,2,1,0:T(8,128)(2,1)} %bitcast.83, bf16[4,49,16,256]{3,2,1,0:T(8,128)(2,1)} %get-tuple-element.106.refs_1_, ...), custom_call_target="tpu_custom_call" | custom-call | tf_op jit(solution)/shard_map/back_out/pallas_call | solution.py:372
  181.1 24.7 %back_spatial.1 = (f32[14,14,16,256]{3,2,1,0:T(8,128)}, bf16[49,64,128]{2,1,0:T(8,128)(2,1)}, bf16[2304,256]{1,0:T(8,128)(2,1)}, f32[96,256]{1,0:T(8,128)}, f32[4,2,128]{2,1,0:T(2,128)}) custom-call(f32[14,14,16,256]{3,2,1,0:T(8,128)} %bitcast.97, f32[14,14,16,256]{3,2,1,0:T(8,128)} %get-tuple-element.95.refs_1_, f32[14,14,16,256]{3,2,1,0:T(8,128)} %bitcast.92, ...), custom_call_target="tpu_custom_call" | custom-call | tf_op jit(solution)/shard_map/back_spatial/pallas_call | solution.py:372
  205.8 0.0 copy-start.1
  205.8 20.5 %back_join.1 = (bf16[1280,256]{1,0:T(8,128)(2,1)}, bf16[4,49,16,1024]{3,2,1,0:T(8,128)(2,1)}, f32[4,49,16,256]{3,2,1,0:T(8,128)}, f32[7,2,4,8,256]{4,3,2,1,0:T(8,128)}, f32[8,128]{1,0:T(8,128)}) custom-call(bf16[4,49,16,1024]{3,2,1,0:T(8,128)(2,1)} %bitcast.84, bf16[4,49,16,256]{3,2,1,0:T(8,128)(2,1)} %get-tuple-element.106.refs_1_, ...), custom_call_target="tpu_custom_call" | custom-call | tf_op jit(solution)/shard_map/back_join/pallas_call | solution.py:372
  226.4 0.0 copy-done.1
  226.4 0.7 slice_bitcast_fusion.8
  227.1 0.7 slice_bitcast_fusion.15
  227.8 0.7 slice_bitcast_fusion.4
  228.4 17.5 %exchange_8.1 = (f32[4,2,128]{2,1,0:T(2,128)}, f32[7,2,4,8,256]{4,3,2,1,0:T(8,128)}) custom-call(f32[8,128]{1,0:T(8,128)} %get-tuple-element.129.refs_0_, f32[2,32,128]{2,1,0:T(8,128)} %get-tuple-element.84.refs_6_.refs_11_.refs_7_.refs_1_.refs_21_.refs_16_, f32[5,3,128]{2,1,0:T(4,128)} %get-tuple-element.89.refs_5_.refs_12_.refs_23_.refs_9_.refs_6_.refs_2_, ...), custom_call_target="tpu_custom_call" | custom-call | tf_op jit(solution)/shard_map/exchange_8/pallas_call | solution.py:324
  246.0 0.0 copy-start
  246.0 12.0 %last.1 = (bf16[4,49,64,128]{3,2,1,0:T(8,128)(2,1)}, bf16[640,256]{1,0:T(8,128)(2,1)}) custom-call(f32[4,49,16,256]{3,2,1,0:T(8,128)} %get-tuple-element.127.refs_0_, f32[4,49,16,256]{3,2,1,0:T(8,128)} %get-tuple-element.85.refs_1_.refs_5_, bf16[4,49,16,640]{3,2,1,0:T(8,128)(2,1)} %get-tuple-element.128.refs_2_, ...), custom_call_target="tpu_custom_call" | custom-call | tf_op jit(solution)/shard_map/last/pallas_call | solution.py:372
  258.0 0.0 copy-done
  258.0 0.7 concatenate.7
  258.7 0.7 concatenate.6
  259.3 76.0 %reduce_9.1.src_ref = bf16[10752,256]{1,0:T(8,128)(2,1)} custom-call(bf16[6144,256]{1,0:T(8,128)(2,1)} %get-tuple-element.135.refs_0_, bf16[2304,256]{1,0:T(8,128)(2,1)} %get-tuple-element.136.refs_1_, bf16[1280,256]{1,0:T(8,128)(2,1)} %get-tuple-element.137.refs_2_, bf16[640,256]{1,0:T(8,128)(2,1)} %get-tuple-element.138.refs_3_, ...), custom_call_target="tpu_custom_call" | custom-call | tf_op jit(solution)/shard_map/reduce_9/pallas_call | solution.py:1106
  335.3 5.4 %unpack.1 = (f32[1280,1024]{1,0:T(8,128)}, f32[256,1024]{1,0:T(8,128)}, f32[2304,256]{1,0:T(8,128)}, f32[1280,256]{1,0:T(8,128)}, f32[640,256]{1,0:T(8,128)}, /*index=5*/f32[96,256]{1,0:T(8,128)}) custom-call(bf16[10752,256]{1,0:T(8,128)(2,1)} %reduce_9.1.src_ref), custom_call_target="tpu_custom_call" | custom-call | tf_op jit(solution)/shard_map/unpack/pallas_call | solution.py:1150
  340.7 1.3 fusion.1
  342.1 0.8 slice_bitcast_fusion.2
  342.8 0.7 copy.30
  (2 shorter events, 0.0 us)
Async XLA Ops:
  205.8 20.5 %copy-start.1 = (f32[4,2,128]{2,1,0:T(2,128)S(1)}, f32[4,2,128]{2,1,0:T(2,128)}, u32[]{:S(2)}) copy-start(f32[4,2,128]{2,1,0:T(2,128)} %get-tuple-element.125.refs_8_) | copy-start | bytes 12292
  246.0 12.0 %copy-start = (f32[4,2,128]{2,1,0:T(2,128)S(1)}, f32[4,2,128]{2,1,0:T(2,128)}, u32[]{:S(2)}) copy-start(f32[4,2,128]{2,1,0:T(2,128)} %get-tuple-element.133.refs_7_) | copy-start | bytes 12292

commit v4 on v3

--- a/solution.py
+++ b/solution.py
@@ -115,14 +115,14 @@
 def exchange_hello(cfg):
     g1, g2, _, _, peer1, peer2, nxt, prv = exchange_peers(cfg)
     peers = [peer1(k) for k in range(1, g1)] + [peer2(k) for k in range(1, g2)]
-    if cfg.up or cfg.down:
+    if cfg.greets:
         peers += [nxt, prv]
     for peer in peers:
         pl.semaphore_signal(pltpu.get_barrier_semaphore(), inc=1, device_id=peer, device_id_type=MESH)
     return len(peers)
 
 
-def exchange_run(cfg, ins, outs, scratch, meanwhile=None):
+def exchange_run(cfg, ins, outs, scratch, meanwhile=None, post=None):
     fwd, bwd = cfg.fwd, cfg.bwd
     nf = sum(c[2] for c in fwd)
     nb = max((c[6] + c[4] for c in bwd), default=0)
@@ -134,7 +134,7 @@
     pq_out = outs.pop(0) if nb else None
     from_prev = outs.pop(0) if cfg.up else None
     from_next = outs.pop(0) if cfg.down else None
-    slots1, slots2, mid, tot, send1, recv1, send2, recv2, up_land, up_sems, down_land, down_sems = scratch[3:]
+    slots1, slots2, mid, tot, send1, recv1, send2, recv2, up_land, up_sems, down_land, down_sems = scratch[3:15]
     g1, g2, r1, r2, peer1, peer2, nxt, prv = exchange_peers(cfg)
 
     halos = []
@@ -265,6 +265,20 @@
         pq_out[3, at : at + count, :] = dg
         at += count
 
+    if cfg.post:
+        post_sent, post_land, post_sems = scratch[15:]
+        post(pq_out, post_sent)
+        late = pltpu.make_async_remote_copy(
+            src_ref=post_sent,
+            dst_ref=post_land,
+            send_sem=post_sems.at[0],
+            recv_sem=post_sems.at[1],
+            device_id=prv,
+            device_id_type=MESH,
+        )
+        late.start()
+        late.wait()
+        outs.pop(0)[...] = post_land[...]
     for c in halos:
         c.wait()
     if cfg.up:
@@ -278,8 +292,9 @@
 
 
 class Exchange:
-    def __init__(self, sizes, cid, rows_n, fwd=(), bwd=(), up=None, down=None):
-        self.cid, self.fwd, self.bwd, self.up, self.down = cid, fwd, bwd, up, down
+    def __init__(self, sizes, cid, rows_n, fwd=(), bwd=(), up=None, down=None, post=None):
+        self.cid, self.fwd, self.bwd, self.up, self.down, self.post = cid, fwd, bwd, up, down, post
+        self.greets = bool(up or down or post)
         g1, g2, r = sizes[0] * 4, sizes[1] // 4, pad8(rows_n)
         self.outs = []
         nf, nn = sum(c[2] for c in fwd), sum(c[4] for c in bwd)
@@ -288,6 +303,8 @@
         if nn:
             self.outs.append(((4, nn, LANES), F32))
         self.outs += [(h, F32) for h in (up, down) if h]
+        if post:
+            self.outs.append((post, BF16))
         none = (8, LANES)
         self.stats = (r, LANES)
         self.work = [
@@ -304,6 +321,8 @@
             pltpu.VMEM(down or none, F32),
             pltpu.SemaphoreType.DMA((2,)),
         ]
+        if post:
+            self.work += [pltpu.VMEM(post, BF16), pltpu.VMEM(post, BF16), pltpu.SemaphoreType.DMA((2,))]
         self.local = [pltpu.VMEM(self.stats, F32), pltpu.VMEM(up or none, F32), pltpu.VMEM(down or none, F32)]
 
 
@@ -385,7 +404,7 @@
 
 def len_peers(ex):
     paths, length = lax.axis_size("path"), lax.axis_size("frames")
-    return paths * 4 - 1 + length // 4 - 1 + (2 if ex.up or ex.down else 0)
+    return paths * 4 - 1 + length // 4 - 1 + (2 if ex.greets else 0)
 
 
 def whole(array):
@@ -721,7 +740,7 @@
 
 def k_back_out(x_ref, lact_ref, dy_ref, sp_ref, sact_ref, sb_ref, dfb_ref, fb_ref, fa_ref, ftap_ref, hp_ref, hn_ref,
                c1_ref, c2_ref, c3_ref, c4_ref, q5_ref, m16_ref, m64_ref, wso_ref, wback_ref,
-               gw_ref, dsp_ref, dsb_ref, dfa_ref, gmid_ref, st_ref, s1, s2, t1, t2, gsc, gso, gmid):
+               gw_ref, gs_ref, dsp_ref, dsb_ref, dfa_ref, gmid_ref, st_ref, s1, s2, t1, t2, gsc, gso, gmid):
     i = pl.program_id(0)
     s_n, p_n, t_n, c = sb_ref.shape
     sact = flat(sact_ref[...])
@@ -798,120 +817,36 @@
         for n in range(blocks):
             cols = slice(n * wide, (n + 1) * wide)
             gw_ref[n * tall : (n + 1) * tall, :] = gsc[:, cols].astype(BF16)
-            at = blocks * tall + n * low_tall
-            gw_ref[at : at + low_tall, :] = gso[:, cols].astype(BF16)
+            gs_ref[n * low_tall : (n + 1) * low_tall, :] = gso[:, cols].astype(BF16)
+        if blocks * tall < gw_ref.shape[0]:
+            gw_ref[blocks * tall :, :] = jnp.zeros((gw_ref.shape[0] - blocks * tall, wide), BF16)
 
     return late
 
 
-def k_back_spatial(dsb_ref, sb_ref, sa_ref, spad_ref, x_ref, dfa_ref, fa_ref, gout_ref, gmid_ref, c1_ref, c2_ref, c3_ref, q6_ref,
-                   m16_ref, m64_ref, wsp_ref,
-                   dsa_ref, dlow_ref, gw_ref, gf_ref, st_ref, s1, s2, pad_ref, gsp, gin):
+def k_slow_grad(x_ref, lact_ref, low_ref, dsp_ref, win_ref, wsc_ref, gx_ref, gw_ref, gsi):
     i = pl.program_id(0)
-    h_n, w_n, t_n, c = sb_ref.shape
-
-    @pl.when(i == 0)
-    def _():
-        scale = rows(c3_ref, 0, 4, 2)
-        p_row, q_row = rows(q6_ref, 0, 0, 2), rows(q6_ref, 1, 0, 2)
-        zero_ref(pad_ref)
-
-        @pl.loop(0, h_n)
-        def _(h):
-            d = back_norm(scale, p_row, q_row, dsb_ref[h], sb_ref[h], m16_ref[0:1, :, 0:1])
-            pad_ref[h + 1, 1 : w_n + 1] = d.astype(BF16)
-
-    per = h_n // STEPS
-    h0 = i * per
-    acc = None
-    turned = flat(pad_ref[pl.ds(h0 + 1, per), 1 : w_n + 1]).T
-    for a in range(3):
-        for b in range(3):
-            k = 3 * a + b
-            patch = flat(spad_ref[pl.ds(h0 + a, per), b : b + w_n])
-            cols = slice(k * c, (k + 1) * c)
-            gsp[:, cols] = jnp.where(i == 0, 0.0, gsp[:, cols]) + dot(turned, patch)
-            block = pad_ref[pl.ds(h0 + 2 - a, per), 2 - b : 2 - b + w_n]
-            part = dot_nt(flat(block), wsp_ref[k])
-            acc = part if acc is None else acc + part
-    z = sa_ref[...].reshape(per * w_n, t_n, c)
-    back = acc.reshape(z.shape) * slope(z * rows(c2_ref, 0, 1, 2) + rows(c2_ref, 1, 1, 2))
-    dsa_ref[...] = back.reshape(dsa_ref.shape)
-    sum_add(i, back, s1)
-    sum_add(i, back * (z * rows(c2_ref, 2, 1, 2) - rows(c2_ref, 3, 1, 2)), s2)
-
-    low = back_norm(
-        rows(c1_ref, 0, 0, 1), rows(q6_ref, 0, 2, 1), rows(q6_ref, 1, 2, 1), dfa_ref[...], fa_ref[...], m64_ref[0:1]
-    ).astype(BF16)
-    dlow_ref[...] = low
-    packed = jnp.concatenate([flat(x_ref[s]) for s in range(x_ref.shape[0])], axis=1)
-    add_to(i, gin, dot_tn(flat(low), packed))
+    s_n, p_n, t_n, c = low_ref.shape
+    low, dsp = flat(low_ref[...]), flat(dsp_ref[...])
+    turned = low.T
+    blocks = gx_ref.shape[-1] // c
+    for n in range(blocks + 1):
+        part = slice(n * c, (n + 1) * c)
+        joined = flat(x_ref[:, :, :, part] if n < blocks else lact_ref[...])
+        gsi[:, part] = jnp.where(i == 0, 0.0, gsi[:, part]) + dot(turned, joined)
+        if n < blocks:
+            d = dot_nt(dsp, wsc_ref[part, :]) + dot_nt(low, win_ref[part, :])
+            gx_ref[:, :, :, part] = d.astype(BF16).reshape(s_n, p_n, t_n, c)
 
     @pl.when(i == STEPS - 1)
     def _():
-        zero_ref(st_ref)
-        put_rows(st_ref, 0, sum_end(s1))
-        put_rows(st_ref, 2, sum_end(s2))
-
-    def late():
-        for k in range(9):
-            gw_ref[k * c : (k + 1) * c, :] = gsp[:, k * c : (k + 1) * c].T.astype(BF16)
-        gf_ref[0:32, 0:LANES] = fold_wide(gin, x_ref.shape[0])
-        gf_ref[0:32, LANES:] = gout_ref[...]
-        gf_ref[32:64, 0:LANES] = gmid_ref[0:32, :]
-        gf_ref[32:64, LANES:] = gmid_ref[32:64, :]
-        gf_ref[64:96, 0:LANES] = gmid_ref[64:96, :]
-        gf_ref[64:96, LANES:] = jnp.zeros((32, LANES), F32)
-
-    return late
-
-
-def k_back_join(x_ref, lact_ref, dsa_ref, sa_ref, dsp_ref, lat_ref, c1_ref, c2_ref, q7_ref, m16_ref, win_ref, wsc_ref,
-                gw_ref, gx_ref, dlat_ref, down_ref, st_ref, s1, s2, gsi):
-    i = pl.program_id(0)
-    s_n, p_n, t_n, c = sa_ref.shape
-    shape = (s_n * p_n, t_n, c)
-    low = back_norm(
-        rows(c2_ref, 0, 1, 2), rows(q7_ref, 0, 0, 2), rows(q7_ref, 1, 0, 2),
-        dsa_ref[...].reshape(shape), sa_ref[...].reshape(shape), m16_ref[0:1, :, 0:1],
-    ).astype(BF16)
-    low = flat(low)
-    dsp = flat(dsp_ref[...])
-    turned = low.T
-    wide = 256
-    blocks = win_ref.shape[0] // wide
-    for n in range(blocks):
-        part = slice(n * wide, (n + 1) * wide)
-        joined = flat(x_ref[:, :, :, part] if n < blocks - 1 else lact_ref[...])
-        gsi[:, part] = jnp.where(i == 0, 0.0, gsi[:, part]) + dot(turned, joined)
-        d = dot_nt(dsp, wsc_ref[part, :]) + dot_nt(low, win_ref[part, :])
-        if n < blocks - 1:
-            gx_ref[:, :, :, n * wide : (n + 1) * wide] = d.astype(BF16).reshape(s_n, p_n, t_n, wide)
-    z = lat_ref[...].reshape(shape)
-    back = d.reshape(shape) * slope(z * rows(c1_ref, 0, 1, 2) + rows(c1_ref, 1, 1, 2))
-    dlat_ref[...] = back.reshape(dlat_ref.shape)
-    sum_add(i, back, s1)
-    sum_add(i, back * (z * rows(c1_ref, 2, 1, 2) - rows(c1_ref, 3, 1, 2)), s2)
-    fill = jnp.broadcast_to(m16_ref[0, 0:1, 0:1], (1, c))
-    for k, value in enumerate((flat(back), flat(z))):
-        for s in range(s_n):
-            for p in range(p_n):
-                r = (s * p_n + p) * t_n
-                down_ref[0, k, s, p : p + 1, :] = value[r : r + 1, :]
-            down_ref[0, k, s, p_n : p_n + 1, :] = fill
-
-    @pl.when(i == STEPS - 1)
-    def _():
-        zero_ref(st_ref)
-        put_rows(st_ref, 0, sum_end(s1))
-        put_rows(st_ref, 2, sum_end(s2))
-        for n in range(blocks):
-            part = slice(n * wide, (n + 1) * wide)
+        for n in range(blocks + 1):
+            part = slice(n * c, (n + 1) * c)
             gw_ref[part, :] = gsi[:, part].T.astype(BF16)
 
 
-def k_last(dlat_ref, lat_ref, taps_ref, hn_ref, df_ref, dlow_ref, c1_ref, q8_ref, m16_ref,
-           wlat_ref, wfa_ref, gx_ref, gw_ref, gs, glat):
+def k_fast_grad(dlat_ref, lat_ref, taps_ref, hn_ref, df_ref, dlow_ref, c1_ref, q8_ref, m16_ref, wlat_ref, wfa_ref,
+                gx_ref, gw_ref, gs, glat):
     i = pl.program_id(0)
     s_n, p_n, t_n, c = lat_ref.shape
     shape = (s_n * p_n, t_n, c)
@@ -920,13 +855,17 @@
         back_norm(scale, p_row, q_row, dlat_ref[...].reshape(shape), lat_ref[...].reshape(shape), m16_ref[0:1, :, 0:1])
     ).astype(BF16)
     add_to(i, glat, dot_tn(low, flat(taps_ref[...])))
-    ends = []
-    for s in range(s_n):
-        small = back_norm(
-            scale, p_row, q_row, hn_ref[0, 0, s], hn_ref[0, 1, s], hn_ref[0, 0, s, p_n : p_n + 1, :]
-        )
-        small = small.astype(BF16).astype(F32)
-        ends += [jnp.broadcast_to(small[p : p + 1, :], (t_n, c)) for p in range(p_n)]
+
+    @pl.when(i == STEPS - 1)
+    def _():
+        for k in range(glat.shape[1] // LANES):
+            part = slice(k * LANES, (k + 1) * LANES)
+            gw_ref[part, :] = glat[:, part].T.astype(BF16)
+
+    small = hn_ref[0].astype(F32)
+    ends = [
+        jnp.broadcast_to(small[s * 8 + p : s * 8 + p + 1, :], (t_n, c)) for s in range(s_n) for p in range(p_n)
+    ]
     ends = jnp.concatenate(ends, axis=0).reshape(shape)
     n = low.shape[0]
     moved = pltpu.roll(low.astype(F32), n - 1, 0).reshape(shape)
@@ -944,12 +883,6 @@
         total = flat(df_ref[:, :, cols]) + back[:, cols] + gs[s * n : (s + 1) * n, :]
         gx_ref[s] = total.astype(BF16).reshape(gx_ref.shape[1:])
 
-    @pl.when(i == STEPS - 1)
-    def _():
-        for k in range(glat.shape[1] // LANES):
-            part = slice(k * LANES, (k + 1) * LANES)
-            gw_ref[part, :] = glat[:, part].T.astype(BF16)
-
 
 def each(first, last, body):
     def step(k, carry):
@@ -961,31 +894,401 @@
 NEAR = 4
 
 
-def reduce_kernel(cfg, *refs):
-    offsets, heights, ch, far = cfg
-    n_in = len(offsets)
-    ins = refs[:n_in]
-    (out_ref, x, land_a, buf_b, land_b, buf_c, land_c, acc,
-     sem_a, sem_b, sem_c, sem_d, sem_e, sem_f) = refs[n_in:]
-    me_p, me_f = lax.axis_index("path"), lax.axis_index("frames")
-    me_q, me_r = lax.rem(me_f, NEAR), lax.div(me_f, NEAR)
-    other = 1 - me_p
-
-    def at(path, q, r):
-        return pl.ds(pl.multiple_of(((path * NEAR + q) * far + r) * ch, 16), ch)
-
-    def q_of(k):
-        return lax.rem(me_q + k, NEAR)
-
-    def r_of(k):
-        return lax.rem(me_r + k, far)
-
+class Cube:
+    def __init__(self, ch, far):
+        self.ch, self.far = ch, far
+        self.p, self.f = lax.axis_index("path"), lax.axis_index("frames")
+        self.q, self.r = lax.rem(self.f, NEAR), lax.div(self.f, NEAR)
+        self.sibling = (1 - self.p, self.f)
+
+    def q_of(self, k):
+        return lax.rem(self.q + k, NEAR)
+
+    def r_of(self, k):
+        return lax.rem(self.r + k, self.far)
+
+    def plane(self, k):
+        return (self.p, self.r * NEAR + self.q_of(k))
+
+    def line(self, k):
+        return (self.p, self.r_of(k) * NEAR + self.q)
+
+    def at(self, path, q, r):
+        return pl.ds(pl.multiple_of(((path * NEAR + q) * self.far + r) * self.ch, 16), self.ch)
+
+
+def remote(src, dst, sem, index, device):
+    return pltpu.make_async_remote_copy(
+        src_ref=src, dst_ref=dst, send_sem=sem.at[(0, *index)], recv_sem=sem.at[(1, *index)],
+        device_id=device, device_id_type=MESH)
+
+
+def rows_for(sizes, n):
+    unit = 16 * sizes[0] * sizes[1]
+    return -(-n // unit) * unit
+
+
+class Stream:
+    def __init__(self, sizes, rows_n, width):
+        self.sizes, self.rows_n, self.width = sizes, rows_n, width
+        self.far = sizes[1] // NEAR
+        self.ch = rows_n // (sizes[0] * sizes[1])
+        self.chunk = (self.ch, width)
+        self.near_shape = (self.far, *self.chunk)
+        quad = pltpu.VMEM((NEAR, *self.near_shape), BF16)
+        quad_sems, line_sems = pltpu.SemaphoreType.DMA((2, NEAR, self.far)), pltpu.SemaphoreType.DMA((2, self.far))
+        self.near_scratch = [quad, quad, quad, pltpu.VMEM(self.chunk, F32), quad_sems, quad_sems]
+        self.line_scratch = [pltpu.VMEM(self.near_shape, BF16), pltpu.VMEM(self.chunk, F32), line_sems]
+        self.share_scratch = [line_sems, quad_sems, quad_sems, pltpu.SemaphoreType.DMA]
+
+
+class Near:
+    def __init__(self, stream, x, out, scratch):
+        self.x, self.out, self.far, self.c = x, out, stream.far, Cube(stream.ch, stream.far)
+        self.land_a, self.buf_b, self.land_b, self.acc, self.sem_a, self.sem_b = scratch
+
+    def pair(self, k, m):
+        c = self.c
+        return remote(self.x.at[c.at(1 - c.p, c.q_of(k), c.r_of(m + 1))], self.land_a.at[k, m], self.sem_a, (k, m), c.sibling)
+
+    def plane(self, k, m):
+        return remote(self.buf_b.at[k, m], self.land_b.at[k, m], self.sem_b, (k, m), self.c.plane(k))
+
+    def start(self):
+        def one(m):
+            each(1, NEAR, lambda k: self.pair(k, m).start())
+            self.pair(0, m).start()
+
+        each(0, self.far, one)
+
+    def add_pair(self, first, last):
+        c = self.c
+
+        def one(k, m):
+            self.pair(k, m).wait_recv()
+            mine = self.x[c.at(c.p, c.q_of(k), c.r_of(m + 1)), :]
+            self.buf_b[k, m] = (mine.astype(F32) + self.land_a[k, m].astype(F32)).astype(BF16)
+            self.plane(k, m).start()
+
+        each(first, last, lambda m: each(1, NEAR, lambda k: one(k, m)))
+
+    def add_plane(self, first, last, then=None):
+        c = self.c
+
+        def one(m):
+            self.pair(0, m).wait_recv()
+            self.acc[...] = self.x[c.at(c.p, c.q, c.r_of(m + 1)), :].astype(F32) + self.land_a[0, m].astype(F32)
+
+            def more(k):
+                self.plane(k, m).wait_recv()
+                self.acc[...] += self.land_b[k, m].astype(F32)
+
+            each(1, NEAR, more)
+            self.out[m] = self.acc[...].astype(BF16)
+            if then is not None:
+                then(m)
+
+        each(first, last, one)
+
+    def end(self):
+        each(0, self.far, lambda m: each(0, NEAR, lambda k: self.pair(k, m).wait_send()))
+        each(0, self.far, lambda m: each(1, NEAR, lambda k: self.plane(k, m).wait_send()))
+
+
+class Line:
+    def __init__(self, stream, near, scratch):
+        self.near, self.far, self.c = near, stream.far, Cube(stream.ch, stream.far)
+        self.land, self.acc, self.sem = scratch
+
+    def line(self, m):
+        return remote(self.near.at[m], self.land.at[m], self.sem, (m,), self.c.line(m + 1))
+
+    def start(self, first, last):
+        each(first, min(last, self.far - 1), lambda m: self.line(m).start())
+
+    def total(self):
+        self.acc[...] = self.near[self.far - 1].astype(F32)
+
+        def one(m):
+            self.line(m).wait_recv()
+            self.acc[...] += self.land[m].astype(F32)
+
+        each(0, self.far - 1, one)
+        return self.acc[...].astype(BF16)
+
+    def end(self):
+        each(0, self.far - 1, lambda m: self.line(m).wait_send())
+
+
+class Share:
+    def __init__(self, stream, res, out, scratch):
+        self.res, self.out, self.far, self.c = res, out, stream.far, Cube(stream.ch, stream.far)
+        self.sem_d, self.sem_e, self.sem_f, self.sem_own = scratch
+
+    def own(self):
+        return self.out.at[self.c.at(self.c.p, self.c.q, self.c.r)]
+
+    def keep(self):
+        return pltpu.make_async_copy(self.res, self.own(), self.sem_own)
+
+    def line_back(self, k):
+        return remote(self.res, self.own(), self.sem_d, (k,), self.c.line(k))
+
+    def part(self, q, m):
+        return self.out.at[self.c.at(self.c.p, q, self.c.r_of(self.far - m))]
+
+    def plane_back(self, k, m, src=None):
+        dst = self.part(self.c.q, m)
+        return remote(dst if src is None else src, dst, self.sem_e, (k, m), self.c.plane(k))
+
+    def pair_back(self, k, m, src=None):
+        dst = self.part(self.c.q_of(NEAR - k), m)
+        return remote(dst if src is None else src, dst, self.sem_f, (k, m), self.c.sibling)
+
+    def start_line(self):
+        each(1, self.far, lambda k: self.line_back(k).start())
+
+    def start_plane(self):
+        each(1, NEAR, lambda k: self.plane_back(k, 0, self.res).start())
+        self.pair_back(0, 0, self.res).start()
+        self.keep().start()
+
+    def relay(self, first, last):
+        def one(m):
+            self.line_back(m).wait_recv()
+            each(1, NEAR, lambda k: self.plane_back(k, m).start())
+            self.pair_back(0, m).start()
+
+        each(first, last, one)
+
+    def hand_on(self, first, last):
+        def one(k, m):
+            self.plane_back(k, m).wait_recv()
+            self.pair_back(k, m).start()
+
+        each(first, last, lambda m: each(1, NEAR, lambda k: one(k, m)))
+
+    def end(self):
+        each(0, self.far, lambda m: each(0, NEAR, lambda k: self.pair_back(k, m).wait()))
+        self.keep().wait()
+        each(1, self.far, lambda k: self.line_back(k).wait_send())
+        each(0, self.far, lambda m: each(1, NEAR, lambda k: self.plane_back(k, m).wait_send()))
+
+
+def k_tail(cfg, *refs):
+    st_a, st_b, ex7, ex8, side = cfg
+    it = iter(refs)
+
+    def take(n):
+        return [next(it) for _ in range(n)]
+
+    hbm = take(13)
+    gb, c1, c2, c3, q6, m16, m64, g_fout, g_fmid = take(9)
+    low_out, dlow_out, dlat_out, gf, q7, q8, hn, res_a, near_b = take(9)
+    local = take(13)
+    gw_a, dsb, sb, spad, wsp, sa, x_fast, dfa, fa, w_in, w_sc, dsp, lat = local
+    pad, gsp, gin, low, dlow, gw_b, near_a, ends, s1, s2, t1, t2, sems, out_sems = take(14)
+    near1, line1, near2 = take(len(st_a.near_scratch)), take(len(st_a.line_scratch)), take(len(st_b.near_scratch))
+    scr7 = take(len(ex7.local) + len(ex7.work))
+    scr8 = take(len(ex8.local) + len(ex8.work))
+    n_in = w_in.shape[0]
+    srcs = list(hbm)
+    for k in (9, 10):
+        srcs[k] = hbm[k].at[pl.ds(hbm[k].shape[0] - n_in, n_in)]
+    loads = [pltpu.make_async_copy(src, dst, sems.at[k]) for k, (src, dst) in enumerate(zip(srcs, local))]
+    count = exchange_hello(ex8)
+    for load in loads:
+        load.start()
+    near = Near(st_a, gw_a, near_a, near1)
+    line = Line(st_a, near_a, line1)
+    near_two = Near(st_b, gw_b, near_b, near2)
+    far = st_a.far
+    t_n, c = pad.shape[2], pad.shape[3]
+    wide = side * t_n
+    per = side // STEPS
+    fill = m16[0:1, :, 0:1]
+
+    def waits(*names):
+        for k in names:
+            loads[k].wait()
+
+    waits(1, 2)
+    scale, p_row, q_row = rows(c3, 0, 4, 2), rows(q6, 0, 0, 2), rows(q6, 1, 0, 2)
+    zero_ref(pad)
+
+    def fill_pad(h):
+        part = pl.ds(h * wide, wide)
+        d = back_norm(
+            scale, p_row, q_row, dsb[part].reshape(side, t_n, c), sb[part].reshape(side, t_n, c), fill
+        )
+        pad[h + 1, 1 : side + 1] = d.astype(BF16)
+
+    each(0, side, fill_pad)
+    waits(0)
+    pl.semaphore_wait(pltpu.get_barrier_semaphore(), count)
+    near.start()
+    waits(3, 4, 5, 6, 7, 8)
+    f_n = x_fast.shape[2]
+    p_n = x_fast.shape[1] // STEPS
+
+    def spatial(i):
+        h0 = i * per
+        turned = flat(pad[pl.ds(h0 + 1, per), 1 : side + 1]).T
+        acc = None
+        for a in range(3):
+            for b in range(3):
+                k = 3 * a + b
+                patch = flat(spad[pl.ds(h0 + a, per), b : b + side])
+                cols = slice(k * c, (k + 1) * c)
+                gsp[:, cols] = jnp.where(i == 0, 0.0, gsp[:, cols]) + dot(turned, patch)
+                block = pad[pl.ds(h0 + 2 - a, per), 2 - b : 2 - b + side]
+                part = dot_nt(flat(block), wsp[k])
+                acc = part if acc is None else acc + part
+        span = pl.ds(i * per * wide, per * wide)
+        z = sa[span]
+        back = acc * slope(z * rows(c2, 0, 1, 2) + rows(c2, 1, 1, 2))
+        dsb[span] = back
+        unit = z * rows(c2, 2, 1, 2) - rows(c2, 3, 1, 2)
+        sum_add(i, back.reshape(per * side, t_n, c), s1)
+        sum_add(i, (back * unit).reshape(per * side, t_n, c), s2)
+        f_span = pl.ds(i * p_n, p_n)
+        small = back_norm(
+            rows(c1, 0, 0, 1), rows(q6, 0, 2, 1), rows(q6, 1, 2, 1), dfa[f_span], fa[f_span], m64[0:1]
+        ).astype(BF16)
+        dlow[f_span] = small
+        packed = jnp.concatenate([flat(x_fast[s, f_span]) for s in range(x_fast.shape[0])], axis=1)
+        add_to(i, gin, dot_tn(flat(small), packed))
+        pl.when(i == 0)(lambda: near.add_pair(0, far // 2))
+        pl.when(i == 1)(lambda: near.add_pair(far // 2, far))
+
+    each(0, STEPS, spatial)
+    stats = scr7[0]
+    zero_ref(stats)
+    put_rows(stats, 0, sum_end(s1))
+    put_rows(stats, 2, sum_end(s2))
+    stores = [pltpu.make_async_copy(dlow, dlow_out, out_sems.at[0])]
+    stores[0].start()
+
+    def late():
+        for k in range(9):
+            gw_b[k * c : (k + 1) * c, :] = gsp[:, k * c : (k + 1) * c].T.astype(BF16)
+        if 9 * c < gw_b.shape[0]:
+            gw_b[9 * c :, :] = jnp.zeros((gw_b.shape[0] - 9 * c, c), BF16)
+        n = g_fout.shape[0]
+        gf[0:n, 0:LANES] = fold_wide(gin, x_fast.shape[0])
+        gf[0:n, LANES:] = g_fout[...]
+        gf[n : 2 * n, 0:LANES] = g_fmid[0:n, :]
+        gf[n : 2 * n, LANES:] = g_fmid[n : 2 * n, :]
+        gf[2 * n :, 0:LANES] = g_fmid[2 * n :, :]
+        gf[2 * n :, LANES:] = jnp.zeros((n, LANES), F32)
+
+    exchange_run(ex7, [gb, c2], [q7], scr7, late)
+    near_two.start()
+    near.add_plane(0, far - 1, lambda m: line.line(m).start())
+    near.add_plane(far - 1, far)
+    waits(9, 10, 11, 12)
+    scale7, p7, q7_row = rows(c2, 0, 1, 2), rows(q7, 0, 0, 2), rows(q7, 1, 0, 2)
+    block = per * wide
+
+    def join(i):
+        span = pl.ds(i * block, block)
+        shape = (per * side, t_n, c)
+        d = back_norm(scale7, p7, q7_row, dsb[span].reshape(shape), sa[span].reshape(shape), fill)
+        small = flat(d).astype(BF16)
+        low[span] = small
+        d = dot_nt(dsp[span], w_sc[...]) + dot_nt(small, w_in[...])
+        z = lat[span]
+        back = d * slope(z * rows(c1, 0, 1, 2) + rows(c1, 1, 1, 2))
+        sb[span] = back
+        unit = z * rows(c1, 2, 1, 2) - rows(c1, 3, 1, 2)
+        sum_add(i, back.reshape(shape), t1)
+        sum_add(i, (back * unit).reshape(shape), t2)
+        pl.when(i == 2)(lambda: near_two.add_pair(0, far))
+
+    each(0, STEPS, join)
+    stores.append(pltpu.make_async_copy(low, low_out, out_sems.at[1]))
+    stores.append(pltpu.make_async_copy(sb, dlat_out, out_sems.at[2]))
+    stores[1].start()
+    stores[2].start()
+    stats = scr8[0]
+    zero_ref(stats)
+    put_rows(stats, 0, sum_end(t1))
+    put_rows(stats, 2, sum_end(t2))
+
+    def post(q, sent):
+        zero_ref(ends)
+        for s in range(x_fast.shape[0]):
+            for step in range(STEPS):
+                for p in range(p_n):
+                    at = ((s * STEPS + step) * p_n + p) * t_n
+                    ends[0, step, s * 8 + p : s * 8 + p + 1, :] = sb[at : at + 1, :]
+                    ends[1, step, s * 8 + p : s * 8 + p + 1, :] = lat[at : at + 1, :]
+        d = back_norm(rows(c1, 0, 1, 2), rows(q, 0, 0, 2), rows(q, 1, 0, 2), ends[0], ends[1], m16[0, 0:1, 0:1])
+        sent[...] = d.astype(BF16)
+
+    exchange_run(ex8, [gb, c1], [q8, hn], scr8, None, post)
+    res_a[...] = line.total()
+    near_two.add_plane(0, far)
+    for store in stores:
+        store.wait()
+    line.end()
+    near.end()
+    near_two.end()
+
+
+def back_tail(st_a, st_b, ex7, ex8, hbm, small, side, t_n, c):
+    vm, anywhere = pl.BlockSpec(memory_space=pltpu.VMEM), pl.BlockSpec(memory_space=pl.ANY)
+    inner, f_n = hbm[7].shape[:2]
+    n = side * side * t_n
+    outs = [((n, c), BF16), ((inner, f_n, LANES), BF16), ((n, c), F32), (small[-1].shape[0:1] + (2 * LANES,), F32),
+            *ex7.outs, *ex8.outs, (st_a.chunk, BF16), (st_b.near_shape, BF16)]
+    local = [pltpu.VMEM((c,) + a.shape[1:] if k in (9, 10) else a.shape, a.dtype) for k, a in enumerate(hbm)]
+    width = hbm[6].shape[0] * hbm[6].shape[3]
+    scratch = [
+        pltpu.VMEM((side + 2, side + 2, t_n, c), BF16), pltpu.VMEM((c, 9 * c), F32), pltpu.VMEM((LANES, width), F32),
+        pltpu.VMEM((n, c), BF16), pltpu.VMEM((inner, f_n, LANES), BF16), pltpu.VMEM((st_b.rows_n, c), BF16),
+        pltpu.VMEM(st_a.near_shape, BF16), pltpu.VMEM((2, *ex8.post), F32), *[pltpu.VMEM((t_n, c), F32)] * 4,
+        pltpu.SemaphoreType.DMA((len(hbm),)), pltpu.SemaphoreType.DMA((3,)),
+        *st_a.near_scratch, *st_a.line_scratch, *st_b.near_scratch, *ex7.local, *ex7.work, *ex8.local, *ex8.work,
+    ]
+    return pl.pallas_call(
+        functools.partial(k_tail, (st_a, st_b, ex7, ex8, side)),
+        out_shape=[jax.ShapeDtypeStruct(s, d) for s, d in outs],
+        in_specs=[anywhere] * len(hbm) + [vm] * len(small),
+        out_specs=[anywhere] * 3 + [vm] * (len(outs) - 3),
+        scratch_shapes=[*local, *scratch],
+        compiler_params=pltpu.CompilerParams(collective_id=ex8.cid, has_side_effects=True, vmem_limit_bytes=VMEM_LIMIT),
+        name="tail",
+    )(*hbm, *small)
+
+
+def final_kernel(cfg, *refs):
+    first, second, third, both, offsets, heights = cfg
+    n = len(offsets)
+    (res_a, near_b), ins, (out_a, out_bc), refs = refs[:2], refs[2 : 2 + n], refs[2 + n : 4 + n], refs[4 + n :]
+    x, near_c, res = refs[:3]
+    at = [3]
+
+    def take(scratch):
+        at[0] += len(scratch)
+        return refs[at[0] - len(scratch) : at[0]]
+
+    far = first.far
+    share_a = Share(first, res_a, out_a, take(first.share_scratch))
+    line_b = Line(second, near_b, take(second.line_scratch))
+    near = Near(third, x, near_c, take(third.near_scratch))
+    line_c = Line(third, near_c, take(third.line_scratch))
+    share = Share(both, res, out_bc, take(both.share_scratch))
+
+    c = near.c
     barrier = pltpu.get_barrier_semaphore()
-    pl.semaphore_signal(barrier, inc=1, device_id=(other, me_f), device_id_type=MESH)
-    each(1, NEAR, lambda k: pl.semaphore_signal(
-        barrier, inc=1, device_id=(me_p, me_r * NEAR + q_of(k)), device_id_type=MESH))
-    each(1, far, lambda k: pl.semaphore_signal(
-        barrier, inc=1, device_id=(me_p, r_of(k) * NEAR + me_q), device_id_type=MESH))
+
+    def greet(device):
+        pl.semaphore_signal(barrier, inc=1, device_id=device, device_id_type=MESH)
+
+    greet(c.sibling)
+    each(1, NEAR, lambda k: greet(c.plane(k)))
+    each(1, far, lambda k: greet(c.line(k)))
     end = 0
     for ref, off, height in zip(ins, offsets, heights):
         x[off : off + height, :] = ref[...].astype(BF16)
@@ -994,173 +1297,107 @@
         x[end:, :] = jnp.zeros((x.shape[0] - end, x.shape[1]), BF16)
     pl.semaphore_wait(barrier, NEAR + far - 1)
 
-    def copy(src, dst, sem, index, device):
-        return pltpu.make_async_remote_copy(
-            src_ref=src, dst_ref=dst, send_sem=sem.at[(0, *index)], recv_sem=sem.at[(1, *index)],
-            device_id=device, device_id_type=MESH)
-
-    sibling = (other, me_f)
-
-    def pair(k, m):
-        return copy(x.at[at(other, q_of(k), r_of(m + 1))], land_a.at[k, m], sem_a, (k, m), sibling)
-
-    def plane(k, m):
-        return copy(buf_b.at[k, m], land_b.at[k, m], sem_b, (k, m), (me_p, me_r * NEAR + q_of(k)))
-
-    def line(m):
-        return copy(buf_c.at[m], land_c.at[m], sem_c, (m,), (me_p, r_of(m + 1) * NEAR + me_q))
-
-    def own(q, r):
-        return out_ref.at[at(me_p, q, r)]
-
-    def line_back(k):
-        return copy(own(me_q, me_r), own(me_q, me_r), sem_d, (k,), (me_p, r_of(k) * NEAR + me_q))
-
-    def plane_back(k, m):
-        part = own(me_q, r_of(far - m))
-        return copy(part, part, sem_e, (k, m), (me_p, me_r * NEAR + q_of(k)))
-
-    def pair_back(k, m):
-        part = own(q_of(NEAR - k), r_of(far - m))
-        return copy(part, part, sem_f, (k, m), sibling)
-
-    def both(body, first=0):
-        each(0, far, lambda m: each(first, NEAR, lambda k: body(k, m)))
-
-    def start_pair(m):
-        each(1, NEAR, lambda k: pair(k, m).start())
-        pair(0, m).start()
-
-    each(0, far, start_pair)
-
-    def add_pair(k, m):
-        pair(k, m).wait_recv()
-        buf_b[k, m] = (x[at(me_p, q_of(k), r_of(m + 1)), :].astype(F32) + land_a[k, m].astype(F32)).astype(BF16)
-        plane(k, m).start()
-
-    both(add_pair, 1)
-
-    def add_plane(m):
-        pair(0, m).wait_recv()
-        acc[...] = x[at(me_p, me_q, r_of(m + 1)), :].astype(F32) + land_a[0, m].astype(F32)
-
-        def more(k):
-            plane(k, m).wait_recv()
-            acc[...] += land_b[k, m].astype(F32)
-
-        each(1, NEAR, more)
-
-    def send_line(m):
-        add_plane(m)
-        buf_c[m] = acc[...].astype(BF16)
-        line(m).start()
-
-    each(0, far - 1, send_line)
-    add_plane(far - 1)
-
-    def add_line(m):
-        line(m).wait_recv()
-        acc[...] += land_c[m].astype(F32)
-
-    each(0, far - 1, add_line)
-    out_ref[at(me_p, me_q, me_r), :] = acc[...].astype(BF16)
-    each(1, far, lambda k: line_back(k).start())
-
-    def share(m):
-        each(1, NEAR, lambda k: plane_back(k, m).start())
-        pair_back(0, m).start()
-
-    share(0)
-
-    def relay(m):
-        line_back(m).wait_recv()
-        share(m)
-
-    each(1, far, relay)
-
-    def hand_on(k, m):
-        plane_back(k, m).wait_recv()
-        pair_back(k, m).start()
-
-    both(hand_on, 1)
-    both(lambda k, m: pair_back(k, m).wait())
-    both(lambda k, m: pair(k, m).wait_send())
-    both(lambda k, m: plane(k, m).wait_send(), 1)
-    each(0, far - 1, lambda m: line(m).wait_send())
-    each(1, far, lambda k: line_back(k).wait_send())
-    both(lambda k, m: plane_back(k, m).wait_send(), 1)
-
-
-def reduce_all(sizes, cid, parts):
-    paths, length = sizes
-    far = length // NEAR
-    unit = 16 * paths * length
+    near.start()
+    line_b.start(0, far)
+    share_a.start_line()
+    near.add_pair(0, far)
+    share_a.start_plane()
+    res[0 : second.ch, :] = line_b.total()
+    near.add_plane(0, far - 1, lambda m: line_c.line(m).start())
+    near.add_plane(far - 1, far)
+    share_a.relay(1, far)
+    res[second.ch :, :] = line_c.total()
+    share.start_line()
+    share.start_plane()
+    share_a.hand_on(0, far)
+    share.relay(1, far)
+    share.hand_on(0, far)
+    share_a.end()
+    share.end()
+    line_b.end()
+    line_c.end()
+    near.end()
+
+
+def final_sum(sizes, cid, first, second, res_a, near_b, parts):
+    width = res_a.shape[1]
     heights = tuple(p.shape[0] for p in parts)
     offsets = tuple(sum(heights[:k]) for k in range(len(parts)))
-    total = -(-sum(heights) // unit) * unit
-    ch = total // (paths * length)
-    vm = pl.BlockSpec(memory_space=pltpu.VMEM)
-    width = parts[0].shape[1]
-    quad = pltpu.VMEM((NEAR, far, ch, width), BF16)
-    single = pltpu.VMEM((far, ch, width), BF16)
-    out = pl.pallas_call(
-        functools.partial(reduce_kernel, (offsets, heights, ch, far)),
-        out_shape=jax.ShapeDtypeStruct((total, width), BF16),
-        in_specs=[vm] * len(parts),
-        out_specs=vm,
+    third = Stream(sizes, rows_for(sizes, sum(heights)), width)
+    both = Stream(sizes, second.rows_n + third.rows_n, width)
+    vm, hbm = pl.BlockSpec(memory_space=pltpu.VMEM), pl.BlockSpec(memory_space=pl.ANY)
+    out_a, out_bc = pl.pallas_call(
+        functools.partial(final_kernel, (first, second, third, both, offsets, heights)),
+        out_shape=[jax.ShapeDtypeStruct((s.rows_n, width), BF16) for s in (first, both)],
+        in_specs=[vm] * (2 + len(parts)),
+        out_specs=[hbm] * 2,
         scratch_shapes=[
-            pltpu.VMEM((total, width), BF16), quad, quad, quad, single, single,
-            pltpu.VMEM((ch, width), F32),
-            *[pltpu.SemaphoreType.DMA((2, NEAR, far))] * 2,
-            *[pltpu.SemaphoreType.DMA((2, far))] * 2,
-            *[pltpu.SemaphoreType.DMA((2, NEAR, far))] * 2,
+            pltpu.VMEM((third.rows_n, width), BF16), pltpu.VMEM(third.near_shape, BF16), pltpu.VMEM(both.chunk, BF16),
+            *first.share_scratch, *second.line_scratch, *third.near_scratch, *third.line_scratch, *both.share_scratch,
         ],
         compiler_params=pltpu.CompilerParams(collective_id=cid, has_side_effects=True, vmem_limit_bytes=VMEM_LIMIT),
-        name=f"reduce_{cid}",
-    )(*parts)
-    return out
-
-
-def k_unpack(pieces, src_ref, *refs):
-    n_out = len(refs) - 4
-    outs, (low, wide, sem_in, sem_out) = refs[:n_out], refs[n_out:]
-
-    def fetch(k):
-        row, height = pieces[k][:2]
-        part = pl.ds(row, height)
-        return pltpu.make_async_copy(src_ref.at[part], low.at[part], sem_in.at[k])
+        name="final_sum",
+    )(res_a, near_b, *parts)
+    return out_a, out_bc.reshape(-1, both.ch, width), third
+
+
+def k_unpack(pieces, cut, *refs):
+    (src_a, src_b), outs, (low_a, low_b, low_c, wide, sem_a, sem_b, sem_out) = refs[:2], refs[2:-7], refs[-7:]
+    lows = (low_a, low_b, low_c)
+    flats = [low_a, low_b.reshape(-1, low_b.shape[-1]), low_c.reshape(-1, low_c.shape[-1])]
+    starts = [sum(p[2] for p in pieces[:k]) for k in range(len(pieces))]
+
+    def fetch_a(k):
+        _, row, height, _, _ = pieces[k]
+        return pltpu.make_async_copy(src_a.at[pl.ds(row, height)], low_a.at[pl.ds(row, height)], sem_a.at[k])
+
+    def fetch_b(k):
+        part = src_b.at[:, pl.ds(0, cut)] if k == 1 else src_b.at[:, pl.ds(cut, src_b.shape[1] - cut)]
+        return pltpu.make_async_copy(part, lows[k], sem_b.at[k])
 
     def store(k):
-        row, height, out, col = pieces[k]
-        part = outs[out] if col is None else outs[out].at[:, pl.ds(col, src_ref.shape[1])]
-        return pltpu.make_async_copy(wide.at[pl.ds(row, height)], part, sem_out.at[k])
-
-    for k in range(len(pieces)):
-        fetch(k).start()
-    for k, (row, height, _, _) in enumerate(pieces):
-        fetch(k).wait()
-        wide[row : row + height, :] = low[row : row + height, :].astype(F32)
+        _, _, height, out, col = pieces[k]
+        part = outs[out] if col is None else outs[out].at[:, pl.ds(col, wide.shape[1])]
+        return pltpu.make_async_copy(wide.at[pl.ds(starts[k], height)], part, sem_out.at[k])
+
+    for k, piece in enumerate(pieces):
+        if piece[0] == 0:
+            fetch_a(k).start()
+    for k in (1, 2):
+        fetch_b(k).start()
+    seen = 0
+    for k, (src, row, height, _, _) in enumerate(pieces):
+        if src == 0:
+            fetch_a(k).wait()
+        elif src != seen:
+            fetch_b(src).wait()
+            seen = src
+        wide[starts[k] : starts[k] + height, :] = flats[src][row : row + height, :].astype(F32)
         store(k).start()
     for k in range(len(pieces)):
         store(k).wait()
 
 
-def unpack(reduced, pieces, shapes):
+def unpack(src_a, src_b, cut, pieces, shapes):
     hbm = pl.BlockSpec(memory_space=pl.ANY)
+    n, _, width = src_b.shape
     return pl.pallas_call(
-        functools.partial(k_unpack, pieces),
+        functools.partial(k_unpack, pieces, cut),
         out_shape=[jax.ShapeDtypeStruct(s, F32) for s in shapes],
-        in_specs=[hbm],
+        in_specs=[hbm] * 2,
         out_specs=[hbm] * len(shapes),
         scratch_shapes=[
-            pltpu.VMEM(reduced.shape, BF16),
-            pltpu.VMEM(reduced.shape, F32),
+            pltpu.VMEM(src_a.shape, BF16),
+            pltpu.VMEM((n, cut, width), BF16),
+            pltpu.VMEM((n, src_b.shape[1] - cut, width), BF16),
+            pltpu.VMEM((sum(p[2] for p in pieces), width), F32),
             pltpu.SemaphoreType.DMA((len(pieces),)),
+            pltpu.SemaphoreType.DMA((3,)),
             pltpu.SemaphoreType.DMA((len(pieces),)),
         ],
         compiler_params=pltpu.CompilerParams(vmem_limit_bytes=VMEM_LIMIT),
         name="unpack",
-    )(reduced)
+    )(src_a, src_b)
 
 
 def k_prep(x_hbm, fill_ref, clip_ref, norm_ref, wfi_ref, wfm_ref, wfo_ref,
@@ -1395,11 +1632,14 @@
     q5, hp, hn = exchange_alone(ex5, st, gb, [c4, c2], up, down)
 
     c_cat = w_slow_in.shape[0]
-    gw_out, dsp, dsb, dfa, g_fmid, q6 = call(
+    width = in_slow
+    stream_a = Stream(sizes, rows_for(sizes, c_cat * c_slow // width), width)
+    stream_b = Stream(sizes, rows_for(sizes, 9 * in_slow), width)
+    gw_short, gw_sout, dsp, dsb, dfa, g_fmid, q6 = call(
         k_back_out,
         [sb_(x_slow), sb_(lact), sb_(dy), sb_(sp), sb_(sact), sb_(sb4), fb_(dfb), fb_(fb), fb_(fa), fb_(ftap), blocked(hp, 0, 1), blocked(hn, 0, 1),
          whole(c1), whole(c2), whole(c3), whole(c4), whole(q5), whole(m16), whole(m64), whole(w_slow_out), whole(wback)],
-        [out_whole(((c_cat + in_slow) * c_slow // in_slow, in_slow), BF16), slow_out(c_slow, BF16),
+        [out_whole((stream_a.rows_n, width), BF16), out_whole((c_slow, width), BF16), slow_out(c_slow, BF16),
          slow_out(in_slow, F32), fast_out(LANES, F32), out_whole((3 * in_fast, LANES), F32), STAT],
         [*acc(t_n, in_slow, 2), *acc(f_n, LANES, 2), *acc(c_cat, c_slow, 1), *acc(in_slow, c_slow, 1),
          *acc(LANES, 3 * LANES, 1)],
@@ -1408,54 +1648,44 @@
         [gb, c3, c1],
     )
 
-    grid = (side, side, t_n, in_slow)
-    dsa, dfa_low, gw_mid, gw_fast, q7 = call(
-        k_back_spatial,
-        [whole(dsb.reshape(grid)), whole(sb), blocked(sa.reshape(grid), 0, rows_n), whole(pad), sb_(x_fast), fb_(dfa), fb_(fa),
-         whole(g_fout), whole(g_fmid), whole(c1), whole(c2), whole(c3), whole(q6), whole(m16), whole(m64), whole(wsp)],
-        [out_blocked(grid, F32, 0, rows_n), fast_out(LANES, BF16), out_whole((9 * in_slow, in_slow), BF16),
-         out_whole((3 * in_fast, 2 * LANES), F32), STAT],
-        [*acc(t_n, in_slow, 2), pltpu.VMEM((side + 2, side + 2, t_n, in_slow), BF16), *acc(in_slow, 9 * in_slow, 1),
-         *acc(LANES, groups * c_fast, 1)],
-        "back_spatial",
+    def rows2(a):
+        return a.reshape(-1, a.shape[-1])
+
+    dsa_low, dfa_low, dlat, gw_fast, q7, q8, hn, res_a, near_b = back_tail(
+        stream_a, stream_b,
         Exchange(sizes, 7, 4, bwd=(("plain", 0, 1, 8, 2, 0, 2),)),
-        [gb, c2],
+        Exchange(sizes, 7, 4, bwd=(("plain", 0, 1, 6, 2, 0, 2),), post=(STEPS, groups * 8, c_lat)),
+        [gw_short, rows2(dsb), rows2(sb), pad, wsp, rows2(sa), x_fast, dfa, fa, w_slow_in, w_shortcut, rows2(dsp), rows2(lat)],
+        [gb, c1, c2, c3, q6, m16, m64, g_fout, g_fmid],
+        side, t_n, in_slow,
     )
-
-    gw_in, slow_gx, dlat, down, st = call(
-        k_back_join,
-        [sb_(x_slow), sb_(lact), sb_(dsa.reshape(sl + (in_slow,))), sb_(sa), sb_(dsp), sb_(lat), whole(c1), whole(c2), whole(q7), whole(m16),
-         whole(w_slow_in), whole(w_shortcut)],
-        [out_whole((c_cat, in_slow), BF16), slow_out(c_slow, BF16), slow_out(c_lat, F32),
-         out_blocked((STEPS, 2, groups, 8, c_lat), F32, 0, 1), stat(4)],
-        [*acc(t_n, c_lat, 2), *acc(in_slow, c_cat, 1)],
-        "back_join",
+    slow_gx, gw_in = call(
+        k_slow_grad,
+        [sb_(x_slow), sb_(lact), sb_(dsa_low.reshape(sl + (in_slow,))), sb_(dsp), whole(w_slow_in), whole(w_shortcut)],
+        [slow_out(c_slow, BF16), out_whole((c_cat, in_slow), BF16)], acc(in_slow, c_cat, 1), "slow_grad",
     )
-    ex8 = Exchange(sizes, 8, 4, bwd=(("plain", 0, 1, 6, 2, 0, 2),), down=down.shape)
-    q8, hn = exchange_alone(ex8, st, gb, [c1], None, down)
-
     fast_gx, gw_lat = call(
-        k_last,
-        [sb_(dlat), sb_(lat), sb_(taps), blocked(hn, 0, 1), fb_(df), fb_(dfa_low), whole(c1), whole(q8), whole(m16),
-         whole(wlat), whole(wfa)],
+        k_fast_grad,
+        [sb_(dlat.reshape(sl + (c_lat,))), sb_(lat), sb_(taps), blocked(hn, 0, 1), fb_(df), fb_(dfa_low), whole(c1), whole(q8),
+         whole(m16), whole(wlat), whole(wfa)],
         [out_blocked((groups, inner, f_n, c_fast), BF16, 1, p_n), out_whole((5 * c_fast, c_lat), BF16)],
         [pltpu.VMEM((groups * p_n * f_n, c_fast), F32), *acc(c_lat, 5 * c_fast, 1)],
-        "last",
+        "fast_grad",
     )
-
-    reduced = reduce_all(sizes, 9, [gw_out, gw_mid, gw_in, gw_lat, gw_fast])
+    sum_a, sum_bc, _ = final_sum(sizes, 9, stream_a, stream_b, res_a, near_b, [gw_sout, gw_in, gw_lat, gw_fast])
     blocks = c_slow // in_slow
-    pieces, at = [], 0
-    for out, tall in ((0, c_cat), (1, in_slow)):
-        for n in range(blocks):
-            pieces.append((at, tall, out, n * in_slow))
-            at += tall
-    for out, tall in ((2, gw_mid.shape[0]), (3, c_cat), (4, gw_lat.shape[0]), (5, gw_fast.shape[0])):
-        pieces.append((at, tall, out, None))
+    pieces = [(0, n * c_cat, c_cat, 0, n * width) for n in range(blocks)]
+    pieces.append((1, 0, 9 * in_slow, 2, None))
+    at = 0
+    for n in range(blocks):
+        pieces.append((2, at, in_slow, 1, n * width))
+        at += in_slow
+    for out, tall in ((3, c_cat), (4, gw_lat.shape[0]), (5, gw_fast.shape[0])):
+        pieces.append((2, at, tall, out, None))
         at += tall
     g_short, g_sout, gw_mid, gw_in, gw_lat, gw_fast = unpack(
-        reduced, tuple(pieces),
-        [(c_cat, c_slow), (in_slow, c_slow), gw_mid.shape, (c_cat, in_slow), gw_lat.shape, gw_fast.shape],
+        sum_a, sum_bc, stream_b.ch, tuple(pieces),
+        [(c_cat, c_slow), (in_slow, c_slow), (9 * in_slow, width), (c_cat, in_slow), gw_lat.shape, gw_fast.shape],
     )
     taps_t = [gw_fast[in_fast : 2 * in_fast, :in_fast], gw_fast[in_fast : 2 * in_fast, c_fast : c_fast + in_fast],
               gw_fast[2 * in_fast :, :in_fast]]

time: 345 us -> 324 us (0.939)
  Pallas kernels: 334 us -> 314 us
    pallas_call x9 -> x8, Pallas kernels: 196 us -> 169 us  [call(): pl.pallas_call(body, grid=(STEPS,), in_specs=[pl.BlockSpec(b, m) for _, b...]
    pallas_call x2 -> x3, Pallas kernels: 81.3 us -> 105 us  [the longest x1 51.3 us: back_tail(): pl.pallas_call(functools.partial(k_tail, (st_a, st_b, ex7, ex8, side)), o...]
    pallas_call x3 -> x2, Pallas kernels: 42 us -> 24.4 us  [exchange_alone(): pl.pallas_call(kernel, out_shape=[jax.ShapeDtypeStruct(s, d) for s, d in...]
where the time goes in v4:
time: 324 us; the launch traced here: 323 us
  Pallas kernels  314 us (97%)
  local copies, waits for them, and re-layouts  7.55 us (2%)
    pallas_call x8, Pallas kernels, call(): pl.pallas_call(body, grid=(STEPS,), in_specs=[pl.BlockSpec(b, m) for _, b...  169 us
    pallas_call x1, Pallas kernels, back_tail(): pl.pallas_call(functools.partial(k_tail, (st_a, st_b, ex7, ex8, side)), o...  51.3 us
    pallas_call x1, Pallas kernels, final_sum(): pl.pallas_call(functools.partial(final_kernel, (first, second, third, bot...  48.4 us
    pallas_call x2, Pallas kernels, exchange_alone(): pl.pallas_call(kernel, out_shape=[jax.ShapeDtypeStruct(s, d) for s, d in...  24.4 us
    pallas_call x1, Pallas kernels, prepare(): pl.pallas_call(k_prep, out_shape=[jax.ShapeDtypeStruct(s, d) for s, d in...  14.8 us

profile of v4, /device:TPU:0, one launch (start us, length us, event | category | flops | bytes accessed | tf_op | source)
XLA Modules:
  0.0 322.6 jit_solution(7394763496926758530)
XLA Ops:
  0.6 0.8 fusion
  1.4 0.6 copy.33
  2.0 14.8 %prepare.1 = (f32[7,4,8,256]{3,2,1,0:T(8,128)}, f32[2,32,128]{2,1,0:T(8,128)}, f32[3,16,128]{2,1,0:T(8,128)}, f32[3,64,128]{2,1,0:T(8,128)}, bf16[128,512]{1,0:T...) custom-call(bf16[4,49,64,128]{3,2,1,0:T(8,128)(2,1)} %bitcast.91, ...), custom_call_target="tpu_custom_call" | custom-call | tf_op jit(solution)/shard_map/prepare/pallas_call | solution.py:1496
  16.8 15.3 %first.1 = (f32[49,64,128]{2,1,0:T(8,128)}, f32[4,49,16,256]{3,2,1,0:T(8,128)}, bf16[4,49,16,640]{3,2,1,0:T(8,128)(2,1)}, f32[5,3,128]{2,1,0:T(4,128)}, f32[7,8,128]{2,1,0:T(8,128)}, /*index=5*/f32[7,8,128]{2,1,0:T(8,128)}) custom-call(bf16[4,49,64,128]{3,2,1,0:T(8,128)(2,1)} %bitcast.92, f32[7,4,8,256]{3,2,1,0:T(8,128)} %get-tuple-element.82.refs_1_, ...), custom_call_target="tpu_custom_call" | custom-call | tf_op jit(solution)/shard_map/first/pallas_call | solution.py:391
  32.1 29.1 %join.1 = (bf16[4,49,16,256]{3,2,1,0:T(8,128)(2,1)}, bf16[49,64,384]{2,1,0:T(8,128)(2,1)}, f32[4,49,16,256]{3,2,1,0:T(8,128)}, f32[4,49,16,1024]{3,2,1,0:T(8,128...) custom-call(bf16[4,49,16,1024]{3,2,1,0:T(8,128)(2,1)} %bitcast.88, f32[4,49,16,256]{3,2,1,0:T(8,128)} %get-tuple-element.87.refs_1_, ...), custom_call_target="tpu_custom_call" | custom-call | tf_op jit(solution)/shard_map/join/pallas_call | solution.py:391
  61.2 18.8 %spatial.1 = (bf16[16,16,16,256]{3,2,1,0:T(8,128)(2,1)}, f32[14,14,16,256]{3,2,1,0:T(8,128)}, bf16[49,64,128]{2,1,0:T(8,128)(2,1)}, f32[5,6,128]{2,1,0:T(8,128)}) custom-call(f32[14,14,16,256]{3,2,1,0:T(8,128)} %bitcast.100, f32[49,64,128]{2,1,0:T(8,128)} %get-tuple-element.94.refs_1_.refs_5_.refs_7_, ...), custom_call_target="tpu_custom_call" | custom-call | tf_op jit(solution)/shard_map/spatial/pallas_call | solution.py:391
  80.0 13.8 %expand.1 = (bf16[4,49,16,256]{3,2,1,0:T(8,128)(2,1)}, bf16[4,49,64,128]{3,2,1,0:T(8,128)(2,1)}, f32[49,64,512]{2,1,0:T(8,128)}, f32[32,128]{1,0:T(8,128)}) custom-call(f32[4,49,16,256]{3,2,1,0:T(8,128)} %bitcast.96, bf16[49,64,128]{2,1,0:T(8,128)(2,1)} %get-tuple-element.98.refs_1_.refs_4_, bf16[4,49,64,128]{3,2,1,0:T(8,128)(2,1)} %bitcast.93, ...), custom_call_target="tpu_custom_call" | custom-call | tf_op jit(solution)/shard_map/expand/pallas_call | solution.py:391
  93.8 11.7 %exchange_4.1 = (f32[5,8,128]{2,1,0:T(8,128)}, f32[4,4,128]{2,1,0:T(4,128)}) custom-call(f32[32,128]{1,0:T(8,128)} %get-tuple-element.103.refs_0_, f32[2,32,128]{2,1,0:T(8,128)} %get-tuple-element.86.refs_6_.refs_11_.refs_7_.refs_1_.refs_21_.refs_13_, f32[5,6,128]{2,1,0:T(8,128)} %get-tuple-element.99.refs_4_.refs_2_.refs_7_.refs_14_.refs_22_.refs_16_), custom_call_target="tpu_custom_call" | custom-call | tf_op jit(solution)/shard_map/exchange_4/pallas_call | solution.py:343
  105.5 0.7 slice_bitcast_fusion.14
  106.2 23.8 %out.1 = (bf16[4,49,16,1024]{3,2,1,0:T(8,128)(2,1)}, f32[4,49,16,1024]{3,2,1,0:T(8,128)}, f32[49,64,128]{2,1,0:T(8,128)}, f32[32,128]{1,0:T(8,128)}, f32[7,2,8,1...) custom-call(bf16[4,49,16,256]{3,2,1,0:T(8,128)(2,1)} %get-tuple-element.100.refs_0_.refs_4_, ...), custom_call_target="tpu_custom_call" | custom-call | tf_op jit(solution)/shard_map/out/pallas_call | solution.py:391
  130.0 12.7 %exchange_5.1 = (f32[4,17,128]{2,1,0:T(8,128)}, f32[7,2,8,128]{3,2,1,0:T(8,128)}, f32[7,2,8,128]{3,2,1,0:T(8,128)}) custom-call(f32[32,128]{1,0:T(8,128)} %get-tuple-element.112.refs_0_, f32[2,32,128]{2,1,0:T(8,128)} %get-tuple-element.86.refs_6_.refs_11_.refs_7_.refs_1_.refs_21_.refs_13_, f32[5,8,128]{2,1,0:T(8,128)} %get-tuple-element.104.refs_8_.refs_2_.refs_15_, ...), custom_call_target="tpu_custom_call" | custom-call | tf_op jit(solution)/shard_map/exchange_5/pallas_call | solution.py:343
  142.7 38.2 %back_out.1 = (bf16[5120,256]{1,0:T(8,128)(2,1)}, bf16[1024,256]{1,0:T(8,128)(2,1)}, bf16[4,49,16,1024]{3,2,1,0:T(8,128)(2,1)}, f32[4,49,16,256]{3,2,1,0:T(8,128...) custom-call(bf16[4,49,16,1024]{3,2,1,0:T(8,128)(2,1)} %bitcast.89, ...), custom_call_target="tpu_custom_call" | custom-call | tf_op jit(solution)/shard_map/back_out/pallas_call | solution.py:391
  180.9 51.3 %tail.1 = (bf16[3136,256]{1,0:T(8,128)(2,1)}, bf16[49,64,128]{2,1,0:T(8,128)(2,1)}, f32[3136,256]{1,0:T(8,128)}, f32[96,256]{1,0:T(8,128)}, f32[4,2,128]{2,1,0:T...) custom-call(bf16[5120,256]{1,0:T(8,128)(2,1)} %get-tuple-element.119, ...), custom_call_target="tpu_custom_call" | custom-call | tf_op jit(solution)/shard_map/tail/pallas_call | solution.py:1254
  232.2 16.8 %slow_grad.1 = (bf16[4,49,16,1024]{3,2,1,0:T(8,128)(2,1)}, bf16[1280,256]{1,0:T(8,128)(2,1)}) custom-call(bf16[4,49,16,1024]{3,2,1,0:T(8,128)(2,1)} %bitcast.90, bf16[4,49,16,256]{3,2,1,0:T(8,128)(2,1)} %get-tuple-element.108.refs_1_, bf16[4,49,16,256]{3,2,1,0:T(8,128)(2,1)} %bitcast.109, bf16[4,49,16,1024]{3,2,1,0:T(8,128)(2,1)} %get-tuple-element.123.refs_3_, ...), custom_call_target="tpu_custom_call" | custom-call | tf_op jit(solution)/shard_map/slow_grad/pallas_call | solution.py:391
  249.1 0.0 copy-start
  249.1 0.0 copy-start.1
  249.1 13.3 %fast_grad.1 = (bf16[4,49,64,128]{3,2,1,0:T(8,128)(2,1)}, bf16[640,256]{1,0:T(8,128)(2,1)}) custom-call(f32[4,49,16,256]{3,2,1,0:T(8,128)} %bitcast.105, f32[4,49,16,256]{3,2,1,0:T(8,128)} %get-tuple-element.87.refs_1_, bf16[4,49,16,640]{3,2,1,0:T(8,128)(2,1)} %get-tuple-element.130.refs_2_, bf16[7,32,256]{2,1,0:T(8,128)(2,1)} %get-tuple-element.131.refs_3_, ...), custom_call_target="tpu_custom_call" | custom-call | tf_op jit(solution)/shard_map/fast_grad/pallas_call | solution.py:391
  262.4 0.0 copy-done
  262.4 0.0 copy-done.1
  262.4 0.7 slice_bitcast_fusion.15
  263.1 0.7 slice_bitcast_fusion.4
  263.8 0.7 slice_bitcast_fusion.8
  264.5 0.7 concatenate.7
  265.2 0.7 concatenate.6
  265.9 48.4 %final_sum.1 = (bf16[5120,256]{1,0:T(8,128)(2,1)}, bf16[5632,256]{1,0:T(8,128)(2,1)}) custom-call(bf16[160,256]{1,0:T(8,128)(2,1)} %get-tuple-element.135.refs_0_, bf16[4,80,256]{2,1,0:T(8,128)(2,1)} %get-tuple-element.136.refs_1_, bf16[1024,256]{1,0:T(8,128)(2,1)} %get-tuple-element.137.refs_2_, bf16[1280,256]{1,0:T(8,128)(2,1)} %get-tuple-element.138.refs_3_, ...), custom_call_target="tpu_custom_call" | custom-call | tf_op jit(solution)/shard_map/final_sum/pallas_call | solution.py:1329
  314.3 5.6 %unpack.1 = (f32[1280,1024]{1,0:T(8,128)}, f32[256,1024]{1,0:T(8,128)}, f32[2304,256]{1,0:T(8,128)}, f32[1280,256]{1,0:T(8,128)}, f32[640,256]{1,0:T(8,128)}, /*index=5*/f32[96,256]{1,0:T(8,128)}) custom-call(bf16[5120,256]{1,0:T(8,128)(2,1)} %get-tuple-element.141.refs_0_, bf16[32,176,256]{2,1,0:T(8,128)(2,1)} %bitcast.108), custom_call_target="tpu_custom_call" | custom-call | tf_op jit(solution)/shard_map/unpack/pallas_call | solution.py:1384
  319.8 1.3 fusion.1
  321.2 0.8 slice_bitcast_fusion.2
  321.9 0.7 copy.30
  (2 shorter events, 0.0 us)
Async XLA Ops:
  249.1 13.3 %copy-start = (f32[4,2,128]{2,1,0:T(2,128)S(1)}, f32[4,2,128]{2,1,0:T(2,128)}, u32[]{:S(2)}) copy-start(f32[4,2,128]{2,1,0:T(2,128)} %get-tuple-element.133.refs_7_) | copy-start | bytes 12292
  249.1 13.4 %copy-start.1 = (f32[4,2,128]{2,1,0:T(2,128)S(1)}, f32[4,2,128]{2,1,0:T(2,128)}, u32[]{:S(2)}) copy-start(f32[4,2,128]{2,1,0:T(2,128)} %get-tuple-element.149) | copy-start | bytes 12292

commit v5 on v4

--- a/solution.py
+++ b/solution.py
@@ -326,40 +326,21 @@
         self.local = [pltpu.VMEM(self.stats, F32), pltpu.VMEM(up or none, F32), pltpu.VMEM(down or none, F32)]
 
 
-def exchange_alone(ex, stats, gb, coefs=(), up=None, down=None):
-    vm = pl.BlockSpec(memory_space=pltpu.VMEM)
-    operands = [stats, gb, *coefs] + [h for h in (up, down) if h is not None]
-    n_in, n_out = len(operands), len(ex.outs)
-
-    def kernel(*refs):
-        ins, outs, work = refs[:n_in], refs[n_in : n_in + n_out], refs[n_in + n_out :]
-        count = exchange_hello(ex)
-        pl.semaphore_wait(pltpu.get_barrier_semaphore(), count)
-        halos = list(ins[2 + len(coefs) :])
-        up_ref = halos.pop(0) if ex.up else None
-        down_ref = halos.pop(0) if ex.down else None
-        exchange_run(ex, ins[1 : 2 + len(coefs)], outs, [ins[0], up_ref, down_ref, *work])
-
-    return pl.pallas_call(
-        kernel,
-        out_shape=[jax.ShapeDtypeStruct(s, d) for s, d in ex.outs],
-        in_specs=[vm] * n_in,
-        out_specs=[vm] * n_out,
-        scratch_shapes=ex.work,
-        compiler_params=pltpu.CompilerParams(collective_id=ex.cid, has_side_effects=True),
-        name=f"exchange_{ex.cid}",
-    )(*operands)
-
-
 STAT, UP, DOWN = "stat", "up", "down"
 
 
-def call(kernel, ins, outs, scratch=(), name=None, ex=None, ex_ins=()):
+def call(kernel, ins, outs, scratch=(), name=None, ex=None, ex_ins=(), pre=None, pre_ins=()):
     real = [o for o in outs if not isinstance(o, str)]
-    extra_in = [whole(a) for a in ex_ins]
+    given = ins
+    ins = [a for a in given if not isinstance(a, int)]
+    extra_in = [whole(a) for a in (*ex_ins, *pre_ins)]
     extra_out = [out_whole(s, d) for s, d in ex.outs] if ex else []
+    local = [*ex.local, *ex.work] if ex else []
+    n_local = len(local)
+    if pre:
+        extra_out.append(out_whole(*pre.outs[0]))
+        local += [*pre.work, *[pltpu.VMEM(shape, d) for shape, d in pre.outs[1:]]]
     all_in, all_out = [*ins, *extra_in], [*real, *extra_out]
-    local = [*ex.local, *ex.work] if ex else []
     sizes = [len(ins), len(extra_in), len(real), len(extra_out), len(scratch), len(local)]
     ends = [sum(sizes[: k + 1]) for k in range(len(sizes))]
 
@@ -370,10 +351,24 @@
             return
         i = pl.program_id(0)
 
+        p_ins, p_outs, p_scr = x_in[len(ex_ins) :], [], x_scr[n_local:]
+        x_in, x_scr = x_in[: len(ex_ins)], x_scr[:n_local]
+        if pre:
+            n = len(pre.work)
+            p_outs = [x_out[-1], *p_scr[n:]]
+            x_out = x_out[:-1]
+
         @pl.when(i == 0)
         def _():
-            exchange_hello(ex)
-
+            exchange_hello(pre or ex)
+            if pre:
+                pl.semaphore_wait(pltpu.get_barrier_semaphore(), len_peers(pre))
+                exchange_run(pre, p_ins[3:], p_outs, [*p_ins[:3], *p_scr[:n]])
+
+        if pre:
+            it_in = iter(k_in)
+            views = [p_outs[0], *[o.at[pl.ds(i, 1)] for o in p_outs[1:]]]
+            k_in = [views[a] if isinstance(a, int) else next(it_in) for a in given]
         named = {STAT: x_scr[0]}
         if ex.up:
             named[UP] = x_scr[1].at[pl.ds(i, 1)]
@@ -384,7 +379,8 @@
 
         @pl.when(i == STEPS - 1)
         def _():
-            pl.semaphore_wait(pltpu.get_barrier_semaphore(), len_peers(ex))
+            if not pre:
+                pl.semaphore_wait(pltpu.get_barrier_semaphore(), len_peers(ex))
             exchange_run(ex, x_in, x_out, x_scr, late)
 
     params = {"collective_id": ex.cid, "has_side_effects": True} if ex else {}
@@ -435,9 +431,8 @@
     return [jnp.broadcast_to(ref[(*index, slice(p, p + 1))], (height, ref.shape[-1])) for p in range(count)]
 
 
-def k_first(x_ref, tail_ref, m16_ref, m64_ref, wfa_ref, wlat_ref,
+def k_first(i, x_ref, tail_ref, m16_ref, m64_ref, wfa_ref, wlat_ref,
             fa_ref, lat_ref, taps_ref, st_ref, up_ref, down_ref, xs, fm, fv, lm, lv):
-    i = pl.program_id(0)
     x = x_ref[...]
     s_n, p_n, f_n, _ = x.shape
     packed = jnp.concatenate([flat(x[s]) for s in range(s_n)], axis=1)
@@ -500,9 +495,8 @@
     return before, after
 
 
-def k_join(x_ref, lat_ref, fa_ref, hp_ref, hn_ref, c1_ref, m16_ref, m64_ref, win_ref, wsc_ref, wmid_ref,
+def k_join(i, x_ref, lat_ref, fa_ref, hp_ref, hn_ref, c1_ref, m16_ref, m64_ref, win_ref, wsc_ref, wmid_ref,
            lact_ref, ftap_ref, sa_ref, sp_ref, fb_ref, st_ref, am, av, pm, pv, bm, bv):
-    i = pl.program_id(0)
     s_n, p_n, t_n, c_slow = x_ref.shape
     c_lat = lat_ref.shape[-1]
     v = flat(lat_ref[...]) * rows(c1_ref, 0, 1, 2) + rows(c1_ref, 1, 1, 2)
@@ -564,9 +558,8 @@
         put_rows(st_ref, 22, count_row(m16_ref, positions))
 
 
-def k_spatial(sa_ref, fb_ref, c2_ref, m16_ref, m64_ref, wsp_ref, wout_ref,
+def k_spatial(i, sa_ref, fb_ref, c2_ref, m16_ref, m64_ref, wsp_ref, wout_ref,
               pad_ref, sb_ref, fact_ref, st_ref, sm, sv, cm, cv):
-    i = pl.program_id(0)
     h_n, w_n, t_n, c = sa_ref.shape
 
     @pl.when(i == 0)
@@ -609,10 +602,9 @@
         put_rows(st_ref, 12, count_row(m16_ref, h_n * w_n))
 
 
-def k_expand(sb_ref, fact_ref, x_ref, cot_ref, c3_ref, m16_ref, m64_ref, wso_ref, wout_ref,
+def k_expand(i, sb_ref, fact_ref, x_ref, cot_ref, c3_ref, m16_ref, m64_ref, wso_ref, wout_ref,
              sact_ref, fout_ref, df_ref, st_ref, cm, cv, s1, s2):
-    i = pl.program_id(0)
-    s_n, p_n, t_n, c = sb_ref.shape
+    s_n, p_n, t_n = x_ref.shape[0], fact_ref.shape[0], sb_ref.shape[-2]
     v = flat(sb_ref[...]) * rows(c3_ref, 0, 4, 2) + rows(c3_ref, 1, 4, 2)
     sact = (v * sig(v)).astype(BF16)
     sact_ref[...] = sact.reshape(sact_ref.shape)
@@ -648,6 +640,141 @@
         put_rows(st_ref, 16, sum_end(s1))
         put_rows(st_ref, 20, sum_end(s2))
         put_rows(st_ref, 24, count_row(m16_ref, positions))
+
+
+def run_resident(kernel, ex_list, hbm, small, locals_, outs, scratch, name):
+    vm, anywhere = pl.BlockSpec(memory_space=pltpu.VMEM), pl.BlockSpec(memory_space=pl.ANY)
+    for ex in ex_list:
+        outs = [*outs, *[(shape, dtype, False) for shape, dtype in ex.outs]]
+    work = [w for ex in ex_list for w in (*ex.local, *ex.work)]
+    sizes = [len(hbm), len(small), len(outs), len(hbm), len(locals_), len(scratch), 1]
+    ends = [sum(sizes[: k + 1]) for k in range(len(sizes))]
+
+    def body(*refs):
+        h, sm, o, loaded, kept, scr, (sems,) = (refs[e - n : e] for e, n in zip(ends, sizes))
+        rest, at = [], ends[-1]
+        for ex in ex_list:
+            n = len(ex.local) + len(ex.work)
+            rest.append(refs[at : at + n])
+            at += n
+        loads = [pltpu.make_async_copy(a, b, sems.at[k]) for k, (a, b) in enumerate(zip(h, loaded))]
+        greeter = max(ex_list, key=lambda ex: ex.greets)
+        count = exchange_hello(greeter)
+        for load in loads:
+            load.start()
+        kernel(loads, lambda: pl.semaphore_wait(pltpu.get_barrier_semaphore(), count), loaded, sm, kept, scr, o, rest)
+
+    return pl.pallas_call(
+        body,
+        out_shape=[jax.ShapeDtypeStruct(shape, dtype) for shape, dtype, _ in outs],
+        in_specs=[anywhere] * len(hbm) + [vm] * len(small),
+        out_specs=[anywhere if stays else vm for _, _, stays in outs],
+        scratch_shapes=[
+            *[pltpu.VMEM(a.shape, a.dtype) for a in hbm], *[pltpu.VMEM(*k) for k in locals_], *scratch,
+            pltpu.SemaphoreType.DMA((len(hbm),)), *work,
+        ],
+        compiler_params=pltpu.CompilerParams(
+            collective_id=ex_list[0].cid, has_side_effects=True, vmem_limit_bytes=VMEM_LIMIT
+        ),
+        name=name,
+    )(*hbm, *small)
+
+
+def stores_of(pairs, sems):
+    return [pltpu.make_async_copy(a, b, sems.at[k]) for k, (a, b) in enumerate(pairs)]
+
+
+def k_front(exs, loads, met, loaded, small, kept, scratch, outs, work):
+    x_fast, wlat, x_slow, w_in, w_sc = loaded
+    tail_ref, gb, m16, m64, wfa, wmid = small
+    fa, lat, taps, lact, ftap, sa, sp, fb = kept
+    xs, fm, fv, lm, lv, am, av, pm, pv, bm, bv, sems, sp_sems = scratch
+    big, (c1, hp, hn, c2) = outs[:8], outs[8:]
+    p_n = fa.shape[0] // STEPS
+    copies = dict(zip((0, 1, 2, 3, 4, 5, 7), stores_of([p for k, p in enumerate(zip(kept, big)) if k != 6], sems)))
+    st1, up, down = work[0][:3]
+    loads[0].wait()
+    loads[1].wait()
+
+    def first(i):
+        part, one = pl.ds(i * p_n, p_n), pl.ds(i, 1)
+        k_first(i, x_fast.at[:, part], tail_ref.at[one], m16, m64, wfa, wlat, fa.at[part], lat.at[:, part],
+                taps.at[:, part], st1, up.at[one], down.at[one], xs, fm, fv, lm, lv)
+
+    each(0, STEPS, first)
+    met()
+    for k in (0, 1, 2):
+        copies[k].start()
+    exchange_run(exs[0], [gb], [c1, hp, hn], work[0])
+    for k in (2, 3, 4):
+        loads[k].wait()
+
+    def store_sp(i):
+        part = pl.ds(i * p_n, p_n)
+        return pltpu.make_async_copy(sp.at[:, part], big[6].at[:, part], sp_sems.at[i])
+
+    def join(i):
+        part, one = pl.ds(i * p_n, p_n), pl.ds(i, 1)
+        k_join(i, x_slow.at[:, part], lat.at[:, part], fa.at[part], hp.at[one], hn.at[one], c1, m16, m64, w_in, w_sc, wmid,
+               lact.at[:, part], ftap.at[part], sa.at[:, part], sp.at[:, part], fb.at[part], work[1][0],
+               am, av, pm, pv, bm, bv)
+        store_sp(i).start()
+
+    each(0, STEPS, join)
+    for k in (3, 4, 5, 7):
+        copies[k].start()
+    exchange_run(exs[1], [gb], [c2], work[1])
+    each(0, STEPS, lambda i: store_sp(i).wait())
+    for k in (0, 1, 2, 3, 4, 5, 7):
+        copies[k].wait()
+
+
+def k_middle(exs, loads, met, loaded, small, kept, scratch, outs, work):
+    sa, fb, wsp, wso, x_fast, cot = loaded
+    gb, c2, m16, m64, wout = small
+    pad, sb, fact, sact, fast_y, df = kept
+    sm, sv, cm, cv, em, ev, s1, s2, sems, y_sems, df_sems = scratch
+    big, (c3, c4, q4) = outs[:6], outs[6:]
+    p_n = fb.shape[0] // STEPS
+    rows_n = sb.shape[0] // STEPS
+    copies = stores_of(list(zip(kept, big))[:4], sems)
+    for k in (0, 1, 2):
+        loads[k].wait()
+
+    def spatial(i):
+        part, span = pl.ds(i * p_n, p_n), pl.ds(i * rows_n, rows_n)
+        k_spatial(i, sa, fb.at[part], c2, m16, m64, wsp, wout, pad, sb.at[span], fact.at[part], work[0][0], sm, sv, cm, cv)
+
+    each(0, STEPS, spatial)
+    met()
+    for k in (0, 1, 2):
+        copies[k].start()
+    exchange_run(exs[0], [gb], [c3], work[0])
+    for k in (3, 4, 5):
+        loads[k].wait()
+
+    def y_store(i):
+        part = pl.ds(i * p_n, p_n)
+        return pltpu.make_async_copy(fast_y.at[:, part], big[4].at[:, part], y_sems.at[i])
+
+    def df_store(i):
+        part = pl.ds(i * p_n, p_n)
+        return pltpu.make_async_copy(df.at[part], big[5].at[part], df_sems.at[i])
+
+    def expand(i):
+        part, span = pl.ds(i * p_n, p_n), pl.ds(i * rows_n, rows_n)
+        k_expand(i, sb.at[span], fact.at[part], x_fast.at[:, part], cot.at[:, part], c3, m16, m64, wso, wout,
+                 sact.at[span], fast_y.at[:, part], df.at[part], work[1][0], em, ev, s1, s2)
+        y_store(i).start()
+        df_store(i).start()
+
+    each(0, STEPS, expand)
+    copies[3].start()
+    exchange_run(exs[1], [gb, c3], [c4, q4], work[1])
+    each(0, STEPS, lambda i: y_store(i).wait())
+    each(0, STEPS, lambda i: df_store(i).wait())
+    for copy in copies:
+        copy.wait()
 
 
 def back_norm(scale, p, q, dy, z, fill):
@@ -902,7 +1029,8 @@
         self.sibling = (1 - self.p, self.f)
 
     def q_of(self, k):
-        return lax.rem(self.q + k, NEAR)
+        low = (self.q % 2 + k % 2) % 2
+        return (self.q // 2 + k // 2) % 2 * 2 + low
 
     def r_of(self, k):
         return lax.rem(self.r + k, self.far)
@@ -1023,6 +1151,7 @@
 class Share:
     def __init__(self, stream, res, out, scratch):
         self.res, self.out, self.far, self.c = res, out, stream.far, Cube(stream.ch, stream.far)
+        self.cut = stream.ch // 32 * 16
         self.sem_d, self.sem_e, self.sem_f, self.sem_own = scratch
 
     def own(self):
@@ -1042,37 +1171,60 @@
         return remote(dst if src is None else src, dst, self.sem_e, (k, m), self.c.plane(k))
 
     def pair_back(self, k, m, src=None):
-        dst = self.part(self.c.q_of(NEAR - k), m)
+        dst = self.part(self.c.q_of(k), m)
         return remote(dst if src is None else src, dst, self.sem_f, (k, m), self.c.sibling)
 
     def start_line(self):
         each(1, self.far, lambda k: self.line_back(k).start())
 
+    def half(self, k, m):
+        c, cut = self.c, self.cut
+        start = ((c.p * NEAR + c.q_of(k)) * self.far + c.r_of(self.far - m)) * c.ch
+        rows_n = cut if k == 1 else c.ch - cut
+        part = self.out.at[pl.ds(pl.multiple_of(start + (0 if k == 1 else cut), 16), rows_n)]
+        return remote(part, part, self.sem_e, (3 if k == 1 else 0, m), c.plane(3 - k))
+
     def start_plane(self):
-        each(1, NEAR, lambda k: self.plane_back(k, 0, self.res).start())
+        each(1, NEAR - 1, lambda k: self.plane_back(k, 0, self.res).start())
         self.pair_back(0, 0, self.res).start()
         self.keep().start()
 
     def relay(self, first, last):
         def one(m):
             self.line_back(m).wait_recv()
-            each(1, NEAR, lambda k: self.plane_back(k, m).start())
+            each(1, NEAR - 1, lambda k: self.plane_back(k, m).start())
             self.pair_back(0, m).start()
 
         each(first, last, one)
 
     def hand_on(self, first, last):
-        def one(k, m):
-            self.plane_back(k, m).wait_recv()
-            self.pair_back(k, m).start()
-
-        each(first, last, lambda m: each(1, NEAR, lambda k: one(k, m)))
+        def one(m):
+            for k in (1, 2):
+                self.plane_back(k, m).wait_recv()
+                self.half(k, m).start()
+                self.pair_back(k, m).start()
+
+        each(first, last, one)
+
+    def hand_across(self, first, last):
+        def one(m):
+            for k in (1, 2):
+                self.half(k, m).wait_recv()
+            self.pair_back(3, m).start()
+
+        each(first, last, one)
 
     def end(self):
         each(0, self.far, lambda m: each(0, NEAR, lambda k: self.pair_back(k, m).wait()))
         self.keep().wait()
         each(1, self.far, lambda k: self.line_back(k).wait_send())
-        each(0, self.far, lambda m: each(1, NEAR, lambda k: self.plane_back(k, m).wait_send()))
+        each(0, self.far, lambda m: each(1, NEAR - 1, lambda k: self.plane_back(k, m).wait_send()))
+
+        def sent(m):
+            for k in (1, 2):
+                self.half(k, m).wait_send()
+
+        each(0, self.far, sent)
 
 
 def k_tail(cfg, *refs):
@@ -1311,7 +1463,9 @@
     share.start_plane()
     share_a.hand_on(0, far)
     share.relay(1, far)
+    share_a.hand_across(0, far)
     share.hand_on(0, far)
+    share.hand_across(0, far)
     share_a.end()
     share.end()
     line_b.end()
@@ -1342,7 +1496,9 @@
 
 
 def k_unpack(pieces, cut, *refs):
-    (src_a, src_b), outs, (low_a, low_b, low_c, wide, sem_a, sem_b, sem_out) = refs[:2], refs[2:-7], refs[-7:]
+    (src_a, src_b, q4, q5, q6, q7, q8), refs = refs[:7], refs[7:]
+    outs, (low_a, low_b, low_c, wide, line, sem_a, sem_b, sem_out) = refs[:-8], refs[-8:]
+    outs, (gains_out, biases_out, in_out, mid_out, out_out) = outs[:-5], outs[-5:]
     lows = (low_a, low_b, low_c)
     flats = [low_a, low_b.reshape(-1, low_b.shape[-1]), low_c.reshape(-1, low_c.shape[-1])]
     starts = [sum(p[2] for p in pieces[:k]) for k in range(len(pieces))]
@@ -1374,30 +1530,51 @@
             seen = src
         wide[starts[k] : starts[k] + height, :] = flats[src][row : row + height, :].astype(F32)
         store(k).start()
+    lane = lax.broadcasted_iota(jnp.int32, (1, LANES), 1)
+    left = lane < LANES // 2
+    for slab, out in ((3, gains_out), (2, biases_out)):
+        at = 0
+        for q, first, count in ((q4, 0, 1), (q8, 0, 2), (q7, 0, 2), (q6, 0, 2), (q5, 0, 16)):
+            line[at : at + count, :] = q[slab, first : first + count, :]
+            at += count
+        half = pltpu.roll(line[0:at, :], LANES // 2, 1)
+        head = jnp.where(lane < LANES // 4, q6[slab, 2:3, :], q5[slab, 16:17, :])
+        out[0:1, :] = jnp.where(left, head, half[0:1])
+        out[1:at, :] = jnp.where(left, half[0 : at - 1], half[1:at])
+        out[at : at + 1, :] = jnp.where(left, half[at - 1 : at], 0.0)
+    a = in_out.shape[0]
+    last = sum(p[2] for p in pieces if p[0] == 2)
+    small = flats[2][last : last + 3 * a, :]
+    in_out[...] = small[0:a, 0:LANES].astype(F32)
+    out_out[...] = small[0:a, LANES:].astype(F32)
+    eye = (lax.broadcasted_iota(jnp.int32, (a, a), 0) == lax.broadcasted_iota(jnp.int32, (a, a), 1)).astype(BF16)
+    for k, (row, col) in enumerate(((a, 0), (a, LANES), (2 * a, 0))):
+        mid_out[k] = dot_tn(small[row : row + a, col : col + LANES], eye)[0:a, :]
     for k in range(len(pieces)):
         store(k).wait()
 
 
-def unpack(src_a, src_b, cut, pieces, shapes):
-    hbm = pl.BlockSpec(memory_space=pl.ANY)
+def unpack(src_a, src_b, cut, pieces, shapes, small_shapes, norm_sums):
+    hbm, vm = pl.BlockSpec(memory_space=pl.ANY), pl.BlockSpec(memory_space=pltpu.VMEM)
     n, _, width = src_b.shape
     return pl.pallas_call(
         functools.partial(k_unpack, pieces, cut),
-        out_shape=[jax.ShapeDtypeStruct(s, F32) for s in shapes],
-        in_specs=[hbm] * 2,
-        out_specs=[hbm] * len(shapes),
+        out_shape=[jax.ShapeDtypeStruct(s, F32) for s in (*shapes, *small_shapes)],
+        in_specs=[hbm] * 2 + [vm] * len(norm_sums),
+        out_specs=[hbm] * len(shapes) + [vm] * len(small_shapes),
         scratch_shapes=[
             pltpu.VMEM(src_a.shape, BF16),
             pltpu.VMEM((n, cut, width), BF16),
             pltpu.VMEM((n, src_b.shape[1] - cut, width), BF16),
             pltpu.VMEM((sum(p[2] for p in pieces), width), F32),
+            pltpu.VMEM((24, LANES), F32),
             pltpu.SemaphoreType.DMA((len(pieces),)),
             pltpu.SemaphoreType.DMA((3,)),
             pltpu.SemaphoreType.DMA((len(pieces),)),
         ],
         compiler_params=pltpu.CompilerParams(vmem_limit_bytes=VMEM_LIMIT),
         name="unpack",
-    )(src_a, src_b)
+    )(src_a, src_b, *norm_sums)
 
 
 def k_prep(x_hbm, fill_ref, clip_ref, norm_ref, wfi_ref, wfm_ref, wfo_ref,
@@ -1565,53 +1742,41 @@
 
     small = (STEPS, 8, LANES)
 
-    fa, lat, taps, c1, hp, hn = call(
-        k_first,
-        [sb_(x_fast), blocked(tail, 0, 1), whole(m16), whole(m64), whole(wfa), whole(wlat)],
-        [fast_out(LANES, F32), slow_out(c_lat, F32), slow_out(5 * c_fast, BF16), STAT, UP, DOWN],
-        [pltpu.VMEM((groups * p_n * f_n, c_fast), F32), *acc(f_n, LANES, 2), *acc(t_n, c_lat, 2)],
-        "first",
+    sems7 = pltpu.SemaphoreType.DMA((STEPS,))
+    exs = [
         Exchange(sizes, 1, 7, fwd=(("lane4", 0, 1), ("plain", 6, 2)), up=small, down=small),
-        [gb],
+        Exchange(sizes, 1, 23, fwd=(("lane4", 1, 1), ("plain", 8, 2), ("plain", 20, 8))),
+    ]
+    kept = [
+        (fp + (LANES,), F32), (sl + (c_lat,), F32), (sl + (5 * c_fast,), BF16), (sl + (c_lat,), BF16),
+        (fp + (3 * LANES,), BF16), (sl + (in_slow,), F32), (sl + (c_slow,), F32), (fp + (LANES,), F32),
+    ]
+    fa, lat, taps, lact, ftap, sa, sp, fb, c1, hp, hn, c2 = run_resident(
+        functools.partial(k_front, exs), exs,
+        [x_fast, wlat, x_slow, w_slow_in, w_shortcut], [tail, gb, m16, m64, wfa, wmid],
+        kept, [(*k, True) for k in kept],
+        [pltpu.VMEM((groups * p_n * f_n, c_fast), F32), *acc(f_n, LANES, 2), *acc(t_n, c_lat, 2), *acc(t_n, in_slow, 2),
+         *acc(t_n, c_slow, 2), *acc(f_n, LANES, 2), pltpu.SemaphoreType.DMA((8,)), sems7],
+        "front",
     )
 
-    lact, ftap, sa, sp, fb, c2 = call(
-        k_join,
-        [sb_(x_slow), sb_(lat), fb_(fa), blocked(hp, 0, 1), blocked(hn, 0, 1), whole(c1), whole(m16), whole(m64),
-         whole(w_slow_in), whole(w_shortcut), whole(wmid)],
-        [slow_out(c_lat, BF16), fast_out(3 * LANES, BF16), slow_out(in_slow, F32), slow_out(c_slow, F32),
-         fast_out(LANES, F32), STAT],
-        [*acc(t_n, in_slow, 2), *acc(t_n, c_slow, 2), *acc(f_n, LANES, 2)],
-        "join",
-        Exchange(sizes, 2, 23, fwd=(("lane4", 1, 1), ("plain", 8, 2), ("plain", 20, 8))),
-        [gb],
+    exs = [
+        Exchange(sizes, 3, 13, fwd=(("row4", 2, 4), ("plain", 10, 2))),
+        Exchange(sizes, 3, 25, fwd=(("plain", 12, 8),), bwd=(("row4", 0, 0, 2, 4, 0, 4),)),
+    ]
+    kept = [
+        ((side + 2, side + 2, t_n, in_slow), BF16), ((pixels, t_n, in_slow), F32), (fp + (LANES,), BF16),
+        ((pixels, t_n, in_slow), BF16), ((groups, inner, f_n, c_fast), BF16), (fp + (groups * c_fast,), F32),
+    ]
+    pad, sb, fact, sact, fast_y, df, c3, c4, q4 = run_resident(
+        functools.partial(k_middle, exs), exs,
+        [sa.reshape(side, side, t_n, in_slow), fb, wsp, w_slow_out, x_fast, cot_fast], [gb, c2, m16, m64, wout],
+        kept, [(*k, True) for k in kept],
+        [*acc(t_n, in_slow, 2), *acc(f_n, groups * c_fast, 2), *acc(t_n, c_slow, 2), *acc(f_n, groups * c_fast, 2),
+         pltpu.SemaphoreType.DMA((4,)), sems7, sems7],
+        "middle",
     )
-
-    rows_n = side // STEPS
-    pad, sb, fact, c3 = call(
-        k_spatial,
-        [whole(sa.reshape(side, side, t_n, in_slow)),
-         fb_(fb), whole(c2), whole(m16), whole(m64), whole(wsp), whole(wout)],
-        [out_whole((side + 2, side + 2, t_n, in_slow), BF16),
-         out_blocked((side, side, t_n, in_slow), F32, 0, rows_n), fast_out(LANES, BF16), STAT],
-        [*acc(t_n, in_slow, 2), *acc(f_n, groups * c_fast, 2)],
-        "spatial",
-        Exchange(sizes, 3, 13, fwd=(("row4", 2, 4), ("plain", 10, 2))),
-        [gb],
-    )
-
-    sb4 = sb.reshape(sl + (in_slow,))
-    sact, fast_y, df, st = call(
-        k_expand,
-        [sb_(sb4), fb_(fact), sb_(x_fast), sb_(cot_fast), whole(c3), whole(m16), whole(m64), whole(w_slow_out), whole(wout)],
-        [slow_out(in_slow, BF16), out_blocked((groups, inner, f_n, c_fast), BF16, 1, p_n),
-         fast_out(groups * c_fast, F32), stat(25)],
-        [*acc(t_n, c_slow, 2), *acc(f_n, groups * c_fast, 2)],
-        "expand",
-    )
-    c4, q4 = exchange_alone(
-        Exchange(sizes, 4, 25, fwd=(("plain", 12, 8),), bwd=(("row4", 0, 0, 2, 4, 0, 4),)), st, gb, [c3]
-    )
+    sb4, sact = sb.reshape(sl + (in_slow,)), sact.reshape(sl + (in_slow,))
 
     halo_pair = out_blocked((STEPS, 2, 8, LANES), F32, 0, 1)
     slow_y, dy, dfb, g_fout, up, down, st = call(
@@ -1625,20 +1790,18 @@
     )
     pair = (STEPS, 2, 8, LANES)
     ex5 = Exchange(
-        sizes, 5, 26,
+        sizes, 6, 26,
         bwd=(("plain", 0, 0, 12, 8, 0, 8), ("plain", 1, 3, 20, 8, 0, 16), ("lane4", 1, 0, 1, 1, 24, 25)),
         up=pair, down=pair,
     )
-    q5, hp, hn = exchange_alone(ex5, st, gb, [c4, c2], up, down)
-
     c_cat = w_slow_in.shape[0]
     width = in_slow
     stream_a = Stream(sizes, rows_for(sizes, c_cat * c_slow // width), width)
     stream_b = Stream(sizes, rows_for(sizes, 9 * in_slow), width)
-    gw_short, gw_sout, dsp, dsb, dfa, g_fmid, q6 = call(
+    gw_short, gw_sout, dsp, dsb, dfa, g_fmid, q6, q5 = call(
         k_back_out,
-        [sb_(x_slow), sb_(lact), sb_(dy), sb_(sp), sb_(sact), sb_(sb4), fb_(dfb), fb_(fb), fb_(fa), fb_(ftap), blocked(hp, 0, 1), blocked(hn, 0, 1),
-         whole(c1), whole(c2), whole(c3), whole(c4), whole(q5), whole(m16), whole(m64), whole(w_slow_out), whole(wback)],
+        [sb_(x_slow), sb_(lact), sb_(dy), sb_(sp), sb_(sact), sb_(sb4), fb_(dfb), fb_(fb), fb_(fa), fb_(ftap), 1, 2,
+         whole(c1), whole(c2), whole(c3), whole(c4), 0, whole(m16), whole(m64), whole(w_slow_out), whole(wback)],
         [out_whole((stream_a.rows_n, width), BF16), out_whole((c_slow, width), BF16), slow_out(c_slow, BF16),
          slow_out(in_slow, F32), fast_out(LANES, F32), out_whole((3 * in_fast, LANES), F32), STAT],
         [*acc(t_n, in_slow, 2), *acc(f_n, LANES, 2), *acc(c_cat, c_slow, 1), *acc(in_slow, c_slow, 1),
@@ -1646,6 +1809,8 @@
         "back_out",
         Exchange(sizes, 6, 6, bwd=(("plain", 0, 4, 10, 2, 0, 2), ("lane4", 1, 0, 0, 1, 4, 5))),
         [gb, c3, c1],
+        ex5,
+        [st, up, down, gb, c4, c2],
     )
 
     def rows2(a):
@@ -1655,7 +1820,7 @@
         stream_a, stream_b,
         Exchange(sizes, 7, 4, bwd=(("plain", 0, 1, 8, 2, 0, 2),)),
         Exchange(sizes, 7, 4, bwd=(("plain", 0, 1, 6, 2, 0, 2),), post=(STEPS, groups * 8, c_lat)),
-        [gw_short, rows2(dsb), rows2(sb), pad, wsp, rows2(sa), x_fast, dfa, fa, w_slow_in, w_shortcut, rows2(dsp), rows2(lat)],
+        [gw_short, rows2(dsb), rows2(sb4), pad, wsp, rows2(sa), x_fast, dfa, fa, w_slow_in, w_shortcut, rows2(dsp), rows2(lat)],
         [gb, c1, c2, c3, q6, m16, m64, g_fout, g_fmid],
         side, t_n, in_slow,
     )
@@ -1680,43 +1845,34 @@
     for n in range(blocks):
         pieces.append((2, at, in_slow, 1, n * width))
         at += in_slow
-    for out, tall in ((3, c_cat), (4, gw_lat.shape[0]), (5, gw_fast.shape[0])):
+    for out, tall in ((3, c_cat), (4, gw_lat.shape[0])):
         pieces.append((2, at, tall, out, None))
         at += tall
-    g_short, g_sout, gw_mid, gw_in, gw_lat, gw_fast = unpack(
+    norm_rows = -(-gains.shape[0] // LANES)
+    g_short, g_sout, gw_mid, gw_in, gw_lat, gains_grad, biases_grad, g_fin, g_fmid, g_fout = unpack(
         sum_a, sum_bc, stream_b.ch, tuple(pieces),
-        [(c_cat, c_slow), (in_slow, c_slow), (9 * in_slow, width), (c_cat, in_slow), gw_lat.shape, gw_fast.shape],
+        [(c_cat, c_slow), (in_slow, c_slow), (9 * in_slow, width), (c_cat, in_slow), gw_lat.shape],
+        [(norm_rows, LANES), (norm_rows, LANES), (in_fast, c_fast), w_fast_mid.shape, (in_fast, c_fast)],
+        [q4, q5, q6, q7, q8],
     )
-    taps_t = [gw_fast[in_fast : 2 * in_fast, :in_fast], gw_fast[in_fast : 2 * in_fast, c_fast : c_fast + in_fast],
-              gw_fast[2 * in_fast :, :in_fast]]
     grads = (
-        gw_fast[:in_fast, :c_fast].T,
-        jnp.transpose(jnp.stack(taps_t), (0, 2, 1)),
-        gw_fast[:in_fast, c_fast:],
+        g_fin.T,
+        g_fmid,
+        g_fout,
         gw_lat.reshape(w_lateral.shape),
         gw_in,
         gw_mid.reshape(w_slow_mid.shape),
         g_sout,
         g_short,
     )
-
-    def norm_grads(slab):
-        def row(q, at, n):
-            return q[slab, at : at + n].reshape(-1)
-
-        return jnp.concatenate(
-            [row(q6, 2, 1)[:in_fast], row(q5, 16, 1)[:in_fast], row(q4, 0, 1), row(q8, 0, 2), row(q7, 0, 2),
-             row(q6, 0, 2), row(q5, 0, 8), row(q5, 8, 8)]
-        )
-
     return (
         unview(slow_y),
         unview(fast_y),
         unview(slow_gx),
         unview(fast_gx),
         *grads,
-        norm_grads(3),
-        norm_grads(2),
+        gains_grad.reshape(-1)[: gains.shape[0]],
+        biases_grad.reshape(-1)[: biases.shape[0]],
     )
 
 

time: 324 us -> 296 us (0.914)
  Pallas kernels: 314 us -> 291 us
  local copies, waits for them, and re-layouts: 7.55 us -> 2.3 us
    pallas_call x8 -> x4, Pallas kernels: 169 us -> 102 us  [call(): pl.pallas_call(body, grid=(STEPS,), in_specs=[pl.BlockSpec(b, m) for _, b...]
    pallas_call x2, Pallas kernels: 24.4 us -> 73.5 us  [run_resident(): pl.pallas_call(body, out_shape=[jax.ShapeDtypeStruct(shape, dtype) for sh...]
    pallas_call x1, Pallas kernels: 48.4 us -> 41.9 us  [final_sum(): pl.pallas_call(functools.partial(final_kernel, (first, second, third, bot...]
where the time goes in v5:
time: 296 us; the launch traced here: 295 us
  Pallas kernels  291 us (98%)
    pallas_call x4, Pallas kernels, call(): pl.pallas_call(body, grid=(STEPS,), in_specs=[pl.BlockSpec(b, m) for _, b...  102 us
    pallas_call x2, Pallas kernels, run_resident(): pl.pallas_call(body, out_shape=[jax.ShapeDtypeStruct(shape, dtype) for sh...  73.5 us
    pallas_call x1, Pallas kernels, back_tail(): pl.pallas_call(functools.partial(k_tail, (st_a, st_b, ex7, ex8, side)), o...  51.7 us
    pallas_call x1, Pallas kernels, final_sum(): pl.pallas_call(functools.partial(final_kernel, (first, second, third, bot...  41.9 us
    pallas_call x1, Pallas kernels, prepare(): pl.pallas_call(k_prep, out_shape=[jax.ShapeDtypeStruct(s, d) for s, d in...  14.8 us
    pallas_call x1, Pallas kernels, unpack(): pl.pallas_call(functools.partial(k_unpack, pieces, cut), out_shape=[jax.S...  7.26 us

profile of v5, /device:TPU:0, one launch (start us, length us, event | category | flops | bytes accessed | tf_op | source)
XLA Modules:
  0.0 294.8 jit_solution(4228904660040817318)
XLA Ops:
  0.6 0.8 fusion
  1.4 0.6 copy.32
  2.0 14.8 %prepare.1 = (f32[7,4,8,256]{3,2,1,0:T(8,128)}, f32[2,32,128]{2,1,0:T(8,128)}, f32[3,16,128]{2,1,0:T(8,128)}, f32[3,64,128]{2,1,0:T(8,128)}, bf16[128,512]{1,0:T...) custom-call(bf16[4,49,64,128]{3,2,1,0:T(8,128)(2,1)} %bitcast.55, ...), custom_call_target="tpu_custom_call" | custom-call | tf_op jit(solution)/shard_map/prepare/pallas_call | solution.py:1673
  16.8 37.2 %front.1 = (f32[49,64,128]{2,1,0:T(8,128)}, f32[4,49,16,256]{3,2,1,0:T(8,128)}, bf16[4,49,16,640]{3,2,1,0:T(8,128)(2,1)}, bf16[4,49,16,256]{3,2,1,0:T(8,128)(2,1...) custom-call(bf16[4,49,64,128]{3,2,1,0:T(8,128)(2,1)} %bitcast.56, ...), custom_call_target="tpu_custom_call" | custom-call | tf_op jit(solution)/shard_map/front/pallas_call | solution.py:667
  54.1 36.3 %middle.1 = (bf16[16,16,16,256]{3,2,1,0:T(8,128)(2,1)}, f32[196,16,256]{2,1,0:T(8,128)}, bf16[49,64,128]{2,1,0:T(8,128)(2,1)}, bf16[196,16,256]{2,1,0:T(8,128)(2...) custom-call(f32[14,14,16,256]{3,2,1,0:T(8,128)} %bitcast.63, ...), custom_call_target="tpu_custom_call" | custom-call | tf_op jit(solution)/shard_map/middle/pallas_call | solution.py:667
  90.4 23.8 %out.1 = (bf16[4,49,16,1024]{3,2,1,0:T(8,128)(2,1)}, f32[4,49,16,1024]{3,2,1,0:T(8,128)}, f32[49,64,128]{2,1,0:T(8,128)}, f32[32,128]{1,0:T(8,128)}, f32[7,2,8,1...) custom-call(bf16[4,49,16,256]{3,2,1,0:T(8,128)(2,1)} %bitcast.65, ...), custom_call_target="tpu_custom_call" | custom-call | tf_op jit(solution)/shard_map/out/pallas_call | solution.py:387
  114.2 48.3 %back_out.1 = (bf16[5120,256]{1,0:T(8,128)(2,1)}, bf16[1024,256]{1,0:T(8,128)(2,1)}, bf16[4,49,16,1024]{3,2,1,0:T(8,128)(2,1)}, f32[4,49,16,256]{3,2,1,0:T(8,128...) custom-call(bf16[4,49,16,1024]{3,2,1,0:T(8,128)(2,1)} %bitcast.53, ...), custom_call_target="tpu_custom_call" | custom-call | tf_op jit(solution)/shard_map/back_out/pallas_call | solution.py:387
  162.5 51.7 %tail.1 = (bf16[3136,256]{1,0:T(8,128)(2,1)}, bf16[49,64,128]{2,1,0:T(8,128)(2,1)}, f32[3136,256]{1,0:T(8,128)}, f32[96,256]{1,0:T(8,128)}, f32[4,2,128]{2,1,0:T...) custom-call(bf16[5120,256]{1,0:T(8,128)(2,1)} %get-tuple-element.111, ...), custom_call_target="tpu_custom_call" | custom-call | tf_op jit(solution)/shard_map/tail/pallas_call | solution.py:1406
  214.3 16.8 %slow_grad.1 = (bf16[4,49,16,1024]{3,2,1,0:T(8,128)(2,1)}, bf16[1280,256]{1,0:T(8,128)(2,1)}) custom-call(bf16[4,49,16,1024]{3,2,1,0:T(8,128)(2,1)} %bitcast.54, bf16[4,49,16,256]{3,2,1,0:T(8,128)(2,1)} %get-tuple-element.100.refs_1_, bf16[4,49,16,256]{3,2,1,0:T(8,128)(2,1)} %bitcast.75, bf16[4,49,16,1024]{3,2,1,0:T(8,128)(2,1)} %get-tuple-element.115.refs_3_, ...), custom_call_target="tpu_custom_call" | custom-call | tf_op jit(solution)/shard_map/slow_grad/pallas_call | solution.py:387
  231.1 12.9 %fast_grad.1 = (bf16[4,49,64,128]{3,2,1,0:T(8,128)(2,1)}, bf16[640,256]{1,0:T(8,128)(2,1)}) custom-call(f32[4,49,16,256]{3,2,1,0:T(8,128)} %bitcast.70, f32[4,49,16,256]{3,2,1,0:T(8,128)} %get-tuple-element.116.refs_1_, bf16[4,49,16,640]{3,2,1,0:T(8,128)(2,1)} %get-tuple-element.123.refs_2_, bf16[7,32,256]{2,1,0:T(8,128)(2,1)} %get-tuple-element.124.refs_3_, ...), custom_call_target="tpu_custom_call" | custom-call | tf_op jit(solution)/shard_map/fast_grad/pallas_call | solution.py:387
  244.0 41.9 %final_sum.1 = (bf16[5120,256]{1,0:T(8,128)(2,1)}, bf16[5632,256]{1,0:T(8,128)(2,1)}) custom-call(bf16[160,256]{1,0:T(8,128)(2,1)} %get-tuple-element.128.refs_0_, bf16[4,80,256]{2,1,0:T(8,128)(2,1)} %get-tuple-element.129.refs_1_, bf16[1024,256]{1,0:T(8,128)(2,1)} %get-tuple-element.130.refs_2_, bf16[1280,256]{1,0:T(8,128)(2,1)} %get-tuple-element.131.refs_3_, ...), custom_call_target="tpu_custom_call" | custom-call | tf_op jit(solution)/shard_map/final_sum/pallas_call | solution.py:1483
  285.9 0.0 copy-start
  285.9 7.3 %unpack.1 = (f32[1280,1024]{1,0:T(8,128)}, f32[256,1024]{1,0:T(8,128)}, f32[2304,256]{1,0:T(8,128)}, f32[1280,256]{1,0:T(8,128)}, f32[640,256]{1,0:T(8,128)}, /*...) custom-call(bf16[5120,256]{1,0:T(8,128)(2,1)} %get-tuple-element.134.r, ...), custom_call_target="tpu_custom_call" | custom-call | tf_op jit(solution)/shard_map/unpack/pallas_call | solution.py:1560
  293.1 0.0 copy-done
  293.1 1.7 copy.34
Async XLA Ops:
  285.9 7.3 %copy-start = (bf16[4,49,64,128]{3,2,1,0:T(8,128)(2,1)S(1)}, bf16[4,49,64,128]{3,2,1,0:T(8,128)(2,1)}, u32[]{:S(2)}) copy-start(bf16[4,49,64,128]{3,2,1,0:T(8,128)(2,1)} %get-tuple-element.99) | copy-start | bytes 9633796

commit v6 on v5

--- a/solution.py
+++ b/solution.py
@@ -14,7 +14,7 @@
 AXES = ("path", "frames")
 STEPS = 7
 LANES = 128
-VMEM_LIMIT = 56 * 1024 * 1024
+VMEM_LIMIT = 60 * 1024 * 1024
 
 
 def dot(a, b):
@@ -122,7 +122,7 @@
     return len(peers)
 
 
-def exchange_run(cfg, ins, outs, scratch, meanwhile=None, post=None):
+def exchange_run(cfg, ins, outs, scratch, meanwhile=None, post=None, after=None):
     fwd, bwd = cfg.fwd, cfg.bwd
     nf = sum(c[2] for c in fwd)
     nb = max((c[6] + c[4] for c in bwd), default=0)
@@ -277,6 +277,8 @@
             device_id_type=MESH,
         )
         late.start()
+        if after is not None:
+            after()
         late.wait()
         outs.pop(0)[...] = post_land[...]
     for c in halos:
@@ -451,11 +453,12 @@
     t_n = f_n // 4
     first = lax.broadcasted_iota(jnp.int32, (n // t_n, t_n, LANES), 1) == 0
     link = m16_ref[1:2]
+    tail = tail_ref[0].astype(F32)
     taps = []
     for k in range(2):
         halo = jnp.concatenate(
             [
-                jnp.broadcast_to(tail_ref[0, s, p : p + 1, k * LANES : (k + 1) * LANES], (t_n, LANES))
+                jnp.broadcast_to(tail[s * 8 + p : s * 8 + p + 1, k * LANES : (k + 1) * LANES], (t_n, LANES))
                 for s in range(s_n)
                 for p in range(p_n)
             ],
@@ -574,12 +577,8 @@
 
     per = h_n // STEPS
     h0 = i * per
-    acc = None
-    for a in range(3):
-        for b in range(3):
-            k = 3 * a + b
-            part = dot(flat(pad_ref[pl.ds(h0 + a, per), b : b + w_n].reshape(per * w_n, t_n, c)), wsp_ref[k])
-            acc = part if acc is None else acc + part
+    patches = [flat(pad_ref[pl.ds(h0 + a, per), b : b + w_n]) for a in range(3) for b in range(3)]
+    acc = dot(jnp.concatenate(patches, axis=1), wsp_ref[...])
     sb_ref[...] = acc.reshape(sb_ref.shape)
     spread_add(i, acc.reshape(per * w_n, t_n, acc.shape[1]), sm, sv)
 
@@ -642,7 +641,7 @@
         put_rows(st_ref, 24, count_row(m16_ref, positions))
 
 
-def run_resident(kernel, ex_list, hbm, small, locals_, outs, scratch, name):
+def run_resident(kernel, ex_list, hbm, small, locals_, outs, scratch, name, scalars=0):
     vm, anywhere = pl.BlockSpec(memory_space=pltpu.VMEM), pl.BlockSpec(memory_space=pl.ANY)
     for ex in ex_list:
         outs = [*outs, *[(shape, dtype, False) for shape, dtype in ex.outs]]
@@ -667,7 +666,7 @@
     return pl.pallas_call(
         body,
         out_shape=[jax.ShapeDtypeStruct(shape, dtype) for shape, dtype, _ in outs],
-        in_specs=[anywhere] * len(hbm) + [vm] * len(small),
+        in_specs=[anywhere] * len(hbm) + [pl.BlockSpec(memory_space=pltpu.SMEM)] * scalars + [vm] * (len(small) - scalars),
         out_specs=[anywhere if stays else vm for _, _, stays in outs],
         scratch_shapes=[
             *[pltpu.VMEM(a.shape, a.dtype) for a in hbm], *[pltpu.VMEM(*k) for k in locals_], *scratch,
@@ -686,15 +685,35 @@
 
 def k_front(exs, loads, met, loaded, small, kept, scratch, outs, work):
     x_fast, wlat, x_slow, w_in, w_sc = loaded
-    tail_ref, gb, m16, m64, wfa, wmid = small
     fa, lat, taps, lact, ftap, sa, sp, fb = kept
-    xs, fm, fv, lm, lv, am, av, pm, pv, bm, bv, sems, sp_sems = scratch
-    big, (c1, hp, hn, c2) = outs[:8], outs[8:]
+    xs, fm, fv, lm, lv, am, av, pm, pv, bm, bv, sems, sp_sems, ends_f, sent, sent_low, tail_ref, tail_sems = scratch
+    big, ready, (c1, hp, hn, c2) = outs[:8], outs[8:15], outs[15:]
+    gb, m16, m64, wfa, wmid, wback, wout = ready
     p_n = fa.shape[0] // STEPS
     copies = dict(zip((0, 1, 2, 3, 4, 5, 7), stores_of([p for k, p in enumerate(zip(kept, big)) if k != 6], sems)))
     st1, up, down = work[0][:3]
     loads[0].wait()
+    s_n, inner, f_n, ch = x_fast.shape
+    t_n = lat.shape[2]
+    ends_f[...] = flat(x_fast[:, :, f_n - t_n : f_n, :]).astype(F32)
+    zero_ref(sent)
+    for k in range(2):
+        lines = ends_f[pl.ds(t_n - 2 + k, s_n * inner, stride=t_n), :]
+        for s in range(s_n):
+            for step in range(STEPS):
+                at = s * inner + step * p_n
+                sent[step, s * 8 : s * 8 + p_n, k * ch : (k + 1) * ch] = lines[at : at + p_n, :]
+    sent_low[...] = sent[...].astype(BF16)
+    met()
+    nxt = exchange_peers(exs[0])[6]
+    halo = pltpu.make_async_remote_copy(
+        src_ref=sent_low, dst_ref=tail_ref, send_sem=tail_sems.at[0], recv_sem=tail_sems.at[1],
+        device_id=nxt, device_id_type=MESH,
+    )
+    halo.start()
+    small_set_up(*small, *ready, s_n, t_n)
     loads[1].wait()
+    halo.wait()
 
     def first(i):
         part, one = pl.ds(i * p_n, p_n), pl.ds(i, 1)
@@ -702,7 +721,6 @@
                 taps.at[:, part], st1, up.at[one], down.at[one], xs, fm, fv, lm, lv)
 
     each(0, STEPS, first)
-    met()
     for k in (0, 1, 2):
         copies[k].start()
     exchange_run(exs[0], [gb], [c1, hp, hn], work[0])
@@ -873,7 +891,7 @@
     sact = flat(sact_ref[...])
     fill = m16_ref[0:1, :, 0:1]
     wide = 256
-    back = None
+    dscs = []
     turned = jnp.concatenate([flat(x_ref[...]), flat(lact_ref[...])], axis=1).T
     sact_turned = sact.T
     for n in range(wso_ref.shape[1] // wide):
@@ -893,9 +911,9 @@
         dsp_ref[:, :, :, cols] = dsp.reshape(s_n, p_n, t_n, wide)
         old = jnp.where(i == 0, 0.0, gsc[:, cols])
         gsc[:, cols] = old + dot(turned, dsp)
-        part = dot_nt(dsc, wso_ref[:, cols])
-        back = part if back is None else back + part
+        dscs.append(dsc)
     z = sb_ref[...].reshape(s_n * p_n, t_n, c)
+    back = dot_nt(jnp.concatenate(dscs, axis=1), wso_ref[...])
     back = back.reshape(z.shape) * slope(z * rows(c3_ref, 0, 4, 2) + rows(c3_ref, 1, 4, 2))
     dsb_ref[...] = back.reshape(dsb_ref.shape)
     sum_add(i, back, s1)
@@ -951,45 +969,20 @@
     return late
 
 
-def k_slow_grad(x_ref, lact_ref, low_ref, dsp_ref, win_ref, wsc_ref, gx_ref, gw_ref, gsi):
-    i = pl.program_id(0)
+def slow_grad(low, dsp, w_in, w_sc, out):
+    s_n, p_n, t_n, c = low.shape
+    small, d_sp = flat(low[...]), flat(dsp[...])
+    for n in range(out.shape[-1] // c):
+        part = slice(n * c, (n + 1) * c)
+        d = dot_nt(d_sp, w_sc[part, :]) + dot_nt(small, w_in[part, :])
+        out[:, :, :, part] = d.astype(BF16).reshape(s_n, p_n, t_n, c)
+
+
+def fast_grad(low_ref, hn, df, dlow, m16, wlat, wfa, out, gs):
     s_n, p_n, t_n, c = low_ref.shape
-    low, dsp = flat(low_ref[...]), flat(dsp_ref[...])
-    turned = low.T
-    blocks = gx_ref.shape[-1] // c
-    for n in range(blocks + 1):
-        part = slice(n * c, (n + 1) * c)
-        joined = flat(x_ref[:, :, :, part] if n < blocks else lact_ref[...])
-        gsi[:, part] = jnp.where(i == 0, 0.0, gsi[:, part]) + dot(turned, joined)
-        if n < blocks:
-            d = dot_nt(dsp, wsc_ref[part, :]) + dot_nt(low, win_ref[part, :])
-            gx_ref[:, :, :, part] = d.astype(BF16).reshape(s_n, p_n, t_n, c)
-
-    @pl.when(i == STEPS - 1)
-    def _():
-        for n in range(blocks + 1):
-            part = slice(n * c, (n + 1) * c)
-            gw_ref[part, :] = gsi[:, part].T.astype(BF16)
-
-
-def k_fast_grad(dlat_ref, lat_ref, taps_ref, hn_ref, df_ref, dlow_ref, c1_ref, q8_ref, m16_ref, wlat_ref, wfa_ref,
-                gx_ref, gw_ref, gs, glat):
-    i = pl.program_id(0)
-    s_n, p_n, t_n, c = lat_ref.shape
     shape = (s_n * p_n, t_n, c)
-    scale, p_row, q_row = rows(c1_ref, 0, 1, 2), rows(q8_ref, 0, 0, 2), rows(q8_ref, 1, 0, 2)
-    low = flat(
-        back_norm(scale, p_row, q_row, dlat_ref[...].reshape(shape), lat_ref[...].reshape(shape), m16_ref[0:1, :, 0:1])
-    ).astype(BF16)
-    add_to(i, glat, dot_tn(low, flat(taps_ref[...])))
-
-    @pl.when(i == STEPS - 1)
-    def _():
-        for k in range(glat.shape[1] // LANES):
-            part = slice(k * LANES, (k + 1) * LANES)
-            gw_ref[part, :] = glat[:, part].T.astype(BF16)
-
-    small = hn_ref[0].astype(F32)
+    low = flat(low_ref[...])
+    small = hn[0].astype(F32)
     ends = [
         jnp.broadcast_to(small[s * 8 + p : s * 8 + p + 1, :], (t_n, c)) for s in range(s_n) for p in range(p_n)
     ]
@@ -997,18 +990,18 @@
     n = low.shape[0]
     moved = pltpu.roll(low.astype(F32), n - 1, 0).reshape(shape)
     place = lax.broadcasted_iota(jnp.int32, shape, 1)
-    following = flat(jnp.where(place == t_n - 1, ends, moved) * m16_ref[2:3, :, 0:1]).astype(BF16)
-    own = dot_nt(low, wlat_ref[2 * LANES : 5 * LANES, :])
-    late = dot_nt(following, wlat_ref[0 : 2 * LANES, :])
+    following = flat(jnp.where(place == t_n - 1, ends, moved) * m16[2:3, :, 0:1]).astype(BF16)
+    own = dot_nt(low, wlat[2 * LANES : 5 * LANES, :])
+    late = dot_nt(following, wlat[0 : 2 * LANES, :])
     gs[pl.ds(0, n, stride=4), :] = own[:, 0:LANES]
     gs[pl.ds(1, n, stride=4), :] = own[:, LANES : 2 * LANES]
     gs[pl.ds(2, n, stride=4), :] = own[:, 2 * LANES :] + late[:, 0:LANES]
     gs[pl.ds(3, n, stride=4), :] = late[:, LANES:]
-    back = dot(flat(dlow_ref[...]), wfa_ref[...])
+    back = dot(flat(dlow[...]), wfa[...])
     for s in range(s_n):
         cols = slice(s * LANES, (s + 1) * LANES)
-        total = flat(df_ref[:, :, cols]) + back[:, cols] + gs[s * n : (s + 1) * n, :]
-        gx_ref[s] = total.astype(BF16).reshape(gx_ref.shape[1:])
+        total = flat(df[:, :, cols]) + back[:, cols] + gs[s * n : (s + 1) * n, :]
+        out[s] = total.astype(BF16).reshape(out.shape[1:])
 
 
 def each(first, last, body):
@@ -1235,11 +1228,13 @@
         return [next(it) for _ in range(n)]
 
     hbm = take(13)
+    x_slow, lact_src, taps_src = take(3)
     gb, c1, c2, c3, q6, m16, m64, g_fout, g_fmid = take(9)
-    low_out, dlow_out, dlat_out, gf, q7, q8, hn, res_a, near_b = take(9)
+    low_out, dlow_out, lat_low_out, gf, gw_in, gw_lat, q7, q8, hn, res_a, near_b = take(11)
     local = take(13)
     gw_a, dsb, sb, spad, wsp, sa, x_fast, dfa, fa, w_in, w_sc, dsp, lat = local
     pad, gsp, gin, low, dlow, gw_b, near_a, ends, s1, s2, t1, t2, sems, out_sems = take(14)
+    x_part, taps_part, gsi, glat, wsp_turned, x_sems, taps_sems, lact_sem = take(8)
     near1, line1, near2 = take(len(st_a.near_scratch)), take(len(st_a.line_scratch)), take(len(st_b.near_scratch))
     scr7 = take(len(ex7.local) + len(ex7.work))
     scr8 = take(len(ex8.local) + len(ex8.work))
@@ -1249,8 +1244,8 @@
         srcs[k] = hbm[k].at[pl.ds(hbm[k].shape[0] - n_in, n_in)]
     loads = [pltpu.make_async_copy(src, dst, sems.at[k]) for k, (src, dst) in enumerate(zip(srcs, local))]
     count = exchange_hello(ex8)
-    for load in loads:
-        load.start()
+    for k in (1, 2, 0, 4, 3, 5, 6, 7, 8, 9, 10, 11, 12):
+        loads[k].start()
     near = Near(st_a, gw_a, near_a, near1)
     line = Line(st_a, near_a, line1)
     near_two = Near(st_b, gw_b, near_b, near2)
@@ -1276,26 +1271,27 @@
         pad[h + 1, 1 : side + 1] = d.astype(BF16)
 
     each(0, side, fill_pad)
-    waits(0)
+    waits(0, 4)
+    for k in range(9):
+        wsp_turned[k * c : (k + 1) * c, :] = wsp[k * c : (k + 1) * c, :].T
     pl.semaphore_wait(pltpu.get_barrier_semaphore(), count)
     near.start()
-    waits(3, 4, 5, 6, 7, 8)
+    waits(3, 5, 6, 7, 8)
     f_n = x_fast.shape[2]
     p_n = x_fast.shape[1] // STEPS
 
     def spatial(i):
         h0 = i * per
         turned = flat(pad[pl.ds(h0 + 1, per), 1 : side + 1]).T
-        acc = None
+        blocks = []
         for a in range(3):
             for b in range(3):
                 k = 3 * a + b
                 patch = flat(spad[pl.ds(h0 + a, per), b : b + side])
                 cols = slice(k * c, (k + 1) * c)
                 gsp[:, cols] = jnp.where(i == 0, 0.0, gsp[:, cols]) + dot(turned, patch)
-                block = pad[pl.ds(h0 + 2 - a, per), 2 - b : 2 - b + side]
-                part = dot_nt(flat(block), wsp[k])
-                acc = part if acc is None else acc + part
+                blocks.append(flat(pad[pl.ds(h0 + 2 - a, per), 2 - b : 2 - b + side]))
+        acc = dot(jnp.concatenate(blocks, axis=1), wsp_turned[...])
         span = pl.ds(i * per * wide, per * wide)
         z = sa[span]
         back = acc * slope(z * rows(c2, 0, 1, 2) + rows(c2, 1, 1, 2))
@@ -1334,13 +1330,28 @@
         gf[2 * n :, 0:LANES] = g_fmid[2 * n :, :]
         gf[2 * n :, LANES:] = jnp.zeros((n, LANES), F32)
 
+    n_pos = side * side
+    lact = spad.reshape(-1, t_n, c).at[pl.ds(0, n_pos)]
+    lat_low = pad.reshape(-1, t_n, c).at[pl.ds(0, n_pos)]
+    lact_load = pltpu.make_async_copy(lact_src, lact, lact_sem)
+    lact_load.start()
+    block = per * wide
+
+    def x_load(i):
+        return pltpu.make_async_copy(x_slow.at[pl.ds(i * block, block)], x_part.at[i % 2], x_sems.at[i % 2])
+
+    def taps_load(i):
+        return pltpu.make_async_copy(taps_src.at[pl.ds(i * block, block)], taps_part.at[i % 2], taps_sems.at[i % 2])
+
+    for i in range(2):
+        x_load(i).start()
+        taps_load(i).start()
     exchange_run(ex7, [gb, c2], [q7], scr7, late)
     near_two.start()
     near.add_plane(0, far - 1, lambda m: line.line(m).start())
     near.add_plane(far - 1, far)
     waits(9, 10, 11, 12)
     scale7, p7, q7_row = rows(c2, 0, 1, 2), rows(q7, 0, 0, 2), rows(q7, 1, 0, 2)
-    block = per * wide
 
     def join(i):
         span = pl.ds(i * block, block)
@@ -1359,15 +1370,23 @@
 
     each(0, STEPS, join)
     stores.append(pltpu.make_async_copy(low, low_out, out_sems.at[1]))
-    stores.append(pltpu.make_async_copy(sb, dlat_out, out_sems.at[2]))
     stores[1].start()
-    stores[2].start()
     stats = scr8[0]
     zero_ref(stats)
     put_rows(stats, 0, sum_end(t1))
     put_rows(stats, 2, sum_end(t2))
 
     def post(q, sent):
+        d = back_norm(rows(c1, 0, 1, 2), rows(q, 0, 0, 2), rows(q, 1, 0, 2), ends[0], ends[1], m16[0, 0:1, 0:1])
+        sent[...] = d.astype(BF16)
+
+    def in_step(i):
+        x_load(i).wait()
+        joined = jnp.concatenate([x_part[i % 2], flat(lact[pl.ds(i * per * side, per * side)])], axis=1)
+        add_to(i, gsi, dot(low[pl.ds(i * block, block)].T, joined))
+        pl.when(i + 2 < STEPS)(lambda: x_load(i + 2).start())
+
+    def in_grad():
         zero_ref(ends)
         for s in range(x_fast.shape[0]):
             for step in range(STEPS):
@@ -1375,10 +1394,29 @@
                     at = ((s * STEPS + step) * p_n + p) * t_n
                     ends[0, step, s * 8 + p : s * 8 + p + 1, :] = sb[at : at + 1, :]
                     ends[1, step, s * 8 + p : s * 8 + p + 1, :] = lat[at : at + 1, :]
-        d = back_norm(rows(c1, 0, 1, 2), rows(q, 0, 0, 2), rows(q, 1, 0, 2), ends[0], ends[1], m16[0, 0:1, 0:1])
-        sent[...] = d.astype(BF16)
-
-    exchange_run(ex8, [gb, c1], [q8, hn], scr8, None, post)
+        lact_load.wait()
+        each(0, STEPS, in_step)
+        for n in range(gsi.shape[1] // c):
+            gw_in[n * c : (n + 1) * c, :] = gsi[:, n * c : (n + 1) * c].T.astype(BF16)
+
+    def lat_step(i):
+        scale8, p8, q8_row = rows(c1, 0, 1, 2), rows(q8, 0, 0, 2), rows(q8, 1, 0, 2)
+        span = pl.ds(i * block, block)
+        shape = (per * side, t_n, c)
+        d = back_norm(scale8, p8, q8_row, sb[span].reshape(shape), lat[span].reshape(shape), fill).astype(BF16)
+        lat_low[pl.ds(i * per * side, per * side)] = d
+        taps_load(i).wait()
+        add_to(i, glat, dot_tn(flat(d), taps_part[i % 2]))
+        pl.when(i + 2 < STEPS)(lambda: taps_load(i + 2).start())
+
+    def lat_grad():
+        each(0, STEPS, lat_step)
+        stores.append(pltpu.make_async_copy(lat_low, lat_low_out, out_sems.at[2]))
+        stores[2].start()
+        for k in range(glat.shape[1] // LANES):
+            gw_lat[k * LANES : (k + 1) * LANES, :] = glat[:, k * LANES : (k + 1) * LANES].T.astype(BF16)
+
+    exchange_run(ex8, [gb, c1], [q8, hn], scr8, in_grad, post, lat_grad)
     res_a[...] = line.total()
     near_two.add_plane(0, far)
     for store in stores:
@@ -1388,11 +1426,14 @@
     near_two.end()
 
 
-def back_tail(st_a, st_b, ex7, ex8, hbm, small, side, t_n, c):
+def back_tail(st_a, st_b, ex7, ex8, hbm, more, small, side, t_n, c):
     vm, anywhere = pl.BlockSpec(memory_space=pltpu.VMEM), pl.BlockSpec(memory_space=pl.ANY)
     inner, f_n = hbm[7].shape[:2]
     n = side * side * t_n
-    outs = [((n, c), BF16), ((inner, f_n, LANES), BF16), ((n, c), F32), (small[-1].shape[0:1] + (2 * LANES,), F32),
+    c_cat, c_taps = more[0].shape[1] + c, more[2].shape[1]
+    part = n // STEPS
+    outs = [((n, c), BF16), ((inner, f_n, LANES), BF16), (more[1].shape, BF16), (small[-1].shape[0:1] + (2 * LANES,), F32),
+            ((c_cat, c), BF16), ((c_taps, c), BF16),
             *ex7.outs, *ex8.outs, (st_a.chunk, BF16), (st_b.near_shape, BF16)]
     local = [pltpu.VMEM((c,) + a.shape[1:] if k in (9, 10) else a.shape, a.dtype) for k, a in enumerate(hbm)]
     width = hbm[6].shape[0] * hbm[6].shape[3]
@@ -1401,39 +1442,41 @@
         pltpu.VMEM((n, c), BF16), pltpu.VMEM((inner, f_n, LANES), BF16), pltpu.VMEM((st_b.rows_n, c), BF16),
         pltpu.VMEM(st_a.near_shape, BF16), pltpu.VMEM((2, *ex8.post), F32), *[pltpu.VMEM((t_n, c), F32)] * 4,
         pltpu.SemaphoreType.DMA((len(hbm),)), pltpu.SemaphoreType.DMA((3,)),
+        pltpu.VMEM((2, part, c_cat - c), BF16), pltpu.VMEM((2, part, c_taps), BF16), pltpu.VMEM((c, c_cat), F32),
+        pltpu.VMEM((c, c_taps), F32), pltpu.VMEM((9 * c, c), BF16), pltpu.SemaphoreType.DMA((2,)), pltpu.SemaphoreType.DMA((2,)), pltpu.SemaphoreType.DMA,
         *st_a.near_scratch, *st_a.line_scratch, *st_b.near_scratch, *ex7.local, *ex7.work, *ex8.local, *ex8.work,
     ]
     return pl.pallas_call(
         functools.partial(k_tail, (st_a, st_b, ex7, ex8, side)),
         out_shape=[jax.ShapeDtypeStruct(s, d) for s, d in outs],
-        in_specs=[anywhere] * len(hbm) + [vm] * len(small),
+        in_specs=[anywhere] * (len(hbm) + len(more)) + [vm] * len(small),
         out_specs=[anywhere] * 3 + [vm] * (len(outs) - 3),
         scratch_shapes=[*local, *scratch],
         compiler_params=pltpu.CompilerParams(collective_id=ex8.cid, has_side_effects=True, vmem_limit_bytes=VMEM_LIMIT),
         name="tail",
-    )(*hbm, *small)
+    )(*hbm, *more, *small)
 
 
 def final_kernel(cfg, *refs):
-    first, second, third, both, offsets, heights = cfg
-    n = len(offsets)
-    (res_a, near_b), ins, (out_a, out_bc), refs = refs[:2], refs[2 : 2 + n], refs[2 + n : 4 + n], refs[4 + n :]
-    x, near_c, res = refs[:3]
-    at = [3]
-
-    def take(scratch):
-        at[0] += len(scratch)
-        return refs[at[0] - len(scratch) : at[0]]
-
-    far = first.far
-    share_a = Share(first, res_a, out_a, take(first.share_scratch))
-    line_b = Line(second, near_b, take(second.line_scratch))
-    near = Near(third, x, near_c, take(third.near_scratch))
-    line_c = Line(third, near_c, take(third.line_scratch))
-    share = Share(both, res, out_bc, take(both.share_scratch))
-
-    c = near.c
+    first, second, third, both, offsets, n_hbm, n_small = cfg
+    it = iter(refs)
+
+    def take(n):
+        return [next(it) for _ in range(n)]
+
+    hbm, small, (out_a, out_bc, gx_out, fast_out) = take(n_hbm), take(n_small), take(4)
+    res_a, near_b, *parts, hn, m16, wlat, wfa = small
+    loaded = take(n_hbm)
+    low, dsp, w_in, w_sc, lat_low, df, dlow = loaded
+    x, near_c, res, gx, fast_gx, gs, sems, gx_sems, fast_sems = take(9)
+    share_a = Share(first, res_a, out_a, take(len(first.share_scratch)))
+    line_b = Line(second, near_b, take(len(second.line_scratch)))
+    near = Near(third, x, near_c, take(len(third.near_scratch)))
+    line_c = Line(third, near_c, take(len(third.line_scratch)))
+    share = Share(both, res, out_bc, take(len(both.share_scratch)))
+    far, c = first.far, near.c
     barrier = pltpu.get_barrier_semaphore()
+    loads = [pltpu.make_async_copy(a, b, sems.at[k]) for k, (a, b) in enumerate(zip(hbm, loaded))]
 
     def greet(device):
         pl.semaphore_signal(barrier, inc=1, device_id=device, device_id_type=MESH)
@@ -1441,10 +1484,10 @@
     greet(c.sibling)
     each(1, NEAR, lambda k: greet(c.plane(k)))
     each(1, far, lambda k: greet(c.line(k)))
-    end = 0
-    for ref, off, height in zip(ins, offsets, heights):
-        x[off : off + height, :] = ref[...].astype(BF16)
-        end = off + height
+    for load in loads:
+        load.start()
+    for ref, first_row, end in zip(parts, offsets, offsets[1:]):
+        x[first_row:end, :] = ref[...].astype(BF16)
     if end < x.shape[0]:
         x[end:, :] = jnp.zeros((x.shape[0] - end, x.shape[1]), BF16)
     pl.semaphore_wait(barrier, NEAR + far - 1)
@@ -1452,52 +1495,101 @@
     near.start()
     line_b.start(0, far)
     share_a.start_line()
+    p_n = dlow.shape[0] // STEPS
+
+    def gx_store(i):
+        part = pl.ds(i * p_n, p_n)
+        return pltpu.make_async_copy(gx.at[:, part], gx_out.at[:, part], gx_sems.at[i])
+
+    def slow_step(i):
+        part = pl.ds(i * p_n, p_n)
+        slow_grad(low.at[:, part], dsp.at[:, part], w_in, w_sc, gx.at[:, part])
+        gx_store(i).start()
+
+    def fast_store(i):
+        part = pl.ds(i * p_n, p_n)
+        return pltpu.make_async_copy(fast_gx.at[:, part], fast_out.at[:, part], fast_sems.at[i])
+
+    def fast_step(i):
+        part = pl.ds(i * p_n, p_n)
+        fast_grad(lat_low.at[:, part], hn.at[pl.ds(i, 1)], df.at[part], dlow.at[part], m16, wlat, wfa,
+                  fast_gx.at[:, part], gs)
+        fast_store(i).start()
+
     near.add_pair(0, far)
     share_a.start_plane()
+    for k in (0, 1, 2, 3):
+        loads[k].wait()
+    each(0, 1, slow_step)
     res[0 : second.ch, :] = line_b.total()
+    share_a.relay(1, far)
+    each(1, 4, slow_step)
     near.add_plane(0, far - 1, lambda m: line_c.line(m).start())
     near.add_plane(far - 1, far)
-    share_a.relay(1, far)
+    share_a.hand_on(0, far // 2)
+    each(4, STEPS, slow_step)
     res[second.ch :, :] = line_c.total()
     share.start_line()
     share.start_plane()
-    share_a.hand_on(0, far)
+    for k in range(4, n_hbm):
+        loads[k].wait()
+    share_a.hand_on(far // 2, far)
+    each(0, 2, fast_step)
     share.relay(1, far)
     share_a.hand_across(0, far)
-    share.hand_on(0, far)
+    each(2, 4, fast_step)
+    share.hand_on(0, far // 2)
+    each(4, STEPS, fast_step)
+    share.hand_on(far // 2, far)
     share.hand_across(0, far)
     share_a.end()
     share.end()
     line_b.end()
     line_c.end()
     near.end()
-
-
-def final_sum(sizes, cid, first, second, res_a, near_b, parts):
-    width = res_a.shape[1]
-    heights = tuple(p.shape[0] for p in parts)
-    offsets = tuple(sum(heights[:k]) for k in range(len(parts)))
-    third = Stream(sizes, rows_for(sizes, sum(heights)), width)
+    each(0, STEPS, lambda i: gx_store(i).wait())
+    each(0, STEPS, lambda i: fast_store(i).wait())
+
+
+def final_sum(sizes, cid, first, second, hbm, small, gx, fast_gx, heights):
+    width = first.width
+    offsets = tuple(sum(heights[:k]) for k in range(len(heights) + 1))
+    third = Stream(sizes, rows_for(sizes, offsets[-1]), width)
     both = Stream(sizes, second.rows_n + third.rows_n, width)
-    vm, hbm = pl.BlockSpec(memory_space=pltpu.VMEM), pl.BlockSpec(memory_space=pl.ANY)
-    out_a, out_bc = pl.pallas_call(
-        functools.partial(final_kernel, (first, second, third, both, offsets, heights)),
-        out_shape=[jax.ShapeDtypeStruct((s.rows_n, width), BF16) for s in (first, both)],
-        in_specs=[vm] * (2 + len(parts)),
-        out_specs=[hbm] * 2,
+    vm, anywhere = pl.BlockSpec(memory_space=pltpu.VMEM), pl.BlockSpec(memory_space=pl.ANY)
+    low, dlow = hbm[0], hbm[6]
+    s_n, p_n, f_n = low.shape[0], low.shape[1] // STEPS, dlow.shape[1]
+    out_a, out_bc, gx, fast_gx = pl.pallas_call(
+        functools.partial(final_kernel, (first, second, third, both, offsets, len(hbm), len(small))),
+        out_shape=[jax.ShapeDtypeStruct(s, BF16) for s in ((first.rows_n, width), (both.rows_n, width), gx, fast_gx)],
+        in_specs=[anywhere] * len(hbm) + [vm] * len(small),
+        out_specs=[anywhere] * 4,
         scratch_shapes=[
+            *[pltpu.VMEM(a.shape, a.dtype) for a in hbm],
             pltpu.VMEM((third.rows_n, width), BF16), pltpu.VMEM(third.near_shape, BF16), pltpu.VMEM(both.chunk, BF16),
+            pltpu.VMEM(gx, BF16), pltpu.VMEM(fast_gx, BF16), pltpu.VMEM((s_n * p_n * f_n, LANES), F32),
+            pltpu.SemaphoreType.DMA((len(hbm),)), pltpu.SemaphoreType.DMA((STEPS,)), pltpu.SemaphoreType.DMA((STEPS,)),
             *first.share_scratch, *second.line_scratch, *third.near_scratch, *third.line_scratch, *both.share_scratch,
         ],
         compiler_params=pltpu.CompilerParams(collective_id=cid, has_side_effects=True, vmem_limit_bytes=VMEM_LIMIT),
         name="final_sum",
-    )(res_a, near_b, *parts)
-    return out_a, out_bc.reshape(-1, both.ch, width), third
+    )(*hbm, *small)
+    return out_a, out_bc.reshape(-1, both.ch, width), gx, fast_gx
 
 
 def k_unpack(pieces, cut, *refs):
-    (src_a, src_b, q4, q5, q6, q7, q8), refs = refs[:7], refs[7:]
-    outs, (low_a, low_b, low_c, wide, line, sem_a, sem_b, sem_out) = refs[:-8], refs[-8:]
+    (src_a, src_b, q4, q5, q6, q7, q8), held, refs = refs[:7], refs[7:10], refs[10:]
+    outs, (low_a, low_b, low_c, wide, line, *kept, sem_a, sem_b, sem_out, sem_held) = refs[:-12], refs[-12:]
+    outs, given = outs[:-3], outs[-3:]
+
+    def moves(srcs, dsts, way):
+        return [
+            pltpu.make_async_copy(a.at[pl.ds(k, 1)], b.at[pl.ds(k, 1)], sem_held.at[way, n, k])
+            for n, (a, b) in enumerate(zip(srcs, dsts))
+            for k in range(a.shape[0])
+        ]
+
+    passes_in, passes = moves(held, kept, 0), moves(kept, given, 1)
     outs, (gains_out, biases_out, in_out, mid_out, out_out) = outs[:-5], outs[-5:]
     lows = (low_a, low_b, low_c)
     flats = [low_a, low_b.reshape(-1, low_b.shape[-1]), low_c.reshape(-1, low_c.shape[-1])]
@@ -1521,6 +1613,8 @@
             fetch_a(k).start()
     for k in (1, 2):
         fetch_b(k).start()
+    for move in passes_in:
+        move.start()
     seen = 0
     for k, (src, row, height, _, _) in enumerate(pieces):
         if src == 0:
@@ -1530,6 +1624,9 @@
             seen = src
         wide[starts[k] : starts[k] + height, :] = flats[src][row : row + height, :].astype(F32)
         store(k).start()
+    for move_in, move in zip(passes_in, passes):
+        move_in.wait()
+        move.start()
     lane = lax.broadcasted_iota(jnp.int32, (1, LANES), 1)
     left = lane < LANES // 2
     for slab, out in ((3, gains_out), (2, biases_out)):
@@ -1552,66 +1649,41 @@
         mid_out[k] = dot_tn(small[row : row + a, col : col + LANES], eye)[0:a, :]
     for k in range(len(pieces)):
         store(k).wait()
-
-
-def unpack(src_a, src_b, cut, pieces, shapes, small_shapes, norm_sums):
+    for move in passes:
+        move.wait()
+
+
+def unpack(src_a, src_b, cut, pieces, shapes, small_shapes, norm_sums, held):
     hbm, vm = pl.BlockSpec(memory_space=pl.ANY), pl.BlockSpec(memory_space=pltpu.VMEM)
     n, _, width = src_b.shape
     return pl.pallas_call(
         functools.partial(k_unpack, pieces, cut),
-        out_shape=[jax.ShapeDtypeStruct(s, F32) for s in (*shapes, *small_shapes)],
-        in_specs=[hbm] * 2 + [vm] * len(norm_sums),
-        out_specs=[hbm] * len(shapes) + [vm] * len(small_shapes),
+        out_shape=[jax.ShapeDtypeStruct(s, F32) for s in (*shapes, *small_shapes)]
+        + [jax.ShapeDtypeStruct(a.shape, a.dtype) for a in held],
+        in_specs=[hbm] * 2 + [vm] * len(norm_sums) + [hbm] * len(held),
+        out_specs=[hbm] * len(shapes) + [vm] * len(small_shapes) + [hbm] * len(held),
         scratch_shapes=[
             pltpu.VMEM(src_a.shape, BF16),
             pltpu.VMEM((n, cut, width), BF16),
             pltpu.VMEM((n, src_b.shape[1] - cut, width), BF16),
             pltpu.VMEM((sum(p[2] for p in pieces), width), F32),
             pltpu.VMEM((24, LANES), F32),
+            *[pltpu.VMEM(a.shape, a.dtype) for a in held],
             pltpu.SemaphoreType.DMA((len(pieces),)),
             pltpu.SemaphoreType.DMA((3,)),
             pltpu.SemaphoreType.DMA((len(pieces),)),
+            pltpu.SemaphoreType.DMA((2, len(held), held[0].shape[0])),
         ],
         compiler_params=pltpu.CompilerParams(vmem_limit_bytes=VMEM_LIMIT),
         name="unpack",
-    )(src_a, src_b, *norm_sums)
-
-
-def k_prep(x_hbm, fill_ref, clip_ref, norm_ref, wfi_ref, wfm_ref, wfo_ref,
-           tail_ref, gb_ref, m16_ref, m64_ref, wfa_ref, wmid_ref, wback_ref, wout_ref,
-           near, rows_f, sent, land, sems, local):
+    )(src_a, src_b, *norm_sums, *held)
+
+
+def small_set_up(fill_ref, clip_ref, norm_ref, wfi_ref, wfm_ref, wfo_ref,
+                 gb_ref, m16_ref, m64_ref, wfa_ref, wmid_ref, wback_ref, wout_ref, s_n, t_n):
     length = lax.axis_size("frames")
     total = lax.axis_size("path") * length
     me = lax.axis_index("path") * length + lax.axis_index("frames")
-
-    def place(index):
-        return (lax.div(index, length), lax.rem(index, length))
-
-    nxt, prv = place(lax.rem(me + 1, total)), place(lax.rem(me + total - 1, total))
-    barrier = pltpu.get_barrier_semaphore()
-    pl.semaphore_signal(barrier, inc=1, device_id=nxt, device_id_type=MESH)
-    pl.semaphore_signal(barrier, inc=1, device_id=prv, device_id_type=MESH)
-    s_n, inner, t_n, c = near.shape
-    f_n = x_hbm.shape[2]
-    fetch = pltpu.make_async_copy(x_hbm.at[:, :, pl.ds(f_n - t_n, t_n), :], near, local)
-    fetch.start()
-    fetch.wait()
-    p_n = inner // STEPS
-    rows_f[...] = near[...].reshape(rows_f.shape).astype(F32)
-    zero_ref(sent)
-    count = s_n * inner
-    for k in range(2):
-        line = rows_f[pl.ds(t_n - 2 + k, count, stride=t_n), :]
-        for s in range(s_n):
-            for step in range(STEPS):
-                at = s * inner + step * p_n
-                sent[step, s, 0:p_n, k * c : (k + 1) * c] = line[at : at + p_n, :]
-    pl.semaphore_wait(barrier, 2)
-    copy = pltpu.make_async_remote_copy(
-        src_ref=sent, dst_ref=land, send_sem=sems.at[0], recv_sem=sems.at[1], device_id=nxt, device_id_type=MESH
-    )
-    copy.start()
-
     lane = lax.broadcasted_iota(jnp.int32, (1, LANES), 1)
     for k in range(2):
         half = pltpu.roll(norm_ref[k], LANES // 2, 1)
@@ -1657,35 +1729,6 @@
         wmid_ref[k * LANES : (k + 1) * LANES, :] = jnp.where(diag, dot_nt(left, spread), 0.0).astype(BF16)
         right = dot_nt(spread, wfm_ref[k]).astype(BF16)
         wback_ref[k * LANES : (k + 1) * LANES, :] = jnp.where(diag, dot_nt(right, spread), 0.0).astype(BF16)
-    copy.wait()
-    tail_ref[...] = land[...]
-
-
-def prepare(x_fast, fill, clip_offset, norms, w_fast_in, w_fast_mid, w_fast_out):
-    s_n, inner, f_n, c = x_fast.shape
-    t_n = fill.shape[0]
-    p_n = inner // STEPS
-    vm = pl.BlockSpec(memory_space=pltpu.VMEM)
-    sm = pl.BlockSpec(memory_space=pltpu.SMEM)
-    tail = (STEPS, s_n, 8, 2 * c)
-    outs = [(tail, F32), ((2, 32, LANES), F32), ((3, t_n, LANES), F32), ((3, f_n, LANES), F32),
-            ((LANES, s_n * c), BF16), ((3 * LANES, LANES), BF16), ((3 * LANES, LANES), BF16), ((LANES, s_n * c), BF16)]
-    return pl.pallas_call(
-        k_prep,
-        out_shape=[jax.ShapeDtypeStruct(s, d) for s, d in outs],
-        in_specs=[pl.BlockSpec(memory_space=pl.ANY), sm, sm, vm, vm, vm, vm],
-        out_specs=[vm] * len(outs),
-        scratch_shapes=[
-            pltpu.VMEM((s_n, inner, t_n, c), BF16),
-            pltpu.VMEM((s_n * inner * t_n, c), F32),
-            pltpu.VMEM(tail, F32),
-            pltpu.VMEM(tail, F32),
-            pltpu.SemaphoreType.DMA((2,)),
-            pltpu.SemaphoreType.DMA,
-        ],
-        compiler_params=pltpu.CompilerParams(collective_id=10, has_side_effects=True, vmem_limit_bytes=VMEM_LIMIT),
-        name="prepare",
-    )(x_fast, fill, clip_offset, norms, w_fast_in.T, w_fast_mid, w_fast_out)
 
 
 def per_device(slow_input, fast_input, clip_offset, fill, w_fast_in, w_fast_mid, w_fast_out, w_lateral,
@@ -1713,11 +1756,8 @@
 
     norms = jnp.stack([gains, biases])
     norms = jnp.pad(norms, ((0, 0), (0, -norms.shape[1] % (8 * LANES)))).reshape(2, -1, LANES)
-    tail, gb, m16, m64, wfa, wmid, wback, wout = prepare(
-        x_fast, fill, clip_offset, norms, w_fast_in, w_fast_mid, w_fast_out
-    )
     wlat = w_lateral.reshape(-1, c_lat)
-    wsp = w_slow_mid.reshape(9, in_slow, in_slow)
+    wsp = w_slow_mid.reshape(-1, in_slow)
 
     sl = (groups, inner, t_n)
     fp = (inner, f_n)
@@ -1751,13 +1791,20 @@
         (fp + (LANES,), F32), (sl + (c_lat,), F32), (sl + (5 * c_fast,), BF16), (sl + (c_lat,), BF16),
         (fp + (3 * LANES,), BF16), (sl + (in_slow,), F32), (sl + (c_slow,), F32), (fp + (LANES,), F32),
     ]
-    fa, lat, taps, lact, ftap, sa, sp, fb, c1, hp, hn, c2 = run_resident(
+    ready = [((2, 32, LANES), F32), ((3, t_n, LANES), F32), ((3, f_n, LANES), F32), ((LANES, groups * c_fast), BF16),
+             ((3 * LANES, LANES), BF16), ((3 * LANES, LANES), BF16), ((LANES, groups * c_fast), BF16)]
+    ends = (STEPS, groups * 8, 2 * c_fast)
+    fa, lat, taps, lact, ftap, sa, sp, fb, gb, m16, m64, wfa, wmid, wback, wout, c1, hp, hn, c2 = run_resident(
         functools.partial(k_front, exs), exs,
-        [x_fast, wlat, x_slow, w_slow_in, w_shortcut], [tail, gb, m16, m64, wfa, wmid],
-        kept, [(*k, True) for k in kept],
+        [x_fast, wlat, x_slow, w_slow_in, w_shortcut],
+        [fill, clip_offset, norms, w_fast_in.T, w_fast_mid, w_fast_out],
+        kept, [*[(*k, True) for k in kept], *[(*k, False) for k in ready]],
         [pltpu.VMEM((groups * p_n * f_n, c_fast), F32), *acc(f_n, LANES, 2), *acc(t_n, c_lat, 2), *acc(t_n, in_slow, 2),
-         *acc(t_n, c_slow, 2), *acc(f_n, LANES, 2), pltpu.SemaphoreType.DMA((8,)), sems7],
+         *acc(t_n, c_slow, 2), *acc(f_n, LANES, 2), pltpu.SemaphoreType.DMA((8,)), sems7,
+         pltpu.VMEM((pixels * t_n, c_fast), F32), pltpu.VMEM(ends, F32), pltpu.VMEM(ends, BF16), pltpu.VMEM(ends, BF16),
+         pltpu.SemaphoreType.DMA((2,))],
         "front",
+        scalars=2,
     )
 
     exs = [
@@ -1816,28 +1863,22 @@
     def rows2(a):
         return a.reshape(-1, a.shape[-1])
 
-    dsa_low, dfa_low, dlat, gw_fast, q7, q8, hn, res_a, near_b = back_tail(
+    dsa_low, dfa_low, lat_low, gw_fast, gw_in, gw_lat, q7, q8, hn, res_a, near_b = back_tail(
         stream_a, stream_b,
         Exchange(sizes, 7, 4, bwd=(("plain", 0, 1, 8, 2, 0, 2),)),
         Exchange(sizes, 7, 4, bwd=(("plain", 0, 1, 6, 2, 0, 2),), post=(STEPS, groups * 8, c_lat)),
         [gw_short, rows2(dsb), rows2(sb4), pad, wsp, rows2(sa), x_fast, dfa, fa, w_slow_in, w_shortcut, rows2(dsp), rows2(lat)],
+        [rows2(x_slow), lact.reshape(pixels, t_n, c_lat), rows2(taps)],
         [gb, c1, c2, c3, q6, m16, m64, g_fout, g_fmid],
         side, t_n, in_slow,
     )
-    slow_gx, gw_in = call(
-        k_slow_grad,
-        [sb_(x_slow), sb_(lact), sb_(dsa_low.reshape(sl + (in_slow,))), sb_(dsp), whole(w_slow_in), whole(w_shortcut)],
-        [slow_out(c_slow, BF16), out_whole((c_cat, in_slow), BF16)], acc(in_slow, c_cat, 1), "slow_grad",
+    heights = (gw_sout.shape[0], c_cat, 5 * c_fast, gw_fast.shape[0])
+    sum_a, sum_bc, slow_gx, fast_gx = final_sum(
+        sizes, 9, stream_a, stream_b,
+        [dsa_low.reshape(sl + (in_slow,)), dsp, w_slow_in, w_shortcut, lat_low.reshape(sl + (c_lat,)), df, dfa_low],
+        [res_a, near_b, gw_sout, gw_in, gw_lat, gw_fast, hn, m16, wlat, wfa],
+        sl + (c_slow,), (groups, inner, f_n, c_fast), heights,
     )
-    fast_gx, gw_lat = call(
-        k_fast_grad,
-        [sb_(dlat.reshape(sl + (c_lat,))), sb_(lat), sb_(taps), blocked(hn, 0, 1), fb_(df), fb_(dfa_low), whole(c1), whole(q8),
-         whole(m16), whole(wlat), whole(wfa)],
-        [out_blocked((groups, inner, f_n, c_fast), BF16, 1, p_n), out_whole((5 * c_fast, c_lat), BF16)],
-        [pltpu.VMEM((groups * p_n * f_n, c_fast), F32), *acc(c_lat, 5 * c_fast, 1)],
-        "fast_grad",
-    )
-    sum_a, sum_bc, _ = final_sum(sizes, 9, stream_a, stream_b, res_a, near_b, [gw_sout, gw_in, gw_lat, gw_fast])
     blocks = c_slow // in_slow
     pieces = [(0, n * c_cat, c_cat, 0, n * width) for n in range(blocks)]
     pieces.append((1, 0, 9 * in_slow, 2, None))
@@ -1845,16 +1886,18 @@
     for n in range(blocks):
         pieces.append((2, at, in_slow, 1, n * width))
         at += in_slow
-    for out, tall in ((3, c_cat), (4, gw_lat.shape[0])):
+    for out, tall in ((3, c_cat), (4, 5 * c_fast)):
         pieces.append((2, at, tall, out, None))
         at += tall
     norm_rows = -(-gains.shape[0] // LANES)
-    g_short, g_sout, gw_mid, gw_in, gw_lat, gains_grad, biases_grad, g_fin, g_fmid, g_fout = unpack(
+    g_short, g_sout, gw_mid, gw_in, gw_lat, gains_grad, biases_grad, g_fin, g_fmid, g_fout, *held = unpack(
         sum_a, sum_bc, stream_b.ch, tuple(pieces),
-        [(c_cat, c_slow), (in_slow, c_slow), (9 * in_slow, width), (c_cat, in_slow), gw_lat.shape],
+        [(c_cat, c_slow), (in_slow, c_slow), (9 * in_slow, width), (c_cat, in_slow), wlat.shape],
         [(norm_rows, LANES), (norm_rows, LANES), (in_fast, c_fast), w_fast_mid.shape, (in_fast, c_fast)],
         [q4, q5, q6, q7, q8],
+        [slow_gx, fast_gx, fast_y],
     )
+    slow_gx, fast_gx, fast_y = held
     grads = (
         g_fin.T,
         g_fmid,

time: 296 us -> 273 us (0.922)
  Pallas kernels: 291 us -> 271 us
    pallas_call x4 -> x2, Pallas kernels: 102 us -> 71.6 us  [call(): pl.pallas_call(body, grid=(STEPS,), in_specs=[pl.BlockSpec(b, m) for _, b...]
    pallas_call x1 -> x0, Pallas kernels: 14.8 us -> none  [prepare(): pl.pallas_call(k_prep, out_shape=[jax.ShapeDtypeStruct(s, d) for s, d in...]
    pallas_call x2, Pallas kernels: 73.5 us -> 82.8 us  [run_resident(): pl.pallas_call(body, out_shape=[jax.ShapeDtypeStruct(shape, dtype) for sh...]
    pallas_call x1, Pallas kernels: 7.26 us -> 15.6 us  [unpack(): pl.pallas_call(functools.partial(k_unpack, pieces, cut), out_shape=[jax.S...]
    pallas_call x1, Pallas kernels: 41.9 us -> 47.3 us  [final_sum(): pl.pallas_call(functools.partial(final_kernel, (first, second, third, bot...]
where the time goes in v6:
time: 273 us
  Pallas kernels  271 us (99%)
    pallas_call x2, Pallas kernels, run_resident(): pl.pallas_call(body, out_shape=[jax.ShapeDtypeStruct(shape, dtype) for sh...  82.8 us
    pallas_call x2, Pallas kernels, call(): pl.pallas_call(body, grid=(STEPS,), in_specs=[pl.BlockSpec(b, m) for _, b...  71.6 us
    pallas_call x1, Pallas kernels, back_tail(): pl.pallas_call(functools.partial(k_tail, (st_a, st_b, ex7, ex8, side)), o...  53.4 us
    pallas_call x1, Pallas kernels, final_sum(): pl.pallas_call(functools.partial(final_kernel, (first, second, third, bot...  47.3 us
    pallas_call x1, Pallas kernels, unpack(): pl.pallas_call(functools.partial(k_unpack, pieces, cut), out_shape=[jax.S...  15.6 us

profile of v6, /device:TPU:0, one launch (start us, length us, event | category | flops | bytes accessed | tf_op | source)
XLA Modules:
  0.0 272.9 jit_solution(3992166895159032497)
XLA Ops:
  0.6 0.8 fusion
  1.4 0.6 copy.32
  2.0 46.7 %front.1 = (f32[49,64,128]{2,1,0:T(8,128)}, f32[4,49,16,256]{3,2,1,0:T(8,128)}, bf16[4,49,16,640]{3,2,1,0:T(8,128)(2,1)}, bf16[4,49,16,256]{3,2,1,0:T(8,128)(2,1...) custom-call(bf16[4,49,64,128]{3,2,1,0:T(8,128)(2,1)} %bitcast.59, ...), custom_call_target="tpu_custom_call" | custom-call | tf_op jit(solution)/shard_map/front/pallas_call | solution.py:666
  48.7 36.1 %middle.1 = (bf16[16,16,16,256]{3,2,1,0:T(8,128)(2,1)}, f32[196,16,256]{2,1,0:T(8,128)}, bf16[49,64,128]{2,1,0:T(8,128)(2,1)}, bf16[196,16,256]{2,1,0:T(8,128)(2...) custom-call(f32[14,14,16,256]{3,2,1,0:T(8,128)} %bitcast.65, ...), custom_call_target="tpu_custom_call" | custom-call | tf_op jit(solution)/shard_map/middle/pallas_call | solution.py:666
  84.8 23.8 %out.1 = (bf16[4,49,16,1024]{3,2,1,0:T(8,128)(2,1)}, f32[4,49,16,1024]{3,2,1,0:T(8,128)}, f32[49,64,128]{2,1,0:T(8,128)}, f32[32,128]{1,0:T(8,128)}, f32[7,2,8,1...) custom-call(bf16[4,49,16,256]{3,2,1,0:T(8,128)(2,1)} %bitcast.68, ...), custom_call_target="tpu_custom_call" | custom-call | tf_op jit(solution)/shard_map/out/pallas_call | solution.py:389
  108.7 47.8 %back_out.1 = (bf16[5120,256]{1,0:T(8,128)(2,1)}, bf16[1024,256]{1,0:T(8,128)(2,1)}, bf16[4,49,16,1024]{3,2,1,0:T(8,128)(2,1)}, f32[4,49,16,256]{3,2,1,0:T(8,128...) custom-call(bf16[4,49,16,1024]{3,2,1,0:T(8,128)(2,1)} %bitcast.57, ...), custom_call_target="tpu_custom_call" | custom-call | tf_op jit(solution)/shard_map/back_out/pallas_call | solution.py:389
  156.5 53.4 %tail.1 = (bf16[3136,256]{1,0:T(8,128)(2,1)}, bf16[49,64,128]{2,1,0:T(8,128)(2,1)}, bf16[196,16,256]{2,1,0:T(8,128)(2,1)}, f32[96,256]{1,0:T(8,128)}, bf16[1280,...) custom-call(bf16[5120,256]{1,0:T(8,128)(2,1)} %get-tuple-element.108, ...), custom_call_target="tpu_custom_call" | custom-call | tf_op jit(solution)/shard_map/tail/pallas_call | solution.py:1449
  209.8 47.3 %final_sum.1 = (bf16[5120,256]{1,0:T(8,128)(2,1)}, bf16[5632,256]{1,0:T(8,128)(2,1)}, bf16[4,49,16,1024]{3,2,1,0:T(8,128)(2,1)}, bf16[4,49,64,128]{3,2,1,0:T(8,128)(2,1)}) custom-call(bf16[4,49,16,256]{3,2,1,0:T(8,128)(2,1)} %bitcast.78, bf16[4,49,16,1024]{3,2,1,0:T(8,128)(2,1)} %get-tuple-element.112.refs_1_, bf16[1280,256]{1,0:T(8,128)(2,1)} %refs_2_.1, ...), custom_call_target="tpu_custom_call" | custom-call | tf_op jit(solution)/shard_map/final_sum/pallas_call | solution.py:1562
  257.1 15.6 %unpack.1 = (f32[1280,1024]{1,0:T(8,128)}, f32[256,1024]{1,0:T(8,128)}, f32[2304,256]{1,0:T(8,128)}, f32[1280,256]{1,0:T(8,128)}, f32[640,256]{1,0:T(8,128)}, /*...) custom-call(bf16[5120,256]{1,0:T(8,128)(2,1)} %get-tuple-element.129, ...), custom_call_target="tpu_custom_call" | custom-call | tf_op jit(solution)/shard_map/unpack/pallas_call | solution.py:1659

commit v7 on v6

--- a/solution.py
+++ b/solution.py
@@ -122,7 +122,7 @@
     return len(peers)
 
 
-def exchange_run(cfg, ins, outs, scratch, meanwhile=None, post=None, after=None):
+def exchange_run(cfg, ins, outs, scratch, meanwhile=None, post=None, after=None, between=None):
     fwd, bwd = cfg.fwd, cfg.bwd
     nf = sum(c[2] for c in fwd)
     nb = max((c[6] + c[4] for c in bwd), default=0)
@@ -212,6 +212,8 @@
         )
         copies2[-1].start()
     slots2[r2] = mid[...]
+    if between is not None:
+        between()
     for c in copies2:
         c.wait_recv()
     combine(slots2, g2, tot)
@@ -499,23 +501,27 @@
 
 
 def k_join(i, x_ref, lat_ref, fa_ref, hp_ref, hn_ref, c1_ref, m16_ref, m64_ref, win_ref, wsc_ref, wmid_ref,
-           lact_ref, ftap_ref, sa_ref, sp_ref, fb_ref, st_ref, am, av, pm, pv, bm, bv):
+           lact_ref, ftap_ref, sa_ref, sp_ref, fb_ref, st_ref, am, av, pm, pv, bm, bv, begun=False):
     s_n, p_n, t_n, c_slow = x_ref.shape
     c_lat = lat_ref.shape[-1]
     v = flat(lat_ref[...]) * rows(c1_ref, 0, 1, 2) + rows(c1_ref, 1, 1, 2)
     lact = (v * sig(v)).astype(BF16)
     lact_ref[...] = lact.reshape(lact_ref.shape)
-    joined = jnp.concatenate([flat(x_ref[...]), lact], axis=1)
+    joined = None if begun else jnp.concatenate([flat(x_ref[...]), lact], axis=1)
     wide = c_lat
     for n in range(1 + wsc_ref.shape[1] // wide):
-        z = dot(joined, win_ref[...] if n == 0 else wsc_ref[:, (n - 1) * wide : n * wide])
+        cols = slice((n - 1) * wide, n * wide)
+        if begun:
+            z = flat(sa_ref[...] if n == 0 else sp_ref[:, :, :, cols])
+            z = z + dot(lact, win_ref[c_slow:, :] if n == 0 else wsc_ref[c_slow:, cols])
+        else:
+            z = dot(joined, win_ref[...] if n == 0 else wsc_ref[:, cols])
         z4 = z.reshape(s_n, p_n, t_n, wide)
         z3 = z.reshape(s_n * p_n, t_n, wide)
         if n == 0:
             sa_ref[...] = z4
             spread_add(i, z3, am, av)
         else:
-            cols = slice((n - 1) * wide, n * wide)
             sp_ref[:, :, :, cols] = z4
             spread_add(i, z3, pm, pv, cols)
 
@@ -723,22 +729,37 @@
     each(0, STEPS, first)
     for k in (0, 1, 2):
         copies[k].start()
-    exchange_run(exs[0], [gb], [c1, hp, hn], work[0])
-    for k in (2, 3, 4):
-        loads[k].wait()
+    c_slow = x_slow.shape[-1]
+
+    def begin(i):
+        part = pl.ds(i * p_n, p_n)
+        xs_part = flat(x_slow[:, part])
+        wide = sa.shape[-1]
+        sa[:, part] = dot(xs_part, w_in[0:c_slow, :]).reshape(s_n, p_n, t_n, wide)
+        for n in range(sp.shape[-1] // wide):
+            cols = slice(n * wide, (n + 1) * wide)
+            sp[:, part, :, cols] = dot(xs_part, w_sc[0:c_slow, cols]).reshape(s_n, p_n, t_n, wide)
+
+    def begin_some():
+        for k in (2, 3, 4):
+            loads[k].wait()
+        each(0, 2, begin)
+
+    exchange_run(exs[0], [gb], [c1, hp, hn], work[0], begin_some, between=lambda: each(2, 3, begin))
 
     def store_sp(i):
         part = pl.ds(i * p_n, p_n)
         return pltpu.make_async_copy(sp.at[:, part], big[6].at[:, part], sp_sems.at[i])
 
-    def join(i):
+    def join(i, begun=False):
         part, one = pl.ds(i * p_n, p_n), pl.ds(i, 1)
         k_join(i, x_slow.at[:, part], lat.at[:, part], fa.at[part], hp.at[one], hn.at[one], c1, m16, m64, w_in, w_sc, wmid,
                lact.at[:, part], ftap.at[part], sa.at[:, part], sp.at[:, part], fb.at[part], work[1][0],
-               am, av, pm, pv, bm, bv)
+               am, av, pm, pv, bm, bv, begun)
         store_sp(i).start()
 
-    each(0, STEPS, join)
+    each(0, 3, lambda i: join(i, True))
+    each(3, STEPS, join)
     for k in (3, 4, 5, 7):
         copies[k].start()
     exchange_run(exs[1], [gb], [c2], work[1])
@@ -1516,31 +1537,31 @@
                   fast_gx.at[:, part], gs)
         fast_store(i).start()
 
+    share_a.start_plane()
     near.add_pair(0, far)
-    share_a.start_plane()
     for k in (0, 1, 2, 3):
         loads[k].wait()
     each(0, 1, slow_step)
     res[0 : second.ch, :] = line_b.total()
     share_a.relay(1, far)
-    each(1, 4, slow_step)
+    share_a.hand_on(0, 1)
+    each(1, 3, slow_step)
     near.add_plane(0, far - 1, lambda m: line_c.line(m).start())
     near.add_plane(far - 1, far)
-    share_a.hand_on(0, far // 2)
-    each(4, STEPS, slow_step)
+    share_a.hand_on(1, far)
+    each(3, 4, slow_step)
     res[second.ch :, :] = line_c.total()
     share.start_line()
     share.start_plane()
+    each(4, STEPS, slow_step)
     for k in range(4, n_hbm):
         loads[k].wait()
-    share_a.hand_on(far // 2, far)
-    each(0, 2, fast_step)
     share.relay(1, far)
     share_a.hand_across(0, far)
-    each(2, 4, fast_step)
-    share.hand_on(0, far // 2)
-    each(4, STEPS, fast_step)
-    share.hand_on(far // 2, far)
+    share.hand_on(0, 1)
+    each(0, 3, fast_step)
+    share.hand_on(1, far)
+    each(3, STEPS, fast_step)
     share.hand_across(0, far)
     share_a.end()
     share.end()

time: 273 us -> 269 us (0.985)
  Pallas kernels: 271 us -> 266 us
    pallas_call x2, Pallas kernels: 82.8 us -> 79.9 us  [run_resident(): pl.pallas_call(body, out_shape=[jax.ShapeDtypeStruct(shape, dtype) for sh...]
where the time goes in v7:
time: 269 us
  Pallas kernels  266 us (99%)
    pallas_call x2, Pallas kernels, run_resident(): pl.pallas_call(body, out_shape=[jax.ShapeDtypeStruct(shape, dtype) for sh...  79.9 us
    pallas_call x2, Pallas kernels, call(): pl.pallas_call(body, grid=(STEPS,), in_specs=[pl.BlockSpec(b, m) for _, b...  71.6 us
    pallas_call x1, Pallas kernels, back_tail(): pl.pallas_call(functools.partial(k_tail, (st_a, st_b, ex7, ex8, side)), o...  53.4 us
    pallas_call x1, Pallas kernels, final_sum(): pl.pallas_call(functools.partial(final_kernel, (first, second, third, bot...  45.9 us
    pallas_call x1, Pallas kernels, unpack(): pl.pallas_call(functools.partial(k_unpack, pieces, cut), out_shape=[jax.S...  15.6 us

profile of v7, /device:TPU:0, one launch (start us, length us, event | category | flops | bytes accessed | tf_op | source)
XLA Modules:
  0.0 268.6 jit_solution(13314802109395631832)
XLA Ops:
  0.6 0.8 fusion
  1.4 0.6 copy.32
  2.0 43.8 %front.1 = (f32[49,64,128]{2,1,0:T(8,128)}, f32[4,49,16,256]{3,2,1,0:T(8,128)}, bf16[4,49,16,640]{3,2,1,0:T(8,128)(2,1)}, bf16[4,49,16,256]{3,2,1,0:T(8,128)(2,1...) custom-call(bf16[4,49,64,128]{3,2,1,0:T(8,128)(2,1)} %bitcast.59, ...), custom_call_target="tpu_custom_call" | custom-call | tf_op jit(solution)/shard_map/front/pallas_call | solution.py:672
  45.8 36.1 %middle.1 = (bf16[16,16,16,256]{3,2,1,0:T(8,128)(2,1)}, f32[196,16,256]{2,1,0:T(8,128)}, bf16[49,64,128]{2,1,0:T(8,128)(2,1)}, bf16[196,16,256]{2,1,0:T(8,128)(2...) custom-call(f32[14,14,16,256]{3,2,1,0:T(8,128)} %bitcast.65, ...), custom_call_target="tpu_custom_call" | custom-call | tf_op jit(solution)/shard_map/middle/pallas_call | solution.py:672
  82.0 23.8 %out.1 = (bf16[4,49,16,1024]{3,2,1,0:T(8,128)(2,1)}, f32[4,49,16,1024]{3,2,1,0:T(8,128)}, f32[49,64,128]{2,1,0:T(8,128)}, f32[32,128]{1,0:T(8,128)}, f32[7,2,8,1...) custom-call(bf16[4,49,16,256]{3,2,1,0:T(8,128)(2,1)} %bitcast.68, ...), custom_call_target="tpu_custom_call" | custom-call | tf_op jit(solution)/shard_map/out/pallas_call | solution.py:391
  105.8 47.8 %back_out.1 = (bf16[5120,256]{1,0:T(8,128)(2,1)}, bf16[1024,256]{1,0:T(8,128)(2,1)}, bf16[4,49,16,1024]{3,2,1,0:T(8,128)(2,1)}, f32[4,49,16,256]{3,2,1,0:T(8,128...) custom-call(bf16[4,49,16,1024]{3,2,1,0:T(8,128)(2,1)} %bitcast.57, ...), custom_call_target="tpu_custom_call" | custom-call | tf_op jit(solution)/shard_map/back_out/pallas_call | solution.py:391
  153.6 53.4 %tail.1 = (bf16[3136,256]{1,0:T(8,128)(2,1)}, bf16[49,64,128]{2,1,0:T(8,128)(2,1)}, bf16[196,16,256]{2,1,0:T(8,128)(2,1)}, f32[96,256]{1,0:T(8,128)}, bf16[1280,...) custom-call(bf16[5120,256]{1,0:T(8,128)(2,1)} %get-tuple-element.108, ...), custom_call_target="tpu_custom_call" | custom-call | tf_op jit(solution)/shard_map/tail/pallas_call | solution.py:1470
  207.0 45.9 %final_sum.1 = (bf16[5120,256]{1,0:T(8,128)(2,1)}, bf16[5632,256]{1,0:T(8,128)(2,1)}, bf16[4,49,16,1024]{3,2,1,0:T(8,128)(2,1)}, bf16[4,49,64,128]{3,2,1,0:T(8,128)(2,1)}) custom-call(bf16[4,49,16,256]{3,2,1,0:T(8,128)(2,1)} %bitcast.78, bf16[4,49,16,1024]{3,2,1,0:T(8,128)(2,1)} %get-tuple-element.112.refs_1_, bf16[1280,256]{1,0:T(8,128)(2,1)} %refs_2_.1, ...), custom_call_target="tpu_custom_call" | custom-call | tf_op jit(solution)/shard_map/final_sum/pallas_call | solution.py:1583
  252.9 15.6 %unpack.1 = (f32[1280,1024]{1,0:T(8,128)}, f32[256,1024]{1,0:T(8,128)}, f32[2304,256]{1,0:T(8,128)}, f32[1280,256]{1,0:T(8,128)}, f32[640,256]{1,0:T(8,128)}, /*...) custom-call(bf16[5120,256]{1,0:T(8,128)(2,1)} %get-tuple-element.129, ...), custom_call_target="tpu_custom_call" | custom-call | tf_op jit(solution)/shard_map/unpack/pallas_call | solution.py:1680

commit v8 on v7

--- a/solution.py
+++ b/solution.py
@@ -745,7 +745,7 @@
             loads[k].wait()
         each(0, 2, begin)
 
-    exchange_run(exs[0], [gb], [c1, hp, hn], work[0], begin_some, between=lambda: each(2, 3, begin))
+    exchange_run(exs[0], [gb], [c1, hp, hn], work[0], begin_some, between=lambda: each(2, 4, begin))
 
     def store_sp(i):
         part = pl.ds(i * p_n, p_n)
@@ -758,8 +758,8 @@
                am, av, pm, pv, bm, bv, begun)
         store_sp(i).start()
 
-    each(0, 3, lambda i: join(i, True))
-    each(3, STEPS, join)
+    each(0, 4, lambda i: join(i, True))
+    each(4, STEPS, join)
     for k in (3, 4, 5, 7):
         copies[k].start()
     exchange_run(exs[1], [gb], [c2], work[1])
@@ -1416,7 +1416,10 @@
                     ends[0, step, s * 8 + p : s * 8 + p + 1, :] = sb[at : at + 1, :]
                     ends[1, step, s * 8 + p : s * 8 + p + 1, :] = lat[at : at + 1, :]
         lact_load.wait()
-        each(0, STEPS, in_step)
+        each(0, 3, in_step)
+
+    def in_grad_rest():
+        each(3, STEPS, in_step)
         for n in range(gsi.shape[1] // c):
             gw_in[n * c : (n + 1) * c, :] = gsi[:, n * c : (n + 1) * c].T.astype(BF16)
 
@@ -1437,7 +1440,7 @@
         for k in range(glat.shape[1] // LANES):
             gw_lat[k * LANES : (k + 1) * LANES, :] = glat[:, k * LANES : (k + 1) * LANES].T.astype(BF16)
 
-    exchange_run(ex8, [gb, c1], [q8, hn], scr8, in_grad, post, lat_grad)
+    exchange_run(ex8, [gb, c1], [q8, hn], scr8, in_grad, post, lat_grad, in_grad_rest)
     res_a[...] = line.total()
     near_two.add_plane(0, far)
     for store in stores:

time: 269 us -> 268 us (level)
  no operation moved by 1% of the time
where the time goes in v8:
time: 268 us
  Pallas kernels  266 us (99%)
    pallas_call x2, Pallas kernels, run_resident(): pl.pallas_call(body, out_shape=[jax.ShapeDtypeStruct(shape, dtype) for sh...  79 us
    pallas_call x2, Pallas kernels, call(): pl.pallas_call(body, grid=(STEPS,), in_specs=[pl.BlockSpec(b, m) for _, b...  72.2 us
    pallas_call x1, Pallas kernels, back_tail(): pl.pallas_call(functools.partial(k_tail, (st_a, st_b, ex7, ex8, side)), o...  52.9 us
    pallas_call x1, Pallas kernels, final_sum(): pl.pallas_call(functools.partial(final_kernel, (first, second, third, bot...  45.9 us
    pallas_call x1, Pallas kernels, unpack(): pl.pallas_call(functools.partial(k_unpack, pieces, cut), out_shape=[jax.S...  15.6 us

profile of v8, /device:TPU:0, one launch (start us, length us, event | category | flops | bytes accessed | tf_op | source)
XLA Modules:
  0.0 267.7 jit_solution(17486006505964437476)
XLA Ops:
  0.6 0.8 fusion
  1.4 0.6 copy.32
  2.0 42.9 %front.1 = (f32[49,64,128]{2,1,0:T(8,128)}, f32[4,49,16,256]{3,2,1,0:T(8,128)}, bf16[4,49,16,640]{3,2,1,0:T(8,128)(2,1)}, bf16[4,49,16,256]{3,2,1,0:T(8,128)(2,1...) custom-call(bf16[4,49,64,128]{3,2,1,0:T(8,128)(2,1)} %bitcast.59, ...), custom_call_target="tpu_custom_call" | custom-call | tf_op jit(solution)/shard_map/front/pallas_call | solution.py:672
  44.9 36.1 %middle.1 = (bf16[16,16,16,256]{3,2,1,0:T(8,128)(2,1)}, f32[196,16,256]{2,1,0:T(8,128)}, bf16[49,64,128]{2,1,0:T(8,128)(2,1)}, bf16[196,16,256]{2,1,0:T(8,128)(2...) custom-call(f32[14,14,16,256]{3,2,1,0:T(8,128)} %bitcast.65, ...), custom_call_target="tpu_custom_call" | custom-call | tf_op jit(solution)/shard_map/middle/pallas_call | solution.py:672
  81.0 23.8 %out.1 = (bf16[4,49,16,1024]{3,2,1,0:T(8,128)(2,1)}, f32[4,49,16,1024]{3,2,1,0:T(8,128)}, f32[49,64,128]{2,1,0:T(8,128)}, f32[32,128]{1,0:T(8,128)}, f32[7,2,8,1...) custom-call(bf16[4,49,16,256]{3,2,1,0:T(8,128)(2,1)} %bitcast.68, ...), custom_call_target="tpu_custom_call" | custom-call | tf_op jit(solution)/shard_map/out/pallas_call | solution.py:391
  104.9 48.3 %back_out.1 = (bf16[5120,256]{1,0:T(8,128)(2,1)}, bf16[1024,256]{1,0:T(8,128)(2,1)}, bf16[4,49,16,1024]{3,2,1,0:T(8,128)(2,1)}, f32[4,49,16,256]{3,2,1,0:T(8,128...) custom-call(bf16[4,49,16,1024]{3,2,1,0:T(8,128)(2,1)} %bitcast.57, ...), custom_call_target="tpu_custom_call" | custom-call | tf_op jit(solution)/shard_map/back_out/pallas_call | solution.py:391
  153.2 52.9 %tail.1 = (bf16[3136,256]{1,0:T(8,128)(2,1)}, bf16[49,64,128]{2,1,0:T(8,128)(2,1)}, bf16[196,16,256]{2,1,0:T(8,128)(2,1)}, f32[96,256]{1,0:T(8,128)}, bf16[1280,...) custom-call(bf16[5120,256]{1,0:T(8,128)(2,1)} %get-tuple-element.108, ...), custom_call_target="tpu_custom_call" | custom-call | tf_op jit(solution)/shard_map/tail/pallas_call | solution.py:1473
  206.1 45.9 %final_sum.1 = (bf16[5120,256]{1,0:T(8,128)(2,1)}, bf16[5632,256]{1,0:T(8,128)(2,1)}, bf16[4,49,16,1024]{3,2,1,0:T(8,128)(2,1)}, bf16[4,49,64,128]{3,2,1,0:T(8,128)(2,1)}) custom-call(bf16[4,49,16,256]{3,2,1,0:T(8,128)(2,1)} %bitcast.78, bf16[4,49,16,1024]{3,2,1,0:T(8,128)(2,1)} %get-tuple-element.112.refs_1_, bf16[1280,256]{1,0:T(8,128)(2,1)} %refs_2_.1, ...), custom_call_target="tpu_custom_call" | custom-call | tf_op jit(solution)/shard_map/final_sum/pallas_call | solution.py:1586
  252.0 15.6 %unpack.1 = (f32[1280,1024]{1,0:T(8,128)}, f32[256,1024]{1,0:T(8,128)}, f32[2304,256]{1,0:T(8,128)}, f32[1280,256]{1,0:T(8,128)}, f32[640,256]{1,0:T(8,128)}, /*...) custom-call(bf16[5120,256]{1,0:T(8,128)(2,1)} %get-tuple-element.129, ...), custom_call_target="tpu_custom_call" | custom-call | tf_op jit(solution)/shard_map/unpack/pallas_call | solution.py:1683

commit v9 on v8

--- a/solution.py
+++ b/solution.py
@@ -1367,9 +1367,12 @@
     for i in range(2):
         x_load(i).start()
         taps_load(i).start()
-    exchange_run(ex7, [gb, c2], [q7], scr7, late)
-    near_two.start()
-    near.add_plane(0, far - 1, lambda m: line.line(m).start())
+    def pull():
+        near_two.start()
+        near.add_plane(0, far // 2, lambda m: line.line(m).start())
+
+    exchange_run(ex7, [gb, c2], [q7], scr7, late, between=pull)
+    near.add_plane(far // 2, far - 1, lambda m: line.line(m).start())
     near.add_plane(far - 1, far)
     waits(9, 10, 11, 12)
     scale7, p7, q7_row = rows(c2, 0, 1, 2), rows(q7, 0, 0, 2), rows(q7, 1, 0, 2)

time: 268 us -> 268 us (level)
  no operation moved by 1% of the time
where the time goes in v9:
time: 268 us; the launch traced here: 267 us
  Pallas kernels  265 us (99%)
    pallas_call x2, Pallas kernels, run_resident(): pl.pallas_call(body, out_shape=[jax.ShapeDtypeStruct(shape, dtype) for sh...  79 us
    pallas_call x2, Pallas kernels, call(): pl.pallas_call(body, grid=(STEPS,), in_specs=[pl.BlockSpec(b, m) for _, b...  72.2 us
    pallas_call x1, Pallas kernels, back_tail(): pl.pallas_call(functools.partial(k_tail, (st_a, st_b, ex7, ex8, side)), o...  52.5 us
    pallas_call x1, Pallas kernels, final_sum(): pl.pallas_call(functools.partial(final_kernel, (first, second, third, bot...  45.9 us
    pallas_call x1, Pallas kernels, unpack(): pl.pallas_call(functools.partial(k_unpack, pieces, cut), out_shape=[jax.S...  15.6 us

profile of v9, /device:TPU:0, one launch (start us, length us, event | category | flops | bytes accessed | tf_op | source)
XLA Modules:
  0.0 267.4 jit_solution(508360956037149421)
XLA Ops:
  0.6 0.8 fusion
  1.4 0.6 copy.32
  2.0 42.9 %front.1 = (f32[49,64,128]{2,1,0:T(8,128)}, f32[4,49,16,256]{3,2,1,0:T(8,128)}, bf16[4,49,16,640]{3,2,1,0:T(8,128)(2,1)}, bf16[4,49,16,256]{3,2,1,0:T(8,128)(2,1...) custom-call(bf16[4,49,64,128]{3,2,1,0:T(8,128)(2,1)} %bitcast.59, ...), custom_call_target="tpu_custom_call" | custom-call | tf_op jit(solution)/shard_map/front/pallas_call | solution.py:672
  44.9 36.1 %middle.1 = (bf16[16,16,16,256]{3,2,1,0:T(8,128)(2,1)}, f32[196,16,256]{2,1,0:T(8,128)}, bf16[49,64,128]{2,1,0:T(8,128)(2,1)}, bf16[196,16,256]{2,1,0:T(8,128)(2...) custom-call(f32[14,14,16,256]{3,2,1,0:T(8,128)} %bitcast.65, ...), custom_call_target="tpu_custom_call" | custom-call | tf_op jit(solution)/shard_map/middle/pallas_call | solution.py:672
  81.0 23.8 %out.1 = (bf16[4,49,16,1024]{3,2,1,0:T(8,128)(2,1)}, f32[4,49,16,1024]{3,2,1,0:T(8,128)}, f32[49,64,128]{2,1,0:T(8,128)}, f32[32,128]{1,0:T(8,128)}, f32[7,2,8,1...) custom-call(bf16[4,49,16,256]{3,2,1,0:T(8,128)(2,1)} %bitcast.68, ...), custom_call_target="tpu_custom_call" | custom-call | tf_op jit(solution)/shard_map/out/pallas_call | solution.py:391
  104.9 48.3 %back_out.1 = (bf16[5120,256]{1,0:T(8,128)(2,1)}, bf16[1024,256]{1,0:T(8,128)(2,1)}, bf16[4,49,16,1024]{3,2,1,0:T(8,128)(2,1)}, f32[4,49,16,256]{3,2,1,0:T(8,128...) custom-call(bf16[4,49,16,1024]{3,2,1,0:T(8,128)(2,1)} %bitcast.57, ...), custom_call_target="tpu_custom_call" | custom-call | tf_op jit(solution)/shard_map/back_out/pallas_call | solution.py:391
  153.2 52.5 %tail.1 = (bf16[3136,256]{1,0:T(8,128)(2,1)}, bf16[49,64,128]{2,1,0:T(8,128)(2,1)}, bf16[196,16,256]{2,1,0:T(8,128)(2,1)}, f32[96,256]{1,0:T(8,128)}, bf16[1280,...) custom-call(bf16[5120,256]{1,0:T(8,128)(2,1)} %get-tuple-element.108, ...), custom_call_target="tpu_custom_call" | custom-call | tf_op jit(solution)/shard_map/tail/pallas_call | solution.py:1476
  205.7 45.9 %final_sum.1 = (bf16[5120,256]{1,0:T(8,128)(2,1)}, bf16[5632,256]{1,0:T(8,128)(2,1)}, bf16[4,49,16,1024]{3,2,1,0:T(8,128)(2,1)}, bf16[4,49,64,128]{3,2,1,0:T(8,128)(2,1)}) custom-call(bf16[4,49,16,256]{3,2,1,0:T(8,128)(2,1)} %bitcast.78, bf16[4,49,16,1024]{3,2,1,0:T(8,128)(2,1)} %get-tuple-element.112.refs_1_, bf16[1280,256]{1,0:T(8,128)(2,1)} %refs_2_.1, ...), custom_call_target="tpu_custom_call" | custom-call | tf_op jit(solution)/shard_map/final_sum/pallas_call | solution.py:1589
  251.6 15.6 %unpack.1 = (f32[1280,1024]{1,0:T(8,128)}, f32[256,1024]{1,0:T(8,128)}, f32[2304,256]{1,0:T(8,128)}, f32[1280,256]{1,0:T(8,128)}, f32[640,256]{1,0:T(8,128)}, /*...) custom-call(bf16[5120,256]{1,0:T(8,128)(2,1)} %get-tuple-element.129, ...), custom_call_target="tpu_custom_call" | custom-call | tf_op jit(solution)/shard_map/unpack/pallas_call | solution.py:1686

commit v10 on v9

--- a/solution.py
+++ b/solution.py
@@ -745,7 +745,7 @@
             loads[k].wait()
         each(0, 2, begin)
 
-    exchange_run(exs[0], [gb], [c1, hp, hn], work[0], begin_some, between=lambda: each(2, 4, begin))
+    exchange_run(exs[0], [gb], [c1, hp, hn], work[0], begin_some, between=lambda: each(2, 5, begin))
 
     def store_sp(i):
         part = pl.ds(i * p_n, p_n)
@@ -758,8 +758,8 @@
                am, av, pm, pv, bm, bv, begun)
         store_sp(i).start()
 
-    each(0, 4, lambda i: join(i, True))
-    each(4, STEPS, join)
+    each(0, 5, lambda i: join(i, True))
+    each(5, STEPS, join)
     for k in (3, 4, 5, 7):
         copies[k].start()
     exchange_run(exs[1], [gb], [c2], work[1])

time: 268 us -> 270 us (level)
  no operation moved by 1% of the time
where the time goes in v10:
time: 270 us; the launch traced here: 269 us
  Pallas kernels  267 us (99%)
    pallas_call x2, Pallas kernels, run_resident(): pl.pallas_call(body, out_shape=[jax.ShapeDtypeStruct(shape, dtype) for sh...  78 us
    pallas_call x2, Pallas kernels, call(): pl.pallas_call(body, grid=(STEPS,), in_specs=[pl.BlockSpec(b, m) for _, b...  73.7 us
    pallas_call x1, Pallas kernels, back_tail(): pl.pallas_call(functools.partial(k_tail, (st_a, st_b, ex7, ex8, side)), o...  52.5 us
    pallas_call x1, Pallas kernels, final_sum(): pl.pallas_call(functools.partial(final_kernel, (first, second, third, bot...  47.2 us
    pallas_call x1, Pallas kernels, unpack(): pl.pallas_call(functools.partial(k_unpack, pieces, cut), out_shape=[jax.S...  15.6 us

profile of v10, /device:TPU:0, one launch (start us, length us, event | category | flops | bytes accessed | tf_op | source)
XLA Modules:
  0.0 269.2 jit_solution(9019520467622791754)
XLA Ops:
  0.6 0.8 fusion
  1.4 0.6 copy.32
  2.0 41.9 %front.1 = (f32[49,64,128]{2,1,0:T(8,128)}, f32[4,49,16,256]{3,2,1,0:T(8,128)}, bf16[4,49,16,640]{3,2,1,0:T(8,128)(2,1)}, bf16[4,49,16,256]{3,2,1,0:T(8,128)(2,1...) custom-call(bf16[4,49,64,128]{3,2,1,0:T(8,128)(2,1)} %bitcast.59, ...), custom_call_target="tpu_custom_call" | custom-call | tf_op jit(solution)/shard_map/front/pallas_call | solution.py:672
  43.9 36.1 %middle.1 = (bf16[16,16,16,256]{3,2,1,0:T(8,128)(2,1)}, f32[196,16,256]{2,1,0:T(8,128)}, bf16[49,64,128]{2,1,0:T(8,128)(2,1)}, bf16[196,16,256]{2,1,0:T(8,128)(2...) custom-call(f32[14,14,16,256]{3,2,1,0:T(8,128)} %bitcast.65, ...), custom_call_target="tpu_custom_call" | custom-call | tf_op jit(solution)/shard_map/middle/pallas_call | solution.py:672
  80.0 23.8 %out.1 = (bf16[4,49,16,1024]{3,2,1,0:T(8,128)(2,1)}, f32[4,49,16,1024]{3,2,1,0:T(8,128)}, f32[49,64,128]{2,1,0:T(8,128)}, f32[32,128]{1,0:T(8,128)}, f32[7,2,8,1...) custom-call(bf16[4,49,16,256]{3,2,1,0:T(8,128)(2,1)} %bitcast.68, ...), custom_call_target="tpu_custom_call" | custom-call | tf_op jit(solution)/shard_map/out/pallas_call | solution.py:391
  103.9 49.8 %back_out.1 = (bf16[5120,256]{1,0:T(8,128)(2,1)}, bf16[1024,256]{1,0:T(8,128)(2,1)}, bf16[4,49,16,1024]{3,2,1,0:T(8,128)(2,1)}, f32[4,49,16,256]{3,2,1,0:T(8,128...) custom-call(bf16[4,49,16,1024]{3,2,1,0:T(8,128)(2,1)} %bitcast.57, ...), custom_call_target="tpu_custom_call" | custom-call | tf_op jit(solution)/shard_map/back_out/pallas_call | solution.py:391
  153.7 52.5 %tail.1 = (bf16[3136,256]{1,0:T(8,128)(2,1)}, bf16[49,64,128]{2,1,0:T(8,128)(2,1)}, bf16[196,16,256]{2,1,0:T(8,128)(2,1)}, f32[96,256]{1,0:T(8,128)}, bf16[1280,...) custom-call(bf16[5120,256]{1,0:T(8,128)(2,1)} %get-tuple-element.108, ...), custom_call_target="tpu_custom_call" | custom-call | tf_op jit(solution)/shard_map/tail/pallas_call | solution.py:1476
  206.2 47.2 %final_sum.1 = (bf16[5120,256]{1,0:T(8,128)(2,1)}, bf16[5632,256]{1,0:T(8,128)(2,1)}, bf16[4,49,16,1024]{3,2,1,0:T(8,128)(2,1)}, bf16[4,49,64,128]{3,2,1,0:T(8,128)(2,1)}) custom-call(bf16[4,49,16,256]{3,2,1,0:T(8,128)(2,1)} %bitcast.78, bf16[4,49,16,1024]{3,2,1,0:T(8,128)(2,1)} %get-tuple-element.112.refs_1_, bf16[1280,256]{1,0:T(8,128)(2,1)} %refs_2_.1, ...), custom_call_target="tpu_custom_call" | custom-call | tf_op jit(solution)/shard_map/final_sum/pallas_call | solution.py:1589
  253.5 15.6 %unpack.1 = (f32[1280,1024]{1,0:T(8,128)}, f32[256,1024]{1,0:T(8,128)}, f32[2304,256]{1,0:T(8,128)}, f32[1280,256]{1,0:T(8,128)}, f32[640,256]{1,0:T(8,128)}, /*...) custom-call(bf16[5120,256]{1,0:T(8,128)(2,1)} %get-tuple-element.129, ...), custom_call_target="tpu_custom_call" | custom-call | tf_op jit(solution)/shard_map/unpack/pallas_call | solution.py:1686
